TPU v7x, 32 devices: a whole 2x2x4 slice. The times are simulated.
32 devices in a mesh: sample: 2 (over x), depth: 16 (over z, y, core).
Axes of the slice: x: 2, y: 2, z: 4, core: 2. Of those that a mesh axis runs over, the one named last changes fastest.
Arguments:
- volume: bfloat16 [2, 16, 32, 2048], P('sample', 'depth'), may hold values from -6 to 6
- conv1_weight: bfloat16 [27, 64, 64], replicated, may hold values from -0.15625 to 0.15625
- conv2_weight: bfloat16 [27, 1024, 1024], P(None, 'depth'), may hold values from -0.0390625 to 0.0390625
- cotangent: bfloat16 [2, 16, 8, 8, 1024], P('sample', 'depth'), may hold values from -6 to 6
Outputs:
- features_out: bfloat16 [2, 16, 8, 8, 1024], P('sample', 'depth')
- grad_volume: bfloat16 [2, 16, 32, 2048], P('sample', 'depth')
- grad_conv1: float32 [27, 64, 64], replicated
- grad_conv2: float32 [27, 1024, 1024], P(None, 'depth')
All inputs are finite; a program needn't handle non-finite values.
Results may differ from a plain program's by a relative error of at most 0.014.
Values may be sent and summed in bfloat16 or wider, within the bound.
No kernel may reach another device: no remote copies, remote signals or barrier semaphores. Data moves between devices by JAX's collectives and lax.ppermute only.
A program may use at most 256 MiB of HBM per device.

v0:
```python
import math

import jax
import jax.numpy as jnp
from jax import lax
from jax.experimental import pallas as pl
from jax.experimental.pallas import tpu as pltpu
from jax.sharding import PartitionSpec as P

C1 = 64
LAT = 32
BLOCK = 4
C2 = 1024
LS = 8
CELLS = LS * LS
GROUP = BLOCK * C1
WINDOW = GROUP + 2 * C1
TAPS = 27
PACK = 2 * C1

root_coef = 0.7978845608028654
cubic_coef = 0.044715

f32 = jnp.float32
bf16 = jnp.bfloat16


def params(mebibytes):
    return pltpu.CompilerParams(vmem_limit_bytes=mebibytes * 1024 * 1024)


def low_lanes(shape):
    return lax.broadcasted_iota(jnp.int32, shape, len(shape) - 1) < C1


def band_kernel(w_ref, out_ref):
    for lateral in range(9):
        for slot in range(BLOCK + 2):
            column = slot if slot <= BLOCK else -1
            for pair in range(BLOCK // 2):
                halves = []
                for own in (2 * pair, 2 * pair + 1):
                    c = column - own + 1
                    if 0 <= c <= 2:
                        halves.append(w_ref[3 * lateral + c])
                    else:
                        halves.append(jnp.zeros((C1, C1), bf16))
                start = lateral * WINDOW + slot * C1
                out_ref[start : start + C1, pair * PACK : (pair + 1) * PACK] = jnp.concatenate(halves, axis=1)


def banded(weight):
    return pl.pallas_call(
        band_kernel,
        out_shape=jax.ShapeDtypeStruct((9 * WINDOW, GROUP), bf16),
        compiler_params=params(16),
        cost_estimate=pl.CostEstimate(flops=0, bytes_accessed=4 << 20, transcendentals=0),
    )(weight)


def write_windows(lhs_ref, a, groups):
    field = jnp.concatenate(groups, axis=0)
    blank = jnp.zeros((LAT, PACK), f32)
    after = jnp.concatenate([g[:, :PACK] for g in groups[1:]] + [blank], axis=0)
    before = jnp.concatenate([blank] + [g[:, GROUP - PACK :] for g in groups[:-1]], axis=0)
    edge = jnp.where(low_lanes(after.shape), after, before)
    window = jnp.concatenate([field, edge], axis=1)
    rows = window.shape[0]
    row = lax.broadcasted_iota(jnp.int32, window.shape, 0) % LAT
    shifted = [
        jnp.where(row == 0, 0.0, pltpu.roll(window, 1, 0)),
        window,
        jnp.where(row == LAT - 1, 0.0, pltpu.roll(window, rows - 1, 0)),
    ]
    for b in range(3):
        start = (3 * a + b) * WINDOW
        lhs_ref[:, start : start + WINDOW] = shifted[b].astype(bf16)


def conv_one_kernel(before_ref, own_ref, after_ref, w_ref, moved_ref, slope_ref, lhs_ref, hid_ref):
    for a, ref in enumerate((before_ref, own_ref, after_ref)):
        write_windows(lhs_ref, a, [ref[:, g * GROUP : (g + 1) * GROUP].astype(f32) for g in range(LS)])
    pre = jnp.dot(lhs_ref[...], w_ref[...], preferred_element_type=f32)
    tanh_val = jnp.tanh(root_coef * (pre + cubic_coef * pre * pre * pre))
    hidden = 0.5 * pre * (1.0 + tanh_val)
    slope_ref[...] = 0.5 * (1.0 + tanh_val) + 0.5 * pre * (1.0 - tanh_val * tanh_val) * root_coef * (
        1.0 + 3.0 * cubic_coef * pre * pre
    )
    for u in range(BLOCK // 2):
        hid_ref[u] = hidden[:, u * PACK : (u + 1) * PACK]
    for r in range(BLOCK):
        for u in range(BLOCK // 2):
            cells = jnp.concatenate(
                [hid_ref[u, pl.ds(BLOCK * i + r, LS, stride=LAT), :] for i in range(LS)], axis=0
            )
            top, bottom = cells[: CELLS // 2], cells[CELLS // 2 :]
            low = low_lanes(top.shape)
            piece = r * BLOCK + 2 * u
            moved_ref[piece] = jnp.where(low, top, pltpu.roll(bottom, C1, 1)).astype(bf16)
            moved_ref[piece + 1] = jnp.where(low, pltpu.roll(top, C1, 1), bottom).astype(bf16)


def conv_one(before, own, after, band):
    rows = LS * LAT
    return pl.pallas_call(
        conv_one_kernel,
        out_shape=(
            jax.ShapeDtypeStruct((BLOCK * BLOCK, CELLS // 2, PACK), bf16),
            jax.ShapeDtypeStruct((rows, GROUP), f32),
            jax.ShapeDtypeStruct((rows, 9 * WINDOW), bf16),
        ),
        scratch_shapes=[pltpu.VMEM((BLOCK // 2, rows, PACK), f32)],
        compiler_params=params(24),
        cost_estimate=pl.CostEstimate(
            flops=2 * rows * 9 * WINDOW * GROUP, bytes_accessed=5 << 20, transcendentals=rows * GROUP
        ),
    )(before, own, after, band)


def shift_cells(field, step):
    if step == 0:
        return field
    column = lax.broadcasted_iota(jnp.int32, field.shape, 1)
    edge = LS - 1 if step > 0 else 0
    return jnp.where(column == edge, 0.0, pltpu.roll(field, (-step) % LS, 1))


def conv_two_kernel(planes, x_ref, w_ref, out_ref, lhs_ref, v_ref):
    @pl.when(pl.program_id(0) == 0)
    def _():
        def clear(p, carry):
            v_ref[:, :, p] = jnp.zeros((3, 2, LS + 2, LS, PACK), f32)
            return carry

        lax.fori_loop(0, planes + 2, clear, 0)

        def spread(p, carry):
            x = x_ref[p].astype(f32)
            turned = pltpu.roll(x, C1, 1)
            for half, parts in enumerate(((x, turned), (turned, x))):
                cells = jnp.concatenate(parts, axis=0).reshape(LS, LS, PACK)
                for c in range(3):
                    v_ref[c, half, p + 1, 1 : LS + 1] = shift_cells(cells, c - 1)
            return carry

        lax.fori_loop(0, planes, spread, 0)

        def gather(p, carry):
            rows = pl.ds(pl.multiple_of(p * CELLS, CELLS), CELLS)
            for m in range((TAPS + 1) // 2):
                t = 2 * m
                low = v_ref[t % 3, 0, p + t // 9, pl.ds((t // 3) % 3, LS)].reshape(CELLS, PACK)
                t = 2 * m + 1
                if t < TAPS:
                    high = v_ref[t % 3, 1, p + t // 9, pl.ds((t // 3) % 3, LS)].reshape(CELLS, PACK)
                    tile = jnp.where(low_lanes(low.shape), low, high)
                    lhs_ref[rows, m * PACK : (m + 1) * PACK] = tile.astype(bf16)
                else:
                    lhs_ref[rows, m * PACK : m * PACK + C1] = low[:, :C1].astype(bf16)
            return carry

        lax.fori_loop(0, planes, gather, 0)

    if w_ref is not None:
        chunk = 4 * CELLS
        for m in range(planes * CELLS // chunk):
            rows = slice(m * chunk, (m + 1) * chunk)
            out_ref[rows] = jnp.dot(lhs_ref[rows], w_ref[...], preferred_element_type=f32).astype(bf16)


def conv_two(pieces, weight):
    planes = pieces.shape[0]
    cells = planes * CELLS
    block = 256
    return pl.pallas_call(
        lambda *refs: conv_two_kernel(planes, *refs),
        grid=(C2 // block,),
        in_specs=[
            pl.BlockSpec(pieces.shape, lambda n: (0, 0, 0)),
            pl.BlockSpec((TAPS * C1, block), lambda n: (0, n)),
        ],
        out_specs=(
            pl.BlockSpec((cells, block), lambda n: (0, n)),
            pl.BlockSpec((cells, TAPS * C1), lambda n: (0, 0)),
        ),
        out_shape=(
            jax.ShapeDtypeStruct((cells, C2), bf16),
            jax.ShapeDtypeStruct((cells, TAPS * C1), bf16),
        ),
        scratch_shapes=[pltpu.VMEM((3, 2, planes + 2, LS + 2, LS, PACK), f32)],
        compiler_params=params(40),
        cost_estimate=pl.CostEstimate(
            flops=2 * cells * TAPS * C1 * C2, bytes_accessed=10 << 20, transcendentals=0
        ),
    )(pieces, weight)


def taps_of(pieces):
    planes = pieces.shape[0]
    cells = planes * CELLS
    return pl.pallas_call(
        lambda x_ref, lhs_ref, v_ref: conv_two_kernel(planes, x_ref, None, None, lhs_ref, v_ref),
        grid=(1,),
        in_specs=[pl.BlockSpec(pieces.shape, lambda n: (0, 0, 0))],
        out_specs=pl.BlockSpec((cells, TAPS * C1), lambda n: (0, 0)),
        out_shape=jax.ShapeDtypeStruct((cells, TAPS * C1), bf16),
        scratch_shapes=[pltpu.VMEM((3, 2, planes + 2, LS + 2, LS, PACK), f32)],
        compiler_params=params(24),
        cost_estimate=pl.CostEstimate(flops=0, bytes_accessed=8 << 20, transcendentals=0),
    )(pieces)


def back_two_kernel(planes, cot_ref, w_ref, out_ref, acc_ref):
    step = pl.program_id(0)

    @pl.when(step == 0)
    def _():
        def clear(p, carry):
            acc_ref[:, :, p] = jnp.zeros((3, 2, LS + 2, LS, PACK), f32)
            return carry

        lax.fori_loop(0, planes + 2, clear, 0)

    taps = w_ref.shape[0] // C1
    slab = 4
    for m in range(planes // slab):
        product = lax.dot_general(
            cot_ref[m * slab * CELLS : (m + 1) * slab * CELLS],
            w_ref[...],
            (((1,), (1,)), ((), ())),
            preferred_element_type=f32,
        )
        for u in range(taps):
            t = taps * step + u

            @pl.when(t < TAPS)
            def _():
                first = (u // 2) * PACK
                tile = product[:, first : first + PACK].reshape(slab, LS, LS, PACK)
                where = (t % 3, u % 2, pl.ds(m * slab + t // 9, slab), pl.ds((t // 3) % 3, LS))
                acc_ref[where] = acc_ref[where] + tile

    @pl.when(step == pl.num_programs(0) - 1)
    def _():
        def finish(p, carry):
            total = None
            for half in range(2):
                part = None
                for c in range(3):
                    term = shift_cells(acc_ref[c, half, p + 1, 1 : LS + 1], 1 - c)
                    part = term if part is None else part + term
                part = part.reshape(CELLS, PACK)
                total = part if half == 0 else total + pltpu.roll(part, C1, 1)
            top, bottom = total[: CELLS // 2], total[CELLS // 2 :]
            out_ref[p] = jnp.where(low_lanes(top.shape), top, pltpu.roll(bottom, C1, 1)).astype(bf16)
            return carry

        lax.fori_loop(0, planes, finish, 0)


def back_two(cot, weight):
    planes = cot.shape[0] // CELLS
    block = 256
    return pl.pallas_call(
        lambda *refs: back_two_kernel(planes, *refs),
        grid=(pl.cdiv(TAPS * C1, block),),
        in_specs=[
            pl.BlockSpec(cot.shape, lambda n: (0, 0)),
            pl.BlockSpec((block, C2), lambda n: (n, 0)),
        ],
        out_specs=pl.BlockSpec((planes, CELLS // 2, PACK), lambda n: (0, 0, 0)),
        out_shape=jax.ShapeDtypeStruct((planes, CELLS // 2, PACK), bf16),
        scratch_shapes=[pltpu.VMEM((3, 2, planes + 2, LS + 2, LS, PACK), f32)],
        compiler_params=params(32),
        cost_estimate=pl.CostEstimate(
            flops=2 * planes * CELLS * TAPS * C1 * C2, bytes_accessed=6 << 20, transcendentals=0
        ),
    )(cot, weight)


def weight_two_kernel(samples, scale, *refs):
    lhs_refs, cot_refs, out_ref = refs[:samples], refs[samples : 2 * samples], refs[2 * samples]
    total = None
    for lhs_ref, cot_ref in zip(lhs_refs, cot_refs):
        term = lax.dot_general(
            lhs_ref[...], cot_ref[...], (((0,), (0,)), ((), ())), preferred_element_type=f32
        )
        total = term if total is None else total + term
    out_ref[...] = total * scale


def weight_two(lhs, cots, scale):
    samples = len(lhs)
    cells = lhs[0].shape[0]
    block = 256
    return pl.pallas_call(
        lambda *refs: weight_two_kernel(samples, scale, *refs),
        grid=(pl.cdiv(TAPS * C1, block),),
        in_specs=[pl.BlockSpec((cells, block), lambda n: (0, n))] * samples
        + [pl.BlockSpec((cells, C2), lambda n: (0, 0))] * samples,
        out_specs=pl.BlockSpec((block, C2), lambda n: (n, 0)),
        out_shape=jax.ShapeDtypeStruct((TAPS * C1, C2), f32),
        compiler_params=params(56),
        cost_estimate=pl.CostEstimate(
            flops=2 * samples * cells * TAPS * C1 * C2, bytes_accessed=20 << 20, transcendentals=0
        ),
    )(*lhs, *cots)


def grad_pre_kernel(pieces_ref, slope_ref, lhs_ref, grad_ref, partial_ref, spread_ref, packed_ref):
    for r in range(BLOCK):
        for u in range(BLOCK // 2):
            piece = r * BLOCK + 2 * u
            first = pieces_ref[piece].astype(f32)
            second = pieces_ref[piece + 1].astype(f32)
            low = low_lanes(first.shape)
            top = jnp.where(low, first, pltpu.roll(second, C1, 1))
            bottom = jnp.where(low, pltpu.roll(first, C1, 1), second)
            for i in range(LS):
                source = top if i < LS // 2 else bottom
                start = (i % (LS // 2)) * LS
                spread_ref[u, pl.ds(BLOCK * i + r, LS, stride=LAT), :] = source[start : start + LS]
    grads = []
    for u in range(BLOCK // 2):
        lanes = slice(u * PACK, (u + 1) * PACK)
        value = (spread_ref[u] * slope_ref[:, lanes]).astype(bf16)
        grad_ref[:, lanes] = value
        grads.append(value)
    grad = jnp.concatenate(grads, axis=1)
    for lateral in range(9):
        window = lhs_ref[:, lateral * WINDOW : (lateral + 1) * WINDOW]
        product = lax.dot_general(window, grad, (((0,), (0,)), ((), ())), preferred_element_type=f32)
        for c in range(3):
            sums = []
            for parity in range(2):
                part = None
                for pair in range(BLOCK // 2):
                    column = 2 * pair + parity + c - 1
                    slot = column if column >= 0 else BLOCK + 1
                    term = product[slot * C1 : (slot + 1) * C1, pair * PACK : (pair + 1) * PACK]
                    part = term if part is None else part + term
                sums.append(part)
            total = sums[0] + pltpu.roll(sums[1], C1, 1)
            top, bottom = total[: C1 // 2], total[C1 // 2 :]
            t = 3 * lateral + c
            packed_ref[t * (C1 // 2) : (t + 1) * (C1 // 2)] = jnp.where(
                low_lanes(top.shape), top, pltpu.roll(bottom, C1, 1)
            )
    packed_ref[TAPS * (C1 // 2) :] = jnp.zeros(((32 - TAPS) * (C1 // 2), PACK), f32)
    for row in range(C1 // 2):
        entry = packed_ref[pl.ds(row, 32, stride=C1 // 2), :]
        partial_ref[row] = entry.astype(bf16)


def grad_pre_of(pieces, slope, lhs):
    rows = LS * LAT
    return pl.pallas_call(
        grad_pre_kernel,
        out_shape=(
            jax.ShapeDtypeStruct((rows, GROUP), bf16),
            jax.ShapeDtypeStruct((C1 // 2, 32, PACK), bf16),
        ),
        scratch_shapes=[
            pltpu.VMEM((BLOCK // 2, rows, PACK), f32),
            pltpu.VMEM((32 * (C1 // 2), PACK), f32),
        ],
        compiler_params=params(24),
        cost_estimate=pl.CostEstimate(
            flops=2 * rows * 9 * WINDOW * GROUP, bytes_accessed=3 << 20, transcendentals=0
        ),
    )(pieces, slope, lhs)


def back_one_kernel(before_ref, own_ref, after_ref, w_ref, out_ref, lhs_ref):
    for a, ref in enumerate((before_ref, own_ref, after_ref)):
        write_windows(lhs_ref, a, [ref[g * LAT : (g + 1) * LAT].astype(f32) for g in range(LS)])
    result = jnp.dot(lhs_ref[...], w_ref[...], preferred_element_type=f32)
    for g in range(LS):
        out_ref[:, g * GROUP : (g + 1) * GROUP] = result[g * LAT : (g + 1) * LAT].astype(bf16)


def back_one(before, own, after, band):
    rows = LS * LAT
    return pl.pallas_call(
        back_one_kernel,
        out_shape=jax.ShapeDtypeStruct((LAT, LAT * C1), bf16),
        scratch_shapes=[pltpu.VMEM((rows, 9 * WINDOW), bf16)],
        compiler_params=params(24),
        cost_estimate=pl.CostEstimate(
            flops=2 * rows * 9 * WINDOW * GROUP, bytes_accessed=3 << 20, transcendentals=0
        ),
    )(before, own, after, band)


def unpack_kernel(packed_ref, out_ref, wide_ref):
    wide_ref[...] = packed_ref[...].astype(f32).reshape(wide_ref.shape)
    for t in range(TAPS):
        entry = wide_ref[pl.ds(t, C1 // 2, stride=32), :]
        out_ref[t] = jnp.concatenate([entry[:, :C1], entry[:, C1:]], axis=0)


def unpack(packed):
    return pl.pallas_call(
        unpack_kernel,
        out_shape=jax.ShapeDtypeStruct((TAPS, C1, C1), f32),
        scratch_shapes=[pltpu.VMEM((32 * (C1 // 2), PACK), f32)],
        compiler_params=params(16),
        cost_estimate=pl.CostEstimate(flops=0, bytes_accessed=1 << 20, transcendentals=0),
    )(packed)


def neighbours(value, axis):
    count = lax.axis_size(axis)
    before = lax.ppermute(value, axis, [(i, i + 1) for i in range(count - 1)])
    after = lax.ppermute(value, axis, [(i + 1, i) for i in range(count - 1)])
    return before, after


def over_samples(value):
    count = lax.axis_size("sample")
    return [value] + [
        lax.ppermute(value, "sample", [(i, (i + shift) % count) for i in range(count)])
        for shift in range(1, count)
    ]


def on_device(volume, conv1_weight, conv2_weight, cotangent):
    samples = lax.axis_size("sample")
    shards = lax.axis_size("depth")
    flat_two = conv2_weight.reshape(TAPS * C1, C2)
    own = volume.reshape(LAT, LAT * C1)

    cots = lax.all_gather(cotangent.reshape(CELLS, C2), "depth", axis=0, tiled=True)
    before, after = neighbours(own, "depth")

    back_weight = jnp.swapaxes(conv1_weight[::-1], 1, 2)
    band = banded(conv1_weight)
    back_band = banded(back_weight)

    moved, slope, windows = conv_one(before, own, after, band)
    pieces = lax.all_to_all(moved, "depth", split_axis=0, concat_axis=0, tiled=True)

    partial, own_taps = conv_two(pieces, flat_two)
    features = lax.psum_scatter(partial, "depth", scatter_dimension=0, tiled=True)

    grad_pieces = back_two(cots, flat_two)
    grad_pieces = lax.all_to_all(grad_pieces, "depth", split_axis=0, concat_axis=0, tiled=True)
    grad_pre, partial_one = grad_pre_of(grad_pieces, slope, windows)
    grad_before, grad_after = neighbours(grad_pre, "depth")

    devices = samples * shards
    both = ("sample", "depth")
    scale_one = 1.0 / math.sqrt(samples * shards * LAT * LAT)
    shares = partial_one.reshape(devices, -1, PACK)
    shares = lax.all_to_all(shares, both, split_axis=0, concat_axis=0, tiled=True)
    summed = (jnp.sum(shares.astype(f32), axis=0) * scale_one).astype(bf16)
    summed = jnp.broadcast_to(summed[None], shares.shape)
    summed = lax.all_to_all(summed, both, split_axis=0, concat_axis=0, tiled=True)
    grad_conv1 = unpack(summed.reshape(C1 // 2, 32, PACK))

    grad_volume = back_one(grad_before, grad_pre, grad_after, back_band)

    scale_two = 1.0 / math.sqrt(samples * shards * CELLS)
    all_taps = [own_taps] + [taps_of(value) for value in over_samples(pieces)[1:]]
    grad_conv2 = weight_two(all_taps, over_samples(cots), scale_two)

    return (
        features.reshape(cotangent.shape),
        grad_volume.reshape(volume.shape),
        grad_conv1,
        grad_conv2.reshape(conv2_weight.shape),
    )


def solution(mesh):
    return jax.shard_map(
        on_device,
        mesh=mesh,
        in_specs=(
            P("sample", "depth", None, None),
            P(),
            P(None, "depth", None),
            P("sample", "depth", None, None, None),
        ),
        out_specs=(
            P("sample", "depth", None, None, None),
            P("sample", "depth", None, None),
            P(),
            P(None, "depth", None),
        ),
        check_vma=False,
    )
```

profile of v0, /device:TPU:0, one launch (start us, length us, event | category | flops | bytes accessed | tf_op | source)
XLA Modules:
  0.0 146.3 jit_solution(5295235828702454674)
XLA Ops:
  8.0 2.4 %collective-permute-start = (bf16[32,2048]{1,0:T(8,128)(2,1)}, bf16[32,2048]{1,0:T(8,128)(2,1)S(1)}, u32[]{:S(2)}, u32[]{:S(2)}) collective-permute-start(bf16[32,2048]{1,0:T(8,128)(2,1)} %bitcast.8), channel_id=1, source_target_pairs={{0,1},{1,2},{2,3},{3,4},{4,5},{5,6},{6,7},{7,8},{8,9},{9,10},{10,1... | collective-permute-start | bytes 393224 | tf_op jit(solution)/shard_map/ppermute | solution.py:414
  10.3 1.3 collective-permute-start.1
  13.0 2.9 %collective-permute-done.1.after_ref = bf16[32,2048]{1,0:T(8,128)(2,1)S(1)} collective-permute-done((bf16[32,2048]{1,0:T(8,128)(2,1)}, bf16[32,2048]{1,0:T(8,128)(2,1)S(1)}, u32[]{:S(2)}, u32[]{:S(2)}) %collective-permute-start.1) | collective-permute-done | bytes 131104 | tf_op jit(solution)/shard_map/ppermute | solution.py:415
  17.0 17.6 %all_to_all.20.refs_0_ = bf16[16,32,128]{2,1,0:T(8,128)(2,1)S(1)} all-to-all(bf16[16,32,128]{2,1,0:T(8,128)(2,1)S(1)} %get-tuple-element.11), channel_id=1, replica_groups=mesh['sample'=2,'depth'=16] {'depth'}, dimensions={0} | all-to-all | bytes 262144 | tf_op jit(solution)/shard_map/all_to_all | solution.py:441
  34.6 8.1 %shard_map.77 = (bf16[1024,1024]{1,0:T(8,128)(2,1)}, bf16[1024,1728]{1,0:T(8,128)(2,1)S(1)}) custom-call(bf16[16,32,128]{2,1,0:T(8,128)(2,1)S(1)} %all_to_all.20.refs_0_, bf16[1728,1024]{1,0:T(8,128)(2,1)S(1)} %bitcast.11), custom_call_target="tpu_custom_call" | custom-call | flops 3623878656 | bytes 10485760 | tf_op jit(solution)/shard_map/pallas_call | solution.py:175
  42.7 1.8 %copy-done.7 = bf16[1024,1728]{1,0:T(8,128)(2,1)} copy-done((bf16[1024,1728]{1,0:T(8,128)(2,1)}, bf16[1024,1728]{1,0:T(8,128)(2,1)S(1)}, u32[]{:S(2)}) %copy-start.7) | copy-done | bytes 3538968
  44.5 11.2 %all-gather.2.cloned.1.call-done.refs_0_.refs_2_ = bf16[1024,1024]{1,0:T(8,128)(2,1)} async-done(((bf16[64,1024]{1,0:T(8,128)(2,1)}), bf16[1024,1024]{1,0:T(8,128)(2,1)}) %all-gather.2.cloned.1.call-update) | async-done | bytes 2097168 | tf_op jit(solution)/shard_map/all_gather | solution.py:433
  55.6 1.4 collective-permute-start.5
  57.1 2.0 %copy-done.5 = bf16[27,64,1024]{2,1,0:T(8,128)(2,1)S(1)} copy-done((bf16[27,64,1024]{2,1,0:T(8,128)(2,1)S(1)}, bf16[27,64,1024]{2,1,0:T(8,128)(2,1)}, u32[]{:S(2)}) %copy-start.5) | copy-done | bytes 3538968
  59.1 1.6 %copy-done.6 = bf16[1024,1024]{1,0:T(8,128)(2,1)S(1)} copy-done((bf16[1024,1024]{1,0:T(8,128)(2,1)S(1)}, bf16[1024,1024]{1,0:T(8,128)(2,1)}, u32[]{:S(2)}) %copy-start.6) | copy-done | bytes 2097176
  60.7 18.5 %shard_map.78 = bf16[16,32,128]{2,1,0:T(8,128)(2,1)S(1)} custom-call(bf16[1024,1024]{1,0:T(8,128)(2,1)S(1)} %copy-done.6, bf16[1728,1024]{1,0:T(8,128)(2,1)S(1)} %bitcast.12), custom_call_target="tpu_custom_call" | custom-call | flops 3623878656 | bytes 6291456 | tf_op jit(solution)/shard_map/pallas_call | solution.py:264
  79.2 11.4 %all_to_all.21.pieces_ref = bf16[16,32,128]{2,1,0:T(8,128)(2,1)S(1)} all-to-all(bf16[16,32,128]{2,1,0:T(8,128)(2,1)S(1)} %shard_map.78), channel_id=1, replica_groups=mesh['sample'=2,'depth'=16] {'depth'}, dimensions={0} | all-to-all | bytes 262144 | tf_op jit(solution)/shard_map/all_to_all | solution.py:447
  90.5 2.7 %shard_map.79 = (bf16[256,256]{1,0:T(8,128)(2,1)S(1)}, bf16[32,32,128]{2,1,0:T(8,128)(2,1)S(1)}) custom-call(bf16[16,32,128]{2,1,0:T(8,128)(2,1)S(1)} %all_to_all.21.pieces_ref, f32[256,256]{1,0:T(8,128)S(1)} %get-tuple-element.13.slope_ref, bf16[256,3456]{1,0:T(8,128)(2,1)S(1)} %get-tuple-element.14.lhs_ref), custom_call_target="tpu_custom_call" | custom-call | flops 452984832 | bytes 3145728 | tf_op jit(solution)/shard_map/pallas_call | solution.py:357
  93.2 15.0 %all_to_all.22 = bf16[32,32,128]{2,1,0:T(8,128)(2,1)S(1)} all-to-all(bf16[32,32,128]{2,1,0:T(8,128)(2,1)S(1)} %get-tuple-element.16), channel_id=1, replica_groups=mesh['sample'=2,'depth'=16] {'sample','depth'}, dimensions={0} | all-to-all | bytes 524288 | tf_op jit(solution)/shard_map/all_to_all | solution.py:455
  109.0 2.6 %all-to-all-start.3 = ((bf16[32,32,128]{2,1,0:T(8,128)(2,1)}), bf16[32,32,128]{2,1,0:T(8,128)(2,1)S(1)}, u32[]{:S(2)}, u32[]{:S(2)}) async-start(bf16[32,32,128]{2,1,0:T(8,128)(2,1)} %broadcast_in_dim.2), calls=%async_computation.4 | async-start | bytes 524288 | tf_op jit(solution)/shard_map/all_to_all | solution.py:458
  111.6 1.7 %collective-permute-start.4 = (bf16[16,32,128]{2,1,0:T(8,128)(2,1)S(1)}, bf16[16,32,128]{2,1,0:T(8,128)(2,1)S(1)}, u32[]{:S(2)}, u32[]{:S(2)}) collective-permute-start(bf16[16,32,128]{2,1,0:T(8,128)(2,1)S(1)} %all_to_all.20.refs_0_), channel_id=1, source_target_pairs={{0,16},{16,0},{1,17},{17,1},{2,18},{18,2},{3,19},{19,3},{4,20},{20... | collective-permute-start | bytes 393224 | tf_op jit(solution)/shard_map/ppermute | solution.py:422
  113.3 1.8 %collective-permute-start.2 = (bf16[256,256]{1,0:T(8,128)(2,1)S(1)}, bf16[256,256]{1,0:T(8,128)(2,1)S(1)}, u32[]{:S(2)}, u32[]{:S(2)}) collective-permute-start(bf16[256,256]{1,0:T(8,128)(2,1)S(1)} %get-tuple-element.15.own_ref), channel_id=1, source_target_pairs={{0,1},{1,2},{2,3},{3,4},{4,5},{5,6},{6,7},{7,8},{8,9},{9,10},{10,1... | collective-permute-start | bytes 393224 | tf_op jit(solution)/shard_map/ppermute | solution.py:414
  115.1 1.3 collective-permute-start.3
  117.1 2.0 %collective-permute-done.4.x_ref = bf16[16,32,128]{2,1,0:T(8,128)(2,1)S(1)} collective-permute-done((bf16[16,32,128]{2,1,0:T(8,128)(2,1)S(1)}, bf16[16,32,128]{2,1,0:T(8,128)(2,1)S(1)}, u32[]{:S(2)}, u32[]{:S(2)}) %collective-permute-start.4) | collective-permute-done | bytes 131104 | tf_op jit(solution)/shard_map/ppermute | solution.py:422
  119.1 2.2 %shard_map.83.refs_1_ = bf16[1024,1728]{1,0:T(8,128)(2,1)S(1)} custom-call(bf16[16,32,128]{2,1,0:T(8,128)(2,1)S(1)} %collective-permute-done.4.x_ref), custom_call_target="tpu_custom_call" | custom-call | bytes 8388608 | tf_op jit(solution)/shard_map/pallas_call | solution.py:201
  121.4 1.8 %copy-done = bf16[1024,1728]{1,0:T(8,128)(2,1)} copy-done((bf16[1024,1728]{1,0:T(8,128)(2,1)}, bf16[1024,1728]{1,0:T(8,128)(2,1)S(1)}, u32[]{:S(2)}) %copy-start) | copy-done | bytes 3538968
  123.2 1.4 shard_map.81
  124.7 1.3 shard_map.82
  126.0 13.5 %shard_map.84 = f32[1728,1024]{1,0:T(8,128)} custom-call(bf16[1024,1728]{1,0:T(8,128)(2,1)} %copy-done.7, bf16[1024,1728]{1,0:T(8,128)(2,1)} %copy-done, bf16[1024,1024]{1,0:T(8,128)(2,1)} %all-gather.2.cloned.1.call-done.refs_0_.refs_2_, bf16[1024,1024]{1,0:T(8,128)(2,1)} %collective-permute-done.5.refs_3_), custom_call_target="tpu_custom_call" | custom-call | flops 7247757312 | bytes 20971520 | tf_op jit(solution)/shard_map/pallas_call | solution.py:296
  (30 shorter events, 4.8 us)
Async XLA Ops:
  7.2 8.7 %copy-start.3 = (bf16[1,1,32,2048]{3,2,1,0:T(8,128)(2,1)S(1)}, bf16[1,1,32,2048]{3,2,1,0:T(8,128)(2,1)}, u32[]{:S(2)}) copy-start(bf16[1,1,32,2048]{3,2,1,0:T(8,128)(2,1)} %param.4) | copy-start | bytes 393220
  7.2 48.5 %all-gather.2.cloned.1.call-start = ((), (), s32[]{:S(2)}) async-start(), calls=%async_computation.6 | async-start | bytes 2228224 | tf_op jit(solution)/shard_map/all_gather | solution.py:433
  7.9 131.6 %reduce-scatter.2.cloned.1.call-start = ((), (), s32[]{:S(2)}) async-start(), calls=%async_computation.5 | async-start | bytes 2228224 | tf_op jit(solution)/shard_map/reduce_scatter | solution.py:444
  8.0 5.1 %collective-permute-start = (bf16[32,2048]{1,0:T(8,128)(2,1)}, bf16[32,2048]{1,0:T(8,128)(2,1)S(1)}, u32[]{:S(2)}, u32[]{:S(2)}) collective-permute-start(bf16[32,2048]{1,0:T(8,128)(2,1)} %bitcast.8), channel_id=1, source_target_pairs={{0,1},{1,2},{2,3},{3,4},{4,5},{5,6},{6,7},{7,8},{8,9},{9,10},{10,1... | collective-permute-start | bytes 393224 | tf_op jit(solution)/shard_map/ppermute | solution.py:414
  10.3 5.6 %collective-permute-start.1 = (bf16[32,2048]{1,0:T(8,128)(2,1)}, bf16[32,2048]{1,0:T(8,128)(2,1)S(1)}, u32[]{:S(2)}, u32[]{:S(2)}) collective-permute-start(bf16[32,2048]{1,0:T(8,128)(2,1)} %bitcast.9), channel_id=1, source_target_pairs={{1,0},{2,1},{3,2},{4,3},{5,4},{6,5},{7,6},{8,7},{9,8},{10,9},{11,1... | collective-permute-start | bytes 393224 | tf_op jit(solution)/shard_map/ppermute | solution.py:415
  11.6 1.0 copy-start.1
  12.6 22.0 %copy-start.4 = (bf16[27,64,1024]{2,1,0:T(8,128)(2,1)S(1)}, bf16[27,64,1024]{2,1,0:T(8,128)(2,1)}, u32[]{:S(2)}) copy-start(bf16[27,64,1024]{2,1,0:T(8,128)(2,1)} %param.6) | copy-start | bytes 10616836
  42.7 1.8 %copy-start.7 = (bf16[1024,1728]{1,0:T(8,128)(2,1)}, bf16[1024,1728]{1,0:T(8,128)(2,1)S(1)}, u32[]{:S(2)}) copy-start(bf16[1024,1728]{1,0:T(8,128)(2,1)S(1)} %get-tuple-element.17.refs_0_) | copy-start | bytes 10616836
  55.6 70.4 %collective-permute-start.5 = (bf16[1024,1024]{1,0:T(8,128)(2,1)}, bf16[1024,1024]{1,0:T(8,128)(2,1)}, u32[]{:S(2)}, u32[]{:S(2)}) collective-permute-start(bf16[1024,1024]{1,0:T(8,128)(2,1)} %all-gather.2.cloned.1.call-done.refs_0_.refs_2_), channel_id=1, source_target_pairs={{0,16},{16,0},{1,17},{17,1},{2,18},{18,2},{3,19},{19,3},{4,20},{20... | collective-permute-start | bytes 6291464 | tf_op jit(solution)/shard_map/ppermute | solution.py:422
  57.1 2.0 %copy-start.5 = (bf16[27,64,1024]{2,1,0:T(8,128)(2,1)S(1)}, bf16[27,64,1024]{2,1,0:T(8,128)(2,1)}, u32[]{:S(2)}) copy-start(bf16[27,64,1024]{2,1,0:T(8,128)(2,1)} %param.6) | copy-start | bytes 10616836
  59.1 1.6 %copy-start.6 = (bf16[1024,1024]{1,0:T(8,128)(2,1)S(1)}, bf16[1024,1024]{1,0:T(8,128)(2,1)}, u32[]{:S(2)}) copy-start(bf16[1024,1024]{1,0:T(8,128)(2,1)} %all-gather.2.cloned.1.call-done.refs_0_.refs_2_) | copy-start | bytes 6291460
  79.2 37.3 %copy-start.2 = (bf16[27,64,64]{2,1,0:T(8,128)(2,1)S(1)}, bf16[27,64,64]{2,1,0:T(8,128)(2,1)}, u32[]{:S(2)}) copy-start(bf16[27,64,64]{2,1,0:T(8,128)(2,1)} %w_ref.1) | copy-start | bytes 663556
  109.0 15.7 %all-to-all-start.3 = ((bf16[32,32,128]{2,1,0:T(8,128)(2,1)}), bf16[32,32,128]{2,1,0:T(8,128)(2,1)S(1)}, u32[]{:S(2)}, u32[]{:S(2)}) async-start(bf16[32,32,128]{2,1,0:T(8,128)(2,1)} %broadcast_in_dim.2), calls=%async_computation.4 | async-start | bytes 524288 | tf_op jit(solution)/shard_map/all_to_all | solution.py:458
  111.6 7.5 %collective-permute-start.4 = (bf16[16,32,128]{2,1,0:T(8,128)(2,1)S(1)}, bf16[16,32,128]{2,1,0:T(8,128)(2,1)S(1)}, u32[]{:S(2)}, u32[]{:S(2)}) collective-permute-start(bf16[16,32,128]{2,1,0:T(8,128)(2,1)S(1)} %all_to_all.20.refs_0_), channel_id=1, source_target_pairs={{0,16},{16,0},{1,17},{17,1},{2,18},{18,2},{3,19},{19,3},{4,20},{20... | collective-permute-start | bytes 393224 | tf_op jit(solution)/shard_map/ppermute | solution.py:422
  113.3 9.9 %collective-permute-start.2 = (bf16[256,256]{1,0:T(8,128)(2,1)S(1)}, bf16[256,256]{1,0:T(8,128)(2,1)S(1)}, u32[]{:S(2)}, u32[]{:S(2)}) collective-permute-start(bf16[256,256]{1,0:T(8,128)(2,1)S(1)} %get-tuple-element.15.own_ref), channel_id=1, source_target_pairs={{0,1},{1,2},{2,3},{3,4},{4,5},{5,6},{6,7},{7,8},{8,9},{9,10},{10,1... | collective-permute-start | bytes 393224 | tf_op jit(solution)/shard_map/ppermute | solution.py:414
  115.1 8.1 %collective-permute-start.3 = (bf16[256,256]{1,0:T(8,128)(2,1)S(1)}, bf16[256,256]{1,0:T(8,128)(2,1)S(1)}, u32[]{:S(2)}, u32[]{:S(2)}) collective-permute-start(bf16[256,256]{1,0:T(8,128)(2,1)S(1)} %get-tuple-element.15.own_ref), channel_id=1, source_target_pairs={{1,0},{2,1},{3,2},{4,3},{5,4},{6,5},{7,6},{8,7},{9,8},{10,9},{11,1... | collective-permute-start | bytes 393224 | tf_op jit(solution)/shard_map/ppermute | solution.py:415
  121.4 1.8 %copy-start = (bf16[1024,1728]{1,0:T(8,128)(2,1)}, bf16[1024,1728]{1,0:T(8,128)(2,1)S(1)}, u32[]{:S(2)}) copy-start(bf16[1024,1728]{1,0:T(8,128)(2,1)S(1)} %shard_map.83.refs_1_) | copy-start | bytes 10616836
Sparse Core Ops, SparseCore 0:
  10.2 45.4 all-gather.1
  60.0 64.9 reduce-scatter.1
where the time goes:
time: 147 us; the launch traced here: 146 us
  Pallas kernels  49.4 us (34%)
  blocking collectives  44 us (30%)
  waiting for transfers between devices  16.9 us (11%)
  between operations  14.2 us (10%)
  starting transfers between devices  12.5 us (9%)
  local copies, waits for them, and re-layouts  9.24 us (6%)
    pallas_call x1, Pallas kernels, back_two(): pl.pallas_call(lambda *refs: back_two_kernel(planes, *refs), grid=(pl.cdi...  18.5 us
    all_to_all x1, blocking collectives, on_device(): lax.all_to_all(moved, 'depth', split_axis=0, concat_axis=0, tiled=True)  17.6 us
    all_to_all x1, blocking collectives, on_device(): lax.all_to_all(shares, both, split_axis=0, concat_axis=0, tiled=True)  15 us
    pallas_call x1, Pallas kernels, weight_two(): pl.pallas_call(lambda *refs: weight_two_kernel(samples, scale, *refs), gr...  13.5 us
    all_to_all x1, blocking collectives, on_device(): lax.all_to_all(grad_pieces, 'depth', split_axis=0, concat_axis=0, tiled=T...  11.4 us
    all_gather x1, waiting for transfers between devices, on_device(): lax.all_gather(cotangent.reshape(CELLS, C2), 'depth', axis=0, tiled=True)  11.2 us
    unnamed x17, local copies, waits for them, and re-layouts  8.47 us
    pallas_call x1, Pallas kernels, conv_two(): pl.pallas_call(lambda *refs: conv_two_kernel(planes, *refs), grid=(C2 //...  8.05 us
  transfers between devices with their start and end apart: 9, of which 4 were waited for; matrix products, arithmetic and copies ran while one was open for 1% of the time, Pallas kernels for 34%

commit v1 on v0

--- a/solution.py
+++ b/solution.py
@@ -125,28 +125,68 @@
     return jnp.where(column == edge, 0.0, pltpu.roll(field, (-step) % LS, 1))
 
 
-def conv_two_kernel(planes, x_ref, w_ref, out_ref, lhs_ref, v_ref):
+def turn_kernel(x_ref, out_ref):
+    out_ref[...] = x_ref[...].T
+
+
+def turned(value, block):
+    rows, columns = value.shape
+    return pl.pallas_call(
+        turn_kernel,
+        grid=(columns // block,),
+        in_specs=[pl.BlockSpec((rows, block), lambda n: (0, n))],
+        out_specs=pl.BlockSpec((block, rows), lambda n: (n, 0)),
+        out_shape=jax.ShapeDtypeStruct((columns, rows), value.dtype),
+        compiler_params=params(12),
+        cost_estimate=pl.CostEstimate(flops=0, bytes_accessed=8 * rows * columns, transcendentals=0),
+    )(value)
+
+
+def turn_weight_kernel(rows, x_ref, out_ref):
+    block = x_ref.shape[0]
+    row = lax.broadcasted_iota(jnp.int32, x_ref.shape, 0) + block * pl.program_id(0)
+    out_ref[...] = jnp.where(row < rows, x_ref[...].astype(f32), 0.0).astype(bf16).T
+
+
+def turned_weight(weight, block=256):
+    rows, columns = weight.shape
+    steps = pl.cdiv(rows, block)
+    return pl.pallas_call(
+        lambda *refs: turn_weight_kernel(rows, *refs),
+        grid=(steps,),
+        in_specs=[pl.BlockSpec((block, columns), lambda n: (n, 0))],
+        out_specs=pl.BlockSpec((columns, block), lambda n: (0, n)),
+        out_shape=jax.ShapeDtypeStruct((columns, steps * block), weight.dtype),
+        compiler_params=params(12),
+        cost_estimate=pl.CostEstimate(flops=0, bytes_accessed=16 << 20, transcendentals=0),
+    )(weight)
+
+
+def conv_send_kernel(planes, parity_ref, x_ref, w_ref, out_ref, lhs_ref, v_ref):
+    half_planes = planes // 2
+
     @pl.when(pl.program_id(0) == 0)
     def _():
-        def clear(p, carry):
-            v_ref[:, :, p] = jnp.zeros((3, 2, LS + 2, LS, PACK), f32)
-            return carry
-
-        lax.fori_loop(0, planes + 2, clear, 0)
+        v_ref[:, :, 0] = jnp.zeros((3, 2, LS + 2, LS, PACK), f32)
+        v_ref[:, :, planes + 1] = jnp.zeros((3, 2, LS + 2, LS, PACK), f32)
+        edge = jnp.zeros((LS, PACK), f32)
 
         def spread(p, carry):
             x = x_ref[p].astype(f32)
-            turned = pltpu.roll(x, C1, 1)
-            for half, parts in enumerate(((x, turned), (turned, x))):
+            turn = pltpu.roll(x, C1, 1)
+            for half, parts in enumerate(((x, turn), (turn, x))):
                 cells = jnp.concatenate(parts, axis=0).reshape(LS, LS, PACK)
                 for c in range(3):
+                    v_ref[c, half, p + 1, 0] = edge
                     v_ref[c, half, p + 1, 1 : LS + 1] = shift_cells(cells, c - 1)
+                    v_ref[c, half, p + 1, LS + 1] = edge
             return carry
 
         lax.fori_loop(0, planes, spread, 0)
 
         def gather(p, carry):
-            rows = pl.ds(pl.multiple_of(p * CELLS, CELLS), CELLS)
+            group = jnp.where(p % 2 == parity_ref[0], 0, half_planes)
+            rows = pl.ds(pl.multiple_of((group + p // 2) * CELLS, CELLS), CELLS)
             for m in range((TAPS + 1) // 2):
                 t = 2 * m
                 low = v_ref[t % 3, 0, p + t // 9, pl.ds((t // 3) % 3, LS)].reshape(CELLS, PACK)
@@ -161,56 +201,109 @@
 
         lax.fori_loop(0, planes, gather, 0)
 
-    if w_ref is not None:
-        chunk = 4 * CELLS
-        for m in range(planes * CELLS // chunk):
-            rows = slice(m * chunk, (m + 1) * chunk)
-            out_ref[rows] = jnp.dot(lhs_ref[rows], w_ref[...], preferred_element_type=f32).astype(bf16)
-
-
-def conv_two(pieces, weight):
+    first = half_planes * CELLS
+    out_ref[...] = jnp.dot(lhs_ref[first:], w_ref[...], preferred_element_type=f32).astype(bf16)
+
+
+def conv_send(parity, pieces, weight):
     planes = pieces.shape[0]
     cells = planes * CELLS
     block = 256
     return pl.pallas_call(
-        lambda *refs: conv_two_kernel(planes, *refs),
+        lambda *refs: conv_send_kernel(planes, *refs),
+        grid_spec=pltpu.PrefetchScalarGridSpec(
+            num_scalar_prefetch=1,
+            grid=(C2 // block,),
+            in_specs=[
+                pl.BlockSpec(pieces.shape, lambda n, s: (0, 0, 0)),
+                pl.BlockSpec((TAPS * C1, block), lambda n, s: (0, n)),
+            ],
+            out_specs=(
+                pl.BlockSpec((cells // 2, block), lambda n, s: (0, n)),
+                pl.BlockSpec((cells, TAPS * C1), lambda n, s: (0, 0)),
+            ),
+            scratch_shapes=[pltpu.VMEM((3, 2, planes + 2, LS + 2, LS, PACK), f32)],
+        ),
+        out_shape=(
+            jax.ShapeDtypeStruct((cells // 2, C2), bf16),
+            jax.ShapeDtypeStruct((cells, TAPS * C1), bf16),
+        ),
+        compiler_params=params(24),
+        cost_estimate=pl.CostEstimate(
+            flops=2 * cells * TAPS * C1 * C2, bytes_accessed=10 << 20, transcendentals=0
+        ),
+    )(parity, pieces, weight)
+
+
+def conv_keep_kernel(lhs_ref, w_ref, more_ref, out_ref):
+    product = jnp.dot(lhs_ref[...], w_ref[...], preferred_element_type=f32)
+    out_ref[...] = (product + more_ref[...].astype(f32)).astype(bf16)
+
+
+def conv_keep(lhs, weight, more):
+    cells = more.shape[0]
+    block = 256
+    return pl.pallas_call(
+        conv_keep_kernel,
         grid=(C2 // block,),
         in_specs=[
-            pl.BlockSpec(pieces.shape, lambda n: (0, 0, 0)),
+            pl.BlockSpec((cells, TAPS * C1), lambda n: (0, 0)),
             pl.BlockSpec((TAPS * C1, block), lambda n: (0, n)),
+            pl.BlockSpec((cells, block), lambda n: (0, n)),
         ],
-        out_specs=(
-            pl.BlockSpec((cells, block), lambda n: (0, n)),
-            pl.BlockSpec((cells, TAPS * C1), lambda n: (0, 0)),
-        ),
-        out_shape=(
-            jax.ShapeDtypeStruct((cells, C2), bf16),
-            jax.ShapeDtypeStruct((cells, TAPS * C1), bf16),
-        ),
-        scratch_shapes=[pltpu.VMEM((3, 2, planes + 2, LS + 2, LS, PACK), f32)],
-        compiler_params=params(40),
+        out_specs=pl.BlockSpec((cells, block), lambda n: (0, n)),
+        out_shape=jax.ShapeDtypeStruct((cells, C2), bf16),
+        compiler_params=params(16),
         cost_estimate=pl.CostEstimate(
-            flops=2 * cells * TAPS * C1 * C2, bytes_accessed=10 << 20, transcendentals=0
-        ),
-    )(pieces, weight)
+            flops=2 * cells * TAPS * C1 * C2, bytes_accessed=8 << 20, transcendentals=0
+        ),
+    )(lhs, weight, more)
+
+
+def taps_kernel(planes, x_ref, out_ref, flat_ref):
+    half_cells = planes // 2 * CELLS
+
+    def cells_of(p):
+        x = x_ref[p].astype(f32)
+        return jnp.concatenate([x, pltpu.roll(x, C1, 1)], axis=0)
+
+    for s in range(2):
+        for j in range(planes // 4):
+            pair = jnp.concatenate([cells_of(4 * j + s), cells_of(4 * j + 2 + s)], axis=0)
+            flat_ref[s, :, j * PACK : (j + 1) * PACK] = pair.T[:C1]
+
+    lane = lax.broadcasted_iota(jnp.int32, (C1, half_cells), 1)
+    row, column = (lane // LS) % LS, lane % LS
+    for b in range(3):
+        for c in range(3):
+            inside = (row + b >= 1) & (row + b <= LS) & (column + c >= 1) & (column + c <= LS)
+            step = LS * (b - 1) + c - 1
+            even, odd = (
+                jnp.where(inside, pltpu.roll(flat_ref[s], (-step) % half_cells, 1), 0.0) for s in range(2)
+            )
+            odd_before = jnp.where(lane < CELLS, 0.0, pltpu.roll(odd, CELLS, 1))
+            even_after = jnp.where(
+                lane >= half_cells - CELLS, 0.0, pltpu.roll(even, half_cells - CELLS, 1)
+            )
+            for s, sources in enumerate(((odd_before, even, odd), (even, odd, even_after))):
+                for a in range(3):
+                    t = 9 * a + 3 * b + c
+                    out_ref[s, t * C1 : (t + 1) * C1] = sources[a].astype(bf16)
 
 
 def taps_of(pieces):
     planes = pieces.shape[0]
-    cells = planes * CELLS
-    return pl.pallas_call(
-        lambda x_ref, lhs_ref, v_ref: conv_two_kernel(planes, x_ref, None, None, lhs_ref, v_ref),
-        grid=(1,),
-        in_specs=[pl.BlockSpec(pieces.shape, lambda n: (0, 0, 0))],
-        out_specs=pl.BlockSpec((cells, TAPS * C1), lambda n: (0, 0)),
-        out_shape=jax.ShapeDtypeStruct((cells, TAPS * C1), bf16),
-        scratch_shapes=[pltpu.VMEM((3, 2, planes + 2, LS + 2, LS, PACK), f32)],
-        compiler_params=params(24),
+    half_cells = planes // 2 * CELLS
+    return pl.pallas_call(
+        lambda *refs: taps_kernel(planes, *refs),
+        out_shape=jax.ShapeDtypeStruct((2, TAPS * C1, half_cells), bf16),
+        scratch_shapes=[pltpu.VMEM((2, C1, half_cells), f32)],
+        compiler_params=params(16),
         cost_estimate=pl.CostEstimate(flops=0, bytes_accessed=8 << 20, transcendentals=0),
     )(pieces)
 
 
-def back_two_kernel(planes, cot_ref, w_ref, out_ref, acc_ref):
+def back_two_kernel(planes, parity_ref, own_ref, other_ref, w_ref, out_ref, acc_ref):
     step = pl.program_id(0)
 
     @pl.when(step == 0)
@@ -219,26 +312,23 @@
             acc_ref[:, :, p] = jnp.zeros((3, 2, LS + 2, LS, PACK), f32)
             return carry
 
-        lax.fori_loop(0, planes + 2, clear, 0)
-
-    taps = w_ref.shape[0] // C1
+        lax.fori_loop(0, planes + 3, clear, 0)
+
+    taps = w_ref.shape[1] // C1
     slab = 4
-    for m in range(planes // slab):
-        product = lax.dot_general(
-            cot_ref[m * slab * CELLS : (m + 1) * slab * CELLS],
-            w_ref[...],
-            (((1,), (1,)), ((), ())),
-            preferred_element_type=f32,
-        )
-        for u in range(taps):
-            t = taps * step + u
-
-            @pl.when(t < TAPS)
-            def _():
-                first = (u // 2) * PACK
-                tile = product[:, first : first + PACK].reshape(slab, LS, LS, PACK)
-                where = (t % 3, u % 2, pl.ds(m * slab + t // 9, slab), pl.ds((t // 3) % 3, LS))
-                acc_ref[where] = acc_ref[where] + tile
+    for s, cot_ref in enumerate((own_ref, other_ref)):
+        for m in range(planes // 2 // slab):
+            product = jnp.dot(
+                cot_ref[m * slab * CELLS : (m + 1) * slab * CELLS], w_ref[...], preferred_element_type=f32
+            )
+            for u in range(taps):
+                t = taps * step + u
+                lanes = slice((u // 2) * PACK, (u // 2 + 1) * PACK)
+                for k in range(slab):
+                    plane = 2 * (m * slab + k) + (parity_ref[0] if s == 0 else 1 - parity_ref[0])
+                    tile = product[k * CELLS : (k + 1) * CELLS, lanes].reshape(LS, LS, PACK)
+                    where = (t % 3, u % 2, plane + t // 9, pl.ds((t // 3) % 3, LS))
+                    acc_ref[where] = acc_ref[where] + tile
 
     @pl.when(step == pl.num_programs(0) - 1)
     def _():
@@ -258,53 +348,63 @@
         lax.fori_loop(0, planes, finish, 0)
 
 
-def back_two(cot, weight):
-    planes = cot.shape[0] // CELLS
+def back_two(parity, own, other, weight):
+    planes = 2 * own.shape[0] // CELLS
     block = 256
     return pl.pallas_call(
         lambda *refs: back_two_kernel(planes, *refs),
-        grid=(pl.cdiv(TAPS * C1, block),),
-        in_specs=[
-            pl.BlockSpec(cot.shape, lambda n: (0, 0)),
-            pl.BlockSpec((block, C2), lambda n: (n, 0)),
-        ],
-        out_specs=pl.BlockSpec((planes, CELLS // 2, PACK), lambda n: (0, 0, 0)),
+        grid_spec=pltpu.PrefetchScalarGridSpec(
+            num_scalar_prefetch=1,
+            grid=(weight.shape[1] // block,),
+            in_specs=[
+                pl.BlockSpec(own.shape, lambda n, s: (0, 0)),
+                pl.BlockSpec(own.shape, lambda n, s: (0, 0)),
+                pl.BlockSpec((C2, block), lambda n, s: (0, n)),
+            ],
+            out_specs=pl.BlockSpec((planes, CELLS // 2, PACK), lambda n, s: (0, 0, 0)),
+            scratch_shapes=[pltpu.VMEM((3, 2, planes + 3, LS + 2, LS, PACK), f32)],
+        ),
         out_shape=jax.ShapeDtypeStruct((planes, CELLS // 2, PACK), bf16),
-        scratch_shapes=[pltpu.VMEM((3, 2, planes + 2, LS + 2, LS, PACK), f32)],
-        compiler_params=params(32),
+        compiler_params=params(20),
         cost_estimate=pl.CostEstimate(
             flops=2 * planes * CELLS * TAPS * C1 * C2, bytes_accessed=6 << 20, transcendentals=0
         ),
-    )(cot, weight)
-
-
-def weight_two_kernel(samples, scale, *refs):
-    lhs_refs, cot_refs, out_ref = refs[:samples], refs[samples : 2 * samples], refs[2 * samples]
+    )(parity, own, other, weight)
+
+
+def weight_two_kernel(count, scale, *refs):
+    lhs_refs, cot_refs, out_ref = refs[1 : count + 1], refs[count + 1 : 2 * count + 1], refs[2 * count + 1]
     total = None
     for lhs_ref, cot_ref in zip(lhs_refs, cot_refs):
-        term = lax.dot_general(
-            lhs_ref[...], cot_ref[...], (((0,), (0,)), ((), ())), preferred_element_type=f32
-        )
+        term = jnp.dot(lhs_ref[0], cot_ref[...], preferred_element_type=f32)
         total = term if total is None else total + term
     out_ref[...] = total * scale
 
 
-def weight_two(lhs, cots, scale):
-    samples = len(lhs)
-    cells = lhs[0].shape[0]
-    block = 256
-    return pl.pallas_call(
-        lambda *refs: weight_two_kernel(samples, scale, *refs),
-        grid=(pl.cdiv(TAPS * C1, block),),
-        in_specs=[pl.BlockSpec((cells, block), lambda n: (0, n))] * samples
-        + [pl.BlockSpec((cells, C2), lambda n: (0, 0))] * samples,
-        out_specs=pl.BlockSpec((block, C2), lambda n: (n, 0)),
+def weight_two(parity, taps, cots, scale):
+    lhs = [value for value in taps for _ in range(2)]
+    flat = [value for pair in cots for value in pair]
+    count = len(flat)
+    cells = flat[0].shape[0]
+    block = 3 * 3 * C1
+    specs = [
+        pl.BlockSpec((1, block, cells), lambda n, s: (s[0], n, 0)),
+        pl.BlockSpec((1, block, cells), lambda n, s: (1 - s[0], n, 0)),
+    ] * (count // 2)
+    return pl.pallas_call(
+        lambda *refs: weight_two_kernel(count, scale, *refs),
+        grid_spec=pltpu.PrefetchScalarGridSpec(
+            num_scalar_prefetch=1,
+            grid=(TAPS * C1 // block,),
+            in_specs=specs + [pl.BlockSpec((cells, C2), lambda n, s: (0, 0))] * count,
+            out_specs=pl.BlockSpec((block, C2), lambda n, s: (n, 0)),
+        ),
         out_shape=jax.ShapeDtypeStruct((TAPS * C1, C2), f32),
-        compiler_params=params(56),
+        compiler_params=params(32 if count <= 4 else 56),
         cost_estimate=pl.CostEstimate(
-            flops=2 * samples * cells * TAPS * C1 * C2, bytes_accessed=20 << 20, transcendentals=0
-        ),
-    )(*lhs, *cots)
+            flops=2 * count * cells * TAPS * C1 * C2, bytes_accessed=18 << 20, transcendentals=0
+        ),
+    )(parity, *lhs, *flat)
 
 
 def grad_pre_kernel(pieces_ref, slope_ref, lhs_ref, grad_ref, partial_ref, spread_ref, packed_ref):
@@ -328,8 +428,8 @@
         grads.append(value)
     grad = jnp.concatenate(grads, axis=1)
     for lateral in range(9):
-        window = lhs_ref[:, lateral * WINDOW : (lateral + 1) * WINDOW]
-        product = lax.dot_general(window, grad, (((0,), (0,)), ((), ())), preferred_element_type=f32)
+        window = lhs_ref[lateral * WINDOW : (lateral + 1) * WINDOW]
+        product = jnp.dot(window, grad, preferred_element_type=f32)
         for c in range(3):
             sums = []
             for parity in range(2):
@@ -416,6 +516,11 @@
     return before, after
 
 
+def swap_cores(value):
+    count = lax.axis_size("depth")
+    return lax.ppermute(value, "depth", [(i, i ^ 1) for i in range(count)])
+
+
 def over_samples(value):
     count = lax.axis_size("sample")
     return [value] + [
@@ -429,23 +534,32 @@
     shards = lax.axis_size("depth")
     flat_two = conv2_weight.reshape(TAPS * C1, C2)
     own = volume.reshape(LAT, LAT * C1)
-
-    cots = lax.all_gather(cotangent.reshape(CELLS, C2), "depth", axis=0, tiled=True)
+    parity = (lax.axis_index("depth") % 2).astype(jnp.int32).reshape(1)
+    groups = [list(range(core, shards, 2)) for core in range(2)]
+
+    cot_own = lax.all_gather(
+        cotangent.reshape(CELLS, C2), "depth", axis=0, tiled=True, axis_index_groups=groups
+    )
     before, after = neighbours(own, "depth")
 
     back_weight = jnp.swapaxes(conv1_weight[::-1], 1, 2)
     band = banded(conv1_weight)
     back_band = banded(back_weight)
+    turned_two = turned_weight(flat_two)
 
     moved, slope, windows = conv_one(before, own, after, band)
     pieces = lax.all_to_all(moved, "depth", split_axis=0, concat_axis=0, tiled=True)
 
-    partial, own_taps = conv_two(pieces, flat_two)
-    features = lax.psum_scatter(partial, "depth", scatter_dimension=0, tiled=True)
-
-    grad_pieces = back_two(cots, flat_two)
+    send, own_lhs = conv_send(parity, pieces, flat_two)
+    received = swap_cores(send)
+    kept = conv_keep(own_lhs, flat_two, received)
+    features = lax.all_to_all(kept, "depth", split_axis=0, concat_axis=0, tiled=True, axis_index_groups=groups)
+    features = jnp.sum(features.reshape(-1, CELLS, C2).astype(f32), axis=0).astype(bf16)
+
+    cot_other = swap_cores(cot_own)
+    grad_pieces = back_two(parity, cot_own, cot_other, turned_two)
     grad_pieces = lax.all_to_all(grad_pieces, "depth", split_axis=0, concat_axis=0, tiled=True)
-    grad_pre, partial_one = grad_pre_of(grad_pieces, slope, windows)
+    grad_pre, partial_one = grad_pre_of(grad_pieces, slope, turned(windows, WINDOW))
     grad_before, grad_after = neighbours(grad_pre, "depth")
 
     devices = samples * shards
@@ -461,8 +575,9 @@
     grad_volume = back_one(grad_before, grad_pre, grad_after, back_band)
 
     scale_two = 1.0 / math.sqrt(samples * shards * CELLS)
-    all_taps = [own_taps] + [taps_of(value) for value in over_samples(pieces)[1:]]
-    grad_conv2 = weight_two(all_taps, over_samples(cots), scale_two)
+    all_taps = [taps_of(value) for value in over_samples(pieces)]
+    all_cots = [(cot_own, cot_other)] + [(value, swap_cores(value)) for value in over_samples(cot_own)[1:]]
+    grad_conv2 = weight_two(parity, all_taps, all_cots, scale_two)
 
     return (
         features.reshape(cotangent.shape),

time: 147 us -> 180 us (1.22)
  blocking collectives: 44 us -> 0 us
  waiting for transfers between devices: 16.9 us -> 51.7 us
  starting transfers between devices: 12.5 us -> 42.1 us
  local copies, waits for them, and re-layouts: 9.24 us -> 21.4 us
  Pallas kernels: 49.4 us -> 47.2 us
  other arithmetic: 0.06 us -> 2.15 us
    all_to_all x3 -> x0, blocking collectives: 44 us -> none  [the longest x1 17.6 us: on_device(): lax.all_to_all(moved, 'depth', split_axis=0, concat_axis=0, tiled=True)]
    all_to_all x0 -> x4, starting transfers between devices: none -> 24.2 us  [the longest x1 9.03 us: on_device(): lax.all_to_all(moved, 'depth', split_axis=0, concat_axis=0, tiled=True)]
    ppermute x2, waiting for transfers between devices: 2.02 us -> 23.8 us  [over_samples(): lax.ppermute(value, 'sample', [(i, (i + shift) % count) for i in range(co...]
    all_gather x1, waiting for transfers between devices: 11.2 us -> 23.7 us  [on_device(): lax.all_gather(cotangent.reshape(CELLS, C2), 'depth', axis=0, tiled=True,...]
    unnamed x17 -> x37, local copies, waits for them, and re-layouts: 8.47 us -> 20.6 us
    all_to_all x1, starting transfers between devices: 2.59 us -> 7.25 us  [on_device(): lax.all_to_all(summed, both, split_axis=0, concat_axis=0, tiled=True)]
    pallas_call x4 -> x8, Pallas kernels: 42.2 us -> 38.9 us  [the longest x1 11.1 us: weight_two(): pl.pallas_call(lambda *refs: weight_two_kernel(count, scale, *refs), grid...]
    reduce_sum x0 -> x1, other arithmetic: none -> 2.09 us  [on_device(): jnp.sum(features.reshape(-1, CELLS, C2).astype(f32), axis=0).astype(bf16)]
  transfers between devices with their start and end apart: 9 -> 15, of which waited for: 4 -> 4; matrix products, arithmetic and copies ran while one was open for 1% -> 2% of each run, Pallas kernels for 34% -> 25%
where the time goes in v1:
time: 180 us; the launch traced here: 179 us
  waiting for transfers between devices  51.7 us (29%)
  Pallas kernels  47.2 us (26%)
  starting transfers between devices  42.1 us (23%)
  local copies, waits for them, and re-layouts  21.4 us (12%)
  between operations  14.3 us (8%)
  other arithmetic  2.15 us (1%)
    ppermute x2, waiting for transfers between devices, over_samples(): lax.ppermute(value, 'sample', [(i, (i + shift) % count) for i in range(co...  23.8 us
    all_gather x1, waiting for transfers between devices, on_device(): lax.all_gather(cotangent.reshape(CELLS, C2), 'depth', axis=0, tiled=True,...  23.7 us
    unnamed x37, local copies, waits for them, and re-layouts  20.6 us
    pallas_call x1, Pallas kernels, weight_two(): pl.pallas_call(lambda *refs: weight_two_kernel(count, scale, *refs), grid...  11.1 us
    pallas_call x1, Pallas kernels, back_two(): pl.pallas_call(lambda *refs: back_two_kernel(planes, *refs), grid_spec=pl...  10.3 us
    all_to_all x1, starting transfers between devices, on_device(): lax.all_to_all(moved, 'depth', split_axis=0, concat_axis=0, tiled=True)  9.03 us
    all_to_all x1, starting transfers between devices, on_device(): lax.all_to_all(summed, both, split_axis=0, concat_axis=0, tiled=True)  7.25 us
    pallas_call x1, Pallas kernels, conv_send(): pl.pallas_call(lambda *refs: conv_send_kernel(planes, *refs), grid_spec=p...  6.67 us
  transfers between devices with their start and end apart: 15, of which 4 were waited for; matrix products, arithmetic and copies ran while one was open for 2% of the time, Pallas kernels for 25%

profile of v1, /device:TPU:0, one launch (start us, length us, event | category | flops | bytes accessed | tf_op | source)
XLA Modules:
  0.0 178.8 jit_solution(4514293485601588242)
XLA Ops:
  7.9 2.5 %collective-permute-start = (bf16[32,2048]{1,0:T(8,128)(2,1)}, bf16[32,2048]{1,0:T(8,128)(2,1)S(1)}, u32[]{:S(2)}, u32[]{:S(2)}) collective-permute-start(bf16[32,2048]{1,0:T(8,128)(2,1)} %bitcast.14), channel_id=1, source_target_pairs={{0,1},{1,2},{2,3},{3,4},{4,5},{5,6},{6,7},{7,8},{8,9},{9,10},{10,1... | collective-permute-start | bytes 393224 | tf_op jit(solution)/shard_map/ppermute | solution.py:514
  13.1 2.9 %collective-permute-done.1.after_ref = bf16[32,2048]{1,0:T(8,128)(2,1)S(1)} collective-permute-done((bf16[32,2048]{1,0:T(8,128)(2,1)}, bf16[32,2048]{1,0:T(8,128)(2,1)S(1)}, u32[]{:S(2)}, u32[]{:S(2)}) %collective-permute-start.1) | collective-permute-done | bytes 131104 | tf_op jit(solution)/shard_map/ppermute | solution.py:515
  20.6 9.0 %all-to-all-start = ((bf16[16,32,128]{2,1,0:T(8,128)(2,1)}), bf16[16,32,128]{2,1,0:T(8,128)(2,1)}, u32[]{:S(2)}, u32[]{:S(2)}) async-start(bf16[16,32,128]{2,1,0:T(8,128)(2,1)} %copy-done.14), calls=%async_computation | async-start | bytes 262144 | tf_op jit(solution)/shard_map/all_to_all | solution.py:551
  29.6 23.7 %all-gather.2.cloned.1.call-done.refs_1_.refs_5_ = bf16[512,1024]{1,0:T(8,128)(2,1)} async-done(((bf16[64,1024]{1,0:T(8,128)(2,1)}), bf16[512,1024]{1,0:T(8,128)(2,1)}) %all-gather.2.cloned.1.call-update) | async-done | bytes 1048592 | tf_op jit(solution)/shard_map/all_gather | solution.py:540
  53.3 6.7 %shard_map.77 = (bf16[512,1024]{1,0:T(8,128)(2,1)}, bf16[1024,1728]{1,0:T(8,128)(2,1)S(1)}) custom-call(s32[1]{0:T(128)} %bitcast.refs_0_, bf16[16,32,128]{2,1,0:T(8,128)(2,1)} %all-to-all-done.refs_1_.refs_0_, bf16[1728,1024]{1,0:T(8,128)(2,1)S(1)} %bitcast.10), custom_call_target="tpu_custom_call" | custom-call | flops 3623878656 | bytes 10485760 | tf_op jit(solution)/shard_map/pallas_call | solution.py:212
  62.1 10.3 %shard_map.80 = bf16[16,32,128]{2,1,0:T(8,128)(2,1)S(1)} custom-call(s32[1]{0:T(128)} %bitcast.refs_0_, bf16[512,1024]{1,0:T(8,128)(2,1)S(1)} %copy-done.16, bf16[512,1024]{1,0:T(8,128)(2,1)} %collective-permute-done.3.refs_2_.refs_6_, bf16[1024,1792]{1,0:T(8,128)(2,1)S(1)} %shard_map.79.refs_3_), custom_call_target="tpu_custom_call" | custom-call | flops 3623878656 | bytes 6291456 | tf_op jit(solution)/shard_map/pallas_call | solution.py:354
  73.1 4.2 %all-to-all-start.2 = ((bf16[16,32,128]{2,1,0:T(8,128)(2,1)}), bf16[16,32,128]{2,1,0:T(8,128)(2,1)}, u32[]{:S(2)}, u32[]{:S(2)}) async-start(bf16[16,32,128]{2,1,0:T(8,128)(2,1)} %copy-done.15), calls=%async_computation.2 | async-start | bytes 262144 | tf_op jit(solution)/shard_map/all_to_all | solution.py:561
  77.3 2.0 %copy-done.3 = bf16[1024,1728]{1,0:T(8,128)(2,1)S(1)} copy-done((bf16[1024,1728]{1,0:T(8,128)(2,1)S(1)}, bf16[1024,1728]{1,0:T(8,128)(2,1)}, u32[]{:S(2)}) %copy-start.3) | copy-done | bytes 3538968
  79.3 4.3 %shard_map.78 = bf16[512,1024]{1,0:T(8,128)(2,1)S(1)} custom-call(bf16[1024,1728]{1,0:T(8,128)(2,1)S(1)} %copy-done.3, bf16[1728,1024]{1,0:T(8,128)(2,1)S(1)} %bitcast.12, bf16[512,1024]{1,0:T(8,128)(2,1)} %collective-permute-done.2.more_ref), custom_call_target="tpu_custom_call" | custom-call | flops 1811939328 | bytes 8388608 | tf_op jit(solution)/shard_map/pallas_call | solution.py:246
  85.2 5.2 %all-to-all-start.1 = ((bf16[8,64,1024]{2,1,0:T(8,128)(2,1)}), bf16[8,64,1024]{2,1,0:T(8,128)(2,1)}, u32[]{:S(2)}, u32[]{:S(2)}) async-start(bf16[8,64,1024]{2,1,0:T(8,128)(2,1)} %bitcast.13), calls=%async_computation.1 | async-start | bytes 2097152 | tf_op jit(solution)/shard_map/all_to_all | solution.py:556
  91.9 23.8 %collective-permute-done.7.refs_7_ = bf16[512,1024]{1,0:T(8,128)(2,1)} collective-permute-done((bf16[512,1024]{1,0:T(8,128)(2,1)}, bf16[512,1024]{1,0:T(8,128)(2,1)}, u32[]{:S(2)}, u32[]{:S(2)}) %collective-permute-start.7) | collective-permute-done | bytes 1048608 | tf_op jit(solution)/shard_map/ppermute | solution.py:527
  119.3 2.9 %shard_map.82 = (bf16[256,256]{1,0:T(8,128)(2,1)S(1)}, bf16[32,32,128]{2,1,0:T(8,128)(2,1)}) custom-call(bf16[16,32,128]{2,1,0:T(8,128)(2,1)} %all-to-all-done.2.pieces_ref, f32[256,256]{1,0:T(8,128)S(1)} %copy-done.12, bf16[3456,256]{1,0:T(8,128)(2,1)S(1)} %shard_map.81.lhs_ref), custom_call_target="tpu_custom_call" | custom-call | flops 452984832 | bytes 3145728 | tf_op jit(solution)/shard_map/pallas_call | solution.py:457
  122.2 5.8 %all-to-all-start.3 = ((bf16[32,32,128]{2,1,0:T(8,128)(2,1)}), bf16[32,32,128]{2,1,0:T(8,128)(2,1)S(1)}, u32[]{:S(2)}, u32[]{:S(2)}) async-start(bf16[32,32,128]{2,1,0:T(8,128)(2,1)} %get-tuple-element.17), calls=%async_computation.3 | async-start | bytes 524288 | tf_op jit(solution)/shard_map/all_to_all | solution.py:569
  128.0 1.8 %collective-permute-start.6 = (bf16[16,32,128]{2,1,0:T(8,128)(2,1)}, bf16[16,32,128]{2,1,0:T(8,128)(2,1)S(1)}, u32[]{:S(2)}, u32[]{:S(2)}) collective-permute-start(bf16[16,32,128]{2,1,0:T(8,128)(2,1)} %all-to-all-done.refs_1_.refs_0_), channel_id=1, source_target_pairs={{0,16},{16,0},{1,17},{17,1},{2,18},{18,2},{3,19},{19,3},{4,20},{20... | collective-permute-start | bytes 393224 | tf_op jit(solution)/shard_map/ppermute | solution.py:527
  129.8 1.8 collective-permute-start.4
  134.6 2.3 %shard_map.86.refs_1_.refs_2_ = bf16[2,1728,512]{2,1,0:T(8,128)(2,1)S(1)} custom-call(bf16[16,32,128]{2,1,0:T(8,128)(2,1)} %all-to-all-done.refs_1_.refs_0_), custom_call_target="tpu_custom_call" | custom-call | bytes 8388608 | tf_op jit(solution)/shard_map/pallas_call | solution.py:297
  136.9 1.8 copy-done.4
  140.1 1.7 copy-done.6
  141.9 2.1 %reduce_sum.21 = bf16[64,1024]{1,0:T(8,128)(2,1)} reduce(bf16[8,64,1024]{2,1,0:T(8,128)(2,1)} %all-to-all-done.1, bf16[]{:T(256)} %constant.20.clone.1), dimensions={0}, to_apply=%region_0.1 | reduce | flops 458752 | bytes 1179650 | tf_op jit(solution)/shard_map/reduce_sum | solution.py:557
  146.1 7.2 %all-to-all-start.4 = ((bf16[32,32,128]{2,1,0:T(8,128)(2,1)}), bf16[32,32,128]{2,1,0:T(8,128)(2,1)}, u32[]{:S(2)}, u32[]{:S(2)}) async-start(bf16[32,32,128]{2,1,0:T(8,128)(2,1)} %broadcast_in_dim.2), calls=%async_computation.4 | async-start | bytes 524288 | tf_op jit(solution)/shard_map/all_to_all | solution.py:572
  153.4 2.0 %copy-done.5 = bf16[2,1728,512]{2,1,0:T(8,128)(2,1)S(1)} copy-done((bf16[2,1728,512]{2,1,0:T(8,128)(2,1)S(1)}, bf16[2,1728,512]{2,1,0:T(8,128)(2,1)}, u32[]{:S(2)}) %copy-start.5) | copy-done | bytes 3538968
  155.4 2.0 %copy-done.7 = bf16[2,1728,512]{2,1,0:T(8,128)(2,1)S(1)} copy-done((bf16[2,1728,512]{2,1,0:T(8,128)(2,1)S(1)}, bf16[2,1728,512]{2,1,0:T(8,128)(2,1)}, u32[]{:S(2)}) %copy-start.7) | copy-done | bytes 3538968
  158.6 11.1 %shard_map.88 = f32[1728,1024]{1,0:T(8,128)} custom-call(s32[1]{0:T(128)} %bitcast.refs_0_, bf16[2,1728,512]{2,1,0:T(8,128)(2,1)S(1)} %copy-done.5, bf16[2,1728,512]{2,1,0:T(8,128)(2,1)S(1)} %copy-done.5, bf16[2,1728,512]{2,1,0:T(8,128)(2,1)S(1)} %copy-done.7, bf16[2,1728,512]{2,1,0:T(8,128)(2,1)S(1)} %copy-done.7, bf16[512,1024]{1,0:T(8,128)(2,1)S(1)} %copy-done.17, ...), custom_call_target="tpu_custom_call" | custom-call | flops 7247757312 | bytes 18874368 | tf_op jit(solution)/shard_map/pallas_call | solution.py:394
  169.7 2.2 %shard_map.85 = f32[27,64,64]{2,1,0:T(8,128)} custom-call(bf16[32,32,128]{2,1,0:T(8,128)(2,1)} %all-to-all-done.4.packed_ref), custom_call_target="tpu_custom_call" | custom-call | bytes 1048576 | tf_op jit(solution)/shard_map/pallas_call | solution.py:503
  (63 shorter events, 25.2 us)
Async XLA Ops:
  7.2 46.1 %copy-start = (bf16[27,64,1024]{2,1,0:T(8,128)(2,1)S(1)}, bf16[27,64,1024]{2,1,0:T(8,128)(2,1)}, u32[]{:S(2)}) copy-start(bf16[27,64,1024]{2,1,0:T(8,128)(2,1)} %param.6) | copy-start | bytes 10616836
  7.2 46.1 %all-gather.2.cloned.1.call-start = ((), (), s32[]{:S(2)}) async-start(), calls=%async_computation.5 | async-start | bytes 1179648 | tf_op jit(solution)/shard_map/all_gather | solution.py:540
  7.9 5.2 %collective-permute-start = (bf16[32,2048]{1,0:T(8,128)(2,1)}, bf16[32,2048]{1,0:T(8,128)(2,1)S(1)}, u32[]{:S(2)}, u32[]{:S(2)}) collective-permute-start(bf16[32,2048]{1,0:T(8,128)(2,1)} %bitcast.14), channel_id=1, source_target_pairs={{0,1},{1,2},{2,3},{3,4},{4,5},{5,6},{6,7},{7,8},{8,9},{9,10},{10,1... | collective-permute-start | bytes 393224 | tf_op jit(solution)/shard_map/ppermute | solution.py:514
  10.4 5.6 %collective-permute-start.1 = (bf16[32,2048]{1,0:T(8,128)(2,1)}, bf16[32,2048]{1,0:T(8,128)(2,1)S(1)}, u32[]{:S(2)}, u32[]{:S(2)}) collective-permute-start(bf16[32,2048]{1,0:T(8,128)(2,1)} %bitcast.15), channel_id=1, source_target_pairs={{1,0},{2,1},{3,2},{4,3},{5,4},{6,5},{7,6},{8,7},{9,8},{10,9},{11,1... | collective-permute-start | bytes 393224 | tf_op jit(solution)/shard_map/ppermute | solution.py:515
  20.6 32.7 %all-to-all-start = ((bf16[16,32,128]{2,1,0:T(8,128)(2,1)}), bf16[16,32,128]{2,1,0:T(8,128)(2,1)}, u32[]{:S(2)}, u32[]{:S(2)}) async-start(bf16[16,32,128]{2,1,0:T(8,128)(2,1)} %copy-done.14), calls=%async_computation | async-start | bytes 262144 | tf_op jit(solution)/shard_map/all_to_all | solution.py:551
  53.3 8.8 %collective-permute-start.3 = (bf16[512,1024]{1,0:T(8,128)(2,1)}, bf16[512,1024]{1,0:T(8,128)(2,1)}, u32[]{:S(2)}, u32[]{:S(2)}) collective-permute-start(bf16[512,1024]{1,0:T(8,128)(2,1)} %all-gather.2.cloned.1.call-done.refs_1_.refs_5_), channel_id=1, source_target_pairs={{0,1},{1,0},{2,3},{3,2},{4,5},{5,4},{6,7},{7,6},{8,9},{9,8},{10,11... | collective-permute-start | bytes 3145736 | tf_op jit(solution)/shard_map/ppermute | solution.py:521
  60.0 2.1 %copy-start.2 = (bf16[1024,1728]{1,0:T(8,128)(2,1)}, bf16[1024,1728]{1,0:T(8,128)(2,1)S(1)}, u32[]{:S(2)}) copy-start(bf16[1024,1728]{1,0:T(8,128)(2,1)S(1)} %get-tuple-element.12.lhs_ref) | copy-start | bytes 10616836
  60.0 2.1 %copy-start.16 = (bf16[512,1024]{1,0:T(8,128)(2,1)S(1)}, bf16[512,1024]{1,0:T(8,128)(2,1)}, u32[]{:S(2)}) copy-start(bf16[512,1024]{1,0:T(8,128)(2,1)} %all-gather.2.cloned.1.call-done.refs_1_.refs_5_) | copy-start | bytes 3145732
  60.0 17.3 %collective-permute-start.2 = (bf16[512,1024]{1,0:T(8,128)(2,1)}, bf16[512,1024]{1,0:T(8,128)(2,1)}, u32[]{:S(2)}, u32[]{:S(2)}) collective-permute-start(bf16[512,1024]{1,0:T(8,128)(2,1)} %get-tuple-element.13), channel_id=1, source_target_pairs={{0,1},{1,0},{2,3},{3,2},{4,5},{5,4},{6,7},{7,6},{8,9},{9,8},{10,11... | collective-permute-start | bytes 3145736 | tf_op jit(solution)/shard_map/ppermute | solution.py:521
  73.1 12.1 %all-to-all-start.2 = ((bf16[16,32,128]{2,1,0:T(8,128)(2,1)}), bf16[16,32,128]{2,1,0:T(8,128)(2,1)}, u32[]{:S(2)}, u32[]{:S(2)}) async-start(bf16[16,32,128]{2,1,0:T(8,128)(2,1)} %copy-done.15), calls=%async_computation.2 | async-start | bytes 262144 | tf_op jit(solution)/shard_map/all_to_all | solution.py:561
  77.3 2.0 %copy-start.3 = (bf16[1024,1728]{1,0:T(8,128)(2,1)S(1)}, bf16[1024,1728]{1,0:T(8,128)(2,1)}, u32[]{:S(2)}) copy-start(bf16[1024,1728]{1,0:T(8,128)(2,1)} %copy-done.2) | copy-start | bytes 10616836
  85.2 37.0 %all-to-all-start.1 = ((bf16[8,64,1024]{2,1,0:T(8,128)(2,1)}), bf16[8,64,1024]{2,1,0:T(8,128)(2,1)}, u32[]{:S(2)}, u32[]{:S(2)}) async-start(bf16[8,64,1024]{2,1,0:T(8,128)(2,1)} %bitcast.13), calls=%async_computation.1 | async-start | bytes 2097152 | tf_op jit(solution)/shard_map/all_to_all | solution.py:556
  90.4 25.2 %collective-permute-start.7 = (bf16[512,1024]{1,0:T(8,128)(2,1)}, bf16[512,1024]{1,0:T(8,128)(2,1)}, u32[]{:S(2)}, u32[]{:S(2)}) collective-permute-start(bf16[512,1024]{1,0:T(8,128)(2,1)} %all-gather.2.cloned.1.call-done.refs_1_.refs_5_), channel_id=1, source_target_pairs={{0,16},{16,0},{1,17},{17,1},{2,18},{18,2},{3,19},{19,3},{4,20},{20... | collective-permute-start | bytes 3145736 | tf_op jit(solution)/shard_map/ppermute | solution.py:527
  115.7 37.7 %collective-permute-start.8 = (bf16[512,1024]{1,0:T(8,128)(2,1)}, bf16[512,1024]{1,0:T(8,128)(2,1)}, u32[]{:S(2)}, u32[]{:S(2)}) collective-permute-start(bf16[512,1024]{1,0:T(8,128)(2,1)} %collective-permute-done.7.refs_7_), channel_id=1, source_target_pairs={{0,1},{1,0},{2,3},{3,2},{4,5},{5,4},{6,7},{7,6},{8,9},{9,8},{10,11... | collective-permute-start | bytes 3145736 | tf_op jit(solution)/shard_map/ppermute | solution.py:521
  115.7 1.5 copy-start.9
  122.2 23.1 %all-to-all-start.3 = ((bf16[32,32,128]{2,1,0:T(8,128)(2,1)}), bf16[32,32,128]{2,1,0:T(8,128)(2,1)S(1)}, u32[]{:S(2)}, u32[]{:S(2)}) async-start(bf16[32,32,128]{2,1,0:T(8,128)(2,1)} %get-tuple-element.17), calls=%async_computation.3 | async-start | bytes 524288 | tf_op jit(solution)/shard_map/all_to_all | solution.py:569
  128.0 10.7 %collective-permute-start.6 = (bf16[16,32,128]{2,1,0:T(8,128)(2,1)}, bf16[16,32,128]{2,1,0:T(8,128)(2,1)S(1)}, u32[]{:S(2)}, u32[]{:S(2)}) collective-permute-start(bf16[16,32,128]{2,1,0:T(8,128)(2,1)} %all-to-all-done.refs_1_.refs_0_), channel_id=1, source_target_pairs={{0,16},{16,0},{1,17},{17,1},{2,18},{18,2},{3,19},{19,3},{4,20},{20... | collective-permute-start | bytes 393224 | tf_op jit(solution)/shard_map/ppermute | solution.py:527
  129.8 14.1 %collective-permute-start.4 = (bf16[256,256]{1,0:T(8,128)(2,1)S(1)}, bf16[256,256]{1,0:T(8,128)(2,1)S(1)}, u32[]{:S(2)}, u32[]{:S(2)}) collective-permute-start(bf16[256,256]{1,0:T(8,128)(2,1)S(1)} %get-tuple-element.16.own_ref), channel_id=1, source_target_pairs={{0,1},{1,2},{2,3},{3,4},{4,5},{5,6},{6,7},{7,8},{8,9},{9,10},{10,1... | collective-permute-start | bytes 393224 | tf_op jit(solution)/shard_map/ppermute | solution.py:514
  131.6 12.3 %collective-permute-start.5 = (bf16[256,256]{1,0:T(8,128)(2,1)S(1)}, bf16[256,256]{1,0:T(8,128)(2,1)S(1)}, u32[]{:S(2)}, u32[]{:S(2)}) collective-permute-start(bf16[256,256]{1,0:T(8,128)(2,1)S(1)} %get-tuple-element.16.own_ref), channel_id=1, source_target_pairs={{1,0},{2,1},{3,2},{4,3},{5,4},{6,5},{7,6},{8,7},{9,8},{10,9},{11,1... | collective-permute-start | bytes 393224 | tf_op jit(solution)/shard_map/ppermute | solution.py:515
  136.9 1.8 %copy-start.4 = (bf16[2,1728,512]{2,1,0:T(8,128)(2,1)}, bf16[2,1728,512]{2,1,0:T(8,128)(2,1)S(1)}, u32[]{:S(2)}) copy-start(bf16[2,1728,512]{2,1,0:T(8,128)(2,1)S(1)} %shard_map.86.refs_1_.refs_2_) | copy-start | bytes 10616836
  140.1 1.7 copy-start.6
  146.1 23.6 %all-to-all-start.4 = ((bf16[32,32,128]{2,1,0:T(8,128)(2,1)}), bf16[32,32,128]{2,1,0:T(8,128)(2,1)}, u32[]{:S(2)}, u32[]{:S(2)}) async-start(bf16[32,32,128]{2,1,0:T(8,128)(2,1)} %broadcast_in_dim.2), calls=%async_computation.4 | async-start | bytes 524288 | tf_op jit(solution)/shard_map/all_to_all | solution.py:572
  153.4 2.0 %copy-start.5 = (bf16[2,1728,512]{2,1,0:T(8,128)(2,1)S(1)}, bf16[2,1728,512]{2,1,0:T(8,128)(2,1)}, u32[]{:S(2)}) copy-start(bf16[2,1728,512]{2,1,0:T(8,128)(2,1)} %copy-done.4) | copy-start | bytes 10616836
  155.4 2.0 %copy-start.7 = (bf16[2,1728,512]{2,1,0:T(8,128)(2,1)S(1)}, bf16[2,1728,512]{2,1,0:T(8,128)(2,1)}, u32[]{:S(2)}) copy-start(bf16[2,1728,512]{2,1,0:T(8,128)(2,1)} %copy-done.6) | copy-start | bytes 10616836
  (9 other events, 8.3 us)
Sparse Core Ops, SparseCore 0:
  10.1 43.1 all-gather.1

commit v2 on v0

--- a/solution.py
+++ b/solution.py
@@ -125,14 +125,32 @@
     return jnp.where(column == edge, 0.0, pltpu.roll(field, (-step) % LS, 1))
 
 
+def turn_weight_kernel(rows, x_ref, out_ref):
+    block = x_ref.shape[0]
+    row = lax.broadcasted_iota(jnp.int32, x_ref.shape, 0) + block * pl.program_id(0)
+    out_ref[...] = jnp.where(row < rows, x_ref[...].astype(f32), 0.0).astype(bf16).T
+
+
+def turned_weight(weight, block=256):
+    rows, columns = weight.shape
+    steps = pl.cdiv(rows, block)
+    return pl.pallas_call(
+        lambda *refs: turn_weight_kernel(rows, *refs),
+        grid=(steps,),
+        in_specs=[pl.BlockSpec((block, columns), lambda n: (n, 0))],
+        out_specs=pl.BlockSpec((columns, block), lambda n: (0, n)),
+        out_shape=jax.ShapeDtypeStruct((columns, steps * block), weight.dtype),
+        compiler_params=params(56),
+        cost_estimate=pl.CostEstimate(flops=0, bytes_accessed=16 << 20, transcendentals=0),
+    )(weight)
+
+
 def conv_two_kernel(planes, x_ref, w_ref, out_ref, lhs_ref, v_ref):
     @pl.when(pl.program_id(0) == 0)
     def _():
-        def clear(p, carry):
-            v_ref[:, :, p] = jnp.zeros((3, 2, LS + 2, LS, PACK), f32)
-            return carry
-
-        lax.fori_loop(0, planes + 2, clear, 0)
+        v_ref[:, :, 0] = jnp.zeros((3, 2, LS + 2, LS, PACK), f32)
+        v_ref[:, :, planes + 1] = jnp.zeros((3, 2, LS + 2, LS, PACK), f32)
+        edge = jnp.zeros((LS, PACK), f32)
 
         def spread(p, carry):
             x = x_ref[p].astype(f32)
@@ -140,7 +158,9 @@
             for half, parts in enumerate(((x, turned), (turned, x))):
                 cells = jnp.concatenate(parts, axis=0).reshape(LS, LS, PACK)
                 for c in range(3):
+                    v_ref[c, half, p + 1, 0] = edge
                     v_ref[c, half, p + 1, 1 : LS + 1] = shift_cells(cells, c - 1)
+                    v_ref[c, half, p + 1, LS + 1] = edge
             return carry
 
         lax.fori_loop(0, planes, spread, 0)
@@ -161,11 +181,10 @@
 
         lax.fori_loop(0, planes, gather, 0)
 
-    if w_ref is not None:
-        chunk = 4 * CELLS
-        for m in range(planes * CELLS // chunk):
-            rows = slice(m * chunk, (m + 1) * chunk)
-            out_ref[rows] = jnp.dot(lhs_ref[rows], w_ref[...], preferred_element_type=f32).astype(bf16)
+    chunk = 4 * CELLS
+    for m in range(planes * CELLS // chunk):
+        rows = slice(m * chunk, (m + 1) * chunk)
+        out_ref[rows] = jnp.dot(lhs_ref[rows], w_ref[...], preferred_element_type=f32).astype(bf16)
 
 
 def conv_two(pieces, weight):
@@ -179,76 +198,83 @@
             pl.BlockSpec(pieces.shape, lambda n: (0, 0, 0)),
             pl.BlockSpec((TAPS * C1, block), lambda n: (0, n)),
         ],
-        out_specs=(
-            pl.BlockSpec((cells, block), lambda n: (0, n)),
-            pl.BlockSpec((cells, TAPS * C1), lambda n: (0, 0)),
-        ),
-        out_shape=(
-            jax.ShapeDtypeStruct((cells, C2), bf16),
-            jax.ShapeDtypeStruct((cells, TAPS * C1), bf16),
-        ),
-        scratch_shapes=[pltpu.VMEM((3, 2, planes + 2, LS + 2, LS, PACK), f32)],
-        compiler_params=params(40),
+        out_specs=pl.BlockSpec((cells, block), lambda n: (0, n)),
+        out_shape=jax.ShapeDtypeStruct((cells, C2), bf16),
+        scratch_shapes=[
+            pltpu.VMEM((cells, TAPS * C1), bf16),
+            pltpu.VMEM((3, 2, planes + 2, LS + 2, LS, PACK), f32),
+        ],
+        compiler_params=params(56),
         cost_estimate=pl.CostEstimate(
             flops=2 * cells * TAPS * C1 * C2, bytes_accessed=10 << 20, transcendentals=0
         ),
     )(pieces, weight)
 
 
-def taps_of(pieces):
-    planes = pieces.shape[0]
-    cells = planes * CELLS
-    return pl.pallas_call(
-        lambda x_ref, lhs_ref, v_ref: conv_two_kernel(planes, x_ref, None, None, lhs_ref, v_ref),
-        grid=(1,),
-        in_specs=[pl.BlockSpec(pieces.shape, lambda n: (0, 0, 0))],
-        out_specs=pl.BlockSpec((cells, TAPS * C1), lambda n: (0, 0)),
-        out_shape=jax.ShapeDtypeStruct((cells, TAPS * C1), bf16),
-        scratch_shapes=[pltpu.VMEM((3, 2, planes + 2, LS + 2, LS, PACK), f32)],
-        compiler_params=params(24),
-        cost_estimate=pl.CostEstimate(flops=0, bytes_accessed=8 << 20, transcendentals=0),
-    )(pieces)
-
-
-def back_two_kernel(planes, cot_ref, w_ref, out_ref, acc_ref):
+def plane_copies(device, pieces, refs, target_ref, base, sems):
+    copies = []
+    for differences, ref in zip(pieces, refs):
+        for k, difference in enumerate(differences):
+            row = pl.multiple_of(base + (device ^ difference) * CELLS, CELLS)
+            source = ref.at[pl.ds(k * CELLS, CELLS), :]
+            target = target_ref.at[pl.ds(row, CELLS), :]
+            copies.append(pltpu.make_async_copy(source, target, sems.at[base // CELLS + len(copies)]))
+    return copies
+
+
+def back_two_kernel(planes, pieces, device_ref, *refs):
+    cot_refs = refs[: len(pieces)]
+    w_ref, out_ref, cot_ref, product_ref, sems = refs[len(pieces)], *refs[-4:]
     step = pl.program_id(0)
+    tiles = product_ref.shape[0]
 
     @pl.when(step == 0)
     def _():
-        def clear(p, carry):
-            acc_ref[:, :, p] = jnp.zeros((3, 2, LS + 2, LS, PACK), f32)
-            return carry
-
-        lax.fori_loop(0, planes + 2, clear, 0)
-
-    taps = w_ref.shape[0] // C1
-    slab = 4
-    for m in range(planes // slab):
-        product = lax.dot_general(
-            cot_ref[m * slab * CELLS : (m + 1) * slab * CELLS],
-            w_ref[...],
-            (((1,), (1,)), ((), ())),
-            preferred_element_type=f32,
+        copies = plane_copies(device_ref[0], pieces, cot_refs, cot_ref, 0, sems)
+        for copy in copies:
+            copy.start()
+        empty_plane = jnp.zeros((LS + 2, LS, PACK), f32)
+        empty_row = jnp.zeros((planes, LS, PACK), f32)
+        for m in range(tiles):
+            product_ref[m, 0] = empty_plane
+            product_ref[m, planes + 1] = empty_plane
+            product_ref[m, 1 : planes + 1, 0] = empty_row
+            product_ref[m, 1 : planes + 1, LS + 1] = empty_row
+        for copy in copies:
+            copy.wait()
+
+    wide = w_ref.shape[1] // PACK
+    slab = planes // 4
+    for m in range(4):
+        product = jnp.dot(
+            cot_ref[m * slab * CELLS : (m + 1) * slab * CELLS], w_ref[...], preferred_element_type=f32
         )
-        for u in range(taps):
-            t = taps * step + u
-
-            @pl.when(t < TAPS)
-            def _():
-                first = (u // 2) * PACK
-                tile = product[:, first : first + PACK].reshape(slab, LS, LS, PACK)
-                where = (t % 3, u % 2, pl.ds(m * slab + t // 9, slab), pl.ds((t // 3) % 3, LS))
-                acc_ref[where] = acc_ref[where] + tile
+        for u in range(wide):
+            tile = product[:, u * PACK : (u + 1) * PACK].reshape(slab, LS, LS, PACK)
+            product_ref[wide * step + u, 1 + m * slab : 1 + (m + 1) * slab, 1 : LS + 1] = tile
 
     @pl.when(step == pl.num_programs(0) - 1)
     def _():
         def finish(p, carry):
+            sums = {}
+            for m in range(tiles):
+                taps = [t for t in (2 * m, 2 * m + 1) if t < TAPS]
+                for k, t in enumerate(taps):
+                    a, b = t // 9, (t // 3) % 3
+                    same = len(taps) == 2 and taps[0] // 3 == taps[1] // 3
+                    if same and k == 1:
+                        continue
+                    key = (t % 3, t % 3 + 1) if same else ((t % 3, None) if k == 0 else (None, t % 3))
+                    tile = product_ref[m, p + 2 - a, 2 - b : 2 - b + LS]
+                    sums[key] = tile if key not in sums else sums[key] + tile
             total = None
             for half in range(2):
                 part = None
                 for c in range(3):
-                    term = shift_cells(acc_ref[c, half, p + 1, 1 : LS + 1], 1 - c)
-                    part = term if part is None else part + term
+                    found = [value for key, value in sums.items() if key[half] == c]
+                    for value in found:
+                        term = shift_cells(value, 1 - c)
+                        part = term if part is None else part + term
                 part = part.reshape(CELLS, PACK)
                 total = part if half == 0 else total + pltpu.roll(part, C1, 1)
             top, bottom = total[: CELLS // 2], total[CELLS // 2 :]
@@ -258,53 +284,109 @@
         lax.fori_loop(0, planes, finish, 0)
 
 
-def back_two(cot, weight):
-    planes = cot.shape[0] // CELLS
+def back_two(device, pieces, cots, weight, after):
+    planes = sum(len(piece) for piece in pieces)
     block = 256
-    return pl.pallas_call(
-        lambda *refs: back_two_kernel(planes, *refs),
-        grid=(pl.cdiv(TAPS * C1, block),),
-        in_specs=[
-            pl.BlockSpec(cot.shape, lambda n: (0, 0)),
-            pl.BlockSpec((block, C2), lambda n: (n, 0)),
-        ],
-        out_specs=pl.BlockSpec((planes, CELLS // 2, PACK), lambda n: (0, 0, 0)),
+    tiles = weight.shape[1] // PACK
+    return pl.pallas_call(
+        lambda *refs: back_two_kernel(planes, pieces, *refs),
+        grid_spec=pltpu.PrefetchScalarGridSpec(
+            num_scalar_prefetch=1,
+            grid=(weight.shape[1] // block,),
+            in_specs=[pl.BlockSpec(memory_space=pl.ANY)] * len(cots)
+            + [pl.BlockSpec((C2, block), lambda n, s: (0, n))]
+            + [pl.BlockSpec(memory_space=pl.ANY)] * len(after),
+            out_specs=pl.BlockSpec((planes, CELLS // 2, PACK), lambda n, s: (0, 0, 0)),
+            scratch_shapes=[
+                pltpu.VMEM((planes * CELLS, C2), bf16),
+                pltpu.VMEM((tiles, planes + 2, LS + 2, LS, PACK), f32),
+                pltpu.SemaphoreType.DMA((planes,)),
+            ],
+        ),
         out_shape=jax.ShapeDtypeStruct((planes, CELLS // 2, PACK), bf16),
-        scratch_shapes=[pltpu.VMEM((3, 2, planes + 2, LS + 2, LS, PACK), f32)],
-        compiler_params=params(32),
+        compiler_params=params(56),
         cost_estimate=pl.CostEstimate(
             flops=2 * planes * CELLS * TAPS * C1 * C2, bytes_accessed=6 << 20, transcendentals=0
         ),
-    )(cot, weight)
-
-
-def weight_two_kernel(samples, scale, *refs):
-    lhs_refs, cot_refs, out_ref = refs[:samples], refs[samples : 2 * samples], refs[2 * samples]
-    total = None
-    for lhs_ref, cot_ref in zip(lhs_refs, cot_refs):
-        term = lax.dot_general(
-            lhs_ref[...], cot_ref[...], (((0,), (0,)), ((), ())), preferred_element_type=f32
-        )
-        total = term if total is None else total + term
-    out_ref[...] = total * scale
-
-
-def weight_two(lhs, cots, scale):
-    samples = len(lhs)
-    cells = lhs[0].shape[0]
-    block = 256
-    return pl.pallas_call(
-        lambda *refs: weight_two_kernel(samples, scale, *refs),
-        grid=(pl.cdiv(TAPS * C1, block),),
-        in_specs=[pl.BlockSpec((cells, block), lambda n: (0, n))] * samples
-        + [pl.BlockSpec((cells, C2), lambda n: (0, 0))] * samples,
-        out_specs=pl.BlockSpec((block, C2), lambda n: (n, 0)),
+    )(device, *cots, weight, *after)
+
+
+def weight_two_kernel(planes, pieces, scale, device_ref, *refs):
+    samples = len(pieces)
+    field_refs, cot_refs = refs[:samples], refs[samples:]
+    out_ref, cot_ref, flat_ref, lhs_ref, sems = refs[-5:]
+    cells = planes * CELLS
+    a = pl.program_id(0)
+
+    def all_copies():
+        copies, first = [], 0
+        for s in range(samples):
+            refs_here = cot_refs[first : first + len(pieces[s])]
+            copies += plane_copies(device_ref[0], pieces[s], refs_here, cot_ref, s * cells, sems)
+            first += len(pieces[s])
+        return copies
+
+    @pl.when(a == 0)
+    def _():
+        for copy in all_copies():
+            copy.start()
+        for s in range(samples):
+
+            def cells_of(p):
+                x = field_refs[s][p].astype(f32)
+                return jnp.concatenate([x, pltpu.roll(x, C1, 1)], axis=0)
+
+            for j in range(planes // 2):
+                pair = jnp.concatenate([cells_of(2 * j), cells_of(2 * j + 1)], axis=0)
+                flat_ref[s, :, j * PACK : (j + 1) * PACK] = pair.T[:C1]
+
+    lane = lax.broadcasted_iota(jnp.int32, (C1, cells), 1)
+    plane, row, column = lane // CELLS, (lane // LS) % LS, lane % LS
+    deep = (plane + a >= 1) & (plane + a <= planes)
+    for b in range(3):
+        for c in range(3):
+            inside = deep & (row + b >= 1) & (row + b <= LS) & (column + c >= 1) & (column + c <= LS)
+            shift = lax.rem(2 * cells - (CELLS * (a - 1) + LS * (b - 1) + c - 1), cells)
+            t = 3 * b + c
+            for s in range(samples):
+                value = jnp.where(inside, pltpu.roll(flat_ref[s], shift, 1), 0.0)
+                lhs_ref[t * C1 : (t + 1) * C1, s * cells : (s + 1) * cells] = value.astype(bf16)
+
+    @pl.when(a == 0)
+    def _():
+        for copy in all_copies():
+            copy.wait()
+
+    out_ref[...] = jnp.dot(lhs_ref[...], cot_ref[...], preferred_element_type=f32) * scale
+
+
+def weight_two(device, fields, pieces, cots, scale, after):
+    samples = len(fields)
+    planes = fields[0].shape[0]
+    cells = planes * CELLS
+    block = 9 * C1
+    flat = [value for sample in cots for value in sample]
+    return pl.pallas_call(
+        lambda *refs: weight_two_kernel(planes, pieces, scale, *refs),
+        grid_spec=pltpu.PrefetchScalarGridSpec(
+            num_scalar_prefetch=1,
+            grid=(3,),
+            in_specs=[pl.BlockSpec(field.shape, lambda n, s: (0, 0, 0)) for field in fields]
+            + [pl.BlockSpec(memory_space=pl.ANY)] * (len(flat) + len(after)),
+            out_specs=pl.BlockSpec((block, C2), lambda n, s: (n, 0)),
+            scratch_shapes=[
+                pltpu.VMEM((samples * cells, C2), bf16),
+                pltpu.VMEM((samples, C1, cells), f32),
+                pltpu.VMEM((block, samples * cells), bf16),
+                pltpu.SemaphoreType.DMA((samples * planes,)),
+            ],
+        ),
         out_shape=jax.ShapeDtypeStruct((TAPS * C1, C2), f32),
-        compiler_params=params(56),
+        compiler_params=params(60),
         cost_estimate=pl.CostEstimate(
-            flops=2 * samples * cells * TAPS * C1 * C2, bytes_accessed=20 << 20, transcendentals=0
-        ),
-    )(*lhs, *cots)
+            flops=2 * samples * cells * TAPS * C1 * C2, bytes_accessed=18 << 20, transcendentals=0
+        ),
+    )(device, *fields, *flat, *after)
 
 
 def grad_pre_kernel(pieces_ref, slope_ref, lhs_ref, grad_ref, partial_ref, spread_ref, packed_ref):
@@ -416,6 +498,11 @@
     return before, after
 
 
+def flipped(value, difference):
+    count = lax.axis_size("depth")
+    return lax.ppermute(value, "depth", [(i, i ^ difference) for i in range(count)])
+
+
 def over_samples(value):
     count = lax.axis_size("sample")
     return [value] + [
@@ -429,21 +516,35 @@
     shards = lax.axis_size("depth")
     flat_two = conv2_weight.reshape(TAPS * C1, C2)
     own = volume.reshape(LAT, LAT * C1)
-
-    cots = lax.all_gather(cotangent.reshape(CELLS, C2), "depth", axis=0, tiled=True)
+    device = lax.axis_index("depth").astype(jnp.int32).reshape(1)
+    cot = cotangent.reshape(CELLS, C2)
+
+    core, chip = 1, 2
+    outer = list(range(4, shards, 4))
+    far = [flipped(cot, difference) for difference in outer]
     before, after = neighbours(own, "depth")
+    cot_chip = flipped(cot, chip)
 
     back_weight = jnp.swapaxes(conv1_weight[::-1], 1, 2)
     band = banded(conv1_weight)
     back_band = banded(back_weight)
+    turned_two = turned_weight(flat_two)
 
     moved, slope, windows = conv_one(before, own, after, band)
-    pieces = lax.all_to_all(moved, "depth", split_axis=0, concat_axis=0, tiled=True)
-
-    partial, own_taps = conv_two(pieces, flat_two)
+    fields = lax.all_to_all(moved, "depth", split_axis=0, concat_axis=0, tiled=True)
+
+    near = jnp.concatenate([cot, cot_chip], axis=0)
+    far = jnp.concatenate(far, axis=0)
+    far_chip = flipped(far, chip)
+    cots = [near, far, far_chip]
+    pieces = [[0, chip], outer, [difference + chip for difference in outer]]
+    pieces = pieces + [[difference + core for difference in piece] for piece in pieces]
+
+    partial = conv_two(fields, flat_two)
     features = lax.psum_scatter(partial, "depth", scatter_dimension=0, tiled=True)
 
-    grad_pieces = back_two(cots, flat_two)
+    own_cots = cots + [flipped(value, core) for value in cots]
+    grad_pieces = back_two(device, pieces, own_cots, turned_two, [partial])
     grad_pieces = lax.all_to_all(grad_pieces, "depth", split_axis=0, concat_axis=0, tiled=True)
     grad_pre, partial_one = grad_pre_of(grad_pieces, slope, windows)
     grad_before, grad_after = neighbours(grad_pre, "depth")
@@ -461,8 +562,13 @@
     grad_volume = back_one(grad_before, grad_pre, grad_after, back_band)
 
     scale_two = 1.0 / math.sqrt(samples * shards * CELLS)
-    all_taps = [own_taps] + [taps_of(value) for value in over_samples(pieces)[1:]]
-    grad_conv2 = weight_two(all_taps, over_samples(cots), scale_two)
+    half = jnp.concatenate(cots, axis=0)
+    halves = [[difference for piece in group for difference in piece] for group in (pieces[:3], pieces[3:])]
+    all_pieces, all_cots = [pieces], [own_cots]
+    for value in over_samples(half)[1:]:
+        all_pieces.append(halves)
+        all_cots.append([value, flipped(value, core)])
+    grad_conv2 = weight_two(device, over_samples(fields), all_pieces, all_cots, scale_two, [grad_pre])
 
     return (
         features.reshape(cotangent.shape),

time: 147 us -> 141 us (0.959)
  blocking collectives: 44 us -> 13.7 us
  starting transfers between devices: 12.5 us -> 33.7 us
  Pallas kernels: 49.4 us -> 52.2 us
    all_to_all x2 -> x0, blocking collectives: 32.6 us -> none  [the longest x1 17.6 us: on_device(): lax.all_to_all(moved, 'depth', split_axis=0, concat_axis=0, tiled=True)]
    all_to_all x0 -> x2, waiting for transfers between devices: none -> 13.3 us  [the longest x1 10.1 us: on_device(): lax.all_to_all(shares, both, split_axis=0, concat_axis=0, tiled=True)]
    ppermute x0 -> x9, starting transfers between devices: none -> 12.2 us  [flipped(): lax.ppermute(value, 'depth', [(i, i ^ difference) for i in range(count)])]
    all_gather x1 -> x0, waiting for transfers between devices: 11.2 us -> none  [on_device(): lax.all_gather(cotangent.reshape(CELLS, C2), 'depth', axis=0, tiled=True)]
    all_to_all x0 -> x2, starting transfers between devices: none -> 8.41 us  [the longest x1 5.82 us: on_device(): lax.all_to_all(moved, 'depth', split_axis=0, concat_axis=0, tiled=True)]
    all_to_all x1, waiting for transfers between devices: 0.16 us -> 3.02 us  [on_device(): lax.all_to_all(summed, both, split_axis=0, concat_axis=0, tiled=True)]
    ppermute x2, waiting for transfers between devices: 2.87 us -> 0.48 us  [neighbours(): after = lax.ppermute(value, axis, [(i + 1, i) for i in range(count - 1)])]
    all_to_all x1, blocking collectives: 11.4 us -> 13.7 us  [on_device(): lax.all_to_all(grad_pieces, 'depth', split_axis=0, concat_axis=0, tiled=T...]
  transfers between devices with their start and end apart: 9 -> 19, of which waited for: 4 -> 4; matrix products, arithmetic and copies ran while one was open for 1% -> 4% of each run, Pallas kernels for 34% -> 37%
where the time goes in v2:
time: 141 us; the launch traced here: 139 us
  Pallas kernels  52.2 us (37%)
  starting transfers between devices  33.7 us (24%)
  waiting for transfers between devices  16.9 us (12%)
  between operations  14.3 us (10%)
  blocking collectives  13.7 us (10%)
  local copies, waits for them, and re-layouts  8.45 us (6%)
    pallas_call x1, Pallas kernels, weight_two(): pl.pallas_call(lambda *refs: weight_two_kernel(planes, pieces, scale, *re...  16.3 us
    all_to_all x1, blocking collectives, on_device(): lax.all_to_all(grad_pieces, 'depth', split_axis=0, concat_axis=0, tiled=T...  13.7 us
    ppermute x9, starting transfers between devices, flipped(): lax.ppermute(value, 'depth', [(i, i ^ difference) for i in range(count)])  12.2 us
    pallas_call x1, Pallas kernels, back_two(): pl.pallas_call(lambda *refs: back_two_kernel(planes, pieces, *refs), grid...  12 us
    all_to_all x1, waiting for transfers between devices, on_device(): lax.all_to_all(shares, both, split_axis=0, concat_axis=0, tiled=True)  10.1 us
    pallas_call x1, Pallas kernels, conv_two(): pl.pallas_call(lambda *refs: conv_two_kernel(planes, *refs), grid=(C2 //...  8.76 us
    unnamed x28, local copies, waits for them, and re-layouts  6.91 us
    pallas_call x1, Pallas kernels, turned_weight(): pl.pallas_call(lambda *refs: turn_weight_kernel(rows, *refs), grid=(steps...  6.62 us
  transfers between devices with their start and end apart: 19, of which 4 were waited for; matrix products, arithmetic and copies ran while one was open for 4% of the time, Pallas kernels for 37%

profile of v2, /device:TPU:0, one launch (start us, length us, event | category | flops | bytes accessed | tf_op | source)
XLA Modules:
  0.0 139.4 jit_solution(13293585668082090547)
XLA Ops:
  7.2 2.5 %collective-permute-start = (bf16[32,2048]{1,0:T(8,128)(2,1)}, bf16[32,2048]{1,0:T(8,128)(2,1)S(1)}, u32[]{:S(2)}, u32[]{:S(2)}) collective-permute-start(bf16[32,2048]{1,0:T(8,128)(2,1)} %bitcast.10), channel_id=1, source_target_pairs={{0,1},{1,2},{2,3},{3,4},{4,5},{5,6},{6,7},{7,8},{8,9},{9,10},{10,1... | collective-permute-start | bytes 393224 | tf_op jit(solution)/shard_map/ppermute | solution.py:496
  11.0 4.9 %collective-permute-start.2 = (bf16[64,1024]{1,0:T(8,128)(2,1)}, bf16[64,1024]{1,0:T(8,128)(2,1)S(1)}, u32[]{:S(2)}, u32[]{:S(2)}) collective-permute-start(bf16[64,1024]{1,0:T(8,128)(2,1)} %bitcast.15), channel_id=1, source_target_pairs={{0,2},{1,3},{2,0},{3,1},{4,6},{5,7},{6,4},{7,5},{8,10},{9,11},{10,... | collective-permute-start | bytes 393224 | tf_op jit(solution)/shard_map/ppermute | solution.py:503
  15.9 1.6 %collective-permute-start.3 = (bf16[64,1024]{1,0:T(8,128)(2,1)}, bf16[64,1024]{1,0:T(8,128)(2,1)S(1)}, u32[]{:S(2)}, u32[]{:S(2)}) collective-permute-start(bf16[64,1024]{1,0:T(8,128)(2,1)} %bitcast.16), channel_id=1, source_target_pairs={{0,4},{1,5},{2,6},{3,7},{4,0},{5,1},{6,2},{7,3},{8,12},{9,13},{10,... | collective-permute-start | bytes 393224 | tf_op jit(solution)/shard_map/ppermute | solution.py:503
  17.5 2.6 %collective-permute-start.4 = (bf16[64,1024]{1,0:T(8,128)(2,1)}, bf16[64,1024]{1,0:T(8,128)(2,1)S(1)}, u32[]{:S(2)}, u32[]{:S(2)}) collective-permute-start(bf16[64,1024]{1,0:T(8,128)(2,1)} %bitcast.17), channel_id=1, source_target_pairs={{0,8},{1,9},{2,10},{3,11},{4,12},{5,13},{6,14},{7,15},{8,0},{9,1},... | collective-permute-start | bytes 393224 | tf_op jit(solution)/shard_map/ppermute | solution.py:503
  20.1 1.6 %constant_dynamic-update-slice_fusion.8 = bf16[512,1024]{1,0:T(8,128)(2,1)} fusion(bf16[1,1,8,8,1024]{4,3,2,1,0:T(8,128)(2,1)} %param.7), kind=kLoop, calls=%fused_computation.11 | loop fusion | bytes 262144
  23.4 1.7 %shard_map.76 = (bf16[16,32,128]{2,1,0:T(8,128)(2,1)}, f32[256,256]{1,0:T(8,128)S(1)}, bf16[256,3456]{1,0:T(8,128)(2,1)S(1)}) custom-call(bf16[32,2048]{1,0:T(8,128)(2,1)S(1)} %collective-permute-done.before_ref, bf16[32,2048]{1,0:T(8,128)(2,1)S(1)} %bitcast.12, bf16[32,2048]{1,0:T(8,128)(2,1)S(1)} %collective-permute-done.1.after_ref, ...), custom_call_target="tpu_custom_call" | custom-call | flops 452984832 | bytes 5242880 | tf_op jit(solution)/shard_map/pallas_call | solution.py:105
  25.1 5.8 %all-to-all-start = ((bf16[16,32,128]{2,1,0:T(8,128)(2,1)}), bf16[16,32,128]{2,1,0:T(8,128)(2,1)S(1)}, u32[]{:S(2)}, u32[]{:S(2)}) async-start(bf16[16,32,128]{2,1,0:T(8,128)(2,1)} %get-tuple-element.9), calls=%async_computation | async-start | bytes 262144 | tf_op jit(solution)/shard_map/all_to_all | solution.py:534
  33.7 1.9 %collective-permute-start.6 = (bf16[192,1024]{1,0:T(8,128)(2,1)S(1)}, bf16[192,1024]{1,0:T(8,128)(2,1)S(1)}, u32[]{:S(2)}, u32[]{:S(2)}) collective-permute-start(bf16[192,1024]{1,0:T(8,128)(2,1)S(1)} %get-tuple-element.15.refs_2_.refs_4_), channel_id=1, source_target_pairs={{0,2},{1,3},{2,0},{3,1},{4,6},{5,7},{6,4},{7,5},{8,10},{9,11},{10,... | collective-permute-start | bytes 1179656 | tf_op jit(solution)/shard_map/ppermute | solution.py:503
  35.6 3.2 %all-to-all-done.refs_0_.refs_1_ = bf16[16,32,128]{2,1,0:T(8,128)(2,1)S(1)} async-done(((bf16[16,32,128]{2,1,0:T(8,128)(2,1)}), bf16[16,32,128]{2,1,0:T(8,128)(2,1)S(1)}, u32[]{:S(2)}, u32[]{:S(2)}) %all-to-all-start) | async-done | bytes 131104 | tf_op jit(solution)/shard_map/all_to_all | solution.py:534
  39.5 8.8 %shard_map.77.refs_8_ = bf16[1024,1024]{1,0:T(8,128)(2,1)} custom-call(bf16[16,32,128]{2,1,0:T(8,128)(2,1)} %copy-done.7, bf16[1728,1024]{1,0:T(8,128)(2,1)} %bitcast.13), custom_call_target="tpu_custom_call" | custom-call | flops 3623878656 | bytes 10485760 | tf_op jit(solution)/shard_map/pallas_call | solution.py:194
  49.9 1.5 %collective-permute-start.13 = (bf16[512,1024]{1,0:T(8,128)(2,1)}, bf16[512,1024]{1,0:T(8,128)(2,1)}, u32[]{:S(2)}, u32[]{:S(2)}) collective-permute-start(bf16[512,1024]{1,0:T(8,128)(2,1)} %constant_dynamic-update-slice_fusion.3), channel_id=1, source_target_pairs={{0,16},{16,0},{1,17},{17,1},{2,18},{18,2},{3,19},{19,3},{4,20},{20... | collective-permute-start | bytes 3145736 | tf_op jit(solution)/shard_map/ppermute | solution.py:509
  51.4 6.6 %shard_map.78.refs_7_ = bf16[1024,1792]{1,0:T(8,128)(2,1)} custom-call(bf16[1728,1024]{1,0:T(8,128)(2,1)} %bitcast.14), custom_call_target="tpu_custom_call" | custom-call | bytes 16777216 | tf_op jit(solution)/shard_map/pallas_call | solution.py:137
  58.0 12.0 %shard_map.79 = bf16[16,32,128]{2,1,0:T(8,128)(2,1)} custom-call(s32[1]{0:T(128)} %bitcast.3.refs_0_, bf16[128,1024]{1,0:T(8,128)(2,1)} %copy-done.6, bf16[192,1024]{1,0:T(8,128)(2,1)} %copy-done.9, bf16[192,1024]{1,0:T(8,128)(2,1)} %copy-done.5, bf16[128,1024]{1,0:T(8,128)(2,1)} %collective-permute-done.7.refs_4_.refs_6_, ...), custom_call_target="tpu_custom_call" | custom-call | flops 3623878656 | bytes 6291456 | tf_op jit(solution)/shard_map/pallas_call | solution.py:291
  70.1 13.7 %all_to_all.20.pieces_ref = bf16[16,32,128]{2,1,0:T(8,128)(2,1)S(1)} all-to-all(bf16[16,32,128]{2,1,0:T(8,128)(2,1)} %shard_map.79), channel_id=1, replica_groups=mesh['sample'=2,'depth'=16] {'depth'}, dimensions={0} | all-to-all | bytes 262144 | tf_op jit(solution)/shard_map/all_to_all | solution.py:548
  83.8 3.4 %shard_map.80 = (bf16[256,256]{1,0:T(8,128)(2,1)S(1)}, bf16[32,32,128]{2,1,0:T(8,128)(2,1)}) custom-call(bf16[16,32,128]{2,1,0:T(8,128)(2,1)S(1)} %all_to_all.20.pieces_ref, f32[256,256]{1,0:T(8,128)S(1)} %get-tuple-element.10.slope_ref, bf16[256,3456]{1,0:T(8,128)(2,1)S(1)} %get-tuple-element.11.lhs_ref), custom_call_target="tpu_custom_call" | custom-call | flops 452984832 | bytes 3145728 | tf_op jit(solution)/shard_map/pallas_call | solution.py:439
  87.2 2.6 %all-to-all-start.2 = ((bf16[32,32,128]{2,1,0:T(8,128)(2,1)}), bf16[32,32,128]{2,1,0:T(8,128)(2,1)S(1)}, u32[]{:S(2)}, u32[]{:S(2)}) async-start(bf16[32,32,128]{2,1,0:T(8,128)(2,1)} %get-tuple-element.13), calls=%async_computation.3 | async-start | bytes 524288 | tf_op jit(solution)/shard_map/all_to_all | solution.py:556
  89.9 10.1 %all-to-all-done.2 = bf16[32,32,128]{2,1,0:T(8,128)(2,1)S(1)} async-done(((bf16[32,32,128]{2,1,0:T(8,128)(2,1)}), bf16[32,32,128]{2,1,0:T(8,128)(2,1)S(1)}, u32[]{:S(2)}, u32[]{:S(2)}) %all-to-all-start.2) | async-done | bytes 262176 | tf_op jit(solution)/shard_map/all_to_all | solution.py:556
  100.8 2.6 %all-to-all-start.3 = ((bf16[32,32,128]{2,1,0:T(8,128)(2,1)}), bf16[32,32,128]{2,1,0:T(8,128)(2,1)S(1)}, u32[]{:S(2)}, u32[]{:S(2)}) async-start(bf16[32,32,128]{2,1,0:T(8,128)(2,1)} %broadcast_in_dim.2), calls=%async_computation.4 | async-start | bytes 524288 | tf_op jit(solution)/shard_map/all_to_all | solution.py:559
  103.4 2.0 %collective-permute-start.10 = (bf16[256,256]{1,0:T(8,128)(2,1)S(1)}, bf16[256,256]{1,0:T(8,128)(2,1)S(1)}, u32[]{:S(2)}, u32[]{:S(2)}) collective-permute-start(bf16[256,256]{1,0:T(8,128)(2,1)S(1)} %get-tuple-element.12.own_ref.refs_11_), channel_id=1, source_target_pairs={{0,1},{1,2},{2,3},{3,4},{4,5},{5,6},{6,7},{7,8},{8,9},{9,10},{10,1... | collective-permute-start | bytes 393224 | tf_op jit(solution)/shard_map/ppermute | solution.py:496
  105.5 1.5 %collective-permute-start.11 = (bf16[256,256]{1,0:T(8,128)(2,1)S(1)}, bf16[256,256]{1,0:T(8,128)(2,1)S(1)}, u32[]{:S(2)}, u32[]{:S(2)}) collective-permute-start(bf16[256,256]{1,0:T(8,128)(2,1)S(1)} %get-tuple-element.12.own_ref.refs_11_), channel_id=1, source_target_pairs={{1,0},{2,1},{3,2},{4,3},{5,4},{6,5},{7,6},{8,7},{9,8},{10,9},{11,1... | collective-permute-start | bytes 393224 | tf_op jit(solution)/shard_map/ppermute | solution.py:497
  107.2 1.7 %collective-permute-start.12 = (bf16[16,32,128]{2,1,0:T(8,128)(2,1)S(1)}, bf16[16,32,128]{2,1,0:T(8,128)(2,1)S(1)}, u32[]{:S(2)}, u32[]{:S(2)}) collective-permute-start(bf16[16,32,128]{2,1,0:T(8,128)(2,1)S(1)} %copy-done.8), channel_id=1, source_target_pairs={{0,16},{16,0},{1,17},{17,1},{2,18},{18,2},{3,19},{19,3},{4,20},{20... | collective-permute-start | bytes 393224 | tf_op jit(solution)/shard_map/ppermute | solution.py:509
  109.9 1.4 shard_map.82
  111.2 3.0 %all-to-all-done.3.packed_ref = bf16[32,32,128]{2,1,0:T(8,128)(2,1)S(1)} async-done(((bf16[32,32,128]{2,1,0:T(8,128)(2,1)}), bf16[32,32,128]{2,1,0:T(8,128)(2,1)S(1)}, u32[]{:S(2)}, u32[]{:S(2)}) %all-to-all-start.3) | async-done | bytes 262176 | tf_op jit(solution)/shard_map/all_to_all | solution.py:559
  116.2 16.3 %shard_map.84 = f32[1728,1024]{1,0:T(8,128)} custom-call(s32[1]{0:T(128)} %bitcast.3.refs_0_, bf16[16,32,128]{2,1,0:T(8,128)(2,1)} %copy-done.7, bf16[16,32,128]{2,1,0:T(8,128)(2,1)} %copy-done.10, bf16[128,1024]{1,0:T(8,128)(2,1)} %copy-done.6, bf16[192,1024]{1,0:T(8,128)(2,1)} %copy-done.9, bf16[192,1024]{1,0:T(8,128)(2,1)} %copy-done.5, ...), custom_call_target="tpu_custom_call" | custom-call | flops 7247757312 | bytes 18874368 | tf_op jit(solution)/shard_map/pallas_call | solution.py:369
  (60 shorter events, 12.0 us)
Async XLA Ops:
  7.2 16.2 %copy-start.2 = (bf16[1,1,32,2048]{3,2,1,0:T(8,128)(2,1)S(1)}, bf16[1,1,32,2048]{3,2,1,0:T(8,128)(2,1)}, u32[]{:S(2)}) copy-start(bf16[1,1,32,2048]{3,2,1,0:T(8,128)(2,1)} %param.4) | copy-start | bytes 393220
  7.2 15.9 %copy-start.4 = (bf16[1,1,8,8,1024]{4,3,2,1,0:T(8,128)(2,1)S(1)}, bf16[1,1,8,8,1024]{4,3,2,1,0:T(8,128)(2,1)}, u32[]{:S(2)}) copy-start(bf16[1,1,8,8,1024]{4,3,2,1,0:T(8,128)(2,1)} %param.7) | copy-start | bytes 393220
  7.2 15.9 %collective-permute-start = (bf16[32,2048]{1,0:T(8,128)(2,1)}, bf16[32,2048]{1,0:T(8,128)(2,1)S(1)}, u32[]{:S(2)}, u32[]{:S(2)}) collective-permute-start(bf16[32,2048]{1,0:T(8,128)(2,1)} %bitcast.10), channel_id=1, source_target_pairs={{0,1},{1,2},{2,3},{3,4},{4,5},{5,6},{6,7},{7,8},{8,9},{9,10},{10,1... | collective-permute-start | bytes 393224 | tf_op jit(solution)/shard_map/ppermute | solution.py:496
  9.7 13.7 %collective-permute-start.1 = (bf16[32,2048]{1,0:T(8,128)(2,1)}, bf16[32,2048]{1,0:T(8,128)(2,1)S(1)}, u32[]{:S(2)}, u32[]{:S(2)}) collective-permute-start(bf16[32,2048]{1,0:T(8,128)(2,1)} %bitcast.11), channel_id=1, source_target_pairs={{1,0},{2,1},{3,2},{4,3},{5,4},{6,5},{7,6},{8,7},{9,8},{10,9},{11,1... | collective-permute-start | bytes 393224 | tf_op jit(solution)/shard_map/ppermute | solution.py:497
  11.0 20.0 %collective-permute-start.2 = (bf16[64,1024]{1,0:T(8,128)(2,1)}, bf16[64,1024]{1,0:T(8,128)(2,1)S(1)}, u32[]{:S(2)}, u32[]{:S(2)}) collective-permute-start(bf16[64,1024]{1,0:T(8,128)(2,1)} %bitcast.15), channel_id=1, source_target_pairs={{0,2},{1,3},{2,0},{3,1},{4,6},{5,7},{6,4},{7,5},{8,10},{9,11},{10,... | collective-permute-start | bytes 393224 | tf_op jit(solution)/shard_map/ppermute | solution.py:503
  15.9 15.7 %collective-permute-start.3 = (bf16[64,1024]{1,0:T(8,128)(2,1)}, bf16[64,1024]{1,0:T(8,128)(2,1)S(1)}, u32[]{:S(2)}, u32[]{:S(2)}) collective-permute-start(bf16[64,1024]{1,0:T(8,128)(2,1)} %bitcast.16), channel_id=1, source_target_pairs={{0,4},{1,5},{2,6},{3,7},{4,0},{5,1},{6,2},{7,3},{8,12},{9,13},{10,... | collective-permute-start | bytes 393224 | tf_op jit(solution)/shard_map/ppermute | solution.py:503
  17.5 14.9 %collective-permute-start.4 = (bf16[64,1024]{1,0:T(8,128)(2,1)}, bf16[64,1024]{1,0:T(8,128)(2,1)S(1)}, u32[]{:S(2)}, u32[]{:S(2)}) collective-permute-start(bf16[64,1024]{1,0:T(8,128)(2,1)} %bitcast.17), channel_id=1, source_target_pairs={{0,8},{1,9},{2,10},{3,11},{4,12},{5,13},{6,14},{7,15},{8,0},{9,1},... | collective-permute-start | bytes 393224 | tf_op jit(solution)/shard_map/ppermute | solution.py:503
  23.1 9.9 %collective-permute-start.5 = (bf16[64,1024]{1,0:T(8,128)(2,1)S(1)}, bf16[64,1024]{1,0:T(8,128)(2,1)S(1)}, u32[]{:S(2)}, u32[]{:S(2)}) collective-permute-start(bf16[64,1024]{1,0:T(8,128)(2,1)S(1)} %bitcast.18), channel_id=1, source_target_pairs={{0,12},{1,13},{2,14},{3,15},{4,8},{5,9},{6,10},{7,11},{8,4},{9,5},... | collective-permute-start | bytes 393224 | tf_op jit(solution)/shard_map/ppermute | solution.py:503
  25.1 13.8 %all-to-all-start = ((bf16[16,32,128]{2,1,0:T(8,128)(2,1)}), bf16[16,32,128]{2,1,0:T(8,128)(2,1)S(1)}, u32[]{:S(2)}, u32[]{:S(2)}) async-start(bf16[16,32,128]{2,1,0:T(8,128)(2,1)} %get-tuple-element.9), calls=%async_computation | async-start | bytes 262144 | tf_op jit(solution)/shard_map/all_to_all | solution.py:534
  30.9 101.6 %reduce-scatter.2.cloned.1.call-start = ((), (), s32[]{:S(2)}) async-start(), calls=%async_computation.5 | async-start | bytes 2228224 | tf_op jit(solution)/shard_map/reduce_scatter | solution.py:544
  33.7 14.7 %collective-permute-start.6 = (bf16[192,1024]{1,0:T(8,128)(2,1)S(1)}, bf16[192,1024]{1,0:T(8,128)(2,1)S(1)}, u32[]{:S(2)}, u32[]{:S(2)}) collective-permute-start(bf16[192,1024]{1,0:T(8,128)(2,1)S(1)} %get-tuple-element.15.refs_2_.refs_4_), channel_id=1, source_target_pairs={{0,2},{1,3},{2,0},{3,1},{4,6},{5,7},{6,4},{7,5},{8,10},{9,11},{10,... | collective-permute-start | bytes 1179656 | tf_op jit(solution)/shard_map/ppermute | solution.py:503
  48.3 9.7 %collective-permute-start.8 = (bf16[192,1024]{1,0:T(8,128)(2,1)S(1)}, bf16[192,1024]{1,0:T(8,128)(2,1)}, u32[]{:S(2)}, u32[]{:S(2)}) collective-permute-start(bf16[192,1024]{1,0:T(8,128)(2,1)S(1)} %get-tuple-element.15.refs_2_.refs_4_), channel_id=1, source_target_pairs={{0,1},{1,0},{2,3},{3,2},{4,5},{5,4},{6,7},{7,6},{8,9},{9,8},{10,11... | collective-permute-start | bytes 1179656 | tf_op jit(solution)/shard_map/ppermute | solution.py:503
  48.4 9.6 %collective-permute-start.9 = (bf16[192,1024]{1,0:T(8,128)(2,1)S(1)}, bf16[192,1024]{1,0:T(8,128)(2,1)}, u32[]{:S(2)}, u32[]{:S(2)}) collective-permute-start(bf16[192,1024]{1,0:T(8,128)(2,1)S(1)} %collective-permute-done.6.refs_3_.refs_5_), channel_id=1, source_target_pairs={{0,1},{1,0},{2,3},{3,2},{4,5},{5,4},{6,7},{7,6},{8,9},{9,8},{10,11... | collective-permute-start | bytes 1179656 | tf_op jit(solution)/shard_map/ppermute | solution.py:503
  49.0 9.1 %collective-permute-start.7 = (bf16[128,1024]{1,0:T(8,128)(2,1)S(1)}, bf16[128,1024]{1,0:T(8,128)(2,1)}, u32[]{:S(2)}, u32[]{:S(2)}) collective-permute-start(bf16[128,1024]{1,0:T(8,128)(2,1)S(1)} %pad_maximum_fusion.refs_1_.refs_3_), channel_id=1, source_target_pairs={{0,1},{1,0},{2,3},{3,2},{4,5},{5,4},{6,7},{7,6},{8,9},{9,8},{10,11... | collective-permute-start | bytes 786440 | tf_op jit(solution)/shard_map/ppermute | solution.py:503
  49.9 39.9 %collective-permute-start.13 = (bf16[512,1024]{1,0:T(8,128)(2,1)}, bf16[512,1024]{1,0:T(8,128)(2,1)}, u32[]{:S(2)}, u32[]{:S(2)}) collective-permute-start(bf16[512,1024]{1,0:T(8,128)(2,1)} %constant_dynamic-update-slice_fusion.3), channel_id=1, source_target_pairs={{0,16},{16,0},{1,17},{17,1},{2,18},{18,2},{3,19},{19,3},{4,20},{20... | collective-permute-start | bytes 3145736 | tf_op jit(solution)/shard_map/ppermute | solution.py:509
  70.1 36.9 %copy-start.1 = (bf16[27,64,64]{2,1,0:T(8,128)(2,1)S(1)}, bf16[27,64,64]{2,1,0:T(8,128)(2,1)}, u32[]{:S(2)}) copy-start(bf16[27,64,64]{2,1,0:T(8,128)(2,1)} %w_ref.1) | copy-start | bytes 663556
  83.8 23.5 %copy-start.8 = (bf16[16,32,128]{2,1,0:T(8,128)(2,1)S(1)}, bf16[16,32,128]{2,1,0:T(8,128)(2,1)}, u32[]{:S(2)}) copy-start(bf16[16,32,128]{2,1,0:T(8,128)(2,1)} %copy-done.7) | copy-start | bytes 393220
  87.2 22.7 %copy-start.3 = (bf16[256,256]{1,0:T(8,128)(2,1)}, bf16[256,256]{1,0:T(8,128)(2,1)S(1)}, u32[]{:S(2)}) copy-start(bf16[256,256]{1,0:T(8,128)(2,1)S(1)} %get-tuple-element.12.own_ref.refs_11_) | copy-start | bytes 393220
  87.2 12.9 %all-to-all-start.2 = ((bf16[32,32,128]{2,1,0:T(8,128)(2,1)}), bf16[32,32,128]{2,1,0:T(8,128)(2,1)S(1)}, u32[]{:S(2)}, u32[]{:S(2)}) async-start(bf16[32,32,128]{2,1,0:T(8,128)(2,1)} %get-tuple-element.13), calls=%async_computation.3 | async-start | bytes 524288 | tf_op jit(solution)/shard_map/all_to_all | solution.py:556
  89.8 25.8 %collective-permute-start.14 = (bf16[512,1024]{1,0:T(8,128)(2,1)}, bf16[512,1024]{1,0:T(8,128)(2,1)}, u32[]{:S(2)}, u32[]{:S(2)}) collective-permute-start(bf16[512,1024]{1,0:T(8,128)(2,1)} %collective-permute-done.13.refs_9_), channel_id=1, source_target_pairs={{0,1},{1,0},{2,3},{3,2},{4,5},{5,4},{6,7},{7,6},{8,9},{9,8},{10,11... | collective-permute-start | bytes 3145736 | tf_op jit(solution)/shard_map/ppermute | solution.py:503
  100.8 13.4 %all-to-all-start.3 = ((bf16[32,32,128]{2,1,0:T(8,128)(2,1)}), bf16[32,32,128]{2,1,0:T(8,128)(2,1)S(1)}, u32[]{:S(2)}, u32[]{:S(2)}) async-start(bf16[32,32,128]{2,1,0:T(8,128)(2,1)} %broadcast_in_dim.2), calls=%async_computation.4 | async-start | bytes 524288 | tf_op jit(solution)/shard_map/all_to_all | solution.py:559
  103.4 5.9 %collective-permute-start.10 = (bf16[256,256]{1,0:T(8,128)(2,1)S(1)}, bf16[256,256]{1,0:T(8,128)(2,1)S(1)}, u32[]{:S(2)}, u32[]{:S(2)}) collective-permute-start(bf16[256,256]{1,0:T(8,128)(2,1)S(1)} %get-tuple-element.12.own_ref.refs_11_), channel_id=1, source_target_pairs={{0,1},{1,2},{2,3},{3,4},{4,5},{5,6},{6,7},{7,8},{8,9},{9,10},{10,1... | collective-permute-start | bytes 393224 | tf_op jit(solution)/shard_map/ppermute | solution.py:496
  105.5 4.4 %collective-permute-start.11 = (bf16[256,256]{1,0:T(8,128)(2,1)S(1)}, bf16[256,256]{1,0:T(8,128)(2,1)S(1)}, u32[]{:S(2)}, u32[]{:S(2)}) collective-permute-start(bf16[256,256]{1,0:T(8,128)(2,1)S(1)} %get-tuple-element.12.own_ref.refs_11_), channel_id=1, source_target_pairs={{1,0},{2,1},{3,2},{4,3},{5,4},{6,5},{7,6},{8,7},{9,8},{10,9},{11,1... | collective-permute-start | bytes 393224 | tf_op jit(solution)/shard_map/ppermute | solution.py:497
  107.2 8.3 %collective-permute-start.12 = (bf16[16,32,128]{2,1,0:T(8,128)(2,1)S(1)}, bf16[16,32,128]{2,1,0:T(8,128)(2,1)S(1)}, u32[]{:S(2)}, u32[]{:S(2)}) collective-permute-start(bf16[16,32,128]{2,1,0:T(8,128)(2,1)S(1)} %copy-done.8), channel_id=1, source_target_pairs={{0,16},{16,0},{1,17},{17,1},{2,18},{18,2},{3,19},{19,3},{4,20},{20... | collective-permute-start | bytes 393224 | tf_op jit(solution)/shard_map/ppermute | solution.py:509
  (6 other events, 35.6 us)
Sparse Core Ops, SparseCore 0:
  48.4 60.8 reduce-scatter.1

commit v3 on v2

--- a/solution.py
+++ b/solution.py
@@ -125,27 +125,7 @@
     return jnp.where(column == edge, 0.0, pltpu.roll(field, (-step) % LS, 1))
 
 
-def turn_weight_kernel(rows, x_ref, out_ref):
-    block = x_ref.shape[0]
-    row = lax.broadcasted_iota(jnp.int32, x_ref.shape, 0) + block * pl.program_id(0)
-    out_ref[...] = jnp.where(row < rows, x_ref[...].astype(f32), 0.0).astype(bf16).T
-
-
-def turned_weight(weight, block=256):
-    rows, columns = weight.shape
-    steps = pl.cdiv(rows, block)
-    return pl.pallas_call(
-        lambda *refs: turn_weight_kernel(rows, *refs),
-        grid=(steps,),
-        in_specs=[pl.BlockSpec((block, columns), lambda n: (n, 0))],
-        out_specs=pl.BlockSpec((columns, block), lambda n: (0, n)),
-        out_shape=jax.ShapeDtypeStruct((columns, steps * block), weight.dtype),
-        compiler_params=params(56),
-        cost_estimate=pl.CostEstimate(flops=0, bytes_accessed=16 << 20, transcendentals=0),
-    )(weight)
-
-
-def conv_two_kernel(planes, x_ref, w_ref, out_ref, lhs_ref, v_ref):
+def conv_two_kernel(planes, device_ref, x_ref, w_ref, send_ref, keep_ref, lhs_ref, v_ref):
     @pl.when(pl.program_id(0) == 0)
     def _():
         v_ref[:, :, 0] = jnp.zeros((3, 2, LS + 2, LS, PACK), f32)
@@ -166,7 +146,13 @@
         lax.fori_loop(0, planes, spread, 0)
 
         def gather(p, carry):
-            rows = pl.ds(pl.multiple_of(p * CELLS, CELLS), CELLS)
+            difference = p ^ device_ref[0]
+            place = (
+                (1 - (difference & 1)) * (planes // 2)
+                + ((difference >> 1) & 1) * (planes // 4)
+                + (difference >> 2)
+            )
+            rows = pl.ds(pl.multiple_of(place * CELLS, CELLS), CELLS)
             for m in range((TAPS + 1) // 2):
                 t = 2 * m
                 low = v_ref[t % 3, 0, p + t // 9, pl.ds((t // 3) % 3, LS)].reshape(CELLS, PACK)
@@ -181,34 +167,67 @@
 
         lax.fori_loop(0, planes, gather, 0)
 
-    chunk = 4 * CELLS
-    for m in range(planes * CELLS // chunk):
-        rows = slice(m * chunk, (m + 1) * chunk)
-        out_ref[rows] = jnp.dot(lhs_ref[rows], w_ref[...], preferred_element_type=f32).astype(bf16)
-
-
-def conv_two(pieces, weight):
-    planes = pieces.shape[0]
+    product = jnp.dot(lhs_ref[...], w_ref[...], preferred_element_type=f32).astype(bf16)
+    half = planes // 2 * CELLS
+    send_ref[...] = product[:half]
+    keep_ref[...] = product[half:]
+
+
+def conv_two(device, fields, weight):
+    planes = fields.shape[0]
     cells = planes * CELLS
-    block = 256
+    block = 512
     return pl.pallas_call(
         lambda *refs: conv_two_kernel(planes, *refs),
-        grid=(C2 // block,),
-        in_specs=[
-            pl.BlockSpec(pieces.shape, lambda n: (0, 0, 0)),
-            pl.BlockSpec((TAPS * C1, block), lambda n: (0, n)),
-        ],
-        out_specs=pl.BlockSpec((cells, block), lambda n: (0, n)),
-        out_shape=jax.ShapeDtypeStruct((cells, C2), bf16),
-        scratch_shapes=[
-            pltpu.VMEM((cells, TAPS * C1), bf16),
-            pltpu.VMEM((3, 2, planes + 2, LS + 2, LS, PACK), f32),
-        ],
+        grid_spec=pltpu.PrefetchScalarGridSpec(
+            num_scalar_prefetch=1,
+            grid=(C2 // block,),
+            in_specs=[
+                pl.BlockSpec(fields.shape, lambda n, s: (0, 0, 0)),
+                pl.BlockSpec((TAPS * C1, block), lambda n, s: (0, n)),
+            ],
+            out_specs=(
+                pl.BlockSpec((cells // 2, block), lambda n, s: (0, n)),
+                pl.BlockSpec((cells // 2, block), lambda n, s: (0, n)),
+            ),
+            scratch_shapes=[
+                pltpu.VMEM((cells, TAPS * C1), bf16),
+                pltpu.VMEM((3, 2, planes + 2, LS + 2, LS, PACK), f32),
+            ],
+        ),
+        out_shape=(jax.ShapeDtypeStruct((cells // 2, C2), bf16),) * 2,
         compiler_params=params(56),
         cost_estimate=pl.CostEstimate(
             flops=2 * cells * TAPS * C1 * C2, bytes_accessed=10 << 20, transcendentals=0
         ),
-    )(pieces, weight)
+    )(device, fields, weight)
+
+
+def join_kernel(count, *refs):
+    out_ref, sems = refs[count], refs[count + 1]
+    copies, first = [], 0
+    for k in range(count):
+        rows = refs[k].shape[0]
+        copies.append(pltpu.make_async_copy(refs[k], out_ref.at[pl.ds(first, rows), :], sems.at[k]))
+        first += rows
+    for copy in copies:
+        copy.start()
+    for copy in copies:
+        copy.wait()
+
+
+def joined(values):
+    rows = sum(value.shape[0] for value in values)
+    columns = values[0].shape[1]
+    return pl.pallas_call(
+        lambda *refs: join_kernel(len(values), *refs),
+        in_specs=[pl.BlockSpec(memory_space=pl.ANY)] * len(values),
+        out_specs=pl.BlockSpec(memory_space=pl.ANY),
+        out_shape=jax.ShapeDtypeStruct((rows, columns), values[0].dtype),
+        scratch_shapes=[pltpu.SemaphoreType.DMA((len(values),))],
+        compiler_params=params(56),
+        cost_estimate=pl.CostEstimate(flops=0, bytes_accessed=4 * rows * columns, transcendentals=0),
+    )(*values)
 
 
 def plane_copies(device, pieces, refs, target_ref, base, sems):
@@ -243,15 +262,13 @@
         for copy in copies:
             copy.wait()
 
-    wide = w_ref.shape[1] // PACK
-    slab = planes // 4
-    for m in range(4):
-        product = jnp.dot(
-            cot_ref[m * slab * CELLS : (m + 1) * slab * CELLS], w_ref[...], preferred_element_type=f32
-        )
-        for u in range(wide):
-            tile = product[:, u * PACK : (u + 1) * PACK].reshape(slab, LS, LS, PACK)
-            product_ref[wide * step + u, 1 + m * slab : 1 + (m + 1) * slab, 1 : LS + 1] = tile
+    wide = w_ref.shape[0] // PACK
+    product = lax.dot_general(
+        cot_ref[...], w_ref[...], (((1,), (1,)), ((), ())), preferred_element_type=f32
+    )
+    for u in range(wide):
+        tile = product[:, u * PACK : (u + 1) * PACK].reshape(planes, LS, LS, PACK)
+        product_ref[wide * step + u, 1 : planes + 1, 1 : LS + 1] = tile
 
     @pl.when(step == pl.num_programs(0) - 1)
     def _():
@@ -287,14 +304,15 @@
 def back_two(device, pieces, cots, weight, after):
     planes = sum(len(piece) for piece in pieces)
     block = 256
-    tiles = weight.shape[1] // PACK
+    steps = pl.cdiv(TAPS * C1, block)
+    tiles = steps * block // PACK
     return pl.pallas_call(
         lambda *refs: back_two_kernel(planes, pieces, *refs),
         grid_spec=pltpu.PrefetchScalarGridSpec(
             num_scalar_prefetch=1,
-            grid=(weight.shape[1] // block,),
+            grid=(steps,),
             in_specs=[pl.BlockSpec(memory_space=pl.ANY)] * len(cots)
-            + [pl.BlockSpec((C2, block), lambda n, s: (0, n))]
+            + [pl.BlockSpec((block, C2), lambda n, s: (n, 0))]
             + [pl.BlockSpec(memory_space=pl.ANY)] * len(after),
             out_specs=pl.BlockSpec((planes, CELLS // 2, PACK), lambda n, s: (0, 0, 0)),
             scratch_shapes=[
@@ -311,69 +329,68 @@
     )(device, *cots, weight, *after)
 
 
-def weight_two_kernel(planes, pieces, scale, device_ref, *refs):
+def weight_two_kernel(a, planes, pieces, scale, device_ref, *refs):
     samples = len(pieces)
     field_refs, cot_refs = refs[:samples], refs[samples:]
     out_ref, cot_ref, flat_ref, lhs_ref, sems = refs[-5:]
     cells = planes * CELLS
-    a = pl.program_id(0)
-
-    def all_copies():
-        copies, first = [], 0
-        for s in range(samples):
-            refs_here = cot_refs[first : first + len(pieces[s])]
-            copies += plane_copies(device_ref[0], pieces[s], refs_here, cot_ref, s * cells, sems)
-            first += len(pieces[s])
-        return copies
-
-    @pl.when(a == 0)
-    def _():
-        for copy in all_copies():
-            copy.start()
-        for s in range(samples):
-
-            def cells_of(p):
-                x = field_refs[s][p].astype(f32)
-                return jnp.concatenate([x, pltpu.roll(x, C1, 1)], axis=0)
-
-            for j in range(planes // 2):
-                pair = jnp.concatenate([cells_of(2 * j), cells_of(2 * j + 1)], axis=0)
-                flat_ref[s, :, j * PACK : (j + 1) * PACK] = pair.T[:C1]
-
-    lane = lax.broadcasted_iota(jnp.int32, (C1, cells), 1)
+    copies, first = [], 0
+    for s in range(samples):
+        refs_here = cot_refs[first : first + len(pieces[s])]
+        copies += plane_copies(device_ref[0], pieces[s], refs_here, cot_ref, s * cells, sems)
+        first += len(pieces[s])
+    for copy in copies:
+        copy.start()
+
+    for s in range(samples):
+
+        def cells_of(p):
+            x = field_refs[s][p].astype(f32)
+            return jnp.concatenate([x, pltpu.roll(x, C1, 1)], axis=0)
+
+        for j in range(planes // 2):
+            pair = jnp.concatenate([cells_of(2 * j), cells_of(2 * j + 1)], axis=0)
+            flat_ref[s, :, j * PACK : (j + 1) * PACK] = pair.T[:C1]
+
+    lane = lax.broadcasted_iota(jnp.int32, (1, cells), 1)
     plane, row, column = lane // CELLS, (lane // LS) % LS, lane % LS
-    deep = (plane + a >= 1) & (plane + a <= planes)
     for b in range(3):
         for c in range(3):
-            inside = deep & (row + b >= 1) & (row + b <= LS) & (column + c >= 1) & (column + c <= LS)
-            shift = lax.rem(2 * cells - (CELLS * (a - 1) + LS * (b - 1) + c - 1), cells)
+            inside = (row + b >= 1) & (row + b <= LS) & (column + c >= 1) & (column + c <= LS)
+            if a == 0:
+                inside = inside & (plane > 0)
+            elif a == 2:
+                inside = inside & (plane < planes - 1)
+            mask = inside.astype(f32)
+            shift = (-(CELLS * (a - 1) + LS * (b - 1) + c - 1)) % cells
             t = 3 * b + c
             for s in range(samples):
-                value = jnp.where(inside, pltpu.roll(flat_ref[s], shift, 1), 0.0)
+                value = flat_ref[s]
+                if shift:
+                    value = pltpu.roll(value, shift, 1) * mask
                 lhs_ref[t * C1 : (t + 1) * C1, s * cells : (s + 1) * cells] = value.astype(bf16)
 
-    @pl.when(a == 0)
-    def _():
-        for copy in all_copies():
-            copy.wait()
-
+    for copy in copies:
+        copy.wait()
     out_ref[...] = jnp.dot(lhs_ref[...], cot_ref[...], preferred_element_type=f32) * scale
 
 
-def weight_two(device, fields, pieces, cots, scale, after):
+def weight_two(a, total, device, fields, pieces, cots, scale, after):
     samples = len(fields)
     planes = fields[0].shape[0]
     cells = planes * CELLS
     block = 9 * C1
     flat = [value for sample in cots for value in sample]
-    return pl.pallas_call(
-        lambda *refs: weight_two_kernel(planes, pieces, scale, *refs),
+    extra = list(after) + ([] if total is None else [total])
+    count = 1 + samples + len(flat) + len(extra)
+    return pl.pallas_call(
+        lambda *refs: weight_two_kernel(a, planes, pieces, scale, *refs),
         grid_spec=pltpu.PrefetchScalarGridSpec(
             num_scalar_prefetch=1,
-            grid=(3,),
+            grid=(1,),
             in_specs=[pl.BlockSpec(field.shape, lambda n, s: (0, 0, 0)) for field in fields]
-            + [pl.BlockSpec(memory_space=pl.ANY)] * (len(flat) + len(after)),
-            out_specs=pl.BlockSpec((block, C2), lambda n, s: (n, 0)),
+            + [pl.BlockSpec(memory_space=pl.ANY)] * (len(flat) + len(extra)),
+            out_specs=pl.BlockSpec((block, C2), lambda n, s: (a, 0)),
             scratch_shapes=[
                 pltpu.VMEM((samples * cells, C2), bf16),
                 pltpu.VMEM((samples, C1, cells), f32),
@@ -382,14 +399,16 @@
             ],
         ),
         out_shape=jax.ShapeDtypeStruct((TAPS * C1, C2), f32),
+        input_output_aliases={} if total is None else {count - 1: 0},
         compiler_params=params(60),
         cost_estimate=pl.CostEstimate(
-            flops=2 * samples * cells * TAPS * C1 * C2, bytes_accessed=18 << 20, transcendentals=0
-        ),
-    )(device, *fields, *flat, *after)
-
-
-def grad_pre_kernel(pieces_ref, slope_ref, lhs_ref, grad_ref, partial_ref, spread_ref, packed_ref):
+            flops=2 * samples * cells * 9 * C1 * C2, bytes_accessed=8 << 20, transcendentals=0
+        ),
+    )(device, *fields, *flat, *extra)
+
+
+def grad_pre_kernel(pieces_ref, slope_ref, lhs_ref, *refs):
+    grad_ref, partial_ref, spread_ref, packed_ref = refs[-4:]
     for r in range(BLOCK):
         for u in range(BLOCK // 2):
             piece = r * BLOCK + 2 * u
@@ -434,10 +453,12 @@
         partial_ref[row] = entry.astype(bf16)
 
 
-def grad_pre_of(pieces, slope, lhs):
+def grad_pre_of(pieces, slope, lhs, after):
     rows = LS * LAT
+    whole = pl.BlockSpec(memory_space=pltpu.VMEM)
     return pl.pallas_call(
         grad_pre_kernel,
+        in_specs=[whole] * 3 + [pl.BlockSpec(memory_space=pl.ANY)] * len(after),
         out_shape=(
             jax.ShapeDtypeStruct((rows, GROUP), bf16),
             jax.ShapeDtypeStruct((C1 // 2, 32, PACK), bf16),
@@ -450,7 +471,7 @@
         cost_estimate=pl.CostEstimate(
             flops=2 * rows * 9 * WINDOW * GROUP, bytes_accessed=3 << 20, transcendentals=0
         ),
-    )(pieces, slope, lhs)
+    )(pieces, slope, lhs, *after)
 
 
 def back_one_kernel(before_ref, own_ref, after_ref, w_ref, out_ref, lhs_ref):
@@ -474,21 +495,41 @@
     )(before, own, after, band)
 
 
-def unpack_kernel(packed_ref, out_ref, wide_ref):
+def sum_kernel(scale, shares_ref, *refs):
+    out_ref = refs[-1]
+    total = jnp.sum(shares_ref[...].astype(f32), axis=0) * scale
+    out_ref[...] = jnp.broadcast_to(total.astype(bf16)[None], out_ref.shape)
+
+
+def sum_shares(shares, scale, after):
+    whole = pl.BlockSpec(memory_space=pltpu.VMEM)
+    return pl.pallas_call(
+        lambda *refs: sum_kernel(scale, *refs),
+        in_specs=[whole] + [pl.BlockSpec(memory_space=pl.ANY)] * len(after),
+        out_shape=jax.ShapeDtypeStruct(shares.shape, bf16),
+        compiler_params=params(16),
+        cost_estimate=pl.CostEstimate(flops=0, bytes_accessed=1 << 20, transcendentals=0),
+    )(shares, *after)
+
+
+def unpack_kernel(packed_ref, *refs):
+    out_ref, wide_ref = refs[-2:]
     wide_ref[...] = packed_ref[...].astype(f32).reshape(wide_ref.shape)
     for t in range(TAPS):
         entry = wide_ref[pl.ds(t, C1 // 2, stride=32), :]
         out_ref[t] = jnp.concatenate([entry[:, :C1], entry[:, C1:]], axis=0)
 
 
-def unpack(packed):
+def unpack(packed, after):
+    whole = pl.BlockSpec(memory_space=pltpu.VMEM)
     return pl.pallas_call(
         unpack_kernel,
+        in_specs=[whole] + [pl.BlockSpec(memory_space=pl.ANY)] * len(after),
         out_shape=jax.ShapeDtypeStruct((TAPS, C1, C1), f32),
         scratch_shapes=[pltpu.VMEM((32 * (C1 // 2), PACK), f32)],
         compiler_params=params(16),
         cost_estimate=pl.CostEstimate(flops=0, bytes_accessed=1 << 20, transcendentals=0),
-    )(packed)
+    )(packed, *after)
 
 
 def neighbours(value, axis):
@@ -521,32 +562,48 @@
 
     core, chip = 1, 2
     outer = list(range(4, shards, 4))
+    before, after = neighbours(own, "depth")
     far = [flipped(cot, difference) for difference in outer]
-    before, after = neighbours(own, "depth")
     cot_chip = flipped(cot, chip)
 
     back_weight = jnp.swapaxes(conv1_weight[::-1], 1, 2)
     band = banded(conv1_weight)
     back_band = banded(back_weight)
-    turned_two = turned_weight(flat_two)
 
     moved, slope, windows = conv_one(before, own, after, band)
     fields = lax.all_to_all(moved, "depth", split_axis=0, concat_axis=0, tiled=True)
 
-    near = jnp.concatenate([cot, cot_chip], axis=0)
-    far = jnp.concatenate(far, axis=0)
-    far_chip = flipped(far, chip)
-    cots = [near, far, far_chip]
-    pieces = [[0, chip], outer, [difference + chip for difference in outer]]
+    first = joined([cot, cot_chip] + far)
+    last = flipped(joined(far), chip)
+    pieces = [[0, chip] + outer, [difference + chip for difference in outer]]
     pieces = pieces + [[difference + core for difference in piece] for piece in pieces]
-
-    partial = conv_two(fields, flat_two)
-    features = lax.psum_scatter(partial, "depth", scatter_dimension=0, tiled=True)
-
-    own_cots = cots + [flipped(value, core) for value in cots]
-    grad_pieces = back_two(device, pieces, own_cots, turned_two, [partial])
-    grad_pieces = lax.all_to_all(grad_pieces, "depth", split_axis=0, concat_axis=0, tiled=True)
-    grad_pre, partial_one = grad_pre_of(grad_pieces, slope, windows)
+    all_cots, all_fields = [], over_samples(fields)
+    for value in zip(over_samples(first), over_samples(last)):
+        all_cots.append(list(value) + [flipped(part, core) for part in value])
+    all_pieces = [pieces] * samples
+
+    send, keep = conv_two(device, fields, flat_two)
+    grad_pieces = back_two(device, pieces, all_cots[0], flat_two, [keep])
+
+    received = flipped(send, core)
+    half = keep.shape[0] // 2
+    partial = keep.astype(f32) + received.astype(f32)
+    received = flipped(partial[half:].astype(bf16), chip)
+    partial = partial[:half] + received.astype(f32)
+    features = partial[:CELLS]
+    for k, difference in enumerate(outer):
+        block = partial[(k + 1) * CELLS : (k + 2) * CELLS].astype(bf16)
+        features = features + flipped(block, difference).astype(f32)
+    features = features.astype(bf16)
+
+    scale_two = 1.0 / math.sqrt(samples * shards * CELLS)
+
+    def weight_part(a, total, after):
+        return weight_two(a, total, device, all_fields, all_pieces, all_cots, scale_two, after)
+
+    returned = lax.all_to_all(grad_pieces, "depth", split_axis=0, concat_axis=0, tiled=True)
+    grad_two = weight_part(0, None, [grad_pieces])
+    grad_pre, partial_one = grad_pre_of(returned, slope, windows, [grad_two])
     grad_before, grad_after = neighbours(grad_pre, "depth")
 
     devices = samples * shards
@@ -554,21 +611,13 @@
     scale_one = 1.0 / math.sqrt(samples * shards * LAT * LAT)
     shares = partial_one.reshape(devices, -1, PACK)
     shares = lax.all_to_all(shares, both, split_axis=0, concat_axis=0, tiled=True)
-    summed = (jnp.sum(shares.astype(f32), axis=0) * scale_one).astype(bf16)
-    summed = jnp.broadcast_to(summed[None], shares.shape)
-    summed = lax.all_to_all(summed, both, split_axis=0, concat_axis=0, tiled=True)
-    grad_conv1 = unpack(summed.reshape(C1 // 2, 32, PACK))
-
+    grad_two = weight_part(1, grad_two, [grad_pre])
+    summed = sum_shares(shares, scale_one, [grad_two])
+    shares = lax.all_to_all(summed, both, split_axis=0, concat_axis=0, tiled=True)
+    grad_two = weight_part(2, grad_two, [summed])
     grad_volume = back_one(grad_before, grad_pre, grad_after, back_band)
-
-    scale_two = 1.0 / math.sqrt(samples * shards * CELLS)
-    half = jnp.concatenate(cots, axis=0)
-    halves = [[difference for piece in group for difference in piece] for group in (pieces[:3], pieces[3:])]
-    all_pieces, all_cots = [pieces], [own_cots]
-    for value in over_samples(half)[1:]:
-        all_pieces.append(halves)
-        all_cots.append([value, flipped(value, core)])
-    grad_conv2 = weight_two(device, over_samples(fields), all_pieces, all_cots, scale_two, [grad_pre])
+    grad_conv1 = unpack(shares.reshape(C1 // 2, 32, PACK), [grad_two])
+    grad_conv2 = grad_two
 
     return (
         features.reshape(cotangent.shape),

time: 141 us -> 203 us (1.44)
  Pallas kernels: 52.2 us -> 88.6 us
  waiting for transfers between devices: 16.9 us -> 41.1 us
  starting transfers between devices: 33.7 us -> 51.1 us
  blocking collectives: 13.7 us -> 0 us
  between operations: 14.3 us -> 1 us
  local copies, waits for them, and re-layouts: 8.45 us -> 15.8 us
  other arithmetic: 0.07 us -> 4.25 us
    pallas_call x5 -> x9, Pallas kernels: 36.4 us -> 72.8 us  [the longest x2 34 us: joined(): pl.pallas_call(lambda *refs: join_kernel(len(values), *refs), in_specs=[p...]
    ppermute x2 -> x3, waiting for transfers between devices: 0.01 us -> 22.7 us  [over_samples(): lax.ppermute(value, 'sample', [(i, (i + shift) % count) for i in range(co...]
    ppermute x9 -> x14, waiting for transfers between devices: 0.02 us -> 15.5 us  [flipped(): lax.ppermute(value, 'depth', [(i, i ^ difference) for i in range(count)])]
    all_to_all x1 -> x0, blocking collectives: 13.7 us -> none  [on_device(): lax.all_to_all(grad_pieces, 'depth', split_axis=0, concat_axis=0, tiled=T...]
    all_to_all x1, waiting for transfers between devices: 10.1 us -> 0.01 us  [on_device(): lax.all_to_all(shares, both, split_axis=0, concat_axis=0, tiled=True)]
    unnamed x28 -> x39, local copies, waits for them, and re-layouts: 6.91 us -> 15.6 us
    all_to_all x1, starting transfers between devices: 2.59 us -> 7.94 us  [on_device(): lax.all_to_all(summed, both, split_axis=0, concat_axis=0, tiled=True)]
    all_to_all x0 -> x1, starting transfers between devices: none -> 3.85 us  [on_device(): lax.all_to_all(grad_pieces, 'depth', split_axis=0, concat_axis=0, tiled=T...]
  transfers between devices with their start and end apart: 19 -> 25, of which waited for: 4 -> 6; matrix products, arithmetic and copies ran while one was open for 4% -> 2% of each run, Pallas kernels for 37% -> 42%
where the time goes in v3:
time: 203 us; the launch traced here: 202 us
  Pallas kernels  88.6 us (44%)
  starting transfers between devices  51.1 us (25%)
  waiting for transfers between devices  41.1 us (20%)
  local copies, waits for them, and re-layouts  15.8 us (8%)
  other arithmetic  4.25 us (2%)
    pallas_call x2, Pallas kernels, joined(): pl.pallas_call(lambda *refs: join_kernel(len(values), *refs), in_specs=[p...  34 us
    pallas_call x3, Pallas kernels, weight_two(): pl.pallas_call(lambda *refs: weight_two_kernel(a, planes, pieces, scale,...  24.8 us
    ppermute x3, waiting for transfers between devices, over_samples(): lax.ppermute(value, 'sample', [(i, (i + shift) % count) for i in range(co...  22.7 us
    unnamed x39, local copies, waits for them, and re-layouts  15.6 us
    ppermute x14, waiting for transfers between devices, flipped(): lax.ppermute(value, 'depth', [(i, i ^ difference) for i in range(count)])  15.5 us
    ppermute x14, starting transfers between devices, flipped(): lax.ppermute(value, 'depth', [(i, i ^ difference) for i in range(count)])  14.9 us
    pallas_call x1, Pallas kernels, back_two(): pl.pallas_call(lambda *refs: back_two_kernel(planes, pieces, *refs), grid...  12 us
    all_to_all x1, starting transfers between devices, on_device(): lax.all_to_all(moved, 'depth', split_axis=0, concat_axis=0, tiled=True)  8.97 us
  transfers between devices with their start and end apart: 25, of which 6 were waited for; matrix products, arithmetic and copies ran while one was open for 2% of the time, Pallas kernels for 42%

profile of v3, /device:TPU:0, one launch (start us, length us, event | category | flops | bytes accessed | tf_op | source)
XLA Modules:
  0.0 201.8 jit_solution(422803113394246449)
XLA Ops:
  0.6 2.4 %collective-permute-start = (bf16[32,2048]{1,0:T(8,128)(2,1)}, bf16[32,2048]{1,0:T(8,128)(2,1)S(1)}, u32[]{:S(2)}, u32[]{:S(2)}) collective-permute-start(bf16[32,2048]{1,0:T(8,128)(2,1)} %bitcast.11), channel_id=1, source_target_pairs={{0,1},{1,2},{2,3},{3,4},{4,5},{5,6},{6,7},{7,8},{8,9},{9,10},{10,1... | collective-permute-start | bytes 393224 | tf_op jit(solution)/shard_map/ppermute | solution.py:537
  5.7 2.9 %collective-permute-done.1.after_ref = bf16[32,2048]{1,0:T(8,128)(2,1)S(1)} collective-permute-done((bf16[32,2048]{1,0:T(8,128)(2,1)}, bf16[32,2048]{1,0:T(8,128)(2,1)S(1)}, u32[]{:S(2)}, u32[]{:S(2)}) %collective-permute-start.1) | collective-permute-done | bytes 131104 | tf_op jit(solution)/shard_map/ppermute | solution.py:538
  10.3 9.0 %all-to-all-start = ((bf16[16,32,128]{2,1,0:T(8,128)(2,1)}), bf16[16,32,128]{2,1,0:T(8,128)(2,1)S(1)}, u32[]{:S(2)}, u32[]{:S(2)}) async-start(bf16[16,32,128]{2,1,0:T(8,128)(2,1)} %get-tuple-element.11), calls=%async_computation | async-start | bytes 262144 | tf_op jit(solution)/shard_map/all_to_all | solution.py:574
  21.3 2.4 %collective-permute-start.9 = (bf16[64,1024]{1,0:T(8,128)(2,1)S(1)}, bf16[64,1024]{1,0:T(8,128)(2,1)S(1)}, u32[]{:S(2)}, u32[]{:S(2)}) collective-permute-start(bf16[64,1024]{1,0:T(8,128)(2,1)S(1)} %bitcast.16), channel_id=1, source_target_pairs={{0,8},{1,9},{2,10},{3,11},{4,12},{5,13},{6,14},{7,15},{8,0},{9,1},... | collective-permute-start | bytes 393224 | tf_op jit(solution)/shard_map/ppermute | solution.py:544
  25.7 4.4 %collective-permute-done.8.refs_2_.refs_0_ = bf16[64,1024]{1,0:T(8,128)(2,1)S(1)} collective-permute-done((bf16[64,1024]{1,0:T(8,128)(2,1)S(1)}, bf16[64,1024]{1,0:T(8,128)(2,1)S(1)}, u32[]{:S(2)}, u32[]{:S(2)}) %collective-permute-start.8) | collective-permute-done | bytes 131104 | tf_op jit(solution)/shard_map/ppermute | solution.py:544
  30.1 4.9 %collective-permute-done.9.refs_3_.refs_1_ = bf16[64,1024]{1,0:T(8,128)(2,1)S(1)} collective-permute-done((bf16[64,1024]{1,0:T(8,128)(2,1)S(1)}, bf16[64,1024]{1,0:T(8,128)(2,1)S(1)}, u32[]{:S(2)}, u32[]{:S(2)}) %collective-permute-start.9) | collective-permute-done | bytes 131104 | tf_op jit(solution)/shard_map/ppermute | solution.py:544
  36.3 13.0 %shard_map.79 = bf16[192,1024]{1,0:T(8,128)(2,1)} custom-call(bf16[64,1024]{1,0:T(8,128)(2,1)} %copy-done.14, bf16[64,1024]{1,0:T(8,128)(2,1)} %copy-done.15, bf16[64,1024]{1,0:T(8,128)(2,1)} %copy-done.16), custom_call_target="tpu_custom_call" | custom-call | bytes 786432 | tf_op jit(solution)/shard_map/pallas_call | solution.py:222
  51.5 8.5 %shard_map.77 = (bf16[512,1024]{1,0:T(8,128)(2,1)}, bf16[512,1024]{1,0:T(8,128)(2,1)}) custom-call(s32[1]{0:T(128)} %bitcast.refs_0_, bf16[16,32,128]{2,1,0:T(8,128)(2,1)} %copy-done.12, bf16[1728,1024]{1,0:T(8,128)(2,1)} %bitcast.20), custom_call_target="tpu_custom_call" | custom-call | flops 3623878656 | bytes 10485760 | tf_op jit(solution)/shard_map/pallas_call | solution.py:180
  60.6 21.0 %shard_map.78.refs_1_.refs_3_ = bf16[320,1024]{1,0:T(8,128)(2,1)} custom-call(bf16[64,1024]{1,0:T(8,128)(2,1)} %bitcast.14, bf16[64,1024]{1,0:T(8,128)(2,1)} %copy-done.18, bf16[64,1024]{1,0:T(8,128)(2,1)} %copy-done.14, bf16[64,1024]{1,0:T(8,128)(2,1)} %copy-done.15, bf16[64,1024]{1,0:T(8,128)(2,1)} %copy-done.16), custom_call_target="tpu_custom_call" | custom-call | bytes 1310720 | tf_op jit(solution)/shard_map/pallas_call | solution.py:222
  85.8 14.3 %collective-permute-done.15.refs_7_ = bf16[320,1024]{1,0:T(8,128)(2,1)} collective-permute-done((bf16[320,1024]{1,0:T(8,128)(2,1)}, bf16[320,1024]{1,0:T(8,128)(2,1)}, u32[]{:S(2)}, u32[]{:S(2)}) %collective-permute-start.15) | collective-permute-done | bytes 655392 | tf_op jit(solution)/shard_map/ppermute | solution.py:550
  100.1 8.4 %collective-permute-done.16.refs_8_ = bf16[192,1024]{1,0:T(8,128)(2,1)} collective-permute-done((bf16[192,1024]{1,0:T(8,128)(2,1)S(1)}, bf16[192,1024]{1,0:T(8,128)(2,1)}, u32[]{:S(2)}, u32[]{:S(2)}) %collective-permute-start.16) | collective-permute-done | bytes 393248 | tf_op jit(solution)/shard_map/ppermute | solution.py:550
  109.3 12.0 %shard_map.80.refs_11_ = bf16[16,32,128]{2,1,0:T(8,128)(2,1)} custom-call(s32[1]{0:T(128)} %bitcast.refs_0_, bf16[320,1024]{1,0:T(8,128)(2,1)} %shard_map.78.refs_1_.refs_3_, bf16[192,1024]{1,0:T(8,128)(2,1)} %copy-done.10, bf16[320,1024]{1,0:T(8,128)(2,1)} %copy-done.9, bf16[192,1024]{1,0:T(8,128)(2,1)} %copy-done.11, bf16[1728,1024]{1,0:T(8,128)(2,1)} %bitcast.21, ...), custom_call_target="tpu_custom_call" | custom-call | flops 3623878656 | bytes 6291456 | tf_op jit(solution)/shard_map/pallas_call | solution.py:309
  121.3 3.8 %all-to-all-start.1 = ((bf16[16,32,128]{2,1,0:T(8,128)(2,1)}), bf16[16,32,128]{2,1,0:T(8,128)(2,1)S(1)}, u32[]{:S(2)}, u32[]{:S(2)}) async-start(bf16[16,32,128]{2,1,0:T(8,128)(2,1)} %shard_map.80.refs_11_), calls=%async_computation.1 | async-start | bytes 262144 | tf_op jit(solution)/shard_map/all_to_all | solution.py:604
  131.1 8.3 %shard_map.81.refs_0_.refs_12_ = f32[1728,1024]{1,0:T(8,128)} custom-call(s32[1]{0:T(128)} %bitcast.refs_0_, bf16[16,32,128]{2,1,0:T(8,128)(2,1)} %copy-done.12, bf16[16,32,128]{2,1,0:T(8,128)(2,1)} %copy-done.13, bf16[320,1024]{1,0:T(8,128)(2,1)} %shard_map.78.refs_1_.refs_3_, bf16[192,1024]{1,0:T(8,128)(2,1)} %copy-done.10, bf16[320,1024]{1,0:T(8,128)(2,1)} %copy-done.9, ...), custom_call_target="tpu_custom_call" | custom-call | flops 2415919104 | bytes 8388608 | tf_op jit(solution)/shard_map/pallas_call | solution.py:386
  139.4 3.0 %copy-done = f32[1728,1024]{1,0:T(8,128)S(1)} copy-done((f32[1728,1024]{1,0:T(8,128)S(1)}, f32[1728,1024]{1,0:T(8,128)}, u32[]{:S(2)}) %copy-start) | copy-done | bytes 7077912
  142.4 3.4 %shard_map.82 = (bf16[256,256]{1,0:T(8,128)(2,1)S(1)}, bf16[32,32,128]{2,1,0:T(8,128)(2,1)}) custom-call(bf16[16,32,128]{2,1,0:T(8,128)(2,1)S(1)} %all-to-all-done.1.pieces_ref, f32[256,256]{1,0:T(8,128)S(1)} %get-tuple-element.14.slope_ref, bf16[256,3456]{1,0:T(8,128)(2,1)S(1)} %get-tuple-element.15.lhs_ref, f32[1728,1024]{1,0:T(8,128)S(1)} %copy-done), custom_call_target="tpu_custom_call" | custom-call | flops 452984832 | bytes 3145728 | tf_op jit(solution)/shard_map/pallas_call | solution.py:459
  145.8 4.6 %all-to-all-start.2 = ((bf16[32,32,128]{2,1,0:T(8,128)(2,1)}), bf16[32,32,128]{2,1,0:T(8,128)(2,1)S(1)}, u32[]{:S(2)}, u32[]{:S(2)}) async-start(bf16[32,32,128]{2,1,0:T(8,128)(2,1)} %get-tuple-element.17), calls=%async_computation.2 | async-start | bytes 524288 | tf_op jit(solution)/shard_map/all_to_all | solution.py:613
  154.8 8.3 %shard_map.85.refs_1_.refs_12_ = f32[1728,1024]{1,0:T(8,128)} custom-call(s32[1]{0:T(128)} %bitcast.refs_0_, bf16[16,32,128]{2,1,0:T(8,128)(2,1)} %copy-done.12, bf16[16,32,128]{2,1,0:T(8,128)(2,1)} %copy-done.13, bf16[320,1024]{1,0:T(8,128)(2,1)} %shard_map.78.refs_1_.refs_3_, bf16[192,1024]{1,0:T(8,128)(2,1)} %copy-done.10, ...), custom_call_target="tpu_custom_call", output_to_operand_aliasing={{}: (12, {})} | custom-call | flops 2415919104 | bytes 8388608 | tf_op jit(solution)/shard_map/pallas_call | solution.py:386
  164.4 3.0 %copy-done.1 = f32[1728,1024]{1,0:T(8,128)S(1)} copy-done((f32[1728,1024]{1,0:T(8,128)S(1)}, f32[1728,1024]{1,0:T(8,128)}, u32[]{:S(2)}) %copy-start.1) | copy-done | bytes 7077912
  168.2 7.9 %all-to-all-start.3 = ((bf16[32,32,128]{2,1,0:T(8,128)(2,1)}), bf16[32,32,128]{2,1,0:T(8,128)(2,1)S(1)}, u32[]{:S(2)}, u32[]{:S(2)}) async-start(bf16[32,32,128]{2,1,0:T(8,128)(2,1)} %shard_map.86.refs_11_), calls=%async_computation.3 | async-start | bytes 524288 | tf_op jit(solution)/shard_map/all_to_all | solution.py:616
  177.8 3.7 %collective-permute-start.6 = (bf16[64,1024]{1,0:T(8,128)(2,1)S(1)}, bf16[64,1024]{1,0:T(8,128)(2,1)S(1)}, u32[]{:S(2)}, u32[]{:S(2)}) collective-permute-start(bf16[64,1024]{1,0:T(8,128)(2,1)S(1)} %get-tuple-element.21), channel_id=1, source_target_pairs={{0,12},{1,13},{2,14},{3,15},{4,8},{5,9},{6,10},{7,11},{8,4},{9,5},... | collective-permute-start | bytes 393224 | tf_op jit(solution)/shard_map/ppermute | solution.py:544
  182.3 8.3 %shard_map.87.refs_0_ = f32[1728,1024]{1,0:T(8,128)} custom-call(s32[1]{0:T(128)} %bitcast.refs_0_, bf16[16,32,128]{2,1,0:T(8,128)(2,1)} %copy-done.12, bf16[16,32,128]{2,1,0:T(8,128)(2,1)} %copy-done.13, bf16[320,1024]{1,0:T(8,128)(2,1)} %shard_map.78.refs_1_.refs_3_, bf16[192,1024]{1,0:T(8,128)(2,1)} %copy-done.10, ...), custom_call_target="tpu_custom_call", output_to_operand_aliasing={{}: (12, {})} | custom-call | flops 2415919104 | bytes 8388608 | tf_op jit(solution)/shard_map/pallas_call | solution.py:386
  190.6 6.2 %collective-permute-done.5 = bf16[64,1024]{1,0:T(8,128)(2,1)S(1)} collective-permute-done((bf16[64,1024]{1,0:T(8,128)(2,1)S(1)}, bf16[64,1024]{1,0:T(8,128)(2,1)S(1)}, u32[]{:S(2)}, u32[]{:S(2)}) %collective-permute-start.5) | collective-permute-done | bytes 131104 | tf_op jit(solution)/shard_map/ppermute | solution.py:544
  197.5 3.0 %copy-done.2 = f32[1728,1024]{1,0:T(8,128)S(1)} copy-done((f32[1728,1024]{1,0:T(8,128)S(1)}, f32[1728,1024]{1,0:T(8,128)}, u32[]{:S(2)}) %copy-start.2) | copy-done | bytes 7077912
  (85 shorter events, 34.3 us)
Async XLA Ops:
  0.6 5.1 %collective-permute-start = (bf16[32,2048]{1,0:T(8,128)(2,1)}, bf16[32,2048]{1,0:T(8,128)(2,1)S(1)}, u32[]{:S(2)}, u32[]{:S(2)}) collective-permute-start(bf16[32,2048]{1,0:T(8,128)(2,1)} %bitcast.11), channel_id=1, source_target_pairs={{0,1},{1,2},{2,3},{3,4},{4,5},{5,6},{6,7},{7,8},{8,9},{9,10},{10,1... | collective-permute-start | bytes 393224 | tf_op jit(solution)/shard_map/ppermute | solution.py:537
  3.0 5.6 %collective-permute-start.1 = (bf16[32,2048]{1,0:T(8,128)(2,1)}, bf16[32,2048]{1,0:T(8,128)(2,1)S(1)}, u32[]{:S(2)}, u32[]{:S(2)}) collective-permute-start(bf16[32,2048]{1,0:T(8,128)(2,1)} %bitcast.12), channel_id=1, source_target_pairs={{1,0},{2,1},{3,2},{4,3},{5,4},{6,5},{7,6},{8,7},{9,8},{10,9},{11,1... | collective-permute-start | bytes 393224 | tf_op jit(solution)/shard_map/ppermute | solution.py:538
  10.3 40.5 %all-to-all-start = ((bf16[16,32,128]{2,1,0:T(8,128)(2,1)}), bf16[16,32,128]{2,1,0:T(8,128)(2,1)S(1)}, u32[]{:S(2)}, u32[]{:S(2)}) async-start(bf16[16,32,128]{2,1,0:T(8,128)(2,1)} %get-tuple-element.11), calls=%async_computation | async-start | bytes 262144 | tf_op jit(solution)/shard_map/all_to_all | solution.py:574
  19.3 10.8 %collective-permute-start.8 = (bf16[64,1024]{1,0:T(8,128)(2,1)S(1)}, bf16[64,1024]{1,0:T(8,128)(2,1)S(1)}, u32[]{:S(2)}, u32[]{:S(2)}) collective-permute-start(bf16[64,1024]{1,0:T(8,128)(2,1)S(1)} %bitcast.15), channel_id=1, source_target_pairs={{0,4},{1,5},{2,6},{3,7},{4,0},{5,1},{6,2},{7,3},{8,12},{9,13},{10,... | collective-permute-start | bytes 393224 | tf_op jit(solution)/shard_map/ppermute | solution.py:544
  21.3 13.7 %collective-permute-start.9 = (bf16[64,1024]{1,0:T(8,128)(2,1)S(1)}, bf16[64,1024]{1,0:T(8,128)(2,1)S(1)}, u32[]{:S(2)}, u32[]{:S(2)}) collective-permute-start(bf16[64,1024]{1,0:T(8,128)(2,1)S(1)} %bitcast.16), channel_id=1, source_target_pairs={{0,8},{1,9},{2,10},{3,11},{4,12},{5,13},{6,14},{7,15},{8,0},{9,1},... | collective-permute-start | bytes 393224 | tf_op jit(solution)/shard_map/ppermute | solution.py:544
  23.6 11.3 %collective-permute-start.10 = (bf16[64,1024]{1,0:T(8,128)(2,1)S(1)}, bf16[64,1024]{1,0:T(8,128)(2,1)S(1)}, u32[]{:S(2)}, u32[]{:S(2)}) collective-permute-start(bf16[64,1024]{1,0:T(8,128)(2,1)S(1)} %bitcast.17), channel_id=1, source_target_pairs={{0,12},{1,13},{2,14},{3,15},{4,8},{5,9},{6,10},{7,11},{8,4},{9,5},... | collective-permute-start | bytes 393224 | tf_op jit(solution)/shard_map/ppermute | solution.py:544
  23.7 36.2 %collective-permute-start.7 = (bf16[64,1024]{1,0:T(8,128)(2,1)S(1)}, bf16[64,1024]{1,0:T(8,128)(2,1)S(1)}, u32[]{:S(2)}, u32[]{:S(2)}) collective-permute-start(bf16[64,1024]{1,0:T(8,128)(2,1)S(1)} %bitcast.18), channel_id=1, source_target_pairs={{0,2},{1,3},{2,0},{3,1},{4,6},{5,7},{6,4},{7,5},{8,10},{9,11},{10,... | collective-permute-start | bytes 393224 | tf_op jit(solution)/shard_map/ppermute | solution.py:544
  49.3 34.4 %collective-permute-start.11 = (bf16[192,1024]{1,0:T(8,128)(2,1)}, bf16[192,1024]{1,0:T(8,128)(2,1)S(1)}, u32[]{:S(2)}, u32[]{:S(2)}) collective-permute-start(bf16[192,1024]{1,0:T(8,128)(2,1)} %shard_map.79), channel_id=1, source_target_pairs={{0,2},{1,3},{2,0},{3,1},{4,6},{5,7},{6,4},{7,5},{8,10},{9,11},{10,... | collective-permute-start | bytes 1179656 | tf_op jit(solution)/shard_map/ppermute | solution.py:544
  59.9 65.2 %collective-permute-start.2 = (bf16[512,1024]{1,0:T(8,128)(2,1)}, bf16[512,1024]{1,0:T(8,128)(2,1)}, u32[]{:S(2)}, u32[]{:S(2)}) collective-permute-start(bf16[512,1024]{1,0:T(8,128)(2,1)} %get-tuple-element.13), channel_id=1, source_target_pairs={{0,1},{1,0},{2,3},{3,2},{4,5},{5,4},{6,7},{7,6},{8,9},{9,8},{10,11... | collective-permute-start | bytes 3145736 | tf_op jit(solution)/shard_map/ppermute | solution.py:544
  82.2 17.9 %collective-permute-start.15 = (bf16[320,1024]{1,0:T(8,128)(2,1)}, bf16[320,1024]{1,0:T(8,128)(2,1)}, u32[]{:S(2)}, u32[]{:S(2)}) collective-permute-start(bf16[320,1024]{1,0:T(8,128)(2,1)} %shard_map.78.refs_1_.refs_3_), channel_id=1, source_target_pairs={{0,16},{16,0},{1,17},{17,1},{2,18},{18,2},{3,19},{19,3},{4,20},{20... | collective-permute-start | bytes 1966088 | tf_op jit(solution)/shard_map/ppermute | solution.py:550
  83.7 24.8 %collective-permute-start.16 = (bf16[192,1024]{1,0:T(8,128)(2,1)S(1)}, bf16[192,1024]{1,0:T(8,128)(2,1)}, u32[]{:S(2)}, u32[]{:S(2)}) collective-permute-start(bf16[192,1024]{1,0:T(8,128)(2,1)S(1)} %collective-permute-done.11.refs_2_.refs_4_), channel_id=1, source_target_pairs={{0,16},{16,0},{1,17},{17,1},{2,18},{18,2},{3,19},{19,3},{4,20},{20... | collective-permute-start | bytes 1179656 | tf_op jit(solution)/shard_map/ppermute | solution.py:550
  84.2 24.3 %collective-permute-start.13 = (bf16[192,1024]{1,0:T(8,128)(2,1)S(1)}, bf16[192,1024]{1,0:T(8,128)(2,1)S(1)}, u32[]{:S(2)}, u32[]{:S(2)}) collective-permute-start(bf16[192,1024]{1,0:T(8,128)(2,1)S(1)} %collective-permute-done.11.refs_2_.refs_4_), channel_id=1, source_target_pairs={{0,1},{1,0},{2,3},{3,2},{4,5},{5,4},{6,7},{7,6},{8,9},{9,8},{10,11... | collective-permute-start | bytes 1179656 | tf_op jit(solution)/shard_map/ppermute | solution.py:544
  84.2 46.3 %collective-permute-start.14 = (bf16[16,32,128]{2,1,0:T(8,128)(2,1)}, bf16[16,32,128]{2,1,0:T(8,128)(2,1)S(1)}, u32[]{:S(2)}, u32[]{:S(2)}) collective-permute-start(bf16[16,32,128]{2,1,0:T(8,128)(2,1)} %copy-done.12), channel_id=1, source_target_pairs={{0,16},{16,0},{1,17},{17,1},{2,18},{18,2},{3,19},{19,3},{4,20},{20... | collective-permute-start | bytes 393224 | tf_op jit(solution)/shard_map/ppermute | solution.py:550
  100.1 30.4 %collective-permute-start.17 = (bf16[320,1024]{1,0:T(8,128)(2,1)}, bf16[320,1024]{1,0:T(8,128)(2,1)}, u32[]{:S(2)}, u32[]{:S(2)}) collective-permute-start(bf16[320,1024]{1,0:T(8,128)(2,1)} %collective-permute-done.15.refs_7_), channel_id=1, source_target_pairs={{0,1},{1,0},{2,3},{3,2},{4,5},{5,4},{6,7},{7,6},{8,9},{9,8},{10,11... | collective-permute-start | bytes 1966088 | tf_op jit(solution)/shard_map/ppermute | solution.py:544
  108.5 22.0 %collective-permute-start.18 = (bf16[192,1024]{1,0:T(8,128)(2,1)}, bf16[192,1024]{1,0:T(8,128)(2,1)}, u32[]{:S(2)}, u32[]{:S(2)}) collective-permute-start(bf16[192,1024]{1,0:T(8,128)(2,1)} %collective-permute-done.16.refs_8_), channel_id=1, source_target_pairs={{0,1},{1,0},{2,3},{3,2},{4,5},{5,4},{6,7},{7,6},{8,9},{9,8},{10,11... | collective-permute-start | bytes 1179656 | tf_op jit(solution)/shard_map/ppermute | solution.py:544
  121.3 18.1 %all-to-all-start.1 = ((bf16[16,32,128]{2,1,0:T(8,128)(2,1)}), bf16[16,32,128]{2,1,0:T(8,128)(2,1)S(1)}, u32[]{:S(2)}, u32[]{:S(2)}) async-start(bf16[16,32,128]{2,1,0:T(8,128)(2,1)} %shard_map.80.refs_11_), calls=%async_computation.1 | async-start | bytes 262144 | tf_op jit(solution)/shard_map/all_to_all | solution.py:604
  128.5 47.7 %collective-permute-start.3 = (bf16[256,1024]{1,0:T(8,128)(2,1)S(1)}, bf16[256,1024]{1,0:T(8,128)(2,1)}, u32[]{:S(2)}, u32[]{:S(2)}) collective-permute-start(bf16[256,1024]{1,0:T(8,128)(2,1)S(1)} %slice.45), channel_id=1, source_target_pairs={{0,2},{1,3},{2,0},{3,1},{4,6},{5,7},{6,4},{7,5},{8,10},{9,11},{10,... | collective-permute-start | bytes 1572872 | tf_op jit(solution)/shard_map/ppermute | solution.py:544
  145.8 18.6 %all-to-all-start.2 = ((bf16[32,32,128]{2,1,0:T(8,128)(2,1)}), bf16[32,32,128]{2,1,0:T(8,128)(2,1)S(1)}, u32[]{:S(2)}, u32[]{:S(2)}) async-start(bf16[32,32,128]{2,1,0:T(8,128)(2,1)} %get-tuple-element.17), calls=%async_computation.2 | async-start | bytes 524288 | tf_op jit(solution)/shard_map/all_to_all | solution.py:613
  151.1 11.9 %collective-permute-start.19 = (bf16[256,256]{1,0:T(8,128)(2,1)S(1)}, bf16[256,256]{1,0:T(8,128)(2,1)S(1)}, u32[]{:S(2)}, u32[]{:S(2)}) collective-permute-start(bf16[256,256]{1,0:T(8,128)(2,1)S(1)} %get-tuple-element.16.own_ref.refs_11_), channel_id=1, source_target_pairs={{0,1},{1,2},{2,3},{3,4},{4,5},{5,6},{6,7},{7,8},{8,9},{9,10},{10,1... | collective-permute-start | bytes 393224 | tf_op jit(solution)/shard_map/ppermute | solution.py:537
  153.3 9.8 %collective-permute-start.20 = (bf16[256,256]{1,0:T(8,128)(2,1)S(1)}, bf16[256,256]{1,0:T(8,128)(2,1)S(1)}, u32[]{:S(2)}, u32[]{:S(2)}) collective-permute-start(bf16[256,256]{1,0:T(8,128)(2,1)S(1)} %get-tuple-element.16.own_ref.refs_11_), channel_id=1, source_target_pairs={{1,0},{2,1},{3,2},{4,3},{5,4},{6,5},{7,6},{8,7},{9,8},{10,9},{11,1... | collective-permute-start | bytes 393224 | tf_op jit(solution)/shard_map/ppermute | solution.py:538
  168.2 29.3 %all-to-all-start.3 = ((bf16[32,32,128]{2,1,0:T(8,128)(2,1)}), bf16[32,32,128]{2,1,0:T(8,128)(2,1)S(1)}, u32[]{:S(2)}, u32[]{:S(2)}) async-start(bf16[32,32,128]{2,1,0:T(8,128)(2,1)} %shard_map.86.refs_11_), calls=%async_computation.3 | async-start | bytes 524288 | tf_op jit(solution)/shard_map/all_to_all | solution.py:616
  177.8 12.7 %collective-permute-start.6 = (bf16[64,1024]{1,0:T(8,128)(2,1)S(1)}, bf16[64,1024]{1,0:T(8,128)(2,1)S(1)}, u32[]{:S(2)}, u32[]{:S(2)}) collective-permute-start(bf16[64,1024]{1,0:T(8,128)(2,1)S(1)} %get-tuple-element.21), channel_id=1, source_target_pairs={{0,12},{1,13},{2,14},{3,15},{4,8},{5,9},{6,10},{7,11},{8,4},{9,5},... | collective-permute-start | bytes 393224 | tf_op jit(solution)/shard_map/ppermute | solution.py:544
  181.5 15.3 %collective-permute-start.5 = (bf16[64,1024]{1,0:T(8,128)(2,1)S(1)}, bf16[64,1024]{1,0:T(8,128)(2,1)S(1)}, u32[]{:S(2)}, u32[]{:S(2)}) collective-permute-start(bf16[64,1024]{1,0:T(8,128)(2,1)S(1)} %get-tuple-element.22), channel_id=1, source_target_pairs={{0,8},{1,9},{2,10},{3,11},{4,12},{5,13},{6,14},{7,15},{8,0},{9,1},... | collective-permute-start | bytes 393224 | tf_op jit(solution)/shard_map/ppermute | solution.py:544
  181.5 15.3 %collective-permute-start.4 = (bf16[64,1024]{1,0:T(8,128)(2,1)S(1)}, bf16[64,1024]{1,0:T(8,128)(2,1)S(1)}, u32[]{:S(2)}, u32[]{:S(2)}) collective-permute-start(bf16[64,1024]{1,0:T(8,128)(2,1)S(1)} %get-tuple-element.20), channel_id=1, source_target_pairs={{0,4},{1,5},{2,6},{3,7},{4,0},{5,1},{6,2},{7,3},{8,12},{9,13},{10,... | collective-permute-start | bytes 393224 | tf_op jit(solution)/shard_map/ppermute | solution.py:544
  (20 other events, 113.0 us)

commit v4 on v2

--- a/solution.py
+++ b/solution.py
@@ -125,54 +125,37 @@
     return jnp.where(column == edge, 0.0, pltpu.roll(field, (-step) % LS, 1))
 
 
-def turn_weight_kernel(rows, x_ref, out_ref):
-    block = x_ref.shape[0]
-    row = lax.broadcasted_iota(jnp.int32, x_ref.shape, 0) + block * pl.program_id(0)
-    out_ref[...] = jnp.where(row < rows, x_ref[...].astype(f32), 0.0).astype(bf16).T
-
-
-def turned_weight(weight, block=256):
-    rows, columns = weight.shape
-    steps = pl.cdiv(rows, block)
-    return pl.pallas_call(
-        lambda *refs: turn_weight_kernel(rows, *refs),
-        grid=(steps,),
-        in_specs=[pl.BlockSpec((block, columns), lambda n: (n, 0))],
-        out_specs=pl.BlockSpec((columns, block), lambda n: (0, n)),
-        out_shape=jax.ShapeDtypeStruct((columns, steps * block), weight.dtype),
-        compiler_params=params(56),
-        cost_estimate=pl.CostEstimate(flops=0, bytes_accessed=16 << 20, transcendentals=0),
-    )(weight)
-
-
-def conv_two_kernel(planes, x_ref, w_ref, out_ref, lhs_ref, v_ref):
+def shift_rows(field, step):
+    if step == 0:
+        return field
+    blank = jnp.zeros((1,) + field.shape[1:], field.dtype)
+    parts = [field[1:], blank] if step > 0 else [blank, field[:-1]]
+    return jnp.concatenate(parts, axis=0)
+
+
+def conv_two_kernel(planes, x_ref, w_ref, out_ref, lhs_ref):
+    cells = planes * CELLS
+    lateral = 9 * C1
+
     @pl.when(pl.program_id(0) == 0)
     def _():
-        v_ref[:, :, 0] = jnp.zeros((3, 2, LS + 2, LS, PACK), f32)
-        v_ref[:, :, planes + 1] = jnp.zeros((3, 2, LS + 2, LS, PACK), f32)
-        edge = jnp.zeros((LS, PACK), f32)
-
-        def spread(p, carry):
+        lhs_ref[:CELLS] = jnp.zeros((CELLS, lateral), bf16)
+        lhs_ref[cells + CELLS :] = jnp.zeros((CELLS, lateral), bf16)
+
+        def gather(p, carry):
             x = x_ref[p].astype(f32)
             turned = pltpu.roll(x, C1, 1)
-            for half, parts in enumerate(((x, turned), (turned, x))):
-                cells = jnp.concatenate(parts, axis=0).reshape(LS, LS, PACK)
-                for c in range(3):
-                    v_ref[c, half, p + 1, 0] = edge
-                    v_ref[c, half, p + 1, 1 : LS + 1] = shift_cells(cells, c - 1)
-                    v_ref[c, half, p + 1, LS + 1] = edge
-            return carry
-
-        lax.fori_loop(0, planes, spread, 0)
-
-        def gather(p, carry):
-            rows = pl.ds(pl.multiple_of(p * CELLS, CELLS), CELLS)
-            for m in range((TAPS + 1) // 2):
+            halves = []
+            for parts in ((x, turned), (turned, x)):
+                field = jnp.concatenate(parts, axis=0).reshape(LS, LS, PACK)
+                halves.append([shift_cells(field, c - 1) for c in range(3)])
+            rows = pl.ds(pl.multiple_of((p + 1) * CELLS, CELLS), CELLS)
+            for m in range(5):
                 t = 2 * m
-                low = v_ref[t % 3, 0, p + t // 9, pl.ds((t // 3) % 3, LS)].reshape(CELLS, PACK)
+                low = shift_rows(halves[0][t % 3], t // 3 - 1).reshape(CELLS, PACK)
                 t = 2 * m + 1
-                if t < TAPS:
-                    high = v_ref[t % 3, 1, p + t // 9, pl.ds((t // 3) % 3, LS)].reshape(CELLS, PACK)
+                if t < 9:
+                    high = shift_rows(halves[1][t % 3], t // 3 - 1).reshape(CELLS, PACK)
                     tile = jnp.where(low_lanes(low.shape), low, high)
                     lhs_ref[rows, m * PACK : (m + 1) * PACK] = tile.astype(bf16)
                 else:
@@ -181,34 +164,33 @@
 
         lax.fori_loop(0, planes, gather, 0)
 
-    chunk = 4 * CELLS
-    for m in range(planes * CELLS // chunk):
-        rows = slice(m * chunk, (m + 1) * chunk)
-        out_ref[rows] = jnp.dot(lhs_ref[rows], w_ref[...], preferred_element_type=f32).astype(bf16)
-
-
-def conv_two(pieces, weight):
-    planes = pieces.shape[0]
+    total = None
+    for a in range(3):
+        window = lhs_ref[a * CELLS : a * CELLS + cells]
+        term = jnp.dot(window, w_ref[a * lateral : (a + 1) * lateral], preferred_element_type=f32)
+        total = term if total is None else total + term
+    out_ref[...] = total.astype(bf16)
+
+
+def conv_two(fields, weight):
+    planes = fields.shape[0]
     cells = planes * CELLS
-    block = 256
+    block = 512
     return pl.pallas_call(
         lambda *refs: conv_two_kernel(planes, *refs),
         grid=(C2 // block,),
         in_specs=[
-            pl.BlockSpec(pieces.shape, lambda n: (0, 0, 0)),
+            pl.BlockSpec(fields.shape, lambda n: (0, 0, 0)),
             pl.BlockSpec((TAPS * C1, block), lambda n: (0, n)),
         ],
         out_specs=pl.BlockSpec((cells, block), lambda n: (0, n)),
         out_shape=jax.ShapeDtypeStruct((cells, C2), bf16),
-        scratch_shapes=[
-            pltpu.VMEM((cells, TAPS * C1), bf16),
-            pltpu.VMEM((3, 2, planes + 2, LS + 2, LS, PACK), f32),
-        ],
+        scratch_shapes=[pltpu.VMEM((cells + 2 * CELLS, 9 * C1), bf16)],
         compiler_params=params(56),
         cost_estimate=pl.CostEstimate(
             flops=2 * cells * TAPS * C1 * C2, bytes_accessed=10 << 20, transcendentals=0
         ),
-    )(pieces, weight)
+    )(fields, weight)
 
 
 def plane_copies(device, pieces, refs, target_ref, base, sems):
@@ -218,65 +200,49 @@
             row = pl.multiple_of(base + (device ^ difference) * CELLS, CELLS)
             source = ref.at[pl.ds(k * CELLS, CELLS), :]
             target = target_ref.at[pl.ds(row, CELLS), :]
-            copies.append(pltpu.make_async_copy(source, target, sems.at[base // CELLS + len(copies)]))
+            copies.append(pltpu.make_async_copy(source, target, sems.at[len(copies)]))
     return copies
 
 
 def back_two_kernel(planes, pieces, device_ref, *refs):
     cot_refs = refs[: len(pieces)]
-    w_ref, out_ref, cot_ref, product_ref, sems = refs[len(pieces)], *refs[-4:]
-    step = pl.program_id(0)
-    tiles = product_ref.shape[0]
-
-    @pl.when(step == 0)
+    w_ref, out_ref, cot_ref, sum_ref, sems = refs[len(pieces)], *refs[-4:]
+    b = pl.program_id(0)
+    cells = planes * CELLS
+
+    @pl.when(b == 0)
     def _():
-        copies = plane_copies(device_ref[0], pieces, cot_refs, cot_ref, 0, sems)
+        copies = plane_copies(device_ref[0], pieces, cot_refs, cot_ref, CELLS, sems)
         for copy in copies:
             copy.start()
-        empty_plane = jnp.zeros((LS + 2, LS, PACK), f32)
-        empty_row = jnp.zeros((planes, LS, PACK), f32)
-        for m in range(tiles):
-            product_ref[m, 0] = empty_plane
-            product_ref[m, planes + 1] = empty_plane
-            product_ref[m, 1 : planes + 1, 0] = empty_row
-            product_ref[m, 1 : planes + 1, LS + 1] = empty_row
+        cot_ref[:CELLS] = jnp.zeros((CELLS, C2), bf16)
+        cot_ref[cells + CELLS :] = jnp.zeros((CELLS, C2), bf16)
+        sum_ref[...] = jnp.zeros(sum_ref.shape, f32)
         for copy in copies:
             copy.wait()
 
-    wide = w_ref.shape[1] // PACK
-    slab = planes // 4
-    for m in range(4):
-        product = jnp.dot(
-            cot_ref[m * slab * CELLS : (m + 1) * slab * CELLS], w_ref[...], preferred_element_type=f32
+    total = None
+    for a in range(3):
+        term = lax.dot_general(
+            cot_ref[(2 - a) * CELLS : (2 - a) * CELLS + cells],
+            w_ref[a],
+            (((1,), (1,)), ((), ())),
+            preferred_element_type=f32,
         )
-        for u in range(wide):
-            tile = product[:, u * PACK : (u + 1) * PACK].reshape(slab, LS, LS, PACK)
-            product_ref[wide * step + u, 1 + m * slab : 1 + (m + 1) * slab, 1 : LS + 1] = tile
-
-    @pl.when(step == pl.num_programs(0) - 1)
+        total = term if total is None else total + term
+    rows = pl.ds(b, LS)
+    first = total[:, :PACK].reshape(planes, LS, LS, PACK)
+    sum_ref[0, :, rows] = sum_ref[0, :, rows] + first
+    last = jnp.concatenate([total[:, PACK:], jnp.zeros((cells, C1), f32)], axis=1)
+    sum_ref[1, :, rows] = sum_ref[1, :, rows] + last.reshape(planes, LS, LS, PACK)
+
+    @pl.when(b == 2)
     def _():
         def finish(p, carry):
-            sums = {}
-            for m in range(tiles):
-                taps = [t for t in (2 * m, 2 * m + 1) if t < TAPS]
-                for k, t in enumerate(taps):
-                    a, b = t // 9, (t // 3) % 3
-                    same = len(taps) == 2 and taps[0] // 3 == taps[1] // 3
-                    if same and k == 1:
-                        continue
-                    key = (t % 3, t % 3 + 1) if same else ((t % 3, None) if k == 0 else (None, t % 3))
-                    tile = product_ref[m, p + 2 - a, 2 - b : 2 - b + LS]
-                    sums[key] = tile if key not in sums else sums[key] + tile
-            total = None
-            for half in range(2):
-                part = None
-                for c in range(3):
-                    found = [value for key, value in sums.items() if key[half] == c]
-                    for value in found:
-                        term = shift_cells(value, 1 - c)
-                        part = term if part is None else part + term
-                part = part.reshape(CELLS, PACK)
-                total = part if half == 0 else total + pltpu.roll(part, C1, 1)
+            pair = sum_ref[0, p, 1 : LS + 1]
+            single = sum_ref[1, p, 1 : LS + 1]
+            total = shift_cells(pair, 1) + shift_cells(single, -1)
+            total = total.reshape(CELLS, PACK) + pltpu.roll(pair.reshape(CELLS, PACK), C1, 1)
             top, bottom = total[: CELLS // 2], total[CELLS // 2 :]
             out_ref[p] = jnp.where(low_lanes(top.shape), top, pltpu.roll(bottom, C1, 1)).astype(bf16)
             return carry
@@ -286,20 +252,18 @@
 
 def back_two(device, pieces, cots, weight, after):
     planes = sum(len(piece) for piece in pieces)
-    block = 256
-    tiles = weight.shape[1] // PACK
     return pl.pallas_call(
         lambda *refs: back_two_kernel(planes, pieces, *refs),
         grid_spec=pltpu.PrefetchScalarGridSpec(
             num_scalar_prefetch=1,
-            grid=(weight.shape[1] // block,),
+            grid=(3,),
             in_specs=[pl.BlockSpec(memory_space=pl.ANY)] * len(cots)
-            + [pl.BlockSpec((C2, block), lambda n, s: (0, n))]
+            + [pl.BlockSpec((3, 3 * C1, C2), lambda n, s: (0, n, 0))]
             + [pl.BlockSpec(memory_space=pl.ANY)] * len(after),
             out_specs=pl.BlockSpec((planes, CELLS // 2, PACK), lambda n, s: (0, 0, 0)),
             scratch_shapes=[
-                pltpu.VMEM((planes * CELLS, C2), bf16),
-                pltpu.VMEM((tiles, planes + 2, LS + 2, LS, PACK), f32),
+                pltpu.VMEM(((planes + 2) * CELLS, C2), bf16),
+                pltpu.VMEM((2, planes, LS + 2, LS, PACK), f32),
                 pltpu.SemaphoreType.DMA((planes,)),
             ],
         ),
@@ -308,7 +272,7 @@
         cost_estimate=pl.CostEstimate(
             flops=2 * planes * CELLS * TAPS * C1 * C2, bytes_accessed=6 << 20, transcendentals=0
         ),
-    )(device, *cots, weight, *after)
+    )(device, *cots, weight.reshape(3, 9 * C1, C2), *after)
 
 
 def weight_two_kernel(planes, pieces, scale, device_ref, *refs):
@@ -318,19 +282,18 @@
     cells = planes * CELLS
     a = pl.program_id(0)
 
-    def all_copies():
+    @pl.when(a == 0)
+    def _():
         copies, first = [], 0
         for s in range(samples):
             refs_here = cot_refs[first : first + len(pieces[s])]
-            copies += plane_copies(device_ref[0], pieces[s], refs_here, cot_ref, s * cells, sems)
+            copies += plane_copies(device_ref[0], pieces[s], refs_here, cot_ref.at[s], CELLS, sems.at[s])
             first += len(pieces[s])
-        return copies
-
-    @pl.when(a == 0)
-    def _():
-        for copy in all_copies():
+        for copy in copies:
             copy.start()
         for s in range(samples):
+            cot_ref[s, :CELLS] = jnp.zeros((CELLS, C2), bf16)
+            cot_ref[s, cells + CELLS :] = jnp.zeros((CELLS, C2), bf16)
 
             def cells_of(p):
                 x = field_refs[s][p].astype(f32)
@@ -340,24 +303,28 @@
                 pair = jnp.concatenate([cells_of(2 * j), cells_of(2 * j + 1)], axis=0)
                 flat_ref[s, :, j * PACK : (j + 1) * PACK] = pair.T[:C1]
 
-    lane = lax.broadcasted_iota(jnp.int32, (C1, cells), 1)
-    plane, row, column = lane // CELLS, (lane // LS) % LS, lane % LS
-    deep = (plane + a >= 1) & (plane + a <= planes)
-    for b in range(3):
-        for c in range(3):
-            inside = deep & (row + b >= 1) & (row + b <= LS) & (column + c >= 1) & (column + c <= LS)
-            shift = lax.rem(2 * cells - (CELLS * (a - 1) + LS * (b - 1) + c - 1), cells)
-            t = 3 * b + c
-            for s in range(samples):
-                value = jnp.where(inside, pltpu.roll(flat_ref[s], shift, 1), 0.0)
-                lhs_ref[t * C1 : (t + 1) * C1, s * cells : (s + 1) * cells] = value.astype(bf16)
-
-    @pl.when(a == 0)
-    def _():
-        for copy in all_copies():
+        lane = lax.broadcasted_iota(jnp.int32, (1, cells), 1)
+        row, column = (lane // LS) % LS, lane % LS
+        for b in range(3):
+            for c in range(3):
+                inside = (row + b >= 1) & (row + b <= LS) & (column + c >= 1) & (column + c <= LS)
+                mask = inside.astype(f32)
+                shift = (-(LS * (b - 1) + c - 1)) % cells
+                t = 3 * b + c
+                for s in range(samples):
+                    value = flat_ref[s]
+                    if shift:
+                        value = pltpu.roll(value, shift, 1) * mask
+                    lhs_ref[s, t * C1 : (t + 1) * C1] = value.astype(bf16)
+        for copy in copies:
             copy.wait()
 
-    out_ref[...] = jnp.dot(lhs_ref[...], cot_ref[...], preferred_element_type=f32) * scale
+    rows = pl.ds(pl.multiple_of((2 - a) * CELLS, CELLS), cells)
+    total = None
+    for s in range(samples):
+        term = jnp.dot(lhs_ref[s], cot_ref[s, rows], preferred_element_type=f32)
+        total = term if total is None else total + term
+    out_ref[...] = total * scale
 
 
 def weight_two(device, fields, pieces, cots, scale, after):
@@ -375,21 +342,22 @@
             + [pl.BlockSpec(memory_space=pl.ANY)] * (len(flat) + len(after)),
             out_specs=pl.BlockSpec((block, C2), lambda n, s: (n, 0)),
             scratch_shapes=[
-                pltpu.VMEM((samples * cells, C2), bf16),
+                pltpu.VMEM((samples, (planes + 2) * CELLS, C2), bf16),
                 pltpu.VMEM((samples, C1, cells), f32),
-                pltpu.VMEM((block, samples * cells), bf16),
-                pltpu.SemaphoreType.DMA((samples * planes,)),
+                pltpu.VMEM((samples, block, cells), bf16),
+                pltpu.SemaphoreType.DMA((samples, planes)),
             ],
         ),
         out_shape=jax.ShapeDtypeStruct((TAPS * C1, C2), f32),
-        compiler_params=params(60),
+        compiler_params=params(40 if samples <= 2 else 58),
         cost_estimate=pl.CostEstimate(
             flops=2 * samples * cells * TAPS * C1 * C2, bytes_accessed=18 << 20, transcendentals=0
         ),
     )(device, *fields, *flat, *after)
 
 
-def grad_pre_kernel(pieces_ref, slope_ref, lhs_ref, grad_ref, partial_ref, spread_ref, packed_ref):
+def grad_pre_kernel(pieces_ref, slope_ref, lhs_ref, *refs):
+    grad_ref, partial_ref, spread_ref, packed_ref = refs[-4:]
     for r in range(BLOCK):
         for u in range(BLOCK // 2):
             piece = r * BLOCK + 2 * u
@@ -434,10 +402,12 @@
         partial_ref[row] = entry.astype(bf16)
 
 
-def grad_pre_of(pieces, slope, lhs):
+def grad_pre_of(pieces, slope, lhs, after):
     rows = LS * LAT
+    whole = pl.BlockSpec(memory_space=pltpu.VMEM)
     return pl.pallas_call(
         grad_pre_kernel,
+        in_specs=[whole] * 3 + [pl.BlockSpec(memory_space=pl.ANY)] * len(after),
         out_shape=(
             jax.ShapeDtypeStruct((rows, GROUP), bf16),
             jax.ShapeDtypeStruct((C1 // 2, 32, PACK), bf16),
@@ -450,7 +420,7 @@
         cost_estimate=pl.CostEstimate(
             flops=2 * rows * 9 * WINDOW * GROUP, bytes_accessed=3 << 20, transcendentals=0
         ),
-    )(pieces, slope, lhs)
+    )(pieces, slope, lhs, *after)
 
 
 def back_one_kernel(before_ref, own_ref, after_ref, w_ref, out_ref, lhs_ref):
@@ -474,21 +444,41 @@
     )(before, own, after, band)
 
 
-def unpack_kernel(packed_ref, out_ref, wide_ref):
+def sum_kernel(scale, shares_ref, *refs):
+    out_ref = refs[-1]
+    total = jnp.sum(shares_ref[...].astype(f32), axis=0) * scale
+    out_ref[...] = jnp.broadcast_to(total.astype(bf16)[None], out_ref.shape)
+
+
+def sum_shares(shares, scale, after):
+    whole = pl.BlockSpec(memory_space=pltpu.VMEM)
+    return pl.pallas_call(
+        lambda *refs: sum_kernel(scale, *refs),
+        in_specs=[whole] + [pl.BlockSpec(memory_space=pl.ANY)] * len(after),
+        out_shape=jax.ShapeDtypeStruct(shares.shape, bf16),
+        compiler_params=params(16),
+        cost_estimate=pl.CostEstimate(flops=0, bytes_accessed=1 << 20, transcendentals=0),
+    )(shares, *after)
+
+
+def unpack_kernel(packed_ref, *refs):
+    out_ref, wide_ref = refs[-2:]
     wide_ref[...] = packed_ref[...].astype(f32).reshape(wide_ref.shape)
     for t in range(TAPS):
         entry = wide_ref[pl.ds(t, C1 // 2, stride=32), :]
         out_ref[t] = jnp.concatenate([entry[:, :C1], entry[:, C1:]], axis=0)
 
 
-def unpack(packed):
+def unpack(packed, after):
+    whole = pl.BlockSpec(memory_space=pltpu.VMEM)
     return pl.pallas_call(
         unpack_kernel,
+        in_specs=[whole] + [pl.BlockSpec(memory_space=pl.ANY)] * len(after),
         out_shape=jax.ShapeDtypeStruct((TAPS, C1, C1), f32),
         scratch_shapes=[pltpu.VMEM((32 * (C1 // 2), PACK), f32)],
         compiler_params=params(16),
         cost_estimate=pl.CostEstimate(flops=0, bytes_accessed=1 << 20, transcendentals=0),
-    )(packed)
+    )(packed, *after)
 
 
 def neighbours(value, axis):
@@ -521,32 +511,31 @@
 
     core, chip = 1, 2
     outer = list(range(4, shards, 4))
+    before, after = neighbours(own, "depth")
     far = [flipped(cot, difference) for difference in outer]
-    before, after = neighbours(own, "depth")
     cot_chip = flipped(cot, chip)
 
     back_weight = jnp.swapaxes(conv1_weight[::-1], 1, 2)
     band = banded(conv1_weight)
     back_band = banded(back_weight)
-    turned_two = turned_weight(flat_two)
 
     moved, slope, windows = conv_one(before, own, after, band)
     fields = lax.all_to_all(moved, "depth", split_axis=0, concat_axis=0, tiled=True)
 
-    near = jnp.concatenate([cot, cot_chip], axis=0)
-    far = jnp.concatenate(far, axis=0)
-    far_chip = flipped(far, chip)
-    cots = [near, far, far_chip]
-    pieces = [[0, chip], outer, [difference + chip for difference in outer]]
-    pieces = pieces + [[difference + core for difference in piece] for piece in pieces]
+    cots = [cot, cot_chip] + far + [flipped(value, chip) for value in far]
+    pieces = [0, chip] + outer + [difference + chip for difference in outer]
+    pieces = [[difference] for difference in pieces + [difference + core for difference in pieces]]
+    all_cots = []
+    for value in zip(*[over_samples(value) for value in cots]):
+        all_cots.append(list(value) + [flipped(part, core) for part in value])
+    all_pieces = [pieces] * samples
 
     partial = conv_two(fields, flat_two)
     features = lax.psum_scatter(partial, "depth", scatter_dimension=0, tiled=True)
 
-    own_cots = cots + [flipped(value, core) for value in cots]
-    grad_pieces = back_two(device, pieces, own_cots, turned_two, [partial])
+    grad_pieces = back_two(device, pieces, all_cots[0], flat_two, [partial])
     grad_pieces = lax.all_to_all(grad_pieces, "depth", split_axis=0, concat_axis=0, tiled=True)
-    grad_pre, partial_one = grad_pre_of(grad_pieces, slope, windows)
+    grad_pre, partial_one = grad_pre_of(grad_pieces, slope, windows, [])
     grad_before, grad_after = neighbours(grad_pre, "depth")
 
     devices = samples * shards
@@ -554,21 +543,14 @@
     scale_one = 1.0 / math.sqrt(samples * shards * LAT * LAT)
     shares = partial_one.reshape(devices, -1, PACK)
     shares = lax.all_to_all(shares, both, split_axis=0, concat_axis=0, tiled=True)
-    summed = (jnp.sum(shares.astype(f32), axis=0) * scale_one).astype(bf16)
-    summed = jnp.broadcast_to(summed[None], shares.shape)
-    summed = lax.all_to_all(summed, both, split_axis=0, concat_axis=0, tiled=True)
-    grad_conv1 = unpack(summed.reshape(C1 // 2, 32, PACK))
-
+    scale_two = 1.0 / math.sqrt(samples * shards * CELLS)
+    grad_conv2 = weight_two(
+        device, over_samples(fields), all_pieces, all_cots, scale_two, [grad_pre]
+    )
+    summed = sum_shares(shares, scale_one, [grad_conv2])
+    shares = lax.all_to_all(summed, both, split_axis=0, concat_axis=0, tiled=True)
     grad_volume = back_one(grad_before, grad_pre, grad_after, back_band)
-
-    scale_two = 1.0 / math.sqrt(samples * shards * CELLS)
-    half = jnp.concatenate(cots, axis=0)
-    halves = [[difference for piece in group for difference in piece] for group in (pieces[:3], pieces[3:])]
-    all_pieces, all_cots = [pieces], [own_cots]
-    for value in over_samples(half)[1:]:
-        all_pieces.append(halves)
-        all_cots.append([value, flipped(value, core)])
-    grad_conv2 = weight_two(device, over_samples(fields), all_pieces, all_cots, scale_two, [grad_pre])
+    grad_conv1 = unpack(shares.reshape(C1 // 2, 32, PACK), [])
 
     return (
         features.reshape(cotangent.shape),

time: 141 us -> 157 us (1.11)
  starting transfers between devices: 33.7 us -> 42.9 us
  Pallas kernels: 52.2 us -> 43.6 us
  waiting for transfers between devices: 16.9 us -> 24.5 us
  blocking collectives: 13.7 us -> 18.2 us
  local copies, waits for them, and re-layouts: 8.45 us -> 12.5 us
    ppermute x9 -> x23, waiting for transfers between devices: 0.02 us -> 15.4 us  [flipped(): lax.ppermute(value, 'depth', [(i, i ^ difference) for i in range(count)])]
    all_to_all x1, waiting for transfers between devices: 10.1 us -> 0.01 us  [on_device(): lax.all_to_all(shares, both, split_axis=0, concat_axis=0, tiled=True)]
    ppermute x2 -> x9, starting transfers between devices: 3.23 us -> 9.79 us  [over_samples(): lax.ppermute(value, 'sample', [(i, (i + shift) % count) for i in range(co...]
    pallas_call x3, Pallas kernels: 11.3 us -> 5.43 us  [the longest x1 3.39 us: grad_pre_of(): pl.pallas_call(grad_pre_kernel, in_specs=[whole] * 3 + [pl.BlockSpec(memo...]
    unnamed x28 -> x59, local copies, waits for them, and re-layouts: 6.91 us -> 12.4 us
    ppermute x2 -> x9, waiting for transfers between devices: 0.01 us -> 5.2 us  [over_samples(): lax.ppermute(value, 'sample', [(i, (i + shift) % count) for i in range(co...]
    all_to_all x1, blocking collectives: 13.7 us -> 18.2 us  [on_device(): lax.all_to_all(moved, 'depth', split_axis=0, concat_axis=0, tiled=True)]
    all_to_all x1, starting transfers between devices: 2.59 us -> 6.01 us  [on_device(): lax.all_to_all(shares, both, split_axis=0, concat_axis=0, tiled=True)]
  transfers between devices with their start and end apart: 19 -> 40, of which waited for: 4 -> 10; matrix products, arithmetic and copies ran while one was open for 4% -> 0% of each run, Pallas kernels for 37% -> 21%
where the time goes in v4:
time: 157 us; the launch traced here: 156 us
  Pallas kernels  43.6 us (28%)
  starting transfers between devices  42.9 us (27%)
  waiting for transfers between devices  24.5 us (16%)
  blocking collectives  18.2 us (12%)
  between operations  14.5 us (9%)
  local copies, waits for them, and re-layouts  12.5 us (8%)
    all_to_all x1, blocking collectives, on_device(): lax.all_to_all(moved, 'depth', split_axis=0, concat_axis=0, tiled=True)  18.2 us
    ppermute x23, waiting for transfers between devices, flipped(): lax.ppermute(value, 'depth', [(i, i ^ difference) for i in range(count)])  15.4 us
    pallas_call x1, Pallas kernels, weight_two(): pl.pallas_call(lambda *refs: weight_two_kernel(planes, pieces, scale, *re...  14.4 us
    unnamed x59, local copies, waits for them, and re-layouts  12.4 us
    pallas_call x1, Pallas kernels, back_two(): pl.pallas_call(lambda *refs: back_two_kernel(planes, pieces, *refs), grid...  11.5 us
    ppermute x9, starting transfers between devices, over_samples(): lax.ppermute(value, 'sample', [(i, (i + shift) % count) for i in range(co...  9.79 us
    pallas_call x1, Pallas kernels, conv_two(): pl.pallas_call(lambda *refs: conv_two_kernel(planes, *refs), grid=(C2 //...  9.09 us
    ppermute x23, starting transfers between devices, flipped(): lax.ppermute(value, 'depth', [(i, i ^ difference) for i in range(count)])  8.93 us
  transfers between devices with their start and end apart: 40, of which 10 were waited for; matrix products, arithmetic and copies ran while one was open for 0% of the time, Pallas kernels for 21%

profile of v4, /device:TPU:0, one launch (start us, length us, event | category | flops | bytes accessed | tf_op | source)
XLA Modules:
  0.0 156.1 jit_solution(6619494852102787059)
XLA Ops:
  8.5 3.0 %collective-permute-start = (bf16[32,2048]{1,0:T(8,128)(2,1)}, bf16[32,2048]{1,0:T(8,128)(2,1)S(1)}, u32[]{:S(2)}, u32[]{:S(2)}) collective-permute-start(bf16[32,2048]{1,0:T(8,128)(2,1)} %bitcast.12), channel_id=1, source_target_pairs={{0,1},{1,2},{2,3},{3,4},{4,5},{5,6},{6,7},{7,8},{8,9},{9,10},{10,1... | collective-permute-start | bytes 393224 | tf_op jit(solution)/shard_map/ppermute | solution.py:486
  14.5 18.2 %all_to_all.20.refs_0_.refs_1_ = bf16[16,32,128]{2,1,0:T(8,128)(2,1)} all-to-all(bf16[16,32,128]{2,1,0:T(8,128)(2,1)S(1)} %get-tuple-element.9), channel_id=1, replica_groups=mesh['sample'=2,'depth'=16] {'depth'}, dimensions={0} | all-to-all | bytes 262144 | tf_op jit(solution)/shard_map/all_to_all | solution.py:523
  32.7 9.1 %shard_map.77.refs_18_ = bf16[1024,1024]{1,0:T(8,128)(2,1)} custom-call(bf16[16,32,128]{2,1,0:T(8,128)(2,1)} %all_to_all.20.refs_0_.refs_1_, bf16[1728,1024]{1,0:T(8,128)(2,1)} %bitcast.23), custom_call_target="tpu_custom_call" | custom-call | flops 3623878656 | bytes 10485760 | tf_op jit(solution)/shard_map/pallas_call | solution.py:179
  42.7 1.5 collective-permute-start.20
  45.1 3.5 %collective-permute-start.3 = (bf16[64,1024]{1,0:T(8,128)(2,1)S(1)}, bf16[64,1024]{1,0:T(8,128)(2,1)}, u32[]{:S(2)}, u32[]{:S(2)}) collective-permute-start(bf16[64,1024]{1,0:T(8,128)(2,1)S(1)} %bitcast.19), channel_id=1, source_target_pairs={{0,4},{1,5},{2,6},{3,7},{4,0},{5,1},{6,2},{7,3},{8,12},{9,13},{10,... | collective-permute-start | bytes 393224 | tf_op jit(solution)/shard_map/ppermute | solution.py:493
  48.6 3.8 %collective-permute-done.5.refs_5_.refs_7_ = bf16[64,1024]{1,0:T(8,128)(2,1)S(1)} collective-permute-done((bf16[64,1024]{1,0:T(8,128)(2,1)S(1)}, bf16[64,1024]{1,0:T(8,128)(2,1)S(1)}, u32[]{:S(2)}, u32[]{:S(2)}) %collective-permute-start.5) | collective-permute-done | bytes 131104 | tf_op jit(solution)/shard_map/ppermute | solution.py:493
  52.9 4.4 %collective-permute-done.4.refs_4_.refs_6_ = bf16[64,1024]{1,0:T(8,128)(2,1)} collective-permute-done((bf16[64,1024]{1,0:T(8,128)(2,1)S(1)}, bf16[64,1024]{1,0:T(8,128)(2,1)}, u32[]{:S(2)}, u32[]{:S(2)}) %collective-permute-start.4) | collective-permute-done | bytes 131104 | tf_op jit(solution)/shard_map/ppermute | solution.py:493
  60.2 3.1 %collective-permute-done.8.refs_8_.refs_10_ = bf16[64,1024]{1,0:T(8,128)(2,1)S(1)} collective-permute-done((bf16[64,1024]{1,0:T(8,128)(2,1)S(1)}, bf16[64,1024]{1,0:T(8,128)(2,1)S(1)}, u32[]{:S(2)}, u32[]{:S(2)}) %collective-permute-start.8) | collective-permute-done | bytes 131104 | tf_op jit(solution)/shard_map/ppermute | solution.py:493
  63.8 2.3 %collective-permute-done.7.refs_7_.refs_9_ = bf16[64,1024]{1,0:T(8,128)(2,1)S(1)} collective-permute-done((bf16[64,1024]{1,0:T(8,128)(2,1)}, bf16[64,1024]{1,0:T(8,128)(2,1)S(1)}, u32[]{:S(2)}, u32[]{:S(2)}) %collective-permute-start.7) | collective-permute-done | bytes 131104 | tf_op jit(solution)/shard_map/ppermute | solution.py:493
  66.0 1.8 %collective-permute-done.6.refs_6_.refs_8_ = bf16[64,1024]{1,0:T(8,128)(2,1)S(1)} collective-permute-done((bf16[64,1024]{1,0:T(8,128)(2,1)}, bf16[64,1024]{1,0:T(8,128)(2,1)S(1)}, u32[]{:S(2)}, u32[]{:S(2)}) %collective-permute-start.6) | collective-permute-done | bytes 131104 | tf_op jit(solution)/shard_map/ppermute | solution.py:493
  68.5 1.5 collective-permute-start.22
  71.1 11.5 %shard_map.78 = bf16[16,32,128]{2,1,0:T(8,128)(2,1)} custom-call(s32[1]{0:T(128)} %bitcast.3.refs_0_, bf16[64,1024]{1,0:T(8,128)(2,1)} %bitcast.14, bf16[64,1024]{1,0:T(8,128)(2,1)} %collective-permute-done.2.refs_2_.refs_4_, bf16[64,1024]{1,0:T(8,128)(2,1)} %collective-permute-done.3.refs_3_.refs_5_, ...), custom_call_target="tpu_custom_call" | custom-call | flops 3623878656 | bytes 6291456 | tf_op jit(solution)/shard_map/pallas_call | solution.py:255
  82.7 3.7 %all-to-all-start.1 = ((bf16[16,32,128]{2,1,0:T(8,128)(2,1)}), bf16[16,32,128]{2,1,0:T(8,128)(2,1)S(1)}, u32[]{:S(2)}, u32[]{:S(2)}) async-start(bf16[16,32,128]{2,1,0:T(8,128)(2,1)} %shard_map.78), calls=%async_computation.2 | async-start | bytes 262144 | tf_op jit(solution)/shard_map/all_to_all | solution.py:537
  86.4 1.6 collective-permute-start.27
  90.2 2.9 %collective-permute-done.27.refs_26_ = bf16[64,1024]{1,0:T(8,128)(2,1)} collective-permute-done((bf16[64,1024]{1,0:T(8,128)(2,1)}, bf16[64,1024]{1,0:T(8,128)(2,1)}, u32[]{:S(2)}, u32[]{:S(2)}) %collective-permute-start.27) | collective-permute-done | bytes 131104 | tf_op jit(solution)/shard_map/ppermute | solution.py:499
  93.8 1.5 collective-permute-start.19
  97.1 1.6 %collective-permute-done.25.refs_24_ = bf16[64,1024]{1,0:T(8,128)(2,1)} collective-permute-done((bf16[64,1024]{1,0:T(8,128)(2,1)}, bf16[64,1024]{1,0:T(8,128)(2,1)}, u32[]{:S(2)}, u32[]{:S(2)}) %collective-permute-start.25) | collective-permute-done | bytes 131104 | tf_op jit(solution)/shard_map/ppermute | solution.py:499
  98.7 3.4 %shard_map.79 = (bf16[256,256]{1,0:T(8,128)(2,1)S(1)}, bf16[32,32,128]{2,1,0:T(8,128)(2,1)}) custom-call(bf16[16,32,128]{2,1,0:T(8,128)(2,1)S(1)} %all-to-all-done.1.pieces_ref, f32[256,256]{1,0:T(8,128)S(1)} %get-tuple-element.10.slope_ref, bf16[256,3456]{1,0:T(8,128)(2,1)S(1)} %get-tuple-element.11.lhs_ref), custom_call_target="tpu_custom_call" | custom-call | flops 452984832 | bytes 3145728 | tf_op jit(solution)/shard_map/pallas_call | solution.py:408
  102.1 6.0 %all-to-all-start.2 = ((bf16[32,32,128]{2,1,0:T(8,128)(2,1)}), bf16[32,32,128]{2,1,0:T(8,128)(2,1)S(1)}, u32[]{:S(2)}, u32[]{:S(2)}) async-start(bf16[32,32,128]{2,1,0:T(8,128)(2,1)} %get-tuple-element.13), calls=%async_computation.3 | async-start | bytes 524288 | tf_op jit(solution)/shard_map/all_to_all | solution.py:545
  113.7 14.4 %shard_map.82.refs_1_ = f32[1728,1024]{1,0:T(8,128)} custom-call(s32[1]{0:T(128)} %bitcast.3.refs_0_, bf16[16,32,128]{2,1,0:T(8,128)(2,1)S(1)} %copy-done.4, bf16[16,32,128]{2,1,0:T(8,128)(2,1)} %collective-permute-done.19.refs_2_, bf16[64,1024]{1,0:T(8,128)(2,1)S(1)} %bitcast.21, bf16[64,1024]{1,0:T(8,128)(2,1)} %collective-permute-done.2.refs_2_.refs_4_, ...), custom_call_target="tpu_custom_call" | custom-call | flops 7247757312 | bytes 18874368 | tf_op jit(solution)/shard_map/pallas_call | solution.py:336
  128.1 3.0 %copy-done = f32[1728,1024]{1,0:T(8,128)S(1)} copy-done((f32[1728,1024]{1,0:T(8,128)S(1)}, f32[1728,1024]{1,0:T(8,128)}, u32[]{:S(2)}) %copy-start) | copy-done | bytes 7077912
  131.8 5.8 %all-to-all-start.3 = ((bf16[32,32,128]{2,1,0:T(8,128)(2,1)}), bf16[32,32,128]{2,1,0:T(8,128)(2,1)S(1)}, u32[]{:S(2)}, u32[]{:S(2)}) async-start(bf16[32,32,128]{2,1,0:T(8,128)(2,1)} %shard_map.83), calls=%async_computation.4 | async-start | bytes 524288 | tf_op jit(solution)/shard_map/all_to_all | solution.py:551
  139.0 3.0 %collective-permute-start.17 = (bf16[256,256]{1,0:T(8,128)(2,1)S(1)}, bf16[256,256]{1,0:T(8,128)(2,1)S(1)}, u32[]{:S(2)}, u32[]{:S(2)}) collective-permute-start(bf16[256,256]{1,0:T(8,128)(2,1)S(1)} %get-tuple-element.12.own_ref.refs_35_), channel_id=1, source_target_pairs={{0,1},{1,2},{2,3},{3,4},{4,5},{5,6},{6,7},{7,8},{8,9},{9,10},{10,1... | collective-permute-start | bytes 393224 | tf_op jit(solution)/shard_map/ppermute | solution.py:486
  144.3 3.6 %all-to-all-done.3.packed_ref = bf16[32,32,128]{2,1,0:T(8,128)(2,1)S(1)} async-done(((bf16[32,32,128]{2,1,0:T(8,128)(2,1)}), bf16[32,32,128]{2,1,0:T(8,128)(2,1)S(1)}, u32[]{:S(2)}, u32[]{:S(2)}) %all-to-all-start.3) | async-done | bytes 262176 | tf_op jit(solution)/shard_map/all_to_all | solution.py:551
  (128 shorter events, 27.5 us)
Async XLA Ops:
  7.2 142.1 %reduce-scatter.2.cloned.1.call-start = ((), (), s32[]{:S(2)}) async-start(), calls=%async_computation.5 | async-start | bytes 2228224 | tf_op jit(solution)/shard_map/reduce_scatter | solution.py:534
  44.2 8.2 %collective-permute-start.5 = (bf16[64,1024]{1,0:T(8,128)(2,1)S(1)}, bf16[64,1024]{1,0:T(8,128)(2,1)S(1)}, u32[]{:S(2)}, u32[]{:S(2)}) collective-permute-start(bf16[64,1024]{1,0:T(8,128)(2,1)S(1)} %bitcast.16), channel_id=1, source_target_pairs={{0,12},{1,13},{2,14},{3,15},{4,8},{5,9},{6,10},{7,11},{8,4},{9,5},... | collective-permute-start | bytes 393224 | tf_op jit(solution)/shard_map/ppermute | solution.py:493
  44.9 8.0 %collective-permute-start.9 = (bf16[64,1024]{1,0:T(8,128)(2,1)S(1)}, bf16[64,1024]{1,0:T(8,128)(2,1)S(1)}, u32[]{:S(2)}, u32[]{:S(2)}) collective-permute-start(bf16[64,1024]{1,0:T(8,128)(2,1)S(1)} %bitcast.17), channel_id=1, source_target_pairs={{0,1},{1,0},{2,3},{3,2},{4,5},{5,4},{6,7},{7,6},{8,9},{9,8},{10,11... | collective-permute-start | bytes 393224 | tf_op jit(solution)/shard_map/ppermute | solution.py:493
  44.9 12.4 %collective-permute-start.4 = (bf16[64,1024]{1,0:T(8,128)(2,1)S(1)}, bf16[64,1024]{1,0:T(8,128)(2,1)}, u32[]{:S(2)}, u32[]{:S(2)}) collective-permute-start(bf16[64,1024]{1,0:T(8,128)(2,1)S(1)} %bitcast.18), channel_id=1, source_target_pairs={{0,8},{1,9},{2,10},{3,11},{4,12},{5,13},{6,14},{7,15},{8,0},{9,1},... | collective-permute-start | bytes 393224 | tf_op jit(solution)/shard_map/ppermute | solution.py:493
  45.1 12.9 %collective-permute-start.3 = (bf16[64,1024]{1,0:T(8,128)(2,1)S(1)}, bf16[64,1024]{1,0:T(8,128)(2,1)}, u32[]{:S(2)}, u32[]{:S(2)}) collective-permute-start(bf16[64,1024]{1,0:T(8,128)(2,1)S(1)} %bitcast.19), channel_id=1, source_target_pairs={{0,4},{1,5},{2,6},{3,7},{4,0},{5,1},{6,2},{7,3},{8,12},{9,13},{10,... | collective-permute-start | bytes 393224 | tf_op jit(solution)/shard_map/ppermute | solution.py:493
  48.6 9.5 %collective-permute-start.2 = (bf16[64,1024]{1,0:T(8,128)(2,1)S(1)}, bf16[64,1024]{1,0:T(8,128)(2,1)}, u32[]{:S(2)}, u32[]{:S(2)}) collective-permute-start(bf16[64,1024]{1,0:T(8,128)(2,1)S(1)} %bitcast.20), channel_id=1, source_target_pairs={{0,2},{1,3},{2,0},{3,1},{4,6},{5,7},{6,4},{7,5},{8,10},{9,11},{10,... | collective-permute-start | bytes 393224 | tf_op jit(solution)/shard_map/ppermute | solution.py:493
  58.0 8.0 %collective-permute-start.7 = (bf16[64,1024]{1,0:T(8,128)(2,1)}, bf16[64,1024]{1,0:T(8,128)(2,1)S(1)}, u32[]{:S(2)}, u32[]{:S(2)}) collective-permute-start(bf16[64,1024]{1,0:T(8,128)(2,1)} %collective-permute-done.4.refs_4_.refs_6_), channel_id=1, source_target_pairs={{0,2},{1,3},{2,0},{3,1},{4,6},{5,7},{6,4},{7,5},{8,10},{9,11},{10,... | collective-permute-start | bytes 393224 | tf_op jit(solution)/shard_map/ppermute | solution.py:493
  59.4 8.5 %collective-permute-start.6 = (bf16[64,1024]{1,0:T(8,128)(2,1)}, bf16[64,1024]{1,0:T(8,128)(2,1)S(1)}, u32[]{:S(2)}, u32[]{:S(2)}) collective-permute-start(bf16[64,1024]{1,0:T(8,128)(2,1)} %collective-permute-done.3.refs_3_.refs_5_), channel_id=1, source_target_pairs={{0,2},{1,3},{2,0},{3,1},{4,6},{5,7},{6,4},{7,5},{8,10},{9,11},{10,... | collective-permute-start | bytes 393224 | tf_op jit(solution)/shard_map/ppermute | solution.py:493
  60.1 7.7 %collective-permute-start.11 = (bf16[64,1024]{1,0:T(8,128)(2,1)}, bf16[64,1024]{1,0:T(8,128)(2,1)S(1)}, u32[]{:S(2)}, u32[]{:S(2)}) collective-permute-start(bf16[64,1024]{1,0:T(8,128)(2,1)} %collective-permute-done.3.refs_3_.refs_5_), channel_id=1, source_target_pairs={{0,1},{1,0},{2,3},{3,2},{4,5},{5,4},{6,7},{7,6},{8,9},{9,8},{10,11... | collective-permute-start | bytes 393224 | tf_op jit(solution)/shard_map/ppermute | solution.py:493
  67.9 20.1 %collective-permute-start.23 = (bf16[64,1024]{1,0:T(8,128)(2,1)}, bf16[64,1024]{1,0:T(8,128)(2,1)}, u32[]{:S(2)}, u32[]{:S(2)}) collective-permute-start(bf16[64,1024]{1,0:T(8,128)(2,1)} %collective-permute-done.4.refs_4_.refs_6_), channel_id=1, source_target_pairs={{0,16},{16,0},{1,17},{17,1},{2,18},{18,2},{3,19},{19,3},{4,20},{20... | collective-permute-start | bytes 393224 | tf_op jit(solution)/shard_map/ppermute | solution.py:499
  68.5 19.5 %collective-permute-start.22 = (bf16[64,1024]{1,0:T(8,128)(2,1)}, bf16[64,1024]{1,0:T(8,128)(2,1)}, u32[]{:S(2)}, u32[]{:S(2)}) collective-permute-start(bf16[64,1024]{1,0:T(8,128)(2,1)} %collective-permute-done.3.refs_3_.refs_5_), channel_id=1, source_target_pairs={{0,16},{16,0},{1,17},{17,1},{2,18},{18,2},{3,19},{19,3},{4,20},{20... | collective-permute-start | bytes 393224 | tf_op jit(solution)/shard_map/ppermute | solution.py:499
  70.0 18.6 %collective-permute-start.21 = (bf16[64,1024]{1,0:T(8,128)(2,1)}, bf16[64,1024]{1,0:T(8,128)(2,1)}, u32[]{:S(2)}, u32[]{:S(2)}) collective-permute-start(bf16[64,1024]{1,0:T(8,128)(2,1)} %collective-permute-done.2.refs_2_.refs_4_), channel_id=1, source_target_pairs={{0,16},{16,0},{1,17},{17,1},{2,18},{18,2},{3,19},{19,3},{4,20},{20... | collective-permute-start | bytes 393224 | tf_op jit(solution)/shard_map/ppermute | solution.py:499
  70.5 15.8 %collective-permute-start.28 = (bf16[64,1024]{1,0:T(8,128)(2,1)S(1)}, bf16[64,1024]{1,0:T(8,128)(2,1)}, u32[]{:S(2)}, u32[]{:S(2)}) collective-permute-start(bf16[64,1024]{1,0:T(8,128)(2,1)S(1)} %collective-permute-done.20.refs_19_), channel_id=1, source_target_pairs={{0,1},{1,0},{2,3},{3,2},{4,5},{5,4},{6,7},{7,6},{8,9},{9,8},{10,11... | collective-permute-start | bytes 393224 | tf_op jit(solution)/shard_map/ppermute | solution.py:493
  70.5 18.2 %collective-permute-start.32 = (bf16[64,1024]{1,0:T(8,128)(2,1)S(1)}, bf16[64,1024]{1,0:T(8,128)(2,1)}, u32[]{:S(2)}, u32[]{:S(2)}) collective-permute-start(bf16[64,1024]{1,0:T(8,128)(2,1)S(1)} %collective-permute-done.24.refs_23_), channel_id=1, source_target_pairs={{0,1},{1,0},{2,3},{3,2},{4,5},{5,4},{6,7},{7,6},{8,9},{9,8},{10,11... | collective-permute-start | bytes 393224 | tf_op jit(solution)/shard_map/ppermute | solution.py:493
  82.7 16.0 %all-to-all-start.1 = ((bf16[16,32,128]{2,1,0:T(8,128)(2,1)}), bf16[16,32,128]{2,1,0:T(8,128)(2,1)S(1)}, u32[]{:S(2)}, u32[]{:S(2)}) async-start(bf16[16,32,128]{2,1,0:T(8,128)(2,1)} %shard_map.78), calls=%async_computation.2 | async-start | bytes 262144 | tf_op jit(solution)/shard_map/all_to_all | solution.py:537
  88.0 7.9 %collective-permute-start.26 = (bf16[64,1024]{1,0:T(8,128)(2,1)}, bf16[64,1024]{1,0:T(8,128)(2,1)}, u32[]{:S(2)}, u32[]{:S(2)}) collective-permute-start(bf16[64,1024]{1,0:T(8,128)(2,1)} %copy-done.17), channel_id=1, source_target_pairs={{0,16},{16,0},{1,17},{17,1},{2,18},{18,2},{3,19},{19,3},{4,20},{20... | collective-permute-start | bytes 393224 | tf_op jit(solution)/shard_map/ppermute | solution.py:499
  88.7 10.0 %collective-permute-start.25 = (bf16[64,1024]{1,0:T(8,128)(2,1)}, bf16[64,1024]{1,0:T(8,128)(2,1)}, u32[]{:S(2)}, u32[]{:S(2)}) collective-permute-start(bf16[64,1024]{1,0:T(8,128)(2,1)} %copy-done.19), channel_id=1, source_target_pairs={{0,16},{16,0},{1,17},{17,1},{2,18},{18,2},{3,19},{19,3},{4,20},{20... | collective-permute-start | bytes 393224 | tf_op jit(solution)/shard_map/ppermute | solution.py:499
  93.1 15.0 %collective-permute-start.29 = (bf16[64,1024]{1,0:T(8,128)(2,1)}, bf16[64,1024]{1,0:T(8,128)(2,1)}, u32[]{:S(2)}, u32[]{:S(2)}) collective-permute-start(bf16[64,1024]{1,0:T(8,128)(2,1)} %collective-permute-done.21.refs_20_), channel_id=1, source_target_pairs={{0,1},{1,0},{2,3},{3,2},{4,5},{5,4},{6,7},{7,6},{8,9},{9,8},{10,11... | collective-permute-start | bytes 393224 | tf_op jit(solution)/shard_map/ppermute | solution.py:493
  93.8 14.4 %collective-permute-start.19 = (bf16[16,32,128]{2,1,0:T(8,128)(2,1)S(1)}, bf16[16,32,128]{2,1,0:T(8,128)(2,1)}, u32[]{:S(2)}, u32[]{:S(2)}) collective-permute-start(bf16[16,32,128]{2,1,0:T(8,128)(2,1)S(1)} %copy-done.4), channel_id=1, source_target_pairs={{0,16},{16,0},{1,17},{17,1},{2,18},{18,2},{3,19},{19,3},{4,20},{20... | collective-permute-start | bytes 393224 | tf_op jit(solution)/shard_map/ppermute | solution.py:499
  95.9 12.2 %collective-permute-start.35 = (bf16[64,1024]{1,0:T(8,128)(2,1)}, bf16[64,1024]{1,0:T(8,128)(2,1)}, u32[]{:S(2)}, u32[]{:S(2)}) collective-permute-start(bf16[64,1024]{1,0:T(8,128)(2,1)} %collective-permute-done.27.refs_26_), channel_id=1, source_target_pairs={{0,1},{1,0},{2,3},{3,2},{4,5},{5,4},{6,7},{7,6},{8,9},{9,8},{10,11... | collective-permute-start | bytes 393224 | tf_op jit(solution)/shard_map/ppermute | solution.py:493
  96.6 11.6 %collective-permute-start.34 = (bf16[64,1024]{1,0:T(8,128)(2,1)}, bf16[64,1024]{1,0:T(8,128)(2,1)}, u32[]{:S(2)}, u32[]{:S(2)}) collective-permute-start(bf16[64,1024]{1,0:T(8,128)(2,1)} %collective-permute-done.26.refs_25_), channel_id=1, source_target_pairs={{0,1},{1,0},{2,3},{3,2},{4,5},{5,4},{6,7},{7,6},{8,9},{9,8},{10,11... | collective-permute-start | bytes 393224 | tf_op jit(solution)/shard_map/ppermute | solution.py:493
  98.7 9.5 %collective-permute-start.33 = (bf16[64,1024]{1,0:T(8,128)(2,1)}, bf16[64,1024]{1,0:T(8,128)(2,1)}, u32[]{:S(2)}, u32[]{:S(2)}) collective-permute-start(bf16[64,1024]{1,0:T(8,128)(2,1)} %collective-permute-done.25.refs_24_), channel_id=1, source_target_pairs={{0,1},{1,0},{2,3},{3,2},{4,5},{5,4},{6,7},{7,6},{8,9},{9,8},{10,11... | collective-permute-start | bytes 393224 | tf_op jit(solution)/shard_map/ppermute | solution.py:493
  102.1 25.9 %all-to-all-start.2 = ((bf16[32,32,128]{2,1,0:T(8,128)(2,1)}), bf16[32,32,128]{2,1,0:T(8,128)(2,1)S(1)}, u32[]{:S(2)}, u32[]{:S(2)}) async-start(bf16[32,32,128]{2,1,0:T(8,128)(2,1)} %get-tuple-element.13), calls=%async_computation.3 | async-start | bytes 524288 | tf_op jit(solution)/shard_map/all_to_all | solution.py:545
  131.8 16.1 %all-to-all-start.3 = ((bf16[32,32,128]{2,1,0:T(8,128)(2,1)}), bf16[32,32,128]{2,1,0:T(8,128)(2,1)S(1)}, u32[]{:S(2)}, u32[]{:S(2)}) async-start(bf16[32,32,128]{2,1,0:T(8,128)(2,1)} %shard_map.83), calls=%async_computation.4 | async-start | bytes 524288 | tf_op jit(solution)/shard_map/all_to_all | solution.py:551
  (45 other events, 365.8 us)
Sparse Core Ops, SparseCore 0:
  41.9 60.1 reduce-scatter.1

commit v5 on v4

--- a/solution.py
+++ b/solution.py
@@ -77,7 +77,8 @@
         lhs_ref[:, start : start + WINDOW] = shifted[b].astype(bf16)
 
 
-def conv_one_kernel(before_ref, own_ref, after_ref, w_ref, moved_ref, slope_ref, lhs_ref, hid_ref):
+def conv_one_kernel(before_ref, own_ref, after_ref, w_ref, *refs):
+    moved_ref, slope_ref, lhs_ref, hid_ref = refs[-4:]
     for a, ref in enumerate((before_ref, own_ref, after_ref)):
         write_windows(lhs_ref, a, [ref[:, g * GROUP : (g + 1) * GROUP].astype(f32) for g in range(LS)])
     pre = jnp.dot(lhs_ref[...], w_ref[...], preferred_element_type=f32)
@@ -100,10 +101,12 @@
             moved_ref[piece + 1] = jnp.where(low, pltpu.roll(top, C1, 1), bottom).astype(bf16)
 
 
-def conv_one(before, own, after, band):
+def conv_one(before, own, after, band, waits):
     rows = LS * LAT
+    whole = pl.BlockSpec(memory_space=pltpu.VMEM)
     return pl.pallas_call(
         conv_one_kernel,
+        in_specs=[whole] * 4 + [pl.BlockSpec(memory_space=pltpu.HBM)] * len(waits),
         out_shape=(
             jax.ShapeDtypeStruct((BLOCK * BLOCK, CELLS // 2, PACK), bf16),
             jax.ShapeDtypeStruct((rows, GROUP), f32),
@@ -114,7 +117,7 @@
         cost_estimate=pl.CostEstimate(
             flops=2 * rows * 9 * WINDOW * GROUP, bytes_accessed=5 << 20, transcendentals=rows * GROUP
         ),
-    )(before, own, after, band)
+    )(before, own, after, band, *waits)
 
 
 def shift_cells(field, step):
@@ -125,37 +128,36 @@
     return jnp.where(column == edge, 0.0, pltpu.roll(field, (-step) % LS, 1))
 
 
-def shift_rows(field, step):
-    if step == 0:
-        return field
-    blank = jnp.zeros((1,) + field.shape[1:], field.dtype)
-    parts = [field[1:], blank] if step > 0 else [blank, field[:-1]]
-    return jnp.concatenate(parts, axis=0)
-
-
-def conv_two_kernel(planes, x_ref, w_ref, out_ref, lhs_ref):
-    cells = planes * CELLS
-    lateral = 9 * C1
+def conv_two_kernel(planes, x_ref, w_ref, *refs):
+    out_ref, lhs_ref, v_ref = refs[-3:]
 
     @pl.when(pl.program_id(0) == 0)
     def _():
-        lhs_ref[:CELLS] = jnp.zeros((CELLS, lateral), bf16)
-        lhs_ref[cells + CELLS :] = jnp.zeros((CELLS, lateral), bf16)
-
-        def gather(p, carry):
+        v_ref[:, :, 0] = jnp.zeros((3, 2, LS + 2, LS, PACK), f32)
+        v_ref[:, :, planes + 1] = jnp.zeros((3, 2, LS + 2, LS, PACK), f32)
+        edge = jnp.zeros((LS, PACK), f32)
+
+        def spread(p, carry):
             x = x_ref[p].astype(f32)
             turned = pltpu.roll(x, C1, 1)
-            halves = []
-            for parts in ((x, turned), (turned, x)):
-                field = jnp.concatenate(parts, axis=0).reshape(LS, LS, PACK)
-                halves.append([shift_cells(field, c - 1) for c in range(3)])
-            rows = pl.ds(pl.multiple_of((p + 1) * CELLS, CELLS), CELLS)
-            for m in range(5):
+            for half, parts in enumerate(((x, turned), (turned, x))):
+                cells = jnp.concatenate(parts, axis=0).reshape(LS, LS, PACK)
+                for c in range(3):
+                    v_ref[c, half, p + 1, 0] = edge
+                    v_ref[c, half, p + 1, 1 : LS + 1] = shift_cells(cells, c - 1)
+                    v_ref[c, half, p + 1, LS + 1] = edge
+            return carry
+
+        lax.fori_loop(0, planes, spread, 0)
+
+        def gather(p, carry):
+            rows = pl.ds(pl.multiple_of(p * CELLS, CELLS), CELLS)
+            for m in range((TAPS + 1) // 2):
                 t = 2 * m
-                low = shift_rows(halves[0][t % 3], t // 3 - 1).reshape(CELLS, PACK)
+                low = v_ref[t % 3, 0, p + t // 9, pl.ds((t // 3) % 3, LS)].reshape(CELLS, PACK)
                 t = 2 * m + 1
-                if t < 9:
-                    high = shift_rows(halves[1][t % 3], t // 3 - 1).reshape(CELLS, PACK)
+                if t < TAPS:
+                    high = v_ref[t % 3, 1, p + t // 9, pl.ds((t // 3) % 3, LS)].reshape(CELLS, PACK)
                     tile = jnp.where(low_lanes(low.shape), low, high)
                     lhs_ref[rows, m * PACK : (m + 1) * PACK] = tile.astype(bf16)
                 else:
@@ -164,33 +166,58 @@
 
         lax.fori_loop(0, planes, gather, 0)
 
-    total = None
-    for a in range(3):
-        window = lhs_ref[a * CELLS : a * CELLS + cells]
-        term = jnp.dot(window, w_ref[a * lateral : (a + 1) * lateral], preferred_element_type=f32)
-        total = term if total is None else total + term
-    out_ref[...] = total.astype(bf16)
-
-
-def conv_two(fields, weight):
-    planes = fields.shape[0]
+    chunk = 4 * CELLS
+    for m in range(planes * CELLS // chunk):
+        rows = slice(m * chunk, (m + 1) * chunk)
+        out_ref[rows] = jnp.dot(lhs_ref[rows], w_ref[...], preferred_element_type=f32).astype(bf16)
+
+
+def conv_two(pieces, weight, after):
+    planes = pieces.shape[0]
     cells = planes * CELLS
-    block = 512
+    block = 256
     return pl.pallas_call(
         lambda *refs: conv_two_kernel(planes, *refs),
         grid=(C2 // block,),
         in_specs=[
-            pl.BlockSpec(fields.shape, lambda n: (0, 0, 0)),
+            pl.BlockSpec(pieces.shape, lambda n: (0, 0, 0)),
             pl.BlockSpec((TAPS * C1, block), lambda n: (0, n)),
-        ],
+        ]
+        + [pl.BlockSpec(memory_space=pltpu.HBM)] * len(after),
         out_specs=pl.BlockSpec((cells, block), lambda n: (0, n)),
         out_shape=jax.ShapeDtypeStruct((cells, C2), bf16),
-        scratch_shapes=[pltpu.VMEM((cells + 2 * CELLS, 9 * C1), bf16)],
+        scratch_shapes=[
+            pltpu.VMEM((cells, TAPS * C1), bf16),
+            pltpu.VMEM((3, 2, planes + 2, LS + 2, LS, PACK), f32),
+        ],
         compiler_params=params(56),
         cost_estimate=pl.CostEstimate(
             flops=2 * cells * TAPS * C1 * C2, bytes_accessed=10 << 20, transcendentals=0
         ),
-    )(fields, weight)
+    )(pieces, weight, *after)
+
+
+def join_kernel(count, *refs):
+    out_ref, first = refs[-1], 0
+    for ref in refs[:count]:
+        rows = ref.shape[0]
+        out_ref[first : first + rows] = ref[...]
+        first += rows
+
+
+def joined(values, after=()):
+    rows = sum(value.shape[0] for value in values)
+    columns = values[0].shape[1]
+    return pl.pallas_call(
+        lambda *refs: join_kernel(len(values), *refs),
+        grid=(1,),
+        in_specs=[pl.BlockSpec(value.shape, lambda n: (0, 0)) for value in values]
+        + [pl.BlockSpec(memory_space=pl.ANY)] * len(after),
+        out_specs=pl.BlockSpec((rows, columns), lambda n: (0, 0)),
+        out_shape=jax.ShapeDtypeStruct((rows, columns), values[0].dtype),
+        compiler_params=params(32),
+        cost_estimate=pl.CostEstimate(flops=0, bytes_accessed=4 * rows * columns, transcendentals=0),
+    )(*values, *after)
 
 
 def plane_copies(device, pieces, refs, target_ref, base, sems):
@@ -257,9 +284,9 @@
         grid_spec=pltpu.PrefetchScalarGridSpec(
             num_scalar_prefetch=1,
             grid=(3,),
-            in_specs=[pl.BlockSpec(memory_space=pl.ANY)] * len(cots)
+            in_specs=[pl.BlockSpec(memory_space=pltpu.HBM)] * len(cots)
             + [pl.BlockSpec((3, 3 * C1, C2), lambda n, s: (0, n, 0))]
-            + [pl.BlockSpec(memory_space=pl.ANY)] * len(after),
+            + [pl.BlockSpec(memory_space=pltpu.HBM)] * len(after),
             out_specs=pl.BlockSpec((planes, CELLS // 2, PACK), lambda n, s: (0, 0, 0)),
             scratch_shapes=[
                 pltpu.VMEM(((planes + 2) * CELLS, C2), bf16),
@@ -278,7 +305,7 @@
 def weight_two_kernel(planes, pieces, scale, device_ref, *refs):
     samples = len(pieces)
     field_refs, cot_refs = refs[:samples], refs[samples:]
-    out_ref, cot_ref, flat_ref, lhs_ref, sems = refs[-5:]
+    out_ref, token_ref, cot_ref, flat_ref, lhs_ref, sems = refs[-6:]
     cells = planes * CELLS
     a = pl.program_id(0)
 
@@ -325,6 +352,7 @@
         term = jnp.dot(lhs_ref[s], cot_ref[s, rows], preferred_element_type=f32)
         total = term if total is None else total + term
     out_ref[...] = total * scale
+    token_ref[...] = jnp.zeros(token_ref.shape, f32)
 
 
 def weight_two(device, fields, pieces, cots, scale, after):
@@ -339,8 +367,11 @@
             num_scalar_prefetch=1,
             grid=(3,),
             in_specs=[pl.BlockSpec(field.shape, lambda n, s: (0, 0, 0)) for field in fields]
-            + [pl.BlockSpec(memory_space=pl.ANY)] * (len(flat) + len(after)),
-            out_specs=pl.BlockSpec((block, C2), lambda n, s: (n, 0)),
+            + [pl.BlockSpec(memory_space=pltpu.HBM)] * (len(flat) + len(after)),
+            out_specs=(
+                pl.BlockSpec((block, C2), lambda n, s: (n, 0)),
+                pl.BlockSpec((8, PACK), lambda n, s: (0, 0)),
+            ),
             scratch_shapes=[
                 pltpu.VMEM((samples, (planes + 2) * CELLS, C2), bf16),
                 pltpu.VMEM((samples, C1, cells), f32),
@@ -348,8 +379,11 @@
                 pltpu.SemaphoreType.DMA((samples, planes)),
             ],
         ),
-        out_shape=jax.ShapeDtypeStruct((TAPS * C1, C2), f32),
-        compiler_params=params(40 if samples <= 2 else 58),
+        out_shape=(
+            jax.ShapeDtypeStruct((TAPS * C1, C2), f32),
+            jax.ShapeDtypeStruct((8, PACK), f32),
+        ),
+        compiler_params=params(60),
         cost_estimate=pl.CostEstimate(
             flops=2 * samples * cells * TAPS * C1 * C2, bytes_accessed=18 << 20, transcendentals=0
         ),
@@ -407,7 +441,7 @@
     whole = pl.BlockSpec(memory_space=pltpu.VMEM)
     return pl.pallas_call(
         grad_pre_kernel,
-        in_specs=[whole] * 3 + [pl.BlockSpec(memory_space=pl.ANY)] * len(after),
+        in_specs=[whole] * 3 + [pl.BlockSpec(memory_space=pltpu.HBM)] * len(after),
         out_shape=(
             jax.ShapeDtypeStruct((rows, GROUP), bf16),
             jax.ShapeDtypeStruct((C1 // 2, 32, PACK), bf16),
@@ -454,7 +488,7 @@
     whole = pl.BlockSpec(memory_space=pltpu.VMEM)
     return pl.pallas_call(
         lambda *refs: sum_kernel(scale, *refs),
-        in_specs=[whole] + [pl.BlockSpec(memory_space=pl.ANY)] * len(after),
+        in_specs=[whole] + [pl.BlockSpec(memory_space=pltpu.HBM)] * len(after),
         out_shape=jax.ShapeDtypeStruct(shares.shape, bf16),
         compiler_params=params(16),
         cost_estimate=pl.CostEstimate(flops=0, bytes_accessed=1 << 20, transcendentals=0),
@@ -473,7 +507,7 @@
     whole = pl.BlockSpec(memory_space=pltpu.VMEM)
     return pl.pallas_call(
         unpack_kernel,
-        in_specs=[whole] + [pl.BlockSpec(memory_space=pl.ANY)] * len(after),
+        in_specs=[whole] + [pl.BlockSpec(memory_space=pltpu.HBM)] * len(after),
         out_shape=jax.ShapeDtypeStruct((TAPS, C1, C1), f32),
         scratch_shapes=[pltpu.VMEM((32 * (C1 // 2), PACK), f32)],
         compiler_params=params(16),
@@ -519,23 +553,27 @@
     band = banded(conv1_weight)
     back_band = banded(back_weight)
 
-    moved, slope, windows = conv_one(before, own, after, band)
+    moved, slope, windows = conv_one(before, own, after, band, far)
     fields = lax.all_to_all(moved, "depth", split_axis=0, concat_axis=0, tiled=True)
 
-    cots = [cot, cot_chip] + far + [flipped(value, chip) for value in far]
-    pieces = [0, chip] + outer + [difference + chip for difference in outer]
-    pieces = [[difference] for difference in pieces + [difference + core for difference in pieces]]
-    all_cots = []
-    for value in zip(*[over_samples(value) for value in cots]):
+    far = joined(far, [before, after])
+    first = joined([cot, cot_chip, far])
+    last = flipped(far, chip)
+    pieces = [[0, chip] + outer, [difference + chip for difference in outer]]
+    pieces = pieces + [[difference + core for difference in piece] for piece in pieces]
+    all_cots, all_fields = [], over_samples(fields)
+    for value in zip(over_samples(first), over_samples(last)):
         all_cots.append(list(value) + [flipped(part, core) for part in value])
     all_pieces = [pieces] * samples
-
-    partial = conv_two(fields, flat_two)
+    crossed = [part for value in all_cots[1:] for part in value[:2]]
+    swapped = [part for value in all_cots[1:] for part in value[2:]]
+
+    partial = conv_two(fields, flat_two, [last])
     features = lax.psum_scatter(partial, "depth", scatter_dimension=0, tiled=True)
 
-    grad_pieces = back_two(device, pieces, all_cots[0], flat_two, [partial])
+    grad_pieces = back_two(device, pieces, all_cots[0], flat_two, [partial] + crossed)
     grad_pieces = lax.all_to_all(grad_pieces, "depth", split_axis=0, concat_axis=0, tiled=True)
-    grad_pre, partial_one = grad_pre_of(grad_pieces, slope, windows, [])
+    grad_pre, partial_one = grad_pre_of(grad_pieces, slope, windows, swapped + all_fields[1:])
     grad_before, grad_after = neighbours(grad_pre, "depth")
 
     devices = samples * shards
@@ -544,10 +582,10 @@
     shares = partial_one.reshape(devices, -1, PACK)
     shares = lax.all_to_all(shares, both, split_axis=0, concat_axis=0, tiled=True)
     scale_two = 1.0 / math.sqrt(samples * shards * CELLS)
-    grad_conv2 = weight_two(
-        device, over_samples(fields), all_pieces, all_cots, scale_two, [grad_pre]
+    grad_conv2, token = weight_two(
+        device, all_fields, all_pieces, all_cots, scale_two, [grad_pre]
     )
-    summed = sum_shares(shares, scale_one, [grad_conv2])
+    summed = sum_shares(shares, scale_one, [token])
     shares = lax.all_to_all(summed, both, split_axis=0, concat_axis=0, tiled=True)
     grad_volume = back_one(grad_before, grad_pre, grad_after, back_band)
     grad_conv1 = unpack(shares.reshape(C1 // 2, 32, PACK), [])

time: 157 us -> 156 us (level)
  waiting for transfers between devices: 24.5 us -> 49.1 us
  starting transfers between devices: 42.9 us -> 31.7 us
  local copies, waits for them, and re-layouts: 12.5 us -> 4.7 us
  blocking collectives: 18.2 us -> 12.8 us
    ppermute x9 -> x3, waiting for transfers between devices: 5.2 us -> 25.6 us  [over_samples(): lax.ppermute(value, 'sample', [(i, (i + shift) % count) for i in range(co...]
    unnamed x59 -> x27, local copies, waits for them, and re-layouts: 12.4 us -> 4.67 us
    ppermute x9 -> x3, starting transfers between devices: 9.79 us -> 3.65 us  [over_samples(): lax.ppermute(value, 'sample', [(i, (i + shift) % count) for i in range(co...]
    all_to_all x1, blocking collectives: 18.2 us -> 12.8 us  [on_device(): lax.all_to_all(moved, 'depth', split_axis=0, concat_axis=0, tiled=True)]
    all_to_all x1, starting transfers between devices: 6.01 us -> 2.59 us  [on_device(): lax.all_to_all(shares, both, split_axis=0, concat_axis=0, tiled=True)]
    all_to_all x1, waiting for transfers between devices: 0.01 us -> 3.1 us  [on_device(): lax.all_to_all(grad_pieces, 'depth', split_axis=0, concat_axis=0, tiled=T...]
    ppermute x23 -> x9, starting transfers between devices: 8.93 us -> 6.87 us  [flipped(): lax.ppermute(value, 'depth', [(i, i ^ difference) for i in range(count)])]
    ppermute x23 -> x9, waiting for transfers between devices: 15.4 us -> 16.6 us  [flipped(): lax.ppermute(value, 'depth', [(i, i ^ difference) for i in range(count)])]
  transfers between devices with their start and end apart: 40 -> 20, of which waited for: 10 -> 9; matrix products, arithmetic and copies ran while one was open for 0% -> 0% of each run, Pallas kernels for 21% -> 22%
where the time goes in v5:
time: 156 us; the launch traced here: 155 us
  waiting for transfers between devices  49.1 us (31%)
  Pallas kernels  42.7 us (27%)
  starting transfers between devices  31.7 us (20%)
  between operations  14.3 us (9%)
  blocking collectives  12.8 us (8%)
  local copies, waits for them, and re-layouts  4.7 us (3%)
    ppermute x3, waiting for transfers between devices, over_samples(): lax.ppermute(value, 'sample', [(i, (i + shift) % count) for i in range(co...  25.6 us
    ppermute x9, waiting for transfers between devices, flipped(): lax.ppermute(value, 'depth', [(i, i ^ difference) for i in range(count)])  16.6 us
    pallas_call x1, Pallas kernels, weight_two(): pl.pallas_call(lambda *refs: weight_two_kernel(planes, pieces, scale, *re...  13.8 us
    all_to_all x1, blocking collectives, on_device(): lax.all_to_all(moved, 'depth', split_axis=0, concat_axis=0, tiled=True)  12.8 us
    pallas_call x1, Pallas kernels, back_two(): pl.pallas_call(lambda *refs: back_two_kernel(planes, pieces, *refs), grid...  11.5 us
    pallas_call x1, Pallas kernels, conv_two(): pl.pallas_call(lambda *refs: conv_two_kernel(planes, *refs), grid=(C2 //...  8.78 us
    ppermute x9, starting transfers between devices, flipped(): lax.ppermute(value, 'depth', [(i, i ^ difference) for i in range(count)])  6.87 us
    ppermute x2, starting transfers between devices, neighbours(): before = lax.ppermute(value, axis, [(i, i + 1) for i in range(count - 1)])  6.07 us
  transfers between devices with their start and end apart: 20, of which 9 were waited for; matrix products, arithmetic and copies ran while one was open for 0% of the time, Pallas kernels for 22%

profile of v5, /device:TPU:0, one launch (start us, length us, event | category | flops | bytes accessed | tf_op | source)
XLA Modules:
  0.0 155.3 jit_solution(8727778989873286231)
XLA Ops:
  7.2 1.3 collective-permute-start.1
  8.5 3.0 %collective-permute-start = (bf16[32,2048]{1,0:T(8,128)(2,1)}, bf16[32,2048]{1,0:T(8,128)(2,1)S(1)}, u32[]{:S(2)}, u32[]{:S(2)}) collective-permute-start(bf16[32,2048]{1,0:T(8,128)(2,1)} %bitcast.11), channel_id=1, source_target_pairs={{0,1},{1,2},{2,3},{3,4},{4,5},{5,6},{6,7},{7,8},{8,9},{9,10},{10,1... | collective-permute-start | bytes 393224 | tf_op jit(solution)/shard_map/ppermute | solution.py:520
  11.6 5.5 %collective-permute-start.4 = (bf16[64,1024]{1,0:T(8,128)(2,1)}, bf16[64,1024]{1,0:T(8,128)(2,1)S(1)}, u32[]{:S(2)}, u32[]{:S(2)}) collective-permute-start(bf16[64,1024]{1,0:T(8,128)(2,1)} %bitcast.13), channel_id=1, source_target_pairs={{0,12},{1,13},{2,14},{3,15},{4,8},{5,9},{6,10},{7,11},{8,4},{9,5},... | collective-permute-start | bytes 393224 | tf_op jit(solution)/shard_map/ppermute | solution.py:527
  17.7 4.0 %collective-permute-done.4.refs_2_ = bf16[64,1024]{1,0:T(8,128)(2,1)S(1)} collective-permute-done((bf16[64,1024]{1,0:T(8,128)(2,1)}, bf16[64,1024]{1,0:T(8,128)(2,1)S(1)}, u32[]{:S(2)}, u32[]{:S(2)}) %collective-permute-start.4) | collective-permute-done | bytes 131104 | tf_op jit(solution)/shard_map/ppermute | solution.py:527
  21.7 7.6 %collective-permute-done.3.refs_1_ = bf16[64,1024]{1,0:T(8,128)(2,1)S(1)} collective-permute-done((bf16[64,1024]{1,0:T(8,128)(2,1)}, bf16[64,1024]{1,0:T(8,128)(2,1)S(1)}, u32[]{:S(2)}, u32[]{:S(2)}) %collective-permute-start.3) | collective-permute-done | bytes 131104 | tf_op jit(solution)/shard_map/ppermute | solution.py:527
  32.3 12.8 %all_to_all.20.refs_0_.refs_1_ = bf16[16,32,128]{2,1,0:T(8,128)(2,1)} all-to-all(bf16[16,32,128]{2,1,0:T(8,128)(2,1)S(1)} %get-tuple-element.11), channel_id=1, replica_groups=mesh['sample'=2,'depth'=16] {'depth'}, dimensions={0} | all-to-all | bytes 262144 | tf_op jit(solution)/shard_map/all_to_all | solution.py:557
  45.0 8.8 %shard_map.78.refs_6_ = bf16[1024,1024]{1,0:T(8,128)(2,1)} custom-call(bf16[16,32,128]{2,1,0:T(8,128)(2,1)} %all_to_all.20.refs_0_.refs_1_, bf16[1728,1024]{1,0:T(8,128)(2,1)} %bitcast.19, bf16[192,1024]{1,0:T(8,128)(2,1)} %collective-permute-done.5.refs_2_.refs_4_), custom_call_target="tpu_custom_call" | custom-call | flops 3623878656 | bytes 10485760 | tf_op jit(solution)/shard_map/pallas_call | solution.py:179
  54.7 5.0 %collective-permute-done.6.refs_1_ = bf16[64,1024]{1,0:T(8,128)(2,1)S(1)} collective-permute-done((bf16[64,1024]{1,0:T(8,128)(2,1)S(1)}, bf16[64,1024]{1,0:T(8,128)(2,1)S(1)}, u32[]{:S(2)}, u32[]{:S(2)}) %collective-permute-start.6) | collective-permute-done | bytes 131104 | tf_op jit(solution)/shard_map/ppermute | solution.py:527
  59.8 1.6 %collective-permute-start.9 = (bf16[320,1024]{1,0:T(8,128)(2,1)S(1)}, bf16[320,1024]{1,0:T(8,128)(2,1)}, u32[]{:S(2)}, u32[]{:S(2)}) collective-permute-start(bf16[320,1024]{1,0:T(8,128)(2,1)S(1)} %shard_map.79.refs_1_.refs_3_), channel_id=1, source_target_pairs={{0,16},{16,0},{1,17},{17,1},{2,18},{18,2},{3,19},{19,3},{4,20},{20... | collective-permute-start | bytes 1966088 | tf_op jit(solution)/shard_map/ppermute | solution.py:533
  62.1 15.5 %collective-permute-done.9.refs_7_ = bf16[320,1024]{1,0:T(8,128)(2,1)} collective-permute-done((bf16[320,1024]{1,0:T(8,128)(2,1)S(1)}, bf16[320,1024]{1,0:T(8,128)(2,1)}, u32[]{:S(2)}, u32[]{:S(2)}) %collective-permute-start.9) | collective-permute-done | bytes 655392 | tf_op jit(solution)/shard_map/ppermute | solution.py:533
  77.6 5.6 %collective-permute-done.10.refs_8_ = bf16[192,1024]{1,0:T(8,128)(2,1)} collective-permute-done((bf16[192,1024]{1,0:T(8,128)(2,1)}, bf16[192,1024]{1,0:T(8,128)(2,1)}, u32[]{:S(2)}, u32[]{:S(2)}) %collective-permute-start.10) | collective-permute-done | bytes 393248 | tf_op jit(solution)/shard_map/ppermute | solution.py:533
  83.2 11.5 %shard_map.80 = bf16[16,32,128]{2,1,0:T(8,128)(2,1)} custom-call(s32[1]{0:T(128)} %bitcast.4.refs_0_, bf16[320,1024]{1,0:T(8,128)(2,1)} %copy-done.3, bf16[192,1024]{1,0:T(8,128)(2,1)} %collective-permute-done.5.refs_2_.refs_4_, bf16[320,1024]{1,0:T(8,128)(2,1)} %collective-permute-done.7.refs_3_.refs_5_, ...), custom_call_target="tpu_custom_call" | custom-call | flops 3623878656 | bytes 6291456 | tf_op jit(solution)/shard_map/pallas_call | solution.py:282
  94.7 4.1 %all-to-all-start.1 = ((bf16[16,32,128]{2,1,0:T(8,128)(2,1)}), bf16[16,32,128]{2,1,0:T(8,128)(2,1)S(1)}, u32[]{:S(2)}, u32[]{:S(2)}) async-start(bf16[16,32,128]{2,1,0:T(8,128)(2,1)} %shard_map.80), calls=%async_computation.2 | async-start | bytes 262144 | tf_op jit(solution)/shard_map/all_to_all | solution.py:575
  98.8 1.6 %collective-permute-start.13 = (bf16[16,32,128]{2,1,0:T(8,128)(2,1)}, bf16[16,32,128]{2,1,0:T(8,128)(2,1)S(1)}, u32[]{:S(2)}, u32[]{:S(2)}) collective-permute-start(bf16[16,32,128]{2,1,0:T(8,128)(2,1)} %all_to_all.20.refs_0_.refs_1_), channel_id=1, source_target_pairs={{0,16},{16,0},{1,17},{17,1},{2,18},{18,2},{3,19},{19,3},{4,20},{20... | collective-permute-start | bytes 393224 | tf_op jit(solution)/shard_map/ppermute | solution.py:533
  100.4 4.5 %collective-permute-done.13.refs_2_ = bf16[16,32,128]{2,1,0:T(8,128)(2,1)S(1)} collective-permute-done((bf16[16,32,128]{2,1,0:T(8,128)(2,1)}, bf16[16,32,128]{2,1,0:T(8,128)(2,1)S(1)}, u32[]{:S(2)}, u32[]{:S(2)}) %collective-permute-start.13) | collective-permute-done | bytes 131104 | tf_op jit(solution)/shard_map/ppermute | solution.py:533
  104.8 3.1 %all-to-all-done.1.pieces_ref = bf16[16,32,128]{2,1,0:T(8,128)(2,1)S(1)} async-done(((bf16[16,32,128]{2,1,0:T(8,128)(2,1)}), bf16[16,32,128]{2,1,0:T(8,128)(2,1)S(1)}, u32[]{:S(2)}, u32[]{:S(2)}) %all-to-all-start.1) | async-done | bytes 131104 | tf_op jit(solution)/shard_map/all_to_all | solution.py:575
  109.1 3.4 %shard_map.81 = (bf16[256,256]{1,0:T(8,128)(2,1)S(1)}, bf16[32,32,128]{2,1,0:T(8,128)(2,1)}) custom-call(bf16[16,32,128]{2,1,0:T(8,128)(2,1)S(1)} %all-to-all-done.1.pieces_ref, f32[256,256]{1,0:T(8,128)S(1)} %copy-done.6, bf16[256,3456]{1,0:T(8,128)(2,1)S(1)} %get-tuple-element.13.lhs_ref, bf16[320,1024]{1,0:T(8,128)(2,1)S(1)} %collective-permute-done.11.refs_0_.refs_9_, ...), custom_call_target="tpu_custom_call" | custom-call | flops 452984832 | bytes 3145728 | tf_op jit(solution)/shard_map/pallas_call | solution.py:442
  113.2 2.6 %all-to-all-start.2 = ((bf16[32,32,128]{2,1,0:T(8,128)(2,1)}), bf16[32,32,128]{2,1,0:T(8,128)(2,1)S(1)}, u32[]{:S(2)}, u32[]{:S(2)}) async-start(bf16[32,32,128]{2,1,0:T(8,128)(2,1)} %get-tuple-element.15), calls=%async_computation.3 | async-start | bytes 524288 | tf_op jit(solution)/shard_map/all_to_all | solution.py:583
  115.8 13.8 %shard_map.84 = (f32[1728,1024]{1,0:T(8,128)}, f32[8,128]{1,0:T(8,128)}) custom-call(s32[1]{0:T(128)} %bitcast.4.refs_0_, bf16[16,32,128]{2,1,0:T(8,128)(2,1)} %all_to_all.20.refs_0_.refs_1_, bf16[16,32,128]{2,1,0:T(8,128)(2,1)} %copy-done.11, bf16[320,1024]{1,0:T(8,128)(2,1)} %copy-done.3, bf16[192,1024]{1,0:T(8,128)(2,1)} %collective-permute-done.5.refs_2_.refs_4_, ...), custom_call_target="tpu_custom_call" | custom-call | flops 7247757312 | bytes 18874368 | tf_op jit(solution)/shard_map/pallas_call | solution.py:364
  131.1 5.8 %all-to-all-start.3 = ((bf16[32,32,128]{2,1,0:T(8,128)(2,1)}), bf16[32,32,128]{2,1,0:T(8,128)(2,1)S(1)}, u32[]{:S(2)}, u32[]{:S(2)}) async-start(bf16[32,32,128]{2,1,0:T(8,128)(2,1)} %shard_map.85), calls=%async_computation.4 | async-start | bytes 524288 | tf_op jit(solution)/shard_map/all_to_all | solution.py:589
  136.9 1.3 collective-permute-start.15
  138.2 3.0 %collective-permute-start.14 = (bf16[256,256]{1,0:T(8,128)(2,1)S(1)}, bf16[256,256]{1,0:T(8,128)(2,1)S(1)}, u32[]{:S(2)}, u32[]{:S(2)}) collective-permute-start(bf16[256,256]{1,0:T(8,128)(2,1)S(1)} %copy-done.10), channel_id=1, source_target_pairs={{0,1},{1,2},{2,3},{3,4},{4,5},{5,6},{6,7},{7,8},{8,9},{9,10},{10,1... | collective-permute-start | bytes 393224 | tf_op jit(solution)/shard_map/ppermute | solution.py:520
  142.2 1.4 shard_map.83
  143.6 3.6 %all-to-all-done.3.packed_ref = bf16[32,32,128]{2,1,0:T(8,128)(2,1)S(1)} async-done(((bf16[32,32,128]{2,1,0:T(8,128)(2,1)}), bf16[32,32,128]{2,1,0:T(8,128)(2,1)S(1)}, u32[]{:S(2)}, u32[]{:S(2)}) %all-to-all-start.3) | async-done | bytes 262176 | tf_op jit(solution)/shard_map/all_to_all | solution.py:589
  (58 shorter events, 10.9 us)
Async XLA Ops:
  7.2 24.1 %copy-start.7 = (bf16[1,1,32,2048]{3,2,1,0:T(8,128)(2,1)S(1)}, bf16[1,1,32,2048]{3,2,1,0:T(8,128)(2,1)}, u32[]{:S(2)}) copy-start(bf16[1,1,32,2048]{3,2,1,0:T(8,128)(2,1)} %param.4) | copy-start | bytes 393220
  7.2 141.3 %reduce-scatter.2.cloned.1.call-start = ((), (), s32[]{:S(2)}) async-start(), calls=%async_computation.5 | async-start | bytes 2228224 | tf_op jit(solution)/shard_map/reduce_scatter | solution.py:572
  7.2 10.5 %collective-permute-start.1 = (bf16[32,2048]{1,0:T(8,128)(2,1)}, bf16[32,2048]{1,0:T(8,128)(2,1)S(1)}, u32[]{:S(2)}, u32[]{:S(2)}) collective-permute-start(bf16[32,2048]{1,0:T(8,128)(2,1)} %bitcast.10), channel_id=1, source_target_pairs={{1,0},{2,1},{3,2},{4,3},{5,4},{6,5},{7,6},{8,7},{9,8},{10,9},{11,1... | collective-permute-start | bytes 393224 | tf_op jit(solution)/shard_map/ppermute | solution.py:521
  8.5 9.2 %collective-permute-start = (bf16[32,2048]{1,0:T(8,128)(2,1)}, bf16[32,2048]{1,0:T(8,128)(2,1)S(1)}, u32[]{:S(2)}, u32[]{:S(2)}) collective-permute-start(bf16[32,2048]{1,0:T(8,128)(2,1)} %bitcast.11), channel_id=1, source_target_pairs={{0,1},{1,2},{2,3},{3,4},{4,5},{5,6},{6,7},{7,8},{8,9},{9,10},{10,1... | collective-permute-start | bytes 393224 | tf_op jit(solution)/shard_map/ppermute | solution.py:520
  11.6 10.1 %collective-permute-start.4 = (bf16[64,1024]{1,0:T(8,128)(2,1)}, bf16[64,1024]{1,0:T(8,128)(2,1)S(1)}, u32[]{:S(2)}, u32[]{:S(2)}) collective-permute-start(bf16[64,1024]{1,0:T(8,128)(2,1)} %bitcast.13), channel_id=1, source_target_pairs={{0,12},{1,13},{2,14},{3,15},{4,8},{5,9},{6,10},{7,11},{8,4},{9,5},... | collective-permute-start | bytes 393224 | tf_op jit(solution)/shard_map/ppermute | solution.py:527
  17.0 12.2 %collective-permute-start.3 = (bf16[64,1024]{1,0:T(8,128)(2,1)}, bf16[64,1024]{1,0:T(8,128)(2,1)S(1)}, u32[]{:S(2)}, u32[]{:S(2)}) collective-permute-start(bf16[64,1024]{1,0:T(8,128)(2,1)} %bitcast.14), channel_id=1, source_target_pairs={{0,8},{1,9},{2,10},{3,11},{4,12},{5,13},{6,14},{7,15},{8,0},{9,1},... | collective-permute-start | bytes 393224 | tf_op jit(solution)/shard_map/ppermute | solution.py:527
  17.0 12.2 %collective-permute-start.2 = (bf16[64,1024]{1,0:T(8,128)(2,1)}, bf16[64,1024]{1,0:T(8,128)(2,1)S(1)}, u32[]{:S(2)}, u32[]{:S(2)}) collective-permute-start(bf16[64,1024]{1,0:T(8,128)(2,1)} %bitcast.15), channel_id=1, source_target_pairs={{0,4},{1,5},{2,6},{3,7},{4,0},{5,1},{6,2},{7,3},{8,12},{9,13},{10,... | collective-permute-start | bytes 393224 | tf_op jit(solution)/shard_map/ppermute | solution.py:527
  29.3 15.7 %collective-permute-start.5 = (bf16[192,1024]{1,0:T(8,128)(2,1)S(1)}, bf16[192,1024]{1,0:T(8,128)(2,1)}, u32[]{:S(2)}, u32[]{:S(2)}) collective-permute-start(bf16[192,1024]{1,0:T(8,128)(2,1)S(1)} %shard_map.77.refs_2_), channel_id=1, source_target_pairs={{0,2},{1,3},{2,0},{3,1},{4,6},{5,7},{6,4},{7,5},{8,10},{9,11},{10,... | collective-permute-start | bytes 1179656 | tf_op jit(solution)/shard_map/ppermute | solution.py:527
  54.7 5.0 %collective-permute-start.6 = (bf16[64,1024]{1,0:T(8,128)(2,1)S(1)}, bf16[64,1024]{1,0:T(8,128)(2,1)S(1)}, u32[]{:S(2)}, u32[]{:S(2)}) collective-permute-start(bf16[64,1024]{1,0:T(8,128)(2,1)S(1)} %bitcast.16), channel_id=1, source_target_pairs={{0,2},{1,3},{2,0},{3,1},{4,6},{5,7},{6,4},{7,5},{8,10},{9,11},{10,... | collective-permute-start | bytes 393224 | tf_op jit(solution)/shard_map/ppermute | solution.py:527
  59.8 23.5 %copy-start.3 = (bf16[320,1024]{1,0:T(8,128)(2,1)}, bf16[320,1024]{1,0:T(8,128)(2,1)S(1)}, u32[]{:S(2)}) copy-start(bf16[320,1024]{1,0:T(8,128)(2,1)S(1)} %shard_map.79.refs_1_.refs_3_) | copy-start | bytes 1966084
  59.8 17.8 %collective-permute-start.9 = (bf16[320,1024]{1,0:T(8,128)(2,1)S(1)}, bf16[320,1024]{1,0:T(8,128)(2,1)}, u32[]{:S(2)}, u32[]{:S(2)}) collective-permute-start(bf16[320,1024]{1,0:T(8,128)(2,1)S(1)} %shard_map.79.refs_1_.refs_3_), channel_id=1, source_target_pairs={{0,16},{16,0},{1,17},{17,1},{2,18},{18,2},{3,19},{19,3},{4,20},{20... | collective-permute-start | bytes 1966088 | tf_op jit(solution)/shard_map/ppermute | solution.py:533
  61.3 21.9 %collective-permute-start.7 = (bf16[320,1024]{1,0:T(8,128)(2,1)S(1)}, bf16[320,1024]{1,0:T(8,128)(2,1)}, u32[]{:S(2)}, u32[]{:S(2)}) collective-permute-start(bf16[320,1024]{1,0:T(8,128)(2,1)S(1)} %shard_map.79.refs_1_.refs_3_), channel_id=1, source_target_pairs={{0,1},{1,0},{2,3},{3,2},{4,5},{5,4},{6,7},{7,6},{8,9},{9,8},{10,11... | collective-permute-start | bytes 1966088 | tf_op jit(solution)/shard_map/ppermute | solution.py:527
  61.3 21.9 %collective-permute-start.10 = (bf16[192,1024]{1,0:T(8,128)(2,1)}, bf16[192,1024]{1,0:T(8,128)(2,1)}, u32[]{:S(2)}, u32[]{:S(2)}) collective-permute-start(bf16[192,1024]{1,0:T(8,128)(2,1)} %collective-permute-done.5.refs_2_.refs_4_), channel_id=1, source_target_pairs={{0,16},{16,0},{1,17},{17,1},{2,18},{18,2},{3,19},{19,3},{4,20},{20... | collective-permute-start | bytes 1179656 | tf_op jit(solution)/shard_map/ppermute | solution.py:533
  61.9 21.3 %collective-permute-start.8 = (bf16[192,1024]{1,0:T(8,128)(2,1)}, bf16[192,1024]{1,0:T(8,128)(2,1)}, u32[]{:S(2)}, u32[]{:S(2)}) collective-permute-start(bf16[192,1024]{1,0:T(8,128)(2,1)} %collective-permute-done.5.refs_2_.refs_4_), channel_id=1, source_target_pairs={{0,1},{1,0},{2,3},{3,2},{4,5},{5,4},{6,7},{7,6},{8,9},{9,8},{10,11... | collective-permute-start | bytes 1179656 | tf_op jit(solution)/shard_map/ppermute | solution.py:527
  77.6 30.3 %collective-permute-start.11 = (bf16[320,1024]{1,0:T(8,128)(2,1)}, bf16[320,1024]{1,0:T(8,128)(2,1)S(1)}, u32[]{:S(2)}, u32[]{:S(2)}) collective-permute-start(bf16[320,1024]{1,0:T(8,128)(2,1)} %collective-permute-done.9.refs_7_), channel_id=1, source_target_pairs={{0,1},{1,0},{2,3},{3,2},{4,5},{5,4},{6,7},{7,6},{8,9},{9,8},{10,11... | collective-permute-start | bytes 1966088 | tf_op jit(solution)/shard_map/ppermute | solution.py:527
  83.2 24.7 %collective-permute-start.12 = (bf16[192,1024]{1,0:T(8,128)(2,1)}, bf16[192,1024]{1,0:T(8,128)(2,1)S(1)}, u32[]{:S(2)}, u32[]{:S(2)}) collective-permute-start(bf16[192,1024]{1,0:T(8,128)(2,1)} %collective-permute-done.10.refs_8_), channel_id=1, source_target_pairs={{0,1},{1,0},{2,3},{3,2},{4,5},{5,4},{6,7},{7,6},{8,9},{9,8},{10,11... | collective-permute-start | bytes 1179656 | tf_op jit(solution)/shard_map/ppermute | solution.py:527
  94.7 13.2 %all-to-all-start.1 = ((bf16[16,32,128]{2,1,0:T(8,128)(2,1)}), bf16[16,32,128]{2,1,0:T(8,128)(2,1)S(1)}, u32[]{:S(2)}, u32[]{:S(2)}) async-start(bf16[16,32,128]{2,1,0:T(8,128)(2,1)} %shard_map.80), calls=%async_computation.2 | async-start | bytes 262144 | tf_op jit(solution)/shard_map/all_to_all | solution.py:575
  98.8 6.0 %collective-permute-start.13 = (bf16[16,32,128]{2,1,0:T(8,128)(2,1)}, bf16[16,32,128]{2,1,0:T(8,128)(2,1)S(1)}, u32[]{:S(2)}, u32[]{:S(2)}) collective-permute-start(bf16[16,32,128]{2,1,0:T(8,128)(2,1)} %all_to_all.20.refs_0_.refs_1_), channel_id=1, source_target_pairs={{0,16},{16,0},{1,17},{17,1},{2,18},{18,2},{3,19},{19,3},{4,20},{20... | collective-permute-start | bytes 393224 | tf_op jit(solution)/shard_map/ppermute | solution.py:533
  113.2 16.5 %all-to-all-start.2 = ((bf16[32,32,128]{2,1,0:T(8,128)(2,1)}), bf16[32,32,128]{2,1,0:T(8,128)(2,1)S(1)}, u32[]{:S(2)}, u32[]{:S(2)}) async-start(bf16[32,32,128]{2,1,0:T(8,128)(2,1)} %get-tuple-element.15), calls=%async_computation.3 | async-start | bytes 524288 | tf_op jit(solution)/shard_map/all_to_all | solution.py:583
  115.8 21.1 %copy-start.10 = (bf16[256,256]{1,0:T(8,128)(2,1)S(1)}, bf16[256,256]{1,0:T(8,128)(2,1)}, u32[]{:S(2)}) copy-start(bf16[256,256]{1,0:T(8,128)(2,1)} %copy-done.9) | copy-start | bytes 393220
  115.8 25.5 %copy-start.1 = (bf16[27,64,64]{2,1,0:T(8,128)(2,1)S(1)}, bf16[27,64,64]{2,1,0:T(8,128)(2,1)}, u32[]{:S(2)}) copy-start(bf16[27,64,64]{2,1,0:T(8,128)(2,1)} %w_ref.1) | copy-start | bytes 663556
  131.1 16.1 %all-to-all-start.3 = ((bf16[32,32,128]{2,1,0:T(8,128)(2,1)}), bf16[32,32,128]{2,1,0:T(8,128)(2,1)S(1)}, u32[]{:S(2)}, u32[]{:S(2)}) async-start(bf16[32,32,128]{2,1,0:T(8,128)(2,1)} %shard_map.85), calls=%async_computation.4 | async-start | bytes 524288 | tf_op jit(solution)/shard_map/all_to_all | solution.py:589
  136.9 5.0 %collective-permute-start.15 = (bf16[256,256]{1,0:T(8,128)(2,1)S(1)}, bf16[256,256]{1,0:T(8,128)(2,1)S(1)}, u32[]{:S(2)}, u32[]{:S(2)}) collective-permute-start(bf16[256,256]{1,0:T(8,128)(2,1)S(1)} %copy-done.10), channel_id=1, source_target_pairs={{1,0},{2,1},{3,2},{4,3},{5,4},{6,5},{7,6},{8,7},{9,8},{10,9},{11,1... | collective-permute-start | bytes 393224 | tf_op jit(solution)/shard_map/ppermute | solution.py:521
  138.2 4.0 %collective-permute-start.14 = (bf16[256,256]{1,0:T(8,128)(2,1)S(1)}, bf16[256,256]{1,0:T(8,128)(2,1)S(1)}, u32[]{:S(2)}, u32[]{:S(2)}) collective-permute-start(bf16[256,256]{1,0:T(8,128)(2,1)S(1)} %copy-done.10), channel_id=1, source_target_pairs={{0,1},{1,2},{2,3},{3,4},{4,5},{5,6},{6,7},{7,8},{8,9},{9,10},{10,1... | collective-permute-start | bytes 393224 | tf_op jit(solution)/shard_map/ppermute | solution.py:520
  (9 other events, 43.9 us)
Sparse Core Ops, SparseCore 0:
  54.0 60.7 reduce-scatter.1

commit v6 on v5

--- a/solution.py
+++ b/solution.py
@@ -106,7 +106,7 @@
     whole = pl.BlockSpec(memory_space=pltpu.VMEM)
     return pl.pallas_call(
         conv_one_kernel,
-        in_specs=[whole] * 4 + [pl.BlockSpec(memory_space=pltpu.HBM)] * len(waits),
+        in_specs=[whole] * 4 + [pl.BlockSpec(memory_space=pl.ANY)] * len(waits),
         out_shape=(
             jax.ShapeDtypeStruct((BLOCK * BLOCK, CELLS // 2, PACK), bf16),
             jax.ShapeDtypeStruct((rows, GROUP), f32),
@@ -183,7 +183,7 @@
             pl.BlockSpec(pieces.shape, lambda n: (0, 0, 0)),
             pl.BlockSpec((TAPS * C1, block), lambda n: (0, n)),
         ]
-        + [pl.BlockSpec(memory_space=pltpu.HBM)] * len(after),
+        + [pl.BlockSpec(memory_space=pl.ANY)] * len(after),
         out_specs=pl.BlockSpec((cells, block), lambda n: (0, n)),
         out_shape=jax.ShapeDtypeStruct((cells, C2), bf16),
         scratch_shapes=[
@@ -195,29 +195,6 @@
             flops=2 * cells * TAPS * C1 * C2, bytes_accessed=10 << 20, transcendentals=0
         ),
     )(pieces, weight, *after)
-
-
-def join_kernel(count, *refs):
-    out_ref, first = refs[-1], 0
-    for ref in refs[:count]:
-        rows = ref.shape[0]
-        out_ref[first : first + rows] = ref[...]
-        first += rows
-
-
-def joined(values, after=()):
-    rows = sum(value.shape[0] for value in values)
-    columns = values[0].shape[1]
-    return pl.pallas_call(
-        lambda *refs: join_kernel(len(values), *refs),
-        grid=(1,),
-        in_specs=[pl.BlockSpec(value.shape, lambda n: (0, 0)) for value in values]
-        + [pl.BlockSpec(memory_space=pl.ANY)] * len(after),
-        out_specs=pl.BlockSpec((rows, columns), lambda n: (0, 0)),
-        out_shape=jax.ShapeDtypeStruct((rows, columns), values[0].dtype),
-        compiler_params=params(32),
-        cost_estimate=pl.CostEstimate(flops=0, bytes_accessed=4 * rows * columns, transcendentals=0),
-    )(*values, *after)
 
 
 def plane_copies(device, pieces, refs, target_ref, base, sems):
@@ -284,9 +261,9 @@
         grid_spec=pltpu.PrefetchScalarGridSpec(
             num_scalar_prefetch=1,
             grid=(3,),
-            in_specs=[pl.BlockSpec(memory_space=pltpu.HBM)] * len(cots)
+            in_specs=[pl.BlockSpec(memory_space=pl.ANY)] * len(cots)
             + [pl.BlockSpec((3, 3 * C1, C2), lambda n, s: (0, n, 0))]
-            + [pl.BlockSpec(memory_space=pltpu.HBM)] * len(after),
+            + [pl.BlockSpec(memory_space=pl.ANY)] * len(after),
             out_specs=pl.BlockSpec((planes, CELLS // 2, PACK), lambda n, s: (0, 0, 0)),
             scratch_shapes=[
                 pltpu.VMEM(((planes + 2) * CELLS, C2), bf16),
@@ -367,7 +344,7 @@
             num_scalar_prefetch=1,
             grid=(3,),
             in_specs=[pl.BlockSpec(field.shape, lambda n, s: (0, 0, 0)) for field in fields]
-            + [pl.BlockSpec(memory_space=pltpu.HBM)] * (len(flat) + len(after)),
+            + [pl.BlockSpec(memory_space=pl.ANY)] * (len(flat) + len(after)),
             out_specs=(
                 pl.BlockSpec((block, C2), lambda n, s: (n, 0)),
                 pl.BlockSpec((8, PACK), lambda n, s: (0, 0)),
@@ -441,7 +418,7 @@
     whole = pl.BlockSpec(memory_space=pltpu.VMEM)
     return pl.pallas_call(
         grad_pre_kernel,
-        in_specs=[whole] * 3 + [pl.BlockSpec(memory_space=pltpu.HBM)] * len(after),
+        in_specs=[whole] * 3 + [pl.BlockSpec(memory_space=pl.ANY)] * len(after),
         out_shape=(
             jax.ShapeDtypeStruct((rows, GROUP), bf16),
             jax.ShapeDtypeStruct((C1 // 2, 32, PACK), bf16),
@@ -488,7 +465,7 @@
     whole = pl.BlockSpec(memory_space=pltpu.VMEM)
     return pl.pallas_call(
         lambda *refs: sum_kernel(scale, *refs),
-        in_specs=[whole] + [pl.BlockSpec(memory_space=pltpu.HBM)] * len(after),
+        in_specs=[whole] + [pl.BlockSpec(memory_space=pl.ANY)] * len(after),
         out_shape=jax.ShapeDtypeStruct(shares.shape, bf16),
         compiler_params=params(16),
         cost_estimate=pl.CostEstimate(flops=0, bytes_accessed=1 << 20, transcendentals=0),
@@ -507,7 +484,7 @@
     whole = pl.BlockSpec(memory_space=pltpu.VMEM)
     return pl.pallas_call(
         unpack_kernel,
-        in_specs=[whole] + [pl.BlockSpec(memory_space=pltpu.HBM)] * len(after),
+        in_specs=[whole] + [pl.BlockSpec(memory_space=pl.ANY)] * len(after),
         out_shape=jax.ShapeDtypeStruct((TAPS, C1, C1), f32),
         scratch_shapes=[pltpu.VMEM((32 * (C1 // 2), PACK), f32)],
         compiler_params=params(16),
@@ -545,35 +522,40 @@
 
     core, chip = 1, 2
     outer = list(range(4, shards, 4))
+    far = [flipped(cot, difference) for difference in outer]
     before, after = neighbours(own, "depth")
-    far = [flipped(cot, difference) for difference in outer]
     cot_chip = flipped(cot, chip)
 
     back_weight = jnp.swapaxes(conv1_weight[::-1], 1, 2)
     band = banded(conv1_weight)
     back_band = banded(back_weight)
 
-    moved, slope, windows = conv_one(before, own, after, band, far)
+    moved, slope, windows = conv_one(before, own, after, band, [])
     fields = lax.all_to_all(moved, "depth", split_axis=0, concat_axis=0, tiled=True)
 
-    far = joined(far, [before, after])
-    first = joined([cot, cot_chip, far])
-    last = flipped(far, chip)
-    pieces = [[0, chip] + outer, [difference + chip for difference in outer]]
+    near = jnp.concatenate([cot, cot_chip], axis=0)
+    far = jnp.concatenate(far, axis=0)
+    far_chip = flipped(far, chip)
+    cots = [near, far, far_chip]
+    pieces = [[0, chip], outer, [difference + chip for difference in outer]]
     pieces = pieces + [[difference + core for difference in piece] for piece in pieces]
-    all_cots, all_fields = [], over_samples(fields)
-    for value in zip(over_samples(first), over_samples(last)):
-        all_cots.append(list(value) + [flipped(part, core) for part in value])
-    all_pieces = [pieces] * samples
-    crossed = [part for value in all_cots[1:] for part in value[:2]]
-    swapped = [part for value in all_cots[1:] for part in value[2:]]
-
-    partial = conv_two(fields, flat_two, [last])
+
+    partial = conv_two(fields, flat_two, [])
     features = lax.psum_scatter(partial, "depth", scatter_dimension=0, tiled=True)
 
-    grad_pieces = back_two(device, pieces, all_cots[0], flat_two, [partial] + crossed)
+    own_cots = cots + [flipped(value, core) for value in cots]
+    half = jnp.concatenate(cots, axis=0)
+    halves = [[difference for piece in group for difference in piece] for group in (pieces[:3], pieces[3:])]
+    all_pieces, all_cots = [pieces], [own_cots]
+    for value in over_samples(half)[1:]:
+        all_pieces.append(halves)
+        all_cots.append([value, flipped(value, core)])
+    all_fields = over_samples(fields)
+    swapped = [value[1] for value in all_cots[1:]]
+
+    grad_pieces = back_two(device, pieces, own_cots, flat_two, [partial])
     grad_pieces = lax.all_to_all(grad_pieces, "depth", split_axis=0, concat_axis=0, tiled=True)
-    grad_pre, partial_one = grad_pre_of(grad_pieces, slope, windows, swapped + all_fields[1:])
+    grad_pre, partial_one = grad_pre_of(grad_pieces, slope, windows, swapped)
     grad_before, grad_after = neighbours(grad_pre, "depth")
 
     devices = samples * shards

time: 156 us -> 149 us (0.955)
  starting transfers between devices: 31.7 us -> 45 us
  blocking collectives: 12.8 us -> 0 us
  waiting for transfers between devices: 49.1 us -> 37.9 us
  local copies, waits for them, and re-layouts: 4.7 us -> 6.52 us
    ppermute x3 -> x2, waiting for transfers between devices: 25.6 us -> 9.36 us  [over_samples(): lax.ppermute(value, 'sample', [(i, (i + shift) % count) for i in range(co...]
    all_to_all x1 -> x0, blocking collectives: 12.8 us -> none  [on_device(): lax.all_to_all(moved, 'depth', split_axis=0, concat_axis=0, tiled=True)]
    all_to_all x0 -> x1, starting transfers between devices: none -> 8.78 us  [on_device(): lax.all_to_all(moved, 'depth', split_axis=0, concat_axis=0, tiled=True)]
    ppermute x9, waiting for transfers between devices: 16.6 us -> 10.8 us  [flipped(): lax.ppermute(value, 'depth', [(i, i ^ difference) for i in range(count)])]
    all_to_all x0 -> x1, waiting for transfers between devices: none -> 5.51 us  [on_device(): lax.all_to_all(moved, 'depth', split_axis=0, concat_axis=0, tiled=True)]
    all_to_all x1, waiting for transfers between devices: 3.1 us -> 8.32 us  [on_device(): lax.all_to_all(grad_pieces, 'depth', split_axis=0, concat_axis=0, tiled=T...]
    ppermute x9, starting transfers between devices: 6.87 us -> 10 us  [flipped(): lax.ppermute(value, 'depth', [(i, i ^ difference) for i in range(count)])]
    all_to_all x1, starting transfers between devices: 4.09 us -> 5.72 us  [on_device(): lax.all_to_all(grad_pieces, 'depth', split_axis=0, concat_axis=0, tiled=T...]
  transfers between devices with their start and end apart: 20 -> 20, of which waited for: 9 -> 9; matrix products, arithmetic and copies ran while one was open for 0% -> 2% of each run, Pallas kernels for 22% -> 29%
where the time goes in v6:
time: 149 us; the launch traced here: 148 us
  starting transfers between devices  45 us (30%)
  Pallas kernels  43.3 us (29%)
  waiting for transfers between devices  37.9 us (25%)
  between operations  14.3 us (10%)
  local copies, waits for them, and re-layouts  6.52 us (4%)
    pallas_call x1, Pallas kernels, weight_two(): pl.pallas_call(lambda *refs: weight_two_kernel(planes, pieces, scale, *re...  13.7 us
    pallas_call x1, Pallas kernels, back_two(): pl.pallas_call(lambda *refs: back_two_kernel(planes, pieces, *refs), grid...  11.6 us
    ppermute x9, waiting for transfers between devices, flipped(): lax.ppermute(value, 'depth', [(i, i ^ difference) for i in range(count)])  10.8 us
    ppermute x9, starting transfers between devices, flipped(): lax.ppermute(value, 'depth', [(i, i ^ difference) for i in range(count)])  10 us
    ppermute x2, waiting for transfers between devices, over_samples(): lax.ppermute(value, 'sample', [(i, (i + shift) % count) for i in range(co...  9.36 us
    all_to_all x1, starting transfers between devices, on_device(): lax.all_to_all(moved, 'depth', split_axis=0, concat_axis=0, tiled=True)  8.78 us
    pallas_call x1, Pallas kernels, conv_two(): pl.pallas_call(lambda *refs: conv_two_kernel(planes, *refs), grid=(C2 //...  8.76 us
    all_to_all x1, waiting for transfers between devices, on_device(): lax.all_to_all(grad_pieces, 'depth', split_axis=0, concat_axis=0, tiled=T...  8.32 us
  transfers between devices with their start and end apart: 20, of which 9 were waited for; matrix products, arithmetic and copies ran while one was open for 2% of the time, Pallas kernels for 29%

profile of v6, /device:TPU:0, one launch (start us, length us, event | category | flops | bytes accessed | tf_op | source)
XLA Modules:
  0.0 147.9 jit_solution(4170339953187831971)
XLA Ops:
  7.2 5.1 %collective-permute-start.5 = (bf16[64,1024]{1,0:T(8,128)(2,1)}, bf16[64,1024]{1,0:T(8,128)(2,1)S(1)}, u32[]{:S(2)}, u32[]{:S(2)}) collective-permute-start(bf16[64,1024]{1,0:T(8,128)(2,1)} %bitcast.14), channel_id=1, source_target_pairs={{0,12},{1,13},{2,14},{3,15},{4,8},{5,9},{6,10},{7,11},{8,4},{9,5},... | collective-permute-start | bytes 393224 | tf_op jit(solution)/shard_map/ppermute | solution.py:504
  12.9 1.7 %collective-permute-start.2 = (bf16[64,1024]{1,0:T(8,128)(2,1)}, bf16[64,1024]{1,0:T(8,128)(2,1)S(1)}, u32[]{:S(2)}, u32[]{:S(2)}) collective-permute-start(bf16[64,1024]{1,0:T(8,128)(2,1)} %bitcast.17), channel_id=1, source_target_pairs={{0,2},{1,3},{2,0},{3,1},{4,6},{5,7},{6,4},{7,5},{8,10},{9,11},{10,... | collective-permute-start | bytes 393224 | tf_op jit(solution)/shard_map/ppermute | solution.py:504
  15.5 2.6 %collective-permute-done.2 = bf16[64,1024]{1,0:T(8,128)(2,1)S(1)} collective-permute-done((bf16[64,1024]{1,0:T(8,128)(2,1)}, bf16[64,1024]{1,0:T(8,128)(2,1)S(1)}, u32[]{:S(2)}, u32[]{:S(2)}) %collective-permute-start.2) | collective-permute-done | bytes 131104 | tf_op jit(solution)/shard_map/ppermute | solution.py:504
  18.1 2.9 %collective-permute-done.3 = bf16[64,1024]{1,0:T(8,128)(2,1)S(1)} collective-permute-done((bf16[64,1024]{1,0:T(8,128)(2,1)}, bf16[64,1024]{1,0:T(8,128)(2,1)S(1)}, u32[]{:S(2)}, u32[]{:S(2)}) %collective-permute-start.3) | collective-permute-done | bytes 131104 | tf_op jit(solution)/shard_map/ppermute | solution.py:504
  21.0 2.5 %collective-permute-done.4 = bf16[64,1024]{1,0:T(8,128)(2,1)S(1)} collective-permute-done((bf16[64,1024]{1,0:T(8,128)(2,1)}, bf16[64,1024]{1,0:T(8,128)(2,1)S(1)}, u32[]{:S(2)}, u32[]{:S(2)}) %collective-permute-start.4) | collective-permute-done | bytes 131104 | tf_op jit(solution)/shard_map/ppermute | solution.py:504
  23.7 1.6 %collective-permute-start.6 = (bf16[192,1024]{1,0:T(8,128)(2,1)S(1)}, bf16[192,1024]{1,0:T(8,128)(2,1)S(1)}, u32[]{:S(2)}, u32[]{:S(2)}) collective-permute-start(bf16[192,1024]{1,0:T(8,128)(2,1)S(1)} %get-tuple-element.19.refs_2_.refs_4_), channel_id=1, source_target_pairs={{0,2},{1,3},{2,0},{3,1},{4,6},{5,7},{6,4},{7,5},{8,10},{9,11},{10,... | collective-permute-start | bytes 1179656 | tf_op jit(solution)/shard_map/ppermute | solution.py:504
  26.5 3.0 %collective-permute-start = (bf16[32,2048]{1,0:T(8,128)(2,1)}, bf16[32,2048]{1,0:T(8,128)(2,1)S(1)}, u32[]{:S(2)}, u32[]{:S(2)}) collective-permute-start(bf16[32,2048]{1,0:T(8,128)(2,1)} %bitcast.12), channel_id=1, source_target_pairs={{0,1},{1,2},{2,3},{3,4},{4,5},{5,6},{6,7},{7,8},{8,9},{9,10},{10,1... | collective-permute-start | bytes 393224 | tf_op jit(solution)/shard_map/ppermute | solution.py:497
  31.0 1.7 %shard_map.76 = (bf16[16,32,128]{2,1,0:T(8,128)(2,1)}, f32[256,256]{1,0:T(8,128)S(1)}, bf16[256,3456]{1,0:T(8,128)(2,1)S(1)}) custom-call(bf16[32,2048]{1,0:T(8,128)(2,1)S(1)} %collective-permute-done.before_ref, bf16[32,2048]{1,0:T(8,128)(2,1)S(1)} %bitcast.13, bf16[32,2048]{1,0:T(8,128)(2,1)S(1)} %collective-permute-done.1.after_ref, ...), custom_call_target="tpu_custom_call" | custom-call | flops 452984832 | bytes 5242880 | tf_op jit(solution)/shard_map/pallas_call | solution.py:107
  32.7 8.8 %all-to-all-start = ((bf16[16,32,128]{2,1,0:T(8,128)(2,1)}), bf16[16,32,128]{2,1,0:T(8,128)(2,1)S(1)}, u32[]{:S(2)}, u32[]{:S(2)}) async-start(bf16[16,32,128]{2,1,0:T(8,128)(2,1)} %get-tuple-element.11), calls=%async_computation | async-start | bytes 262144 | tf_op jit(solution)/shard_map/all_to_all | solution.py:534
  42.5 1.5 %collective-permute-start.10 = (bf16[512,1024]{1,0:T(8,128)(2,1)}, bf16[512,1024]{1,0:T(8,128)(2,1)}, u32[]{:S(2)}, u32[]{:S(2)}) collective-permute-start(bf16[512,1024]{1,0:T(8,128)(2,1)} %constant_dynamic-update-slice_fusion.3), channel_id=1, source_target_pairs={{0,16},{16,0},{1,17},{17,1},{2,18},{18,2},{3,19},{19,3},{4,20},{20... | collective-permute-start | bytes 3145736 | tf_op jit(solution)/shard_map/ppermute | solution.py:510
  43.9 5.5 %all-to-all-done.refs_0_.refs_1_ = bf16[16,32,128]{2,1,0:T(8,128)(2,1)S(1)} async-done(((bf16[16,32,128]{2,1,0:T(8,128)(2,1)}), bf16[16,32,128]{2,1,0:T(8,128)(2,1)S(1)}, u32[]{:S(2)}, u32[]{:S(2)}) %all-to-all-start) | async-done | bytes 131104 | tf_op jit(solution)/shard_map/all_to_all | solution.py:534
  50.1 8.8 %shard_map.77.refs_8_ = bf16[1024,1024]{1,0:T(8,128)(2,1)} custom-call(bf16[16,32,128]{2,1,0:T(8,128)(2,1)} %copy-done.9, bf16[1728,1024]{1,0:T(8,128)(2,1)} %bitcast.20), custom_call_target="tpu_custom_call" | custom-call | flops 3623878656 | bytes 10485760 | tf_op jit(solution)/shard_map/pallas_call | solution.py:179
  58.9 9.4 %collective-permute-done.10.refs_9_ = bf16[512,1024]{1,0:T(8,128)(2,1)} collective-permute-done((bf16[512,1024]{1,0:T(8,128)(2,1)}, bf16[512,1024]{1,0:T(8,128)(2,1)}, u32[]{:S(2)}, u32[]{:S(2)}) %collective-permute-start.10) | collective-permute-done | bytes 1048608 | tf_op jit(solution)/shard_map/ppermute | solution.py:510
  70.0 2.8 %collective-permute-done.7.refs_4_.refs_6_ = bf16[128,1024]{1,0:T(8,128)(2,1)S(1)} collective-permute-done((bf16[128,1024]{1,0:T(8,128)(2,1)}, bf16[128,1024]{1,0:T(8,128)(2,1)S(1)}, u32[]{:S(2)}, u32[]{:S(2)}) %collective-permute-start.7) | collective-permute-done | bytes 262176 | tf_op jit(solution)/shard_map/ppermute | solution.py:504
  73.5 11.6 %shard_map.78 = bf16[16,32,128]{2,1,0:T(8,128)(2,1)} custom-call(s32[1]{0:T(128)} %bitcast.3.refs_0_, bf16[128,1024]{1,0:T(8,128)(2,1)} %pad_maximum_fusion.refs_1_.refs_3_, bf16[192,1024]{1,0:T(8,128)(2,1)} %copy-done.11, bf16[192,1024]{1,0:T(8,128)(2,1)} %copy-done.8, bf16[128,1024]{1,0:T(8,128)(2,1)} %copy-done.13, ...), custom_call_target="tpu_custom_call" | custom-call | flops 3623878656 | bytes 6291456 | tf_op jit(solution)/shard_map/pallas_call | solution.py:259
  85.1 5.7 %all-to-all-start.1 = ((bf16[16,32,128]{2,1,0:T(8,128)(2,1)}), bf16[16,32,128]{2,1,0:T(8,128)(2,1)S(1)}, u32[]{:S(2)}, u32[]{:S(2)}) async-start(bf16[16,32,128]{2,1,0:T(8,128)(2,1)} %shard_map.78), calls=%async_computation.2 | async-start | bytes 262144 | tf_op jit(solution)/shard_map/all_to_all | solution.py:557
  90.9 1.5 %collective-permute-start.14 = (bf16[16,32,128]{2,1,0:T(8,128)(2,1)S(1)}, bf16[16,32,128]{2,1,0:T(8,128)(2,1)S(1)}, u32[]{:S(2)}, u32[]{:S(2)}) collective-permute-start(bf16[16,32,128]{2,1,0:T(8,128)(2,1)S(1)} %copy-done.10), channel_id=1, source_target_pairs={{0,16},{16,0},{1,17},{17,1},{2,18},{18,2},{3,19},{19,3},{4,20},{20... | collective-permute-start | bytes 393224 | tf_op jit(solution)/shard_map/ppermute | solution.py:510
  92.4 8.3 %all-to-all-done.1.pieces_ref = bf16[16,32,128]{2,1,0:T(8,128)(2,1)S(1)} async-done(((bf16[16,32,128]{2,1,0:T(8,128)(2,1)}), bf16[16,32,128]{2,1,0:T(8,128)(2,1)S(1)}, u32[]{:S(2)}, u32[]{:S(2)}) %all-to-all-start.1) | async-done | bytes 131104 | tf_op jit(solution)/shard_map/all_to_all | solution.py:557
  100.7 3.4 %shard_map.79 = (bf16[256,256]{1,0:T(8,128)(2,1)S(1)}, bf16[32,32,128]{2,1,0:T(8,128)(2,1)}) custom-call(bf16[16,32,128]{2,1,0:T(8,128)(2,1)S(1)} %all-to-all-done.1.pieces_ref, f32[256,256]{1,0:T(8,128)S(1)} %get-tuple-element.12.slope_ref, bf16[256,3456]{1,0:T(8,128)(2,1)S(1)} %get-tuple-element.13.lhs_ref, ...), custom_call_target="tpu_custom_call" | custom-call | flops 452984832 | bytes 3145728 | tf_op jit(solution)/shard_map/pallas_call | solution.py:419
  104.8 3.0 %all-to-all-start.2 = ((bf16[32,32,128]{2,1,0:T(8,128)(2,1)}), bf16[32,32,128]{2,1,0:T(8,128)(2,1)S(1)}, u32[]{:S(2)}, u32[]{:S(2)}) async-start(bf16[32,32,128]{2,1,0:T(8,128)(2,1)} %get-tuple-element.15), calls=%async_computation.3 | async-start | bytes 524288 | tf_op jit(solution)/shard_map/all_to_all | solution.py:565
  108.4 13.7 %shard_map.82 = (f32[1728,1024]{1,0:T(8,128)}, f32[8,128]{1,0:T(8,128)}) custom-call(s32[1]{0:T(128)} %bitcast.3.refs_0_, bf16[16,32,128]{2,1,0:T(8,128)(2,1)} %copy-done.9, bf16[16,32,128]{2,1,0:T(8,128)(2,1)} %copy-done.14, bf16[128,1024]{1,0:T(8,128)(2,1)} %pad_maximum_fusion.refs_1_.refs_3_, bf16[192,1024]{1,0:T(8,128)(2,1)} %copy-done.11, ...), custom_call_target="tpu_custom_call" | custom-call | flops 7247757312 | bytes 18874368 | tf_op jit(solution)/shard_map/pallas_call | solution.py:341
  123.6 5.8 %all-to-all-start.3 = ((bf16[32,32,128]{2,1,0:T(8,128)(2,1)}), bf16[32,32,128]{2,1,0:T(8,128)(2,1)S(1)}, u32[]{:S(2)}, u32[]{:S(2)}) async-start(bf16[32,32,128]{2,1,0:T(8,128)(2,1)} %shard_map.83), calls=%async_computation.4 | async-start | bytes 524288 | tf_op jit(solution)/shard_map/all_to_all | solution.py:571
  130.7 3.0 %collective-permute-start.12 = (bf16[256,256]{1,0:T(8,128)(2,1)S(1)}, bf16[256,256]{1,0:T(8,128)(2,1)S(1)}, u32[]{:S(2)}, u32[]{:S(2)}) collective-permute-start(bf16[256,256]{1,0:T(8,128)(2,1)S(1)} %copy-done.5), channel_id=1, source_target_pairs={{0,1},{1,2},{2,3},{3,4},{4,5},{5,6},{6,7},{7,8},{8,9},{9,10},{10,1... | collective-permute-start | bytes 393224 | tf_op jit(solution)/shard_map/ppermute | solution.py:497
  136.1 3.6 %all-to-all-done.3.packed_ref = bf16[32,32,128]{2,1,0:T(8,128)(2,1)S(1)} async-done(((bf16[32,32,128]{2,1,0:T(8,128)(2,1)}), bf16[32,32,128]{2,1,0:T(8,128)(2,1)S(1)}, u32[]{:S(2)}, u32[]{:S(2)}) %all-to-all-start.3) | async-done | bytes 262176 | tf_op jit(solution)/shard_map/all_to_all | solution.py:571
  (66 shorter events, 16.0 us)
Async XLA Ops:
  7.2 23.9 %copy-start.3 = (bf16[1,1,32,2048]{3,2,1,0:T(8,128)(2,1)S(1)}, bf16[1,1,32,2048]{3,2,1,0:T(8,128)(2,1)}, u32[]{:S(2)}) copy-start(bf16[1,1,32,2048]{3,2,1,0:T(8,128)(2,1)} %param.4) | copy-start | bytes 393220
  7.2 16.4 %collective-permute-start.5 = (bf16[64,1024]{1,0:T(8,128)(2,1)}, bf16[64,1024]{1,0:T(8,128)(2,1)S(1)}, u32[]{:S(2)}, u32[]{:S(2)}) collective-permute-start(bf16[64,1024]{1,0:T(8,128)(2,1)} %bitcast.14), channel_id=1, source_target_pairs={{0,12},{1,13},{2,14},{3,15},{4,8},{5,9},{6,10},{7,11},{8,4},{9,5},... | collective-permute-start | bytes 393224 | tf_op jit(solution)/shard_map/ppermute | solution.py:504
  12.3 11.3 %collective-permute-start.4 = (bf16[64,1024]{1,0:T(8,128)(2,1)}, bf16[64,1024]{1,0:T(8,128)(2,1)S(1)}, u32[]{:S(2)}, u32[]{:S(2)}) collective-permute-start(bf16[64,1024]{1,0:T(8,128)(2,1)} %bitcast.15), channel_id=1, source_target_pairs={{0,8},{1,9},{2,10},{3,11},{4,12},{5,13},{6,14},{7,15},{8,0},{9,1},... | collective-permute-start | bytes 393224 | tf_op jit(solution)/shard_map/ppermute | solution.py:504
  12.3 8.7 %collective-permute-start.3 = (bf16[64,1024]{1,0:T(8,128)(2,1)}, bf16[64,1024]{1,0:T(8,128)(2,1)S(1)}, u32[]{:S(2)}, u32[]{:S(2)}) collective-permute-start(bf16[64,1024]{1,0:T(8,128)(2,1)} %bitcast.16), channel_id=1, source_target_pairs={{0,4},{1,5},{2,6},{3,7},{4,0},{5,1},{6,2},{7,3},{8,12},{9,13},{10,... | collective-permute-start | bytes 393224 | tf_op jit(solution)/shard_map/ppermute | solution.py:504
  12.9 5.2 %collective-permute-start.2 = (bf16[64,1024]{1,0:T(8,128)(2,1)}, bf16[64,1024]{1,0:T(8,128)(2,1)S(1)}, u32[]{:S(2)}, u32[]{:S(2)}) collective-permute-start(bf16[64,1024]{1,0:T(8,128)(2,1)} %bitcast.17), channel_id=1, source_target_pairs={{0,2},{1,3},{2,0},{3,1},{4,6},{5,7},{6,4},{7,5},{8,10},{9,11},{10,... | collective-permute-start | bytes 393224 | tf_op jit(solution)/shard_map/ppermute | solution.py:504
  23.7 17.9 %collective-permute-start.6 = (bf16[192,1024]{1,0:T(8,128)(2,1)S(1)}, bf16[192,1024]{1,0:T(8,128)(2,1)S(1)}, u32[]{:S(2)}, u32[]{:S(2)}) collective-permute-start(bf16[192,1024]{1,0:T(8,128)(2,1)S(1)} %get-tuple-element.19.refs_2_.refs_4_), channel_id=1, source_target_pairs={{0,2},{1,3},{2,0},{3,1},{4,6},{5,7},{6,4},{7,5},{8,10},{9,11},{10,... | collective-permute-start | bytes 1179656 | tf_op jit(solution)/shard_map/ppermute | solution.py:504
  25.2 5.8 %collective-permute-start.1 = (bf16[32,2048]{1,0:T(8,128)(2,1)}, bf16[32,2048]{1,0:T(8,128)(2,1)S(1)}, u32[]{:S(2)}, u32[]{:S(2)}) collective-permute-start(bf16[32,2048]{1,0:T(8,128)(2,1)} %bitcast.11), channel_id=1, source_target_pairs={{1,0},{2,1},{3,2},{4,3},{5,4},{6,5},{7,6},{8,7},{9,8},{10,9},{11,1... | collective-permute-start | bytes 393224 | tf_op jit(solution)/shard_map/ppermute | solution.py:498
  26.5 4.5 %collective-permute-start = (bf16[32,2048]{1,0:T(8,128)(2,1)}, bf16[32,2048]{1,0:T(8,128)(2,1)S(1)}, u32[]{:S(2)}, u32[]{:S(2)}) collective-permute-start(bf16[32,2048]{1,0:T(8,128)(2,1)} %bitcast.12), channel_id=1, source_target_pairs={{0,1},{1,2},{2,3},{3,4},{4,5},{5,6},{6,7},{7,8},{8,9},{9,10},{10,1... | collective-permute-start | bytes 393224 | tf_op jit(solution)/shard_map/ppermute | solution.py:497
  32.7 16.7 %all-to-all-start = ((bf16[16,32,128]{2,1,0:T(8,128)(2,1)}), bf16[16,32,128]{2,1,0:T(8,128)(2,1)S(1)}, u32[]{:S(2)}, u32[]{:S(2)}) async-start(bf16[16,32,128]{2,1,0:T(8,128)(2,1)} %get-tuple-element.11), calls=%async_computation | async-start | bytes 262144 | tf_op jit(solution)/shard_map/all_to_all | solution.py:534
  41.5 99.5 %reduce-scatter.2.cloned.1.call-start = ((), (), s32[]{:S(2)}) async-start(), calls=%async_computation.5 | async-start | bytes 2228224 | tf_op jit(solution)/shard_map/reduce_scatter | solution.py:544
  42.5 25.8 %collective-permute-start.10 = (bf16[512,1024]{1,0:T(8,128)(2,1)}, bf16[512,1024]{1,0:T(8,128)(2,1)}, u32[]{:S(2)}, u32[]{:S(2)}) collective-permute-start(bf16[512,1024]{1,0:T(8,128)(2,1)} %constant_dynamic-update-slice_fusion.3), channel_id=1, source_target_pairs={{0,16},{16,0},{1,17},{17,1},{2,18},{18,2},{3,19},{19,3},{4,20},{20... | collective-permute-start | bytes 3145736 | tf_op jit(solution)/shard_map/ppermute | solution.py:510
  68.3 32.5 %collective-permute-start.11 = (bf16[512,1024]{1,0:T(8,128)(2,1)}, bf16[512,1024]{1,0:T(8,128)(2,1)S(1)}, u32[]{:S(2)}, u32[]{:S(2)}) collective-permute-start(bf16[512,1024]{1,0:T(8,128)(2,1)} %collective-permute-done.10.refs_9_), channel_id=1, source_target_pairs={{0,1},{1,0},{2,3},{3,2},{4,5},{5,4},{6,7},{7,6},{8,9},{9,8},{10,11... | collective-permute-start | bytes 3145736 | tf_op jit(solution)/shard_map/ppermute | solution.py:504
  68.3 4.6 %collective-permute-start.8 = (bf16[192,1024]{1,0:T(8,128)(2,1)}, bf16[192,1024]{1,0:T(8,128)(2,1)}, u32[]{:S(2)}, u32[]{:S(2)}) collective-permute-start(bf16[192,1024]{1,0:T(8,128)(2,1)} %copy-done.11), channel_id=1, source_target_pairs={{0,1},{1,0},{2,3},{3,2},{4,5},{5,4},{6,7},{7,6},{8,9},{9,8},{10,11... | collective-permute-start | bytes 1179656 | tf_op jit(solution)/shard_map/ppermute | solution.py:504
  68.8 4.1 %collective-permute-start.9 = (bf16[192,1024]{1,0:T(8,128)(2,1)}, bf16[192,1024]{1,0:T(8,128)(2,1)}, u32[]{:S(2)}, u32[]{:S(2)}) collective-permute-start(bf16[192,1024]{1,0:T(8,128)(2,1)} %copy-done.8), channel_id=1, source_target_pairs={{0,1},{1,0},{2,3},{3,2},{4,5},{5,4},{6,7},{7,6},{8,9},{9,8},{10,11... | collective-permute-start | bytes 1179656 | tf_op jit(solution)/shard_map/ppermute | solution.py:504
  69.5 3.3 %collective-permute-start.7 = (bf16[128,1024]{1,0:T(8,128)(2,1)}, bf16[128,1024]{1,0:T(8,128)(2,1)S(1)}, u32[]{:S(2)}, u32[]{:S(2)}) collective-permute-start(bf16[128,1024]{1,0:T(8,128)(2,1)} %pad_maximum_fusion.refs_1_.refs_3_), channel_id=1, source_target_pairs={{0,1},{1,0},{2,3},{3,2},{4,5},{5,4},{6,7},{7,6},{8,9},{9,8},{10,11... | collective-permute-start | bytes 786440 | tf_op jit(solution)/shard_map/ppermute | solution.py:504
  73.5 17.3 %copy-start.10 = (bf16[16,32,128]{2,1,0:T(8,128)(2,1)S(1)}, bf16[16,32,128]{2,1,0:T(8,128)(2,1)}, u32[]{:S(2)}) copy-start(bf16[16,32,128]{2,1,0:T(8,128)(2,1)} %copy-done.9) | copy-start | bytes 393220
  85.1 15.6 %all-to-all-start.1 = ((bf16[16,32,128]{2,1,0:T(8,128)(2,1)}), bf16[16,32,128]{2,1,0:T(8,128)(2,1)S(1)}, u32[]{:S(2)}, u32[]{:S(2)}) async-start(bf16[16,32,128]{2,1,0:T(8,128)(2,1)} %shard_map.78), calls=%async_computation.2 | async-start | bytes 262144 | tf_op jit(solution)/shard_map/all_to_all | solution.py:557
  90.9 16.9 %collective-permute-start.14 = (bf16[16,32,128]{2,1,0:T(8,128)(2,1)S(1)}, bf16[16,32,128]{2,1,0:T(8,128)(2,1)S(1)}, u32[]{:S(2)}, u32[]{:S(2)}) collective-permute-start(bf16[16,32,128]{2,1,0:T(8,128)(2,1)S(1)} %copy-done.10), channel_id=1, source_target_pairs={{0,16},{16,0},{1,17},{17,1},{2,18},{18,2},{3,19},{19,3},{4,20},{20... | collective-permute-start | bytes 393224 | tf_op jit(solution)/shard_map/ppermute | solution.py:510
  104.8 17.4 %all-to-all-start.2 = ((bf16[32,32,128]{2,1,0:T(8,128)(2,1)}), bf16[32,32,128]{2,1,0:T(8,128)(2,1)S(1)}, u32[]{:S(2)}, u32[]{:S(2)}) async-start(bf16[32,32,128]{2,1,0:T(8,128)(2,1)} %get-tuple-element.15), calls=%async_computation.3 | async-start | bytes 524288 | tf_op jit(solution)/shard_map/all_to_all | solution.py:565
  108.4 21.0 %copy-start.5 = (bf16[256,256]{1,0:T(8,128)(2,1)S(1)}, bf16[256,256]{1,0:T(8,128)(2,1)}, u32[]{:S(2)}) copy-start(bf16[256,256]{1,0:T(8,128)(2,1)} %copy-done.4) | copy-start | bytes 393220
  108.4 25.4 %copy-start.1 = (bf16[27,64,64]{2,1,0:T(8,128)(2,1)S(1)}, bf16[27,64,64]{2,1,0:T(8,128)(2,1)}, u32[]{:S(2)}) copy-start(bf16[27,64,64]{2,1,0:T(8,128)(2,1)} %w_ref.1) | copy-start | bytes 663556
  123.6 16.1 %all-to-all-start.3 = ((bf16[32,32,128]{2,1,0:T(8,128)(2,1)}), bf16[32,32,128]{2,1,0:T(8,128)(2,1)S(1)}, u32[]{:S(2)}, u32[]{:S(2)}) async-start(bf16[32,32,128]{2,1,0:T(8,128)(2,1)} %shard_map.83), calls=%async_computation.4 | async-start | bytes 524288 | tf_op jit(solution)/shard_map/all_to_all | solution.py:571
  129.4 5.0 %collective-permute-start.13 = (bf16[256,256]{1,0:T(8,128)(2,1)S(1)}, bf16[256,256]{1,0:T(8,128)(2,1)S(1)}, u32[]{:S(2)}, u32[]{:S(2)}) collective-permute-start(bf16[256,256]{1,0:T(8,128)(2,1)S(1)} %copy-done.5), channel_id=1, source_target_pairs={{1,0},{2,1},{3,2},{4,3},{5,4},{6,5},{7,6},{8,7},{9,8},{10,9},{11,1... | collective-permute-start | bytes 393224 | tf_op jit(solution)/shard_map/ppermute | solution.py:498
  130.7 4.0 %collective-permute-start.12 = (bf16[256,256]{1,0:T(8,128)(2,1)S(1)}, bf16[256,256]{1,0:T(8,128)(2,1)S(1)}, u32[]{:S(2)}, u32[]{:S(2)}) collective-permute-start(bf16[256,256]{1,0:T(8,128)(2,1)S(1)} %copy-done.5), channel_id=1, source_target_pairs={{0,1},{1,2},{2,3},{3,4},{4,5},{5,6},{6,7},{7,8},{8,9},{9,10},{10,1... | collective-permute-start | bytes 393224 | tf_op jit(solution)/shard_map/ppermute | solution.py:497
  (11 other events, 50.6 us)
Sparse Core Ops, SparseCore 0:
  59.0 62.6 reduce-scatter.1

commit v7 on v6

--- a/solution.py
+++ b/solution.py
@@ -195,6 +195,29 @@
             flops=2 * cells * TAPS * C1 * C2, bytes_accessed=10 << 20, transcendentals=0
         ),
     )(pieces, weight, *after)
+
+
+def join_kernel(count, *refs):
+    out_ref, first = refs[-1], 0
+    for ref in refs[:count]:
+        rows = ref.shape[0]
+        out_ref[first : first + rows] = ref[...]
+        first += rows
+
+
+def joined(values, after=()):
+    rows = sum(value.shape[0] for value in values)
+    columns = values[0].shape[1]
+    return pl.pallas_call(
+        lambda *refs: join_kernel(len(values), *refs),
+        grid=(1,),
+        in_specs=[pl.BlockSpec(value.shape, lambda n: (0, 0)) for value in values]
+        + [pl.BlockSpec(memory_space=pl.ANY)] * len(after),
+        out_specs=pl.BlockSpec((rows, columns), lambda n: (0, 0)),
+        out_shape=jax.ShapeDtypeStruct((rows, columns), values[0].dtype),
+        compiler_params=params(32),
+        cost_estimate=pl.CostEstimate(flops=0, bytes_accessed=4 * rows * columns, transcendentals=0),
+    )(*values, *after)
 
 
 def plane_copies(device, pieces, refs, target_ref, base, sems):
@@ -533,29 +556,30 @@
     moved, slope, windows = conv_one(before, own, after, band, [])
     fields = lax.all_to_all(moved, "depth", split_axis=0, concat_axis=0, tiled=True)
 
-    near = jnp.concatenate([cot, cot_chip], axis=0)
-    far = jnp.concatenate(far, axis=0)
+    near = joined([cot, cot_chip], [fields])
+    far = joined(far, [slope])
     far_chip = flipped(far, chip)
     cots = [near, far, far_chip]
     pieces = [[0, chip], outer, [difference + chip for difference in outer]]
     pieces = pieces + [[difference + core for difference in piece] for piece in pieces]
 
-    partial = conv_two(fields, flat_two, [])
+    near_core, far_core = flipped(near, core), flipped(far, core)
+    partial = conv_two(fields, flat_two, [near_core, far_core])
     features = lax.psum_scatter(partial, "depth", scatter_dimension=0, tiled=True)
 
-    own_cots = cots + [flipped(value, core) for value in cots]
-    half = jnp.concatenate(cots, axis=0)
+    own_cots = cots + [near_core, far_core, flipped(far_chip, core)]
+    grad_pieces = back_two(device, pieces, own_cots, flat_two, [partial])
+    returned = lax.all_to_all(grad_pieces, "depth", split_axis=0, concat_axis=0, tiled=True)
+    half = joined(cots, [partial])
     halves = [[difference for piece in group for difference in piece] for group in (pieces[:3], pieces[3:])]
     all_pieces, all_cots = [pieces], [own_cots]
     for value in over_samples(half)[1:]:
+        value = joined([value], [returned])
         all_pieces.append(halves)
         all_cots.append([value, flipped(value, core)])
     all_fields = over_samples(fields)
-    swapped = [value[1] for value in all_cots[1:]]
-
-    grad_pieces = back_two(device, pieces, own_cots, flat_two, [partial])
-    grad_pieces = lax.all_to_all(grad_pieces, "depth", split_axis=0, concat_axis=0, tiled=True)
-    grad_pre, partial_one = grad_pre_of(grad_pieces, slope, windows, swapped)
+
+    grad_pre, partial_one = grad_pre_of(returned, slope, windows, [])
     grad_before, grad_after = neighbours(grad_pre, "depth")
 
     devices = samples * shards

time: 149 us -> 132 us (0.89)
  waiting for transfers between devices: 37.9 us -> 13.6 us
  blocking collectives: 0 us -> 12.3 us
  starting transfers between devices: 45 us -> 38.1 us
  local copies, waits for them, and re-layouts: 6.52 us -> 8.28 us
    all_to_all x0 -> x1, blocking collectives: none -> 12.3 us  [on_device(): lax.all_to_all(grad_pieces, 'depth', split_axis=0, concat_axis=0, tiled=T...]
    ppermute x2, waiting for transfers between devices: 9.36 us -> 0.01 us  [over_samples(): lax.ppermute(value, 'sample', [(i, (i + shift) % count) for i in range(co...]
    all_to_all x1 -> x0, waiting for transfers between devices: 8.32 us -> none  [on_device(): lax.all_to_all(grad_pieces, 'depth', split_axis=0, concat_axis=0, tiled=T...]
    all_to_all x1 -> x0, starting transfers between devices: 5.72 us -> none  [on_device(): lax.all_to_all(grad_pieces, 'depth', split_axis=0, concat_axis=0, tiled=T...]
    all_to_all x1, waiting for transfers between devices: 5.51 us -> 0.86 us  [on_device(): lax.all_to_all(moved, 'depth', split_axis=0, concat_axis=0, tiled=True)]
    ppermute x9, waiting for transfers between devices: 10.8 us -> 8.06 us  [flipped(): lax.ppermute(value, 'depth', [(i, i ^ difference) for i in range(count)])]
    unnamed x36 -> x37, local copies, waits for them, and re-layouts: 5.62 us -> 8.25 us
  transfers between devices with their start and end apart: 20 -> 19, of which waited for: 9 -> 7; matrix products, arithmetic and copies ran while one was open for 2% -> 0% of each run, Pallas kernels for 29% -> 33%
where the time goes in v7:
time: 132 us; the launch traced here: 131 us
  Pallas kernels  44.5 us (34%)
  starting transfers between devices  38.1 us (29%)
  between operations  14.3 us (11%)
  waiting for transfers between devices  13.6 us (10%)
  blocking collectives  12.3 us (9%)
  local copies, waits for them, and re-layouts  8.28 us (6%)
    pallas_call x1, Pallas kernels, weight_two(): pl.pallas_call(lambda *refs: weight_two_kernel(planes, pieces, scale, *re...  13.8 us
    all_to_all x1, blocking collectives, on_device(): lax.all_to_all(grad_pieces, 'depth', split_axis=0, concat_axis=0, tiled=T...  12.3 us
    pallas_call x1, Pallas kernels, back_two(): pl.pallas_call(lambda *refs: back_two_kernel(planes, pieces, *refs), grid...  11.5 us
    all_to_all x1, starting transfers between devices, on_device(): lax.all_to_all(moved, 'depth', split_axis=0, concat_axis=0, tiled=True)  9.93 us
    ppermute x9, starting transfers between devices, flipped(): lax.ppermute(value, 'depth', [(i, i ^ difference) for i in range(count)])  9 us
    pallas_call x1, Pallas kernels, conv_two(): pl.pallas_call(lambda *refs: conv_two_kernel(planes, *refs), grid=(C2 //...  8.77 us
    unnamed x37, local copies, waits for them, and re-layouts  8.25 us
    ppermute x9, waiting for transfers between devices, flipped(): lax.ppermute(value, 'depth', [(i, i ^ difference) for i in range(count)])  8.06 us
  transfers between devices with their start and end apart: 19, of which 7 were waited for; matrix products, arithmetic and copies ran while one was open for 0% of the time, Pallas kernels for 33%

profile of v7, /device:TPU:0, one launch (start us, length us, event | category | flops | bytes accessed | tf_op | source)
XLA Modules:
  0.0 131.2 jit_solution(9650718124116540830)
XLA Ops:
  7.2 1.3 collective-permute-start.1
  8.5 3.0 %collective-permute-start = (bf16[32,2048]{1,0:T(8,128)(2,1)}, bf16[32,2048]{1,0:T(8,128)(2,1)S(1)}, u32[]{:S(2)}, u32[]{:S(2)}) collective-permute-start(bf16[32,2048]{1,0:T(8,128)(2,1)} %bitcast.11), channel_id=1, source_target_pairs={{0,1},{1,2},{2,3},{3,4},{4,5},{5,6},{6,7},{7,8},{8,9},{9,10},{10,1... | collective-permute-start | bytes 393224 | tf_op jit(solution)/shard_map/ppermute | solution.py:520
  11.5 5.5 %collective-permute-start.6 = (bf16[64,1024]{1,0:T(8,128)(2,1)}, bf16[64,1024]{1,0:T(8,128)(2,1)S(1)}, u32[]{:S(2)}, u32[]{:S(2)}) collective-permute-start(bf16[64,1024]{1,0:T(8,128)(2,1)} %bitcast.13), channel_id=1, source_target_pairs={{0,12},{1,13},{2,14},{3,15},{4,8},{5,9},{6,10},{7,11},{8,4},{9,5},... | collective-permute-start | bytes 393224 | tf_op jit(solution)/shard_map/ppermute | solution.py:527
  19.5 1.7 %shard_map.76 = (bf16[16,32,128]{2,1,0:T(8,128)(2,1)}, f32[256,256]{1,0:T(8,128)S(1)}, bf16[256,3456]{1,0:T(8,128)(2,1)S(1)}) custom-call(bf16[32,2048]{1,0:T(8,128)(2,1)S(1)} %collective-permute-done.before_ref, bf16[32,2048]{1,0:T(8,128)(2,1)S(1)} %bitcast.12, bf16[32,2048]{1,0:T(8,128)(2,1)S(1)} %collective-permute-done.1.after_ref, ...), custom_call_target="tpu_custom_call" | custom-call | flops 452984832 | bytes 5242880 | tf_op jit(solution)/shard_map/pallas_call | solution.py:107
  21.2 9.9 %all-to-all-start = ((bf16[16,32,128]{2,1,0:T(8,128)(2,1)}), bf16[16,32,128]{2,1,0:T(8,128)(2,1)S(1)}, u32[]{:S(2)}, u32[]{:S(2)}) async-start(bf16[16,32,128]{2,1,0:T(8,128)(2,1)} %get-tuple-element.11), calls=%async_computation | async-start | bytes 262144 | tf_op jit(solution)/shard_map/all_to_all | solution.py:557
  31.2 2.0 %collective-permute-start.2 = (bf16[64,1024]{1,0:T(8,128)(2,1)S(1)}, bf16[64,1024]{1,0:T(8,128)(2,1)S(1)}, u32[]{:S(2)}, u32[]{:S(2)}) collective-permute-start(bf16[64,1024]{1,0:T(8,128)(2,1)S(1)} %bitcast.16), channel_id=1, source_target_pairs={{0,2},{1,3},{2,0},{3,1},{4,6},{5,7},{6,4},{7,5},{8,10},{9,11},{10,... | collective-permute-start | bytes 393224 | tf_op jit(solution)/shard_map/ppermute | solution.py:527
  33.4 4.9 %collective-permute-done.2.refs_1_ = bf16[64,1024]{1,0:T(8,128)(2,1)S(1)} collective-permute-done((bf16[64,1024]{1,0:T(8,128)(2,1)S(1)}, bf16[64,1024]{1,0:T(8,128)(2,1)S(1)}, u32[]{:S(2)}, u32[]{:S(2)}) %collective-permute-start.2) | collective-permute-done | bytes 131104 | tf_op jit(solution)/shard_map/ppermute | solution.py:527
  41.5 8.8 %shard_map.79.refs_8_.refs_3_ = bf16[1024,1024]{1,0:T(8,128)(2,1)} custom-call(bf16[16,32,128]{2,1,0:T(8,128)(2,1)} %copy-done.8, bf16[1728,1024]{1,0:T(8,128)(2,1)} %bitcast.19, bf16[128,1024]{1,0:T(8,128)(2,1)} %copy-done.16, bf16[192,1024]{1,0:T(8,128)(2,1)} %collective-permute-done.7.refs_3_.refs_5_.refs_7_), custom_call_target="tpu_custom_call" | custom-call | flops 3623878656 | bytes 10485760 | tf_op jit(solution)/shard_map/pallas_call | solution.py:179
  50.8 1.6 %copy-done = bf16[1024,1024]{1,0:T(8,128)(2,1)S(1)} copy-done((bf16[1024,1024]{1,0:T(8,128)(2,1)S(1)}, bf16[1024,1024]{1,0:T(8,128)(2,1)}, u32[]{:S(2)}) %copy-start) | copy-done | bytes 2097176
  52.4 1.1 shard_map.84
  53.5 1.5 %collective-permute-start.13 = (bf16[512,1024]{1,0:T(8,128)(2,1)}, bf16[512,1024]{1,0:T(8,128)(2,1)S(1)}, u32[]{:S(2)}, u32[]{:S(2)}) collective-permute-start(bf16[512,1024]{1,0:T(8,128)(2,1)} %shard_map.84), channel_id=1, source_target_pairs={{0,16},{16,0},{1,17},{17,1},{2,18},{18,2},{3,19},{19,3},{4,20},{20... | collective-permute-start | bytes 3145736 | tf_op jit(solution)/shard_map/ppermute | solution.py:533
  55.0 1.8 %collective-permute-done.9.refs_6_.refs_8_ = bf16[192,1024]{1,0:T(8,128)(2,1)} collective-permute-done((bf16[192,1024]{1,0:T(8,128)(2,1)S(1)}, bf16[192,1024]{1,0:T(8,128)(2,1)}, u32[]{:S(2)}, u32[]{:S(2)}) %collective-permute-start.9) | collective-permute-done | bytes 393248 | tf_op jit(solution)/shard_map/ppermute | solution.py:527
  56.8 11.5 %shard_map.80 = bf16[16,32,128]{2,1,0:T(8,128)(2,1)} custom-call(s32[1]{0:T(128)} %bitcast.4.refs_0_, bf16[128,1024]{1,0:T(8,128)(2,1)} %copy-done.4, bf16[192,1024]{1,0:T(8,128)(2,1)} %copy-done.3, bf16[192,1024]{1,0:T(8,128)(2,1)} %copy-done.10, bf16[128,1024]{1,0:T(8,128)(2,1)} %copy-done.16, ...), custom_call_target="tpu_custom_call" | custom-call | flops 3623878656 | bytes 6291456 | tf_op jit(solution)/shard_map/pallas_call | solution.py:282
  68.3 12.3 %all_to_all.20.pieces_ref.refs_1_ = bf16[16,32,128]{2,1,0:T(8,128)(2,1)S(1)} all-to-all(bf16[16,32,128]{2,1,0:T(8,128)(2,1)} %shard_map.80), channel_id=1, replica_groups=mesh['sample'=2,'depth'=16] {'depth'}, dimensions={0} | all-to-all | bytes 262144 | tf_op jit(solution)/shard_map/all_to_all | solution.py:572
  81.6 1.2 copy-done.7
  83.6 3.4 %shard_map.81 = (bf16[256,256]{1,0:T(8,128)(2,1)S(1)}, bf16[32,32,128]{2,1,0:T(8,128)(2,1)}) custom-call(bf16[16,32,128]{2,1,0:T(8,128)(2,1)S(1)} %all_to_all.20.pieces_ref.refs_1_, f32[256,256]{1,0:T(8,128)S(1)} %get-tuple-element.12.refs_3_.slope_ref, bf16[256,3456]{1,0:T(8,128)(2,1)S(1)} %get-tuple-element.13.lhs_ref), custom_call_target="tpu_custom_call" | custom-call | flops 452984832 | bytes 3145728 | tf_op jit(solution)/shard_map/pallas_call | solution.py:442
  87.7 2.6 %all-to-all-start.2 = ((bf16[32,32,128]{2,1,0:T(8,128)(2,1)}), bf16[32,32,128]{2,1,0:T(8,128)(2,1)S(1)}, u32[]{:S(2)}, u32[]{:S(2)}) async-start(bf16[32,32,128]{2,1,0:T(8,128)(2,1)} %get-tuple-element.15), calls=%async_computation.3 | async-start | bytes 524288 | tf_op jit(solution)/shard_map/all_to_all | solution.py:589
  90.9 13.8 %shard_map.86 = (f32[1728,1024]{1,0:T(8,128)}, f32[8,128]{1,0:T(8,128)}) custom-call(s32[1]{0:T(128)} %bitcast.4.refs_0_, bf16[16,32,128]{2,1,0:T(8,128)(2,1)} %copy-done.8, bf16[16,32,128]{2,1,0:T(8,128)(2,1)} %copy-done.17, bf16[128,1024]{1,0:T(8,128)(2,1)} %copy-done.4, bf16[192,1024]{1,0:T(8,128)(2,1)} %copy-done.3, bf16[192,1024]{1,0:T(8,128)(2,1)} %copy-done.10, ...), custom_call_target="tpu_custom_call" | custom-call | flops 7247757312 | bytes 18874368 | tf_op jit(solution)/shard_map/pallas_call | solution.py:364
  106.2 5.8 %all-to-all-start.3 = ((bf16[32,32,128]{2,1,0:T(8,128)(2,1)}), bf16[32,32,128]{2,1,0:T(8,128)(2,1)S(1)}, u32[]{:S(2)}, u32[]{:S(2)}) async-start(bf16[32,32,128]{2,1,0:T(8,128)(2,1)} %shard_map.87), calls=%async_computation.4 | async-start | bytes 524288 | tf_op jit(solution)/shard_map/all_to_all | solution.py:595
  112.0 1.3 collective-permute-start.11
  113.3 3.0 %collective-permute-start.10 = (bf16[256,256]{1,0:T(8,128)(2,1)S(1)}, bf16[256,256]{1,0:T(8,128)(2,1)S(1)}, u32[]{:S(2)}, u32[]{:S(2)}) collective-permute-start(bf16[256,256]{1,0:T(8,128)(2,1)S(1)} %copy-done.14), channel_id=1, source_target_pairs={{0,1},{1,2},{2,3},{3,4},{4,5},{5,6},{6,7},{7,8},{8,9},{9,10},{10,1... | collective-permute-start | bytes 393224 | tf_op jit(solution)/shard_map/ppermute | solution.py:520
  117.3 1.4 %shard_map.83 = bf16[32,2048]{1,0:T(8,128)(2,1)} custom-call(bf16[256,256]{1,0:T(8,128)(2,1)S(1)} %collective-permute-done.10.before_ref, bf16[256,256]{1,0:T(8,128)(2,1)S(1)} %copy-done.14, bf16[256,256]{1,0:T(8,128)(2,1)S(1)} %collective-permute-done.11.after_ref, bf16[3456,256]{1,0:T(8,128)(2,1)S(1)} %shard_map.82.w_ref), custom_call_target="tpu_custom_call" | custom-call | flops 452984832 | bytes 3145728 | tf_op jit(solution)/shard_map/pallas_call | solution.py:470
  118.6 4.4 %all-to-all-done.3.packed_ref = bf16[32,32,128]{2,1,0:T(8,128)(2,1)S(1)} async-done(((bf16[32,32,128]{2,1,0:T(8,128)(2,1)}), bf16[32,32,128]{2,1,0:T(8,128)(2,1)S(1)}, u32[]{:S(2)}, u32[]{:S(2)}) %all-to-all-start.3) | async-done | bytes 262176 | tf_op jit(solution)/shard_map/all_to_all | solution.py:595
  123.0 1.3 shard_map.88
  (68 shorter events, 11.8 us)
Async XLA Ops:
  7.2 11.9 %collective-permute-start.1 = (bf16[32,2048]{1,0:T(8,128)(2,1)}, bf16[32,2048]{1,0:T(8,128)(2,1)S(1)}, u32[]{:S(2)}, u32[]{:S(2)}) collective-permute-start(bf16[32,2048]{1,0:T(8,128)(2,1)} %bitcast.10), channel_id=1, source_target_pairs={{1,0},{2,1},{3,2},{4,3},{5,4},{6,5},{7,6},{8,7},{9,8},{10,9},{11,1... | collective-permute-start | bytes 393224 | tf_op jit(solution)/shard_map/ppermute | solution.py:521
  8.5 10.6 %collective-permute-start = (bf16[32,2048]{1,0:T(8,128)(2,1)}, bf16[32,2048]{1,0:T(8,128)(2,1)S(1)}, u32[]{:S(2)}, u32[]{:S(2)}) collective-permute-start(bf16[32,2048]{1,0:T(8,128)(2,1)} %bitcast.11), channel_id=1, source_target_pairs={{0,1},{1,2},{2,3},{3,4},{4,5},{5,6},{6,7},{7,8},{8,9},{9,10},{10,1... | collective-permute-start | bytes 393224 | tf_op jit(solution)/shard_map/ppermute | solution.py:520
  11.5 21.7 %collective-permute-start.6 = (bf16[64,1024]{1,0:T(8,128)(2,1)}, bf16[64,1024]{1,0:T(8,128)(2,1)S(1)}, u32[]{:S(2)}, u32[]{:S(2)}) collective-permute-start(bf16[64,1024]{1,0:T(8,128)(2,1)} %bitcast.13), channel_id=1, source_target_pairs={{0,12},{1,13},{2,14},{3,15},{4,8},{5,9},{6,10},{7,11},{8,4},{9,5},... | collective-permute-start | bytes 393224 | tf_op jit(solution)/shard_map/ppermute | solution.py:527
  17.0 16.3 %collective-permute-start.5 = (bf16[64,1024]{1,0:T(8,128)(2,1)}, bf16[64,1024]{1,0:T(8,128)(2,1)S(1)}, u32[]{:S(2)}, u32[]{:S(2)}) collective-permute-start(bf16[64,1024]{1,0:T(8,128)(2,1)} %bitcast.14), channel_id=1, source_target_pairs={{0,8},{1,9},{2,10},{3,11},{4,12},{5,13},{6,14},{7,15},{8,0},{9,1},... | collective-permute-start | bytes 393224 | tf_op jit(solution)/shard_map/ppermute | solution.py:527
  17.0 16.3 %collective-permute-start.4 = (bf16[64,1024]{1,0:T(8,128)(2,1)}, bf16[64,1024]{1,0:T(8,128)(2,1)S(1)}, u32[]{:S(2)}, u32[]{:S(2)}) collective-permute-start(bf16[64,1024]{1,0:T(8,128)(2,1)} %bitcast.15), channel_id=1, source_target_pairs={{0,4},{1,5},{2,6},{3,7},{4,0},{5,1},{6,2},{7,3},{8,12},{9,13},{10,... | collective-permute-start | bytes 393224 | tf_op jit(solution)/shard_map/ppermute | solution.py:527
  18.6 12.6 %copy-start.12 = (bf16[1,1,8,8,1024]{4,3,2,1,0:T(8,128)(2,1)S(1)}, bf16[1,1,8,8,1024]{4,3,2,1,0:T(8,128)(2,1)}, u32[]{:S(2)}) copy-start(bf16[1,1,8,8,1024]{4,3,2,1,0:T(8,128)(2,1)} %param.7) | copy-start | bytes 393220
  21.2 17.9 %all-to-all-start = ((bf16[16,32,128]{2,1,0:T(8,128)(2,1)}), bf16[16,32,128]{2,1,0:T(8,128)(2,1)S(1)}, u32[]{:S(2)}, u32[]{:S(2)}) async-start(bf16[16,32,128]{2,1,0:T(8,128)(2,1)} %get-tuple-element.11), calls=%async_computation | async-start | bytes 262144 | tf_op jit(solution)/shard_map/all_to_all | solution.py:557
  31.2 93.1 %reduce-scatter.2.cloned.1.call-start = ((), (), s32[]{:S(2)}) async-start(), calls=%async_computation.5 | async-start | bytes 2228224 | tf_op jit(solution)/shard_map/reduce_scatter | solution.py:568
  31.2 7.0 %collective-permute-start.2 = (bf16[64,1024]{1,0:T(8,128)(2,1)S(1)}, bf16[64,1024]{1,0:T(8,128)(2,1)S(1)}, u32[]{:S(2)}, u32[]{:S(2)}) collective-permute-start(bf16[64,1024]{1,0:T(8,128)(2,1)S(1)} %bitcast.16), channel_id=1, source_target_pairs={{0,2},{1,3},{2,0},{3,1},{4,6},{5,7},{6,4},{7,5},{8,10},{9,11},{10,... | collective-permute-start | bytes 393224 | tf_op jit(solution)/shard_map/ppermute | solution.py:527
  33.3 17.5 %copy-start.3 = (bf16[192,1024]{1,0:T(8,128)(2,1)}, bf16[192,1024]{1,0:T(8,128)(2,1)S(1)}, u32[]{:S(2)}) copy-start(bf16[192,1024]{1,0:T(8,128)(2,1)S(1)} %shard_map.78.refs_2_.refs_1_.refs_4_) | copy-start | bytes 1179652
  33.3 6.6 %collective-permute-start.7 = (bf16[192,1024]{1,0:T(8,128)(2,1)S(1)}, bf16[192,1024]{1,0:T(8,128)(2,1)}, u32[]{:S(2)}, u32[]{:S(2)}) collective-permute-start(bf16[192,1024]{1,0:T(8,128)(2,1)S(1)} %shard_map.78.refs_2_.refs_1_.refs_4_), channel_id=1, source_target_pairs={{0,1},{1,0},{2,3},{3,2},{4,5},{5,4},{6,7},{7,6},{8,9},{9,8},{10,11... | collective-permute-start | bytes 1179656 | tf_op jit(solution)/shard_map/ppermute | solution.py:527
  39.1 1.6 %collective-permute-start.3 = (bf16[128,1024]{1,0:T(8,128)(2,1)S(1)}, bf16[128,1024]{1,0:T(8,128)(2,1)S(1)}, u32[]{:S(2)}, u32[]{:S(2)}) collective-permute-start(bf16[128,1024]{1,0:T(8,128)(2,1)S(1)} %shard_map.77.refs_1_.refs_0_.refs_3_), channel_id=1, source_target_pairs={{0,1},{1,0},{2,3},{3,2},{4,5},{5,4},{6,7},{7,6},{8,9},{9,8},{10,11... | collective-permute-start | bytes 786440 | tf_op jit(solution)/shard_map/ppermute | solution.py:527
  39.2 11.5 %collective-permute-start.8 = (bf16[192,1024]{1,0:T(8,128)(2,1)S(1)}, bf16[192,1024]{1,0:T(8,128)(2,1)S(1)}, u32[]{:S(2)}, u32[]{:S(2)}) collective-permute-start(bf16[192,1024]{1,0:T(8,128)(2,1)S(1)} %shard_map.78.refs_2_.refs_1_.refs_4_), channel_id=1, source_target_pairs={{0,2},{1,3},{2,0},{3,1},{4,6},{5,7},{6,4},{7,5},{8,10},{9,11},{10,... | collective-permute-start | bytes 1179656 | tf_op jit(solution)/shard_map/ppermute | solution.py:527
  53.5 27.2 %collective-permute-start.13 = (bf16[512,1024]{1,0:T(8,128)(2,1)}, bf16[512,1024]{1,0:T(8,128)(2,1)S(1)}, u32[]{:S(2)}, u32[]{:S(2)}) collective-permute-start(bf16[512,1024]{1,0:T(8,128)(2,1)} %shard_map.84), channel_id=1, source_target_pairs={{0,16},{16,0},{1,17},{17,1},{2,18},{18,2},{3,19},{19,3},{4,20},{20... | collective-permute-start | bytes 3145736 | tf_op jit(solution)/shard_map/ppermute | solution.py:533
  54.9 1.9 %collective-permute-start.9 = (bf16[192,1024]{1,0:T(8,128)(2,1)S(1)}, bf16[192,1024]{1,0:T(8,128)(2,1)}, u32[]{:S(2)}, u32[]{:S(2)}) collective-permute-start(bf16[192,1024]{1,0:T(8,128)(2,1)S(1)} %collective-permute-done.8.refs_3_.refs_2_.refs_5_), channel_id=1, source_target_pairs={{0,1},{1,0},{2,3},{3,2},{4,5},{5,4},{6,7},{7,6},{8,9},{9,8},{10,11... | collective-permute-start | bytes 1179656 | tf_op jit(solution)/shard_map/ppermute | solution.py:527
  68.3 14.7 %copy-start.9 = (bf16[16,32,128]{2,1,0:T(8,128)(2,1)S(1)}, bf16[16,32,128]{2,1,0:T(8,128)(2,1)}, u32[]{:S(2)}) copy-start(bf16[16,32,128]{2,1,0:T(8,128)(2,1)} %copy-done.8) | copy-start | bytes 393220
  82.9 7.4 %collective-permute-start.14 = (bf16[512,1024]{1,0:T(8,128)(2,1)S(1)}, bf16[512,1024]{1,0:T(8,128)(2,1)}, u32[]{:S(2)}, u32[]{:S(2)}) collective-permute-start(bf16[512,1024]{1,0:T(8,128)(2,1)S(1)} %shard_map.85.refs_9_), channel_id=1, source_target_pairs={{0,1},{1,0},{2,3},{3,2},{4,5},{5,4},{6,7},{7,6},{8,9},{9,8},{10,11... | collective-permute-start | bytes 3145736 | tf_op jit(solution)/shard_map/ppermute | solution.py:527
  83.0 7.2 %collective-permute-start.12 = (bf16[16,32,128]{2,1,0:T(8,128)(2,1)S(1)}, bf16[16,32,128]{2,1,0:T(8,128)(2,1)S(1)}, u32[]{:S(2)}, u32[]{:S(2)}) collective-permute-start(bf16[16,32,128]{2,1,0:T(8,128)(2,1)S(1)} %copy-done.9), channel_id=1, source_target_pairs={{0,16},{16,0},{1,17},{17,1},{2,18},{18,2},{3,19},{19,3},{4,20},{20... | collective-permute-start | bytes 393224 | tf_op jit(solution)/shard_map/ppermute | solution.py:533
  87.7 17.0 %all-to-all-start.2 = ((bf16[32,32,128]{2,1,0:T(8,128)(2,1)}), bf16[32,32,128]{2,1,0:T(8,128)(2,1)S(1)}, u32[]{:S(2)}, u32[]{:S(2)}) async-start(bf16[32,32,128]{2,1,0:T(8,128)(2,1)} %get-tuple-element.15), calls=%async_computation.3 | async-start | bytes 524288 | tf_op jit(solution)/shard_map/all_to_all | solution.py:589
  90.9 21.0 %copy-start.14 = (bf16[256,256]{1,0:T(8,128)(2,1)S(1)}, bf16[256,256]{1,0:T(8,128)(2,1)}, u32[]{:S(2)}) copy-start(bf16[256,256]{1,0:T(8,128)(2,1)} %copy-done.13) | copy-start | bytes 393220
  90.9 25.4 %copy-start.2 = (bf16[27,64,64]{2,1,0:T(8,128)(2,1)S(1)}, bf16[27,64,64]{2,1,0:T(8,128)(2,1)}, u32[]{:S(2)}) copy-start(bf16[27,64,64]{2,1,0:T(8,128)(2,1)} %w_ref.1) | copy-start | bytes 663556
  106.2 16.9 %all-to-all-start.3 = ((bf16[32,32,128]{2,1,0:T(8,128)(2,1)}), bf16[32,32,128]{2,1,0:T(8,128)(2,1)S(1)}, u32[]{:S(2)}, u32[]{:S(2)}) async-start(bf16[32,32,128]{2,1,0:T(8,128)(2,1)} %shard_map.87), calls=%async_computation.4 | async-start | bytes 524288 | tf_op jit(solution)/shard_map/all_to_all | solution.py:595
  112.0 5.0 %collective-permute-start.11 = (bf16[256,256]{1,0:T(8,128)(2,1)S(1)}, bf16[256,256]{1,0:T(8,128)(2,1)S(1)}, u32[]{:S(2)}, u32[]{:S(2)}) collective-permute-start(bf16[256,256]{1,0:T(8,128)(2,1)S(1)} %copy-done.14), channel_id=1, source_target_pairs={{1,0},{2,1},{3,2},{4,3},{5,4},{6,5},{7,6},{8,7},{9,8},{10,9},{11,1... | collective-permute-start | bytes 393224 | tf_op jit(solution)/shard_map/ppermute | solution.py:521
  113.3 4.0 %collective-permute-start.10 = (bf16[256,256]{1,0:T(8,128)(2,1)S(1)}, bf16[256,256]{1,0:T(8,128)(2,1)S(1)}, u32[]{:S(2)}, u32[]{:S(2)}) collective-permute-start(bf16[256,256]{1,0:T(8,128)(2,1)S(1)} %copy-done.14), channel_id=1, source_target_pairs={{0,1},{1,2},{2,3},{3,4},{4,5},{5,6},{6,7},{7,8},{8,9},{9,10},{10,1... | collective-permute-start | bytes 393224 | tf_op jit(solution)/shard_map/ppermute | solution.py:520
  (13 other events, 31.7 us)
Sparse Core Ops, SparseCore 0:
  55.1 63.7 reduce-scatter.1

commit v8 on v7

--- a/solution.py
+++ b/solution.py
@@ -129,7 +129,8 @@
 
 
 def conv_two_kernel(planes, x_ref, w_ref, *refs):
-    out_ref, lhs_ref, v_ref = refs[-3:]
+    out_ref, token_ref, lhs_ref, v_ref = refs[-4:]
+    token_ref[...] = jnp.zeros(token_ref.shape, f32)
 
     @pl.when(pl.program_id(0) == 0)
     def _():
@@ -184,8 +185,11 @@
             pl.BlockSpec((TAPS * C1, block), lambda n: (0, n)),
         ]
         + [pl.BlockSpec(memory_space=pl.ANY)] * len(after),
-        out_specs=pl.BlockSpec((cells, block), lambda n: (0, n)),
-        out_shape=jax.ShapeDtypeStruct((cells, C2), bf16),
+        out_specs=(
+            pl.BlockSpec((cells, block), lambda n: (0, n)),
+            pl.BlockSpec((8, PACK), lambda n: (0, 0)),
+        ),
+        out_shape=(jax.ShapeDtypeStruct((cells, C2), bf16), jax.ShapeDtypeStruct((8, PACK), f32)),
         scratch_shapes=[
             pltpu.VMEM((cells, TAPS * C1), bf16),
             pltpu.VMEM((3, 2, planes + 2, LS + 2, LS, PACK), f32),
@@ -218,6 +222,21 @@
         compiler_params=params(32),
         cost_estimate=pl.CostEstimate(flops=0, bytes_accessed=4 * rows * columns, transcendentals=0),
     )(*values, *after)
+
+
+def held_kernel(*refs):
+    pass
+
+
+def held(value, after):
+    return pl.pallas_call(
+        held_kernel,
+        in_specs=[pl.BlockSpec(memory_space=pl.ANY)] * (1 + len(after)),
+        out_specs=pl.BlockSpec(memory_space=pl.ANY),
+        out_shape=jax.ShapeDtypeStruct(value.shape, value.dtype),
+        input_output_aliases={0: 0},
+        compiler_params=params(16),
+    )(value, *after)
 
 
 def plane_copies(device, pieces, refs, target_ref, base, sems):
@@ -557,24 +576,24 @@
     fields = lax.all_to_all(moved, "depth", split_axis=0, concat_axis=0, tiled=True)
 
     near = joined([cot, cot_chip], [fields])
-    far = joined(far, [slope])
+    far = joined(far, [slope, cot_chip])
     far_chip = flipped(far, chip)
     cots = [near, far, far_chip]
     pieces = [[0, chip], outer, [difference + chip for difference in outer]]
     pieces = pieces + [[difference + core for difference in piece] for piece in pieces]
 
     near_core, far_core = flipped(near, core), flipped(far, core)
-    partial = conv_two(fields, flat_two, [near_core, far_core])
+    partial, done = conv_two(fields, flat_two, [near_core, far_core])
     features = lax.psum_scatter(partial, "depth", scatter_dimension=0, tiled=True)
 
     own_cots = cots + [near_core, far_core, flipped(far_chip, core)]
-    grad_pieces = back_two(device, pieces, own_cots, flat_two, [partial])
+    grad_pieces = back_two(device, pieces, own_cots, flat_two, [done])
     returned = lax.all_to_all(grad_pieces, "depth", split_axis=0, concat_axis=0, tiled=True)
-    half = joined(cots, [partial])
+    half = joined(cots, [done])
     halves = [[difference for piece in group for difference in piece] for group in (pieces[:3], pieces[3:])]
     all_pieces, all_cots = [pieces], [own_cots]
     for value in over_samples(half)[1:]:
-        value = joined([value], [returned])
+        value = held(value, [returned])
         all_pieces.append(halves)
         all_cots.append([value, flipped(value, core)])
     all_fields = over_samples(fields)

time: 132 us -> 130 us (0.985)
  waiting for transfers between devices: 13.6 us -> 16.1 us
  local copies, waits for them, and re-layouts: 8.28 us -> 5.93 us
  starting transfers between devices: 38.1 us -> 35.9 us
    all_to_all x1, waiting for transfers between devices: 0.86 us -> 7.33 us  [on_device(): lax.all_to_all(moved, 'depth', split_axis=0, concat_axis=0, tiled=True)]
    ppermute x9, waiting for transfers between devices: 8.06 us -> 3.97 us  [flipped(): lax.ppermute(value, 'depth', [(i, i ^ difference) for i in range(count)])]
    unnamed x37 -> x33, local copies, waits for them, and re-layouts: 8.25 us -> 5.9 us
    all_to_all x1, starting transfers between devices: 9.93 us -> 8.61 us  [on_device(): lax.all_to_all(moved, 'depth', split_axis=0, concat_axis=0, tiled=True)]
  transfers between devices with their start and end apart: 19 -> 19, of which waited for: 7 -> 6; matrix products, arithmetic and copies ran while one was open for 0% -> 0% of each run, Pallas kernels for 33% -> 34%
where the time goes in v8:
time: 130 us; the launch traced here: 129 us
  Pallas kernels  45.4 us (35%)
  starting transfers between devices  35.9 us (28%)
  waiting for transfers between devices  16.1 us (12%)
  between operations  14.3 us (11%)
  blocking collectives  11.5 us (9%)
  local copies, waits for them, and re-layouts  5.93 us (5%)
    pallas_call x1, Pallas kernels, weight_two(): pl.pallas_call(lambda *refs: weight_two_kernel(planes, pieces, scale, *re...  13.8 us
    all_to_all x1, blocking collectives, on_device(): lax.all_to_all(grad_pieces, 'depth', split_axis=0, concat_axis=0, tiled=T...  11.5 us
    pallas_call x1, Pallas kernels, back_two(): pl.pallas_call(lambda *refs: back_two_kernel(planes, pieces, *refs), grid...  11.5 us
    pallas_call x1, Pallas kernels, conv_two(): pl.pallas_call(lambda *refs: conv_two_kernel(planes, *refs), grid=(C2 //...  8.77 us
    all_to_all x1, starting transfers between devices, on_device(): lax.all_to_all(moved, 'depth', split_axis=0, concat_axis=0, tiled=True)  8.61 us
    ppermute x9, starting transfers between devices, flipped(): lax.ppermute(value, 'depth', [(i, i ^ difference) for i in range(count)])  8.04 us
    all_to_all x1, waiting for transfers between devices, on_device(): lax.all_to_all(moved, 'depth', split_axis=0, concat_axis=0, tiled=True)  7.33 us
    ppermute x2, starting transfers between devices, neighbours(): before = lax.ppermute(value, axis, [(i, i + 1) for i in range(count - 1)])  6.07 us
  transfers between devices with their start and end apart: 19, of which 6 were waited for; matrix products, arithmetic and copies ran while one was open for 0% of the time, Pallas kernels for 34%

profile of v8, /device:TPU:0, one launch (start us, length us, event | category | flops | bytes accessed | tf_op | source)
XLA Modules:
  0.0 129.2 jit_solution(15066183390603864056)
XLA Ops:
  7.2 1.3 %collective-permute-start.1 = (bf16[32,2048]{1,0:T(8,128)(2,1)}, bf16[32,2048]{1,0:T(8,128)(2,1)S(1)}, u32[]{:S(2)}, u32[]{:S(2)}) collective-permute-start(bf16[32,2048]{1,0:T(8,128)(2,1)} %bitcast.10), channel_id=1, source_target_pairs={{1,0},{2,1},{3,2},{4,3},{5,4},{6,5},{7,6},{8,7},{9,8},{10,9},{11,1... | collective-permute-start | bytes 393224 | tf_op jit(solution)/shard_map/ppermute | solution.py:540
  8.5 3.0 %collective-permute-start = (bf16[32,2048]{1,0:T(8,128)(2,1)}, bf16[32,2048]{1,0:T(8,128)(2,1)S(1)}, u32[]{:S(2)}, u32[]{:S(2)}) collective-permute-start(bf16[32,2048]{1,0:T(8,128)(2,1)} %bitcast.11), channel_id=1, source_target_pairs={{0,1},{1,2},{2,3},{3,4},{4,5},{5,6},{6,7},{7,8},{8,9},{9,10},{10,1... | collective-permute-start | bytes 393224 | tf_op jit(solution)/shard_map/ppermute | solution.py:539
  11.5 5.5 %collective-permute-start.6 = (bf16[64,1024]{1,0:T(8,128)(2,1)}, bf16[64,1024]{1,0:T(8,128)(2,1)S(1)}, u32[]{:S(2)}, u32[]{:S(2)}) collective-permute-start(bf16[64,1024]{1,0:T(8,128)(2,1)} %bitcast.13), channel_id=1, source_target_pairs={{0,12},{1,13},{2,14},{3,15},{4,8},{5,9},{6,10},{7,11},{8,4},{9,5},... | collective-permute-start | bytes 393224 | tf_op jit(solution)/shard_map/ppermute | solution.py:546
  17.6 1.0 copy-done
  19.5 1.3 %collective-permute-start.2 = (bf16[64,1024]{1,0:T(8,128)(2,1)S(1)}, bf16[64,1024]{1,0:T(8,128)(2,1)S(1)}, u32[]{:S(2)}, u32[]{:S(2)}) collective-permute-start(bf16[64,1024]{1,0:T(8,128)(2,1)S(1)} %bitcast.16), channel_id=1, source_target_pairs={{0,2},{1,3},{2,0},{3,1},{4,6},{5,7},{6,4},{7,5},{8,10},{9,11},{10,... | collective-permute-start | bytes 393224 | tf_op jit(solution)/shard_map/ppermute | solution.py:546
  20.9 1.7 %shard_map.76 = (bf16[16,32,128]{2,1,0:T(8,128)(2,1)}, f32[256,256]{1,0:T(8,128)S(1)}, bf16[256,3456]{1,0:T(8,128)(2,1)S(1)}) custom-call(bf16[32,2048]{1,0:T(8,128)(2,1)S(1)} %collective-permute-done.before_ref, bf16[32,2048]{1,0:T(8,128)(2,1)S(1)} %bitcast.12, bf16[32,2048]{1,0:T(8,128)(2,1)S(1)} %collective-permute-done.1.after_ref, ...), custom_call_target="tpu_custom_call" | custom-call | flops 452984832 | bytes 5242880 | tf_op jit(solution)/shard_map/pallas_call | solution.py:107
  22.6 8.6 %all-to-all-start = ((bf16[16,32,128]{2,1,0:T(8,128)(2,1)}), bf16[16,32,128]{2,1,0:T(8,128)(2,1)S(1)}, u32[]{:S(2)}, u32[]{:S(2)}) async-start(bf16[16,32,128]{2,1,0:T(8,128)(2,1)} %get-tuple-element.13), calls=%async_computation | async-start | bytes 262144 | tf_op jit(solution)/shard_map/all_to_all | solution.py:576
  31.8 7.3 %all-to-all-done.refs_2_.refs_0_.refs_1_ = bf16[16,32,128]{2,1,0:T(8,128)(2,1)S(1)} async-done(((bf16[16,32,128]{2,1,0:T(8,128)(2,1)}), bf16[16,32,128]{2,1,0:T(8,128)(2,1)S(1)}, u32[]{:S(2)}, u32[]{:S(2)}) %all-to-all-start) | async-done | bytes 131104 | tf_op jit(solution)/shard_map/all_to_all | solution.py:576
  39.3 1.4 %collective-permute-done.3.refs_2_.refs_4_.refs_6_ = bf16[128,1024]{1,0:T(8,128)(2,1)S(1)} collective-permute-done((bf16[128,1024]{1,0:T(8,128)(2,1)S(1)}, bf16[128,1024]{1,0:T(8,128)(2,1)S(1)}, u32[]{:S(2)}, u32[]{:S(2)}) %collective-permute-start.3) | collective-permute-done | bytes 262176 | tf_op jit(solution)/shard_map/ppermute | solution.py:546
  41.5 8.8 %shard_map.79 = (bf16[1024,1024]{1,0:T(8,128)(2,1)}, f32[8,128]{1,0:T(8,128)}) custom-call(bf16[16,32,128]{2,1,0:T(8,128)(2,1)} %copy-done.5, bf16[1728,1024]{1,0:T(8,128)(2,1)} %bitcast.19, bf16[128,1024]{1,0:T(8,128)(2,1)} %copy-done.14, bf16[192,1024]{1,0:T(8,128)(2,1)} %collective-permute-done.7.refs_3_.refs_5_.refs_7_), custom_call_target="tpu_custom_call" | custom-call | flops 3623878656 | bytes 10485760 | tf_op jit(solution)/shard_map/pallas_call | solution.py:180
  51.6 2.0 %shard_map.84 = bf16[512,1024]{1,0:T(8,128)(2,1)} custom-call(bf16[128,1024]{1,0:T(8,128)(2,1)S(1)} %shard_map.77.refs_1_.refs_0_.refs_3_, bf16[192,1024]{1,0:T(8,128)(2,1)S(1)} %shard_map.78.refs_2_.refs_1_.refs_4_, bf16[192,1024]{1,0:T(8,128)(2,1)} %collective-permute-done.8.refs_3_.refs_2_.refs_5_, f32[8,128]{1,0:T(8,128)S(1)} %copy-done.11), custom_call_target="tpu_custom_call" | custom-call | bytes 2097152 | tf_op jit(solution)/shard_map/pallas_call | solution.py:215
  53.6 1.5 %collective-permute-start.13 = (bf16[512,1024]{1,0:T(8,128)(2,1)}, bf16[512,1024]{1,0:T(8,128)(2,1)S(1)}, u32[]{:S(2)}, u32[]{:S(2)}) collective-permute-start(bf16[512,1024]{1,0:T(8,128)(2,1)} %shard_map.84), channel_id=1, source_target_pairs={{0,16},{16,0},{1,17},{17,1},{2,18},{18,2},{3,19},{19,3},{4,20},{20... | collective-permute-start | bytes 3145736 | tf_op jit(solution)/shard_map/ppermute | solution.py:552
  55.1 1.9 %collective-permute-done.9.refs_6_.refs_8_ = bf16[192,1024]{1,0:T(8,128)(2,1)S(1)} collective-permute-done((bf16[192,1024]{1,0:T(8,128)(2,1)}, bf16[192,1024]{1,0:T(8,128)(2,1)S(1)}, u32[]{:S(2)}, u32[]{:S(2)}) %collective-permute-start.9) | collective-permute-done | bytes 393248 | tf_op jit(solution)/shard_map/ppermute | solution.py:546
  57.8 11.5 %shard_map.80 = bf16[16,32,128]{2,1,0:T(8,128)(2,1)} custom-call(s32[1]{0:T(128)} %bitcast.4.refs_0_, bf16[128,1024]{1,0:T(8,128)(2,1)} %copy-done.4, bf16[192,1024]{1,0:T(8,128)(2,1)} %copy-done.2, bf16[192,1024]{1,0:T(8,128)(2,1)} %collective-permute-done.8.refs_3_.refs_2_.refs_5_, bf16[128,1024]{1,0:T(8,128)(2,1)} %copy-done.14, ...), custom_call_target="tpu_custom_call" | custom-call | flops 3623878656 | bytes 6291456 | tf_op jit(solution)/shard_map/pallas_call | solution.py:301
  69.3 11.5 %all_to_all.20.pieces_ref.refs_1_ = bf16[16,32,128]{2,1,0:T(8,128)(2,1)S(1)} all-to-all(bf16[16,32,128]{2,1,0:T(8,128)(2,1)} %shard_map.80), channel_id=1, replica_groups=mesh['sample'=2,'depth'=16] {'depth'}, dimensions={0} | all-to-all | bytes 262144 | tf_op jit(solution)/shard_map/all_to_all | solution.py:591
  81.5 3.4 %shard_map.81 = (bf16[256,256]{1,0:T(8,128)(2,1)S(1)}, bf16[32,32,128]{2,1,0:T(8,128)(2,1)}) custom-call(bf16[16,32,128]{2,1,0:T(8,128)(2,1)S(1)} %all_to_all.20.pieces_ref.refs_1_, f32[256,256]{1,0:T(8,128)S(1)} %get-tuple-element.14.refs_3_.slope_ref, bf16[256,3456]{1,0:T(8,128)(2,1)S(1)} %get-tuple-element.17.lhs_ref), custom_call_target="tpu_custom_call" | custom-call | flops 452984832 | bytes 3145728 | tf_op jit(solution)/shard_map/pallas_call | solution.py:461
  85.6 2.6 %all-to-all-start.2 = ((bf16[32,32,128]{2,1,0:T(8,128)(2,1)}), bf16[32,32,128]{2,1,0:T(8,128)(2,1)S(1)}, u32[]{:S(2)}, u32[]{:S(2)}) async-start(bf16[32,32,128]{2,1,0:T(8,128)(2,1)} %get-tuple-element.19), calls=%async_computation.3 | async-start | bytes 524288 | tf_op jit(solution)/shard_map/all_to_all | solution.py:608
  88.8 13.8 %shard_map.86 = (f32[1728,1024]{1,0:T(8,128)}, f32[8,128]{1,0:T(8,128)}) custom-call(s32[1]{0:T(128)} %bitcast.4.refs_0_, bf16[16,32,128]{2,1,0:T(8,128)(2,1)} %copy-done.5, bf16[16,32,128]{2,1,0:T(8,128)(2,1)} %copy-done.15, bf16[128,1024]{1,0:T(8,128)(2,1)} %copy-done.4, bf16[192,1024]{1,0:T(8,128)(2,1)} %copy-done.2, ...), custom_call_target="tpu_custom_call" | custom-call | flops 7247757312 | bytes 18874368 | tf_op jit(solution)/shard_map/pallas_call | solution.py:383
  104.1 5.8 %all-to-all-start.3 = ((bf16[32,32,128]{2,1,0:T(8,128)(2,1)}), bf16[32,32,128]{2,1,0:T(8,128)(2,1)S(1)}, u32[]{:S(2)}, u32[]{:S(2)}) async-start(bf16[32,32,128]{2,1,0:T(8,128)(2,1)} %shard_map.87), calls=%async_computation.4 | async-start | bytes 524288 | tf_op jit(solution)/shard_map/all_to_all | solution.py:614
  109.9 1.3 %collective-permute-start.11 = (bf16[256,256]{1,0:T(8,128)(2,1)S(1)}, bf16[256,256]{1,0:T(8,128)(2,1)S(1)}, u32[]{:S(2)}, u32[]{:S(2)}) collective-permute-start(bf16[256,256]{1,0:T(8,128)(2,1)S(1)} %copy-done.10), channel_id=1, source_target_pairs={{1,0},{2,1},{3,2},{4,3},{5,4},{6,5},{7,6},{8,7},{9,8},{10,9},{11,1... | collective-permute-start | bytes 393224 | tf_op jit(solution)/shard_map/ppermute | solution.py:540
  111.2 3.0 %collective-permute-start.10 = (bf16[256,256]{1,0:T(8,128)(2,1)S(1)}, bf16[256,256]{1,0:T(8,128)(2,1)S(1)}, u32[]{:S(2)}, u32[]{:S(2)}) collective-permute-start(bf16[256,256]{1,0:T(8,128)(2,1)S(1)} %copy-done.10), channel_id=1, source_target_pairs={{0,1},{1,2},{2,3},{3,4},{4,5},{5,6},{6,7},{7,8},{8,9},{9,10},{10,1... | collective-permute-start | bytes 393224 | tf_op jit(solution)/shard_map/ppermute | solution.py:539
  115.2 1.4 %shard_map.83 = bf16[32,2048]{1,0:T(8,128)(2,1)} custom-call(bf16[256,256]{1,0:T(8,128)(2,1)S(1)} %collective-permute-done.10.before_ref, bf16[256,256]{1,0:T(8,128)(2,1)S(1)} %copy-done.10, bf16[256,256]{1,0:T(8,128)(2,1)S(1)} %collective-permute-done.11.after_ref, bf16[3456,256]{1,0:T(8,128)(2,1)S(1)} %shard_map.82.w_ref), custom_call_target="tpu_custom_call" | custom-call | flops 452984832 | bytes 3145728 | tf_op jit(solution)/shard_map/pallas_call | solution.py:489
  116.6 4.5 %all-to-all-done.3.packed_ref = bf16[32,32,128]{2,1,0:T(8,128)(2,1)S(1)} async-done(((bf16[32,32,128]{2,1,0:T(8,128)(2,1)}), bf16[32,32,128]{2,1,0:T(8,128)(2,1)S(1)}, u32[]{:S(2)}, u32[]{:S(2)}) %all-to-all-start.3) | async-done | bytes 262176 | tf_op jit(solution)/shard_map/all_to_all | solution.py:614
  121.1 1.3 shard_map.88
  (64 shorter events, 9.4 us)
Async XLA Ops:
  7.2 11.9 %collective-permute-start.1 = (bf16[32,2048]{1,0:T(8,128)(2,1)}, bf16[32,2048]{1,0:T(8,128)(2,1)S(1)}, u32[]{:S(2)}, u32[]{:S(2)}) collective-permute-start(bf16[32,2048]{1,0:T(8,128)(2,1)} %bitcast.10), channel_id=1, source_target_pairs={{1,0},{2,1},{3,2},{4,3},{5,4},{6,5},{7,6},{8,7},{9,8},{10,9},{11,1... | collective-permute-start | bytes 393224 | tf_op jit(solution)/shard_map/ppermute | solution.py:540
  8.5 12.4 %collective-permute-start = (bf16[32,2048]{1,0:T(8,128)(2,1)}, bf16[32,2048]{1,0:T(8,128)(2,1)S(1)}, u32[]{:S(2)}, u32[]{:S(2)}) collective-permute-start(bf16[32,2048]{1,0:T(8,128)(2,1)} %bitcast.11), channel_id=1, source_target_pairs={{0,1},{1,2},{2,3},{3,4},{4,5},{5,6},{6,7},{7,8},{8,9},{9,10},{10,1... | collective-permute-start | bytes 393224 | tf_op jit(solution)/shard_map/ppermute | solution.py:539
  11.5 19.7 %collective-permute-start.6 = (bf16[64,1024]{1,0:T(8,128)(2,1)}, bf16[64,1024]{1,0:T(8,128)(2,1)S(1)}, u32[]{:S(2)}, u32[]{:S(2)}) collective-permute-start(bf16[64,1024]{1,0:T(8,128)(2,1)} %bitcast.13), channel_id=1, source_target_pairs={{0,12},{1,13},{2,14},{3,15},{4,8},{5,9},{6,10},{7,11},{8,4},{9,5},... | collective-permute-start | bytes 393224 | tf_op jit(solution)/shard_map/ppermute | solution.py:546
  17.0 14.3 %collective-permute-start.5 = (bf16[64,1024]{1,0:T(8,128)(2,1)}, bf16[64,1024]{1,0:T(8,128)(2,1)S(1)}, u32[]{:S(2)}, u32[]{:S(2)}) collective-permute-start(bf16[64,1024]{1,0:T(8,128)(2,1)} %bitcast.14), channel_id=1, source_target_pairs={{0,8},{1,9},{2,10},{3,11},{4,12},{5,13},{6,14},{7,15},{8,0},{9,1},... | collective-permute-start | bytes 393224 | tf_op jit(solution)/shard_map/ppermute | solution.py:546
  17.0 14.3 %collective-permute-start.4 = (bf16[64,1024]{1,0:T(8,128)(2,1)}, bf16[64,1024]{1,0:T(8,128)(2,1)S(1)}, u32[]{:S(2)}, u32[]{:S(2)}) collective-permute-start(bf16[64,1024]{1,0:T(8,128)(2,1)} %bitcast.15), channel_id=1, source_target_pairs={{0,4},{1,5},{2,6},{3,7},{4,0},{5,1},{6,2},{7,3},{8,12},{9,13},{10,... | collective-permute-start | bytes 393224 | tf_op jit(solution)/shard_map/ppermute | solution.py:546
  19.5 11.7 %collective-permute-start.2 = (bf16[64,1024]{1,0:T(8,128)(2,1)S(1)}, bf16[64,1024]{1,0:T(8,128)(2,1)S(1)}, u32[]{:S(2)}, u32[]{:S(2)}) collective-permute-start(bf16[64,1024]{1,0:T(8,128)(2,1)S(1)} %bitcast.16), channel_id=1, source_target_pairs={{0,2},{1,3},{2,0},{3,1},{4,6},{5,7},{6,4},{7,5},{8,10},{9,11},{10,... | collective-permute-start | bytes 393224 | tf_op jit(solution)/shard_map/ppermute | solution.py:546
  22.6 16.6 %all-to-all-start = ((bf16[16,32,128]{2,1,0:T(8,128)(2,1)}), bf16[16,32,128]{2,1,0:T(8,128)(2,1)S(1)}, u32[]{:S(2)}, u32[]{:S(2)}) async-start(bf16[16,32,128]{2,1,0:T(8,128)(2,1)} %get-tuple-element.13), calls=%async_computation | async-start | bytes 262144 | tf_op jit(solution)/shard_map/all_to_all | solution.py:576
  31.2 91.2 %reduce-scatter.2.cloned.1.call-start = ((), (), s32[]{:S(2)}) async-start(), calls=%async_computation.5 | async-start | bytes 2228224 | tf_op jit(solution)/shard_map/reduce_scatter | solution.py:587
  31.3 19.6 %copy-start.2 = (bf16[192,1024]{1,0:T(8,128)(2,1)}, bf16[192,1024]{1,0:T(8,128)(2,1)S(1)}, u32[]{:S(2)}) copy-start(bf16[192,1024]{1,0:T(8,128)(2,1)S(1)} %shard_map.78.refs_2_.refs_1_.refs_4_) | copy-start | bytes 1179652
  31.3 8.0 %collective-permute-start.7 = (bf16[192,1024]{1,0:T(8,128)(2,1)S(1)}, bf16[192,1024]{1,0:T(8,128)(2,1)}, u32[]{:S(2)}, u32[]{:S(2)}) collective-permute-start(bf16[192,1024]{1,0:T(8,128)(2,1)S(1)} %shard_map.78.refs_2_.refs_1_.refs_4_), channel_id=1, source_target_pairs={{0,1},{1,0},{2,3},{3,2},{4,5},{5,4},{6,7},{7,6},{8,9},{9,8},{10,11... | collective-permute-start | bytes 1179656 | tf_op jit(solution)/shard_map/ppermute | solution.py:546
  39.1 11.7 %copy-start.4 = (bf16[128,1024]{1,0:T(8,128)(2,1)}, bf16[128,1024]{1,0:T(8,128)(2,1)S(1)}, u32[]{:S(2)}) copy-start(bf16[128,1024]{1,0:T(8,128)(2,1)S(1)} %shard_map.77.refs_1_.refs_0_.refs_3_) | copy-start | bytes 786436
  39.1 1.6 %collective-permute-start.3 = (bf16[128,1024]{1,0:T(8,128)(2,1)S(1)}, bf16[128,1024]{1,0:T(8,128)(2,1)S(1)}, u32[]{:S(2)}, u32[]{:S(2)}) collective-permute-start(bf16[128,1024]{1,0:T(8,128)(2,1)S(1)} %shard_map.77.refs_1_.refs_0_.refs_3_), channel_id=1, source_target_pairs={{0,1},{1,0},{2,3},{3,2},{4,5},{5,4},{6,7},{7,6},{8,9},{9,8},{10,11... | collective-permute-start | bytes 786440 | tf_op jit(solution)/shard_map/ppermute | solution.py:546
  39.2 11.6 %collective-permute-start.8 = (bf16[192,1024]{1,0:T(8,128)(2,1)S(1)}, bf16[192,1024]{1,0:T(8,128)(2,1)}, u32[]{:S(2)}, u32[]{:S(2)}) collective-permute-start(bf16[192,1024]{1,0:T(8,128)(2,1)S(1)} %shard_map.78.refs_2_.refs_1_.refs_4_), channel_id=1, source_target_pairs={{0,2},{1,3},{2,0},{3,1},{4,6},{5,7},{6,4},{7,5},{8,10},{9,11},{10,... | collective-permute-start | bytes 1179656 | tf_op jit(solution)/shard_map/ppermute | solution.py:546
  53.6 27.3 %collective-permute-start.13 = (bf16[512,1024]{1,0:T(8,128)(2,1)}, bf16[512,1024]{1,0:T(8,128)(2,1)S(1)}, u32[]{:S(2)}, u32[]{:S(2)}) collective-permute-start(bf16[512,1024]{1,0:T(8,128)(2,1)} %shard_map.84), channel_id=1, source_target_pairs={{0,16},{16,0},{1,17},{17,1},{2,18},{18,2},{3,19},{19,3},{4,20},{20... | collective-permute-start | bytes 3145736 | tf_op jit(solution)/shard_map/ppermute | solution.py:552
  55.1 1.9 %collective-permute-start.9 = (bf16[192,1024]{1,0:T(8,128)(2,1)}, bf16[192,1024]{1,0:T(8,128)(2,1)S(1)}, u32[]{:S(2)}, u32[]{:S(2)}) collective-permute-start(bf16[192,1024]{1,0:T(8,128)(2,1)} %collective-permute-done.8.refs_3_.refs_2_.refs_5_), channel_id=1, source_target_pairs={{0,1},{1,0},{2,3},{3,2},{4,5},{5,4},{6,7},{7,6},{8,9},{9,8},{10,11... | collective-permute-start | bytes 1179656 | tf_op jit(solution)/shard_map/ppermute | solution.py:546
  69.3 11.6 %copy-start.6 = (bf16[16,32,128]{2,1,0:T(8,128)(2,1)S(1)}, bf16[16,32,128]{2,1,0:T(8,128)(2,1)}, u32[]{:S(2)}) copy-start(bf16[16,32,128]{2,1,0:T(8,128)(2,1)} %copy-done.5) | copy-start | bytes 393220
  80.9 7.3 %collective-permute-start.14 = (bf16[512,1024]{1,0:T(8,128)(2,1)S(1)}, bf16[512,1024]{1,0:T(8,128)(2,1)}, u32[]{:S(2)}, u32[]{:S(2)}) collective-permute-start(bf16[512,1024]{1,0:T(8,128)(2,1)S(1)} %shard_map.85.refs_9_), channel_id=1, source_target_pairs={{0,1},{1,0},{2,3},{3,2},{4,5},{5,4},{6,7},{7,6},{8,9},{9,8},{10,11... | collective-permute-start | bytes 3145736 | tf_op jit(solution)/shard_map/ppermute | solution.py:546
  80.9 7.3 %collective-permute-start.12 = (bf16[16,32,128]{2,1,0:T(8,128)(2,1)S(1)}, bf16[16,32,128]{2,1,0:T(8,128)(2,1)S(1)}, u32[]{:S(2)}, u32[]{:S(2)}) collective-permute-start(bf16[16,32,128]{2,1,0:T(8,128)(2,1)S(1)} %copy-done.6), channel_id=1, source_target_pairs={{0,16},{16,0},{1,17},{17,1},{2,18},{18,2},{3,19},{19,3},{4,20},{20... | collective-permute-start | bytes 393224 | tf_op jit(solution)/shard_map/ppermute | solution.py:552
  85.6 17.1 %all-to-all-start.2 = ((bf16[32,32,128]{2,1,0:T(8,128)(2,1)}), bf16[32,32,128]{2,1,0:T(8,128)(2,1)S(1)}, u32[]{:S(2)}, u32[]{:S(2)}) async-start(bf16[32,32,128]{2,1,0:T(8,128)(2,1)} %get-tuple-element.19), calls=%async_computation.3 | async-start | bytes 524288 | tf_op jit(solution)/shard_map/all_to_all | solution.py:608
  88.8 21.1 %copy-start.10 = (bf16[256,256]{1,0:T(8,128)(2,1)S(1)}, bf16[256,256]{1,0:T(8,128)(2,1)}, u32[]{:S(2)}) copy-start(bf16[256,256]{1,0:T(8,128)(2,1)} %copy-done.9) | copy-start | bytes 393220
  88.8 25.4 %copy-start.1 = (bf16[27,64,64]{2,1,0:T(8,128)(2,1)S(1)}, bf16[27,64,64]{2,1,0:T(8,128)(2,1)}, u32[]{:S(2)}) copy-start(bf16[27,64,64]{2,1,0:T(8,128)(2,1)} %w_ref.1) | copy-start | bytes 663556
  104.1 17.0 %all-to-all-start.3 = ((bf16[32,32,128]{2,1,0:T(8,128)(2,1)}), bf16[32,32,128]{2,1,0:T(8,128)(2,1)S(1)}, u32[]{:S(2)}, u32[]{:S(2)}) async-start(bf16[32,32,128]{2,1,0:T(8,128)(2,1)} %shard_map.87), calls=%async_computation.4 | async-start | bytes 524288 | tf_op jit(solution)/shard_map/all_to_all | solution.py:614
  109.9 5.0 %collective-permute-start.11 = (bf16[256,256]{1,0:T(8,128)(2,1)S(1)}, bf16[256,256]{1,0:T(8,128)(2,1)S(1)}, u32[]{:S(2)}, u32[]{:S(2)}) collective-permute-start(bf16[256,256]{1,0:T(8,128)(2,1)S(1)} %copy-done.10), channel_id=1, source_target_pairs={{1,0},{2,1},{3,2},{4,3},{5,4},{6,5},{7,6},{8,7},{9,8},{10,9},{11,1... | collective-permute-start | bytes 393224 | tf_op jit(solution)/shard_map/ppermute | solution.py:540
  111.2 4.0 %collective-permute-start.10 = (bf16[256,256]{1,0:T(8,128)(2,1)S(1)}, bf16[256,256]{1,0:T(8,128)(2,1)S(1)}, u32[]{:S(2)}, u32[]{:S(2)}) collective-permute-start(bf16[256,256]{1,0:T(8,128)(2,1)S(1)} %copy-done.10), channel_id=1, source_target_pairs={{0,1},{1,2},{2,3},{3,4},{4,5},{5,6},{6,7},{7,8},{8,9},{9,10},{10,1... | collective-permute-start | bytes 393224 | tf_op jit(solution)/shard_map/ppermute | solution.py:539
  (11 other events, 17.3 us)
Sparse Core Ops, SparseCore 0:
  55.2 61.7 reduce-scatter.1

commit v9 on v8

--- a/solution.py
+++ b/solution.py
@@ -321,33 +321,28 @@
     )(device, *cots, weight.reshape(3, 9 * C1, C2), *after)
 
 
-def weight_two_kernel(planes, pieces, scale, device_ref, *refs):
-    samples = len(pieces)
-    field_refs, cot_refs = refs[:samples], refs[samples:]
+def weight_two_kernel(planes, pieces, scale, based, device_ref, field_ref, *refs):
+    cot_refs = refs[: len(pieces)]
+    base_ref = refs[len(pieces)]
     out_ref, token_ref, cot_ref, flat_ref, lhs_ref, sems = refs[-6:]
     cells = planes * CELLS
     a = pl.program_id(0)
 
     @pl.when(a == 0)
     def _():
-        copies, first = [], 0
-        for s in range(samples):
-            refs_here = cot_refs[first : first + len(pieces[s])]
-            copies += plane_copies(device_ref[0], pieces[s], refs_here, cot_ref.at[s], CELLS, sems.at[s])
-            first += len(pieces[s])
+        copies = plane_copies(device_ref[0], pieces, cot_refs, cot_ref, CELLS, sems)
         for copy in copies:
             copy.start()
-        for s in range(samples):
-            cot_ref[s, :CELLS] = jnp.zeros((CELLS, C2), bf16)
-            cot_ref[s, cells + CELLS :] = jnp.zeros((CELLS, C2), bf16)
-
-            def cells_of(p):
-                x = field_refs[s][p].astype(f32)
-                return jnp.concatenate([x, pltpu.roll(x, C1, 1)], axis=0)
-
-            for j in range(planes // 2):
-                pair = jnp.concatenate([cells_of(2 * j), cells_of(2 * j + 1)], axis=0)
-                flat_ref[s, :, j * PACK : (j + 1) * PACK] = pair.T[:C1]
+        cot_ref[:CELLS] = jnp.zeros((CELLS, C2), bf16)
+        cot_ref[cells + CELLS :] = jnp.zeros((CELLS, C2), bf16)
+
+        def cells_of(p):
+            x = field_ref[p].astype(f32)
+            return jnp.concatenate([x, pltpu.roll(x, C1, 1)], axis=0)
+
+        for j in range(planes // 2):
+            pair = jnp.concatenate([cells_of(2 * j), cells_of(2 * j + 1)], axis=0)
+            flat_ref[:, j * PACK : (j + 1) * PACK] = pair.T[:C1]
 
         lane = lax.broadcasted_iota(jnp.int32, (1, cells), 1)
         row, column = (lane // LS) % LS, lane % LS
@@ -357,56 +352,56 @@
                 mask = inside.astype(f32)
                 shift = (-(LS * (b - 1) + c - 1)) % cells
                 t = 3 * b + c
-                for s in range(samples):
-                    value = flat_ref[s]
-                    if shift:
-                        value = pltpu.roll(value, shift, 1) * mask
-                    lhs_ref[s, t * C1 : (t + 1) * C1] = value.astype(bf16)
+                value = flat_ref[...]
+                if shift:
+                    value = pltpu.roll(value, shift, 1) * mask
+                lhs_ref[t * C1 : (t + 1) * C1] = value.astype(bf16)
         for copy in copies:
             copy.wait()
 
     rows = pl.ds(pl.multiple_of((2 - a) * CELLS, CELLS), cells)
-    total = None
-    for s in range(samples):
-        term = jnp.dot(lhs_ref[s], cot_ref[s, rows], preferred_element_type=f32)
-        total = term if total is None else total + term
-    out_ref[...] = total * scale
+    total = jnp.dot(lhs_ref[...], cot_ref[rows], preferred_element_type=f32) * scale
+    out_ref[...] = total + base_ref[...] if based else total
     token_ref[...] = jnp.zeros(token_ref.shape, f32)
 
 
-def weight_two(device, fields, pieces, cots, scale, after):
-    samples = len(fields)
-    planes = fields[0].shape[0]
+def weight_two(device, field, pieces, cots, scale, base, after):
+    planes = field.shape[0]
     cells = planes * CELLS
     block = 9 * C1
-    flat = [value for sample in cots for value in sample]
-    return pl.pallas_call(
-        lambda *refs: weight_two_kernel(planes, pieces, scale, *refs),
+    extra = ([] if base is None else [base]) + list(after)
+    extra_specs = [pl.BlockSpec(memory_space=pl.ANY)] * len(after)
+    if base is not None:
+        extra_specs = [pl.BlockSpec((block, C2), lambda n, s: (n, 0))] + extra_specs
+    return pl.pallas_call(
+        lambda *refs: weight_two_kernel(planes, pieces, scale, base is not None, *refs),
         grid_spec=pltpu.PrefetchScalarGridSpec(
             num_scalar_prefetch=1,
             grid=(3,),
-            in_specs=[pl.BlockSpec(field.shape, lambda n, s: (0, 0, 0)) for field in fields]
-            + [pl.BlockSpec(memory_space=pl.ANY)] * (len(flat) + len(after)),
+            in_specs=[pl.BlockSpec(field.shape, lambda n, s: (0, 0, 0))]
+            + [pl.BlockSpec(memory_space=pl.ANY)] * len(cots)
+            + extra_specs,
             out_specs=(
                 pl.BlockSpec((block, C2), lambda n, s: (n, 0)),
                 pl.BlockSpec((8, PACK), lambda n, s: (0, 0)),
             ),
             scratch_shapes=[
-                pltpu.VMEM((samples, (planes + 2) * CELLS, C2), bf16),
-                pltpu.VMEM((samples, C1, cells), f32),
-                pltpu.VMEM((samples, block, cells), bf16),
-                pltpu.SemaphoreType.DMA((samples, planes)),
+                pltpu.VMEM(((planes + 2) * CELLS, C2), bf16),
+                pltpu.VMEM((C1, cells), f32),
+                pltpu.VMEM((block, cells), bf16),
+                pltpu.SemaphoreType.DMA((planes,)),
             ],
         ),
         out_shape=(
             jax.ShapeDtypeStruct((TAPS * C1, C2), f32),
             jax.ShapeDtypeStruct((8, PACK), f32),
         ),
+        input_output_aliases={} if base is None else {2 + len(cots): 0},
         compiler_params=params(60),
         cost_estimate=pl.CostEstimate(
-            flops=2 * samples * cells * TAPS * C1 * C2, bytes_accessed=18 << 20, transcendentals=0
-        ),
-    )(device, *fields, *flat, *after)
+            flops=2 * cells * TAPS * C1 * C2, bytes_accessed=12 << 20, transcendentals=0
+        ),
+    )(device, field, *cots, *extra)
 
 
 def grad_pre_kernel(pieces_ref, slope_ref, lhs_ref, *refs):
@@ -589,16 +584,20 @@
     own_cots = cots + [near_core, far_core, flipped(far_chip, core)]
     grad_pieces = back_two(device, pieces, own_cots, flat_two, [done])
     returned = lax.all_to_all(grad_pieces, "depth", split_axis=0, concat_axis=0, tiled=True)
+    scale_two = 1.0 / math.sqrt(samples * shards * CELLS)
+    grad_conv2, token = weight_two(
+        device, fields, pieces, own_cots, scale_two, None, [grad_pieces]
+    )
+    all_fields = over_samples(fields)
+    grad_pre, partial_one = grad_pre_of(returned, slope, windows, [token] + all_fields[1:])
     half = joined(cots, [done])
     halves = [[difference for piece in group for difference in piece] for group in (pieces[:3], pieces[3:])]
     all_pieces, all_cots = [pieces], [own_cots]
     for value in over_samples(half)[1:]:
-        value = held(value, [returned])
+        value = held(value, [grad_pre])
         all_pieces.append(halves)
         all_cots.append([value, flipped(value, core)])
-    all_fields = over_samples(fields)
-
-    grad_pre, partial_one = grad_pre_of(returned, slope, windows, [])
+
     grad_before, grad_after = neighbours(grad_pre, "depth")
 
     devices = samples * shards
@@ -606,10 +605,10 @@
     scale_one = 1.0 / math.sqrt(samples * shards * LAT * LAT)
     shares = partial_one.reshape(devices, -1, PACK)
     shares = lax.all_to_all(shares, both, split_axis=0, concat_axis=0, tiled=True)
-    scale_two = 1.0 / math.sqrt(samples * shards * CELLS)
-    grad_conv2, token = weight_two(
-        device, all_fields, all_pieces, all_cots, scale_two, [grad_pre]
-    )
+    for k in range(1, samples):
+        grad_conv2, token = weight_two(
+            device, all_fields[k], all_pieces[k], all_cots[k], scale_two, grad_conv2, [grad_pre]
+        )
     summed = sum_shares(shares, scale_one, [token])
     shares = lax.all_to_all(summed, both, split_axis=0, concat_axis=0, tiled=True)
     grad_volume = back_one(grad_before, grad_pre, grad_after, back_band)

time: 130 us -> 128 us (0.985)
  blocking collectives: 11.5 us -> 0 us
  Pallas kernels: 45.4 us -> 50.8 us
  starting transfers between devices: 35.9 us -> 40 us
    all_to_all x1 -> x0, blocking collectives: 11.5 us -> none  [on_device(): lax.all_to_all(grad_pieces, 'depth', split_axis=0, concat_axis=0, tiled=T...]
    pallas_call x1 -> x2, Pallas kernels: 13.8 us -> 19.9 us  [weight_two(): pl.pallas_call(lambda *refs: weight_two_kernel(planes, pieces, scale, bas...]
    all_to_all x0 -> x1, starting transfers between devices: none -> 3.52 us  [on_device(): lax.all_to_all(grad_pieces, 'depth', split_axis=0, concat_axis=0, tiled=T...]
    ppermute x2, waiting for transfers between devices: 0.01 us -> 2.74 us  [over_samples(): lax.ppermute(value, 'sample', [(i, (i + shift) % count) for i in range(co...]
    ppermute x9, waiting for transfers between devices: 3.97 us -> 2.06 us  [flipped(): lax.ppermute(value, 'depth', [(i, i ^ difference) for i in range(count)])]
    unnamed x33 -> x39, local copies, waits for them, and re-layouts: 5.9 us -> 5.41 us
  transfers between devices with their start and end apart: 19 -> 20, of which waited for: 6 -> 6; matrix products, arithmetic and copies ran while one was open for 0% -> 0% of each run, Pallas kernels for 34% -> 40%
where the time goes in v9:
time: 128 us; the launch traced here: 127 us
  Pallas kernels  50.8 us (40%)
  starting transfers between devices  40 us (31%)
  waiting for transfers between devices  15.9 us (12%)
  between operations  14.4 us (11%)
  local copies, waits for them, and re-layouts  5.44 us (4%)
    pallas_call x2, Pallas kernels, weight_two(): pl.pallas_call(lambda *refs: weight_two_kernel(planes, pieces, scale, bas...  19.9 us
    pallas_call x1, Pallas kernels, back_two(): pl.pallas_call(lambda *refs: back_two_kernel(planes, pieces, *refs), grid...  11.5 us
    pallas_call x1, Pallas kernels, conv_two(): pl.pallas_call(lambda *refs: conv_two_kernel(planes, *refs), grid=(C2 //...  8.76 us
    all_to_all x1, starting transfers between devices, on_device(): lax.all_to_all(moved, 'depth', split_axis=0, concat_axis=0, tiled=True)  8.61 us
    ppermute x9, starting transfers between devices, flipped(): lax.ppermute(value, 'depth', [(i, i ^ difference) for i in range(count)])  8.1 us
    all_to_all x1, waiting for transfers between devices, on_device(): lax.all_to_all(moved, 'depth', split_axis=0, concat_axis=0, tiled=True)  7.33 us
    ppermute x2, starting transfers between devices, neighbours(): before = lax.ppermute(value, axis, [(i, i + 1) for i in range(count - 1)])  6.07 us
    all_to_all x1, starting transfers between devices, on_device(): lax.all_to_all(summed, both, split_axis=0, concat_axis=0, tiled=True)  5.75 us
  transfers between devices with their start and end apart: 20, of which 6 were waited for; matrix products, arithmetic and copies ran while one was open for 0% of the time, Pallas kernels for 40%

profile of v9, /device:TPU:0, one launch (start us, length us, event | category | flops | bytes accessed | tf_op | source)
XLA Modules:
  0.0 126.6 jit_solution(15350041927756706449)
XLA Ops:
  7.2 1.3 %collective-permute-start.1 = (bf16[32,2048]{1,0:T(8,128)(2,1)}, bf16[32,2048]{1,0:T(8,128)(2,1)S(1)}, u32[]{:S(2)}, u32[]{:S(2)}) collective-permute-start(bf16[32,2048]{1,0:T(8,128)(2,1)} %bitcast.10), channel_id=1, source_target_pairs={{1,0},{2,1},{3,2},{4,3},{5,4},{6,5},{7,6},{8,7},{9,8},{10,9},{11,1... | collective-permute-start | bytes 393224 | tf_op jit(solution)/shard_map/ppermute | solution.py:535
  8.5 3.0 %collective-permute-start = (bf16[32,2048]{1,0:T(8,128)(2,1)}, bf16[32,2048]{1,0:T(8,128)(2,1)S(1)}, u32[]{:S(2)}, u32[]{:S(2)}) collective-permute-start(bf16[32,2048]{1,0:T(8,128)(2,1)} %bitcast.11), channel_id=1, source_target_pairs={{0,1},{1,2},{2,3},{3,4},{4,5},{5,6},{6,7},{7,8},{8,9},{9,10},{10,1... | collective-permute-start | bytes 393224 | tf_op jit(solution)/shard_map/ppermute | solution.py:534
  11.5 5.5 %collective-permute-start.6 = (bf16[64,1024]{1,0:T(8,128)(2,1)}, bf16[64,1024]{1,0:T(8,128)(2,1)S(1)}, u32[]{:S(2)}, u32[]{:S(2)}) collective-permute-start(bf16[64,1024]{1,0:T(8,128)(2,1)} %bitcast.13), channel_id=1, source_target_pairs={{0,12},{1,13},{2,14},{3,15},{4,8},{5,9},{6,10},{7,11},{8,4},{9,5},... | collective-permute-start | bytes 393224 | tf_op jit(solution)/shard_map/ppermute | solution.py:541
  19.5 1.3 %collective-permute-start.2 = (bf16[64,1024]{1,0:T(8,128)(2,1)S(1)}, bf16[64,1024]{1,0:T(8,128)(2,1)S(1)}, u32[]{:S(2)}, u32[]{:S(2)}) collective-permute-start(bf16[64,1024]{1,0:T(8,128)(2,1)S(1)} %bitcast.16), channel_id=1, source_target_pairs={{0,2},{1,3},{2,0},{3,1},{4,6},{5,7},{6,4},{7,5},{8,10},{9,11},{10,... | collective-permute-start | bytes 393224 | tf_op jit(solution)/shard_map/ppermute | solution.py:541
  20.9 1.7 %shard_map.76 = (bf16[16,32,128]{2,1,0:T(8,128)(2,1)}, f32[256,256]{1,0:T(8,128)S(1)}, bf16[256,3456]{1,0:T(8,128)(2,1)S(1)}) custom-call(bf16[32,2048]{1,0:T(8,128)(2,1)S(1)} %collective-permute-done.before_ref, bf16[32,2048]{1,0:T(8,128)(2,1)S(1)} %bitcast.12, bf16[32,2048]{1,0:T(8,128)(2,1)S(1)} %collective-permute-done.1.after_ref, ...), custom_call_target="tpu_custom_call" | custom-call | flops 452984832 | bytes 5242880 | tf_op jit(solution)/shard_map/pallas_call | solution.py:107
  22.6 8.6 %all-to-all-start = ((bf16[16,32,128]{2,1,0:T(8,128)(2,1)}), bf16[16,32,128]{2,1,0:T(8,128)(2,1)S(1)}, u32[]{:S(2)}, u32[]{:S(2)}) async-start(bf16[16,32,128]{2,1,0:T(8,128)(2,1)} %get-tuple-element.15), calls=%async_computation | async-start | bytes 262144 | tf_op jit(solution)/shard_map/all_to_all | solution.py:571
  31.8 7.3 %all-to-all-done.refs_2_.refs_0_.refs_1_ = bf16[16,32,128]{2,1,0:T(8,128)(2,1)S(1)} async-done(((bf16[16,32,128]{2,1,0:T(8,128)(2,1)}), bf16[16,32,128]{2,1,0:T(8,128)(2,1)S(1)}, u32[]{:S(2)}, u32[]{:S(2)}) %all-to-all-start) | async-done | bytes 131104 | tf_op jit(solution)/shard_map/all_to_all | solution.py:571
  39.3 1.4 %collective-permute-done.3.refs_2_.refs_4_.refs_5_ = bf16[128,1024]{1,0:T(8,128)(2,1)S(1)} collective-permute-done((bf16[128,1024]{1,0:T(8,128)(2,1)S(1)}, bf16[128,1024]{1,0:T(8,128)(2,1)S(1)}, u32[]{:S(2)}, u32[]{:S(2)}) %collective-permute-start.3) | collective-permute-done | bytes 262176 | tf_op jit(solution)/shard_map/ppermute | solution.py:541
  41.4 8.8 %shard_map.79 = (bf16[1024,1024]{1,0:T(8,128)(2,1)}, f32[8,128]{1,0:T(8,128)}) custom-call(bf16[16,32,128]{2,1,0:T(8,128)(2,1)} %copy-done.7, bf16[1728,1024]{1,0:T(8,128)(2,1)} %bitcast.19, bf16[128,1024]{1,0:T(8,128)(2,1)} %copy-done.18, bf16[192,1024]{1,0:T(8,128)(2,1)} %copy-done.17), custom_call_target="tpu_custom_call" | custom-call | flops 3623878656 | bytes 10485760 | tf_op jit(solution)/shard_map/pallas_call | solution.py:180
  50.9 2.0 %shard_map.85 = bf16[512,1024]{1,0:T(8,128)(2,1)} custom-call(bf16[128,1024]{1,0:T(8,128)(2,1)S(1)} %shard_map.77.refs_1_.refs_2_.refs_0_, bf16[192,1024]{1,0:T(8,128)(2,1)S(1)} %shard_map.78.refs_2_.refs_3_.refs_1_, bf16[192,1024]{1,0:T(8,128)(2,1)} %collective-permute-done.8.refs_3_.refs_4_.refs_2_, f32[8,128]{1,0:T(8,128)S(1)} %copy-done.13), custom_call_target="tpu_custom_call" | custom-call | bytes 2097152 | tf_op jit(solution)/shard_map/pallas_call | solution.py:215
  52.9 1.5 %collective-permute-start.13 = (bf16[512,1024]{1,0:T(8,128)(2,1)}, bf16[512,1024]{1,0:T(8,128)(2,1)S(1)}, u32[]{:S(2)}, u32[]{:S(2)}) collective-permute-start(bf16[512,1024]{1,0:T(8,128)(2,1)} %shard_map.85), channel_id=1, source_target_pairs={{0,16},{16,0},{1,17},{17,1},{2,18},{18,2},{3,19},{19,3},{4,20},{20... | collective-permute-start | bytes 3145736 | tf_op jit(solution)/shard_map/ppermute | solution.py:547
  55.0 11.5 %shard_map.80.refs_8_ = bf16[16,32,128]{2,1,0:T(8,128)(2,1)} custom-call(s32[1]{0:T(128)} %bitcast.4.refs_0_, bf16[128,1024]{1,0:T(8,128)(2,1)} %copy-done.4, bf16[192,1024]{1,0:T(8,128)(2,1)} %copy-done.2, bf16[192,1024]{1,0:T(8,128)(2,1)} %collective-permute-done.8.refs_3_.refs_4_.refs_2_, bf16[128,1024]{1,0:T(8,128)(2,1)} %copy-done.18, ...), custom_call_target="tpu_custom_call" | custom-call | flops 3623878656 | bytes 6291456 | tf_op jit(solution)/shard_map/pallas_call | solution.py:301
  66.5 3.5 %all-to-all-start.1 = ((bf16[16,32,128]{2,1,0:T(8,128)(2,1)}), bf16[16,32,128]{2,1,0:T(8,128)(2,1)S(1)}, u32[]{:S(2)}, u32[]{:S(2)}) async-start(bf16[16,32,128]{2,1,0:T(8,128)(2,1)} %shard_map.80.refs_8_), calls=%async_computation.2 | async-start | bytes 262144 | tf_op jit(solution)/shard_map/all_to_all | solution.py:586
  70.0 8.7 %shard_map.81 = (f32[1728,1024]{1,0:T(8,128)}, f32[8,128]{1,0:T(8,128)}) custom-call(s32[1]{0:T(128)} %bitcast.4.refs_0_, bf16[16,32,128]{2,1,0:T(8,128)(2,1)} %copy-done.7, bf16[128,1024]{1,0:T(8,128)(2,1)} %copy-done.4, bf16[192,1024]{1,0:T(8,128)(2,1)} %copy-done.2, bf16[192,1024]{1,0:T(8,128)(2,1)} %collective-permute-done.8.refs_3_.refs_4_.refs_2_, ...), custom_call_target="tpu_custom_call" | custom-call | flops 3623878656 | bytes 12582912 | tf_op jit(solution)/shard_map/pallas_call | solution.py:376
  78.8 2.7 %collective-permute-done.10.refs_1_ = bf16[16,32,128]{2,1,0:T(8,128)(2,1)S(1)} collective-permute-done((bf16[16,32,128]{2,1,0:T(8,128)(2,1)S(1)}, bf16[16,32,128]{2,1,0:T(8,128)(2,1)S(1)}, u32[]{:S(2)}, u32[]{:S(2)}) %collective-permute-start.10) | collective-permute-done | bytes 131104 | tf_op jit(solution)/shard_map/ppermute | solution.py:547
  82.2 2.7 %shard_map.82 = (bf16[256,256]{1,0:T(8,128)(2,1)S(1)}, bf16[32,32,128]{2,1,0:T(8,128)(2,1)S(1)}) custom-call(bf16[16,32,128]{2,1,0:T(8,128)(2,1)S(1)} %all-to-all-done.1.pieces_ref, f32[256,256]{1,0:T(8,128)S(1)} %get-tuple-element.16.refs_3_.slope_ref, bf16[256,3456]{1,0:T(8,128)(2,1)S(1)} %get-tuple-element.19.lhs_ref, f32[8,128]{1,0:T(8,128)S(1)} %copy-done.14, ...), custom_call_target="tpu_custom_call" | custom-call | flops 452984832 | bytes 3145728 | tf_op jit(solution)/shard_map/pallas_call | solution.py:456
  85.6 3.2 %all-to-all-start.2 = ((bf16[32,32,128]{2,1,0:T(8,128)(2,1)}), bf16[32,32,128]{2,1,0:T(8,128)(2,1)S(1)}, u32[]{:S(2)}, u32[]{:S(2)}) async-start(bf16[32,32,128]{2,1,0:T(8,128)(2,1)} %copy-done.9), calls=%async_computation.3 | async-start | bytes 524288 | tf_op jit(solution)/shard_map/all_to_all | solution.py:607
  89.8 11.2 %shard_map.87 = (f32[1728,1024]{1,0:T(8,128)}, f32[8,128]{1,0:T(8,128)}) custom-call(s32[1]{0:T(128)} %bitcast.4.refs_0_, bf16[16,32,128]{2,1,0:T(8,128)(2,1)} %copy-done.12, bf16[512,1024]{1,0:T(8,128)(2,1)} %copy-done.3, bf16[512,1024]{1,0:T(8,128)(2,1)} %copy-done.16, f32[1728,1024]{1,0:T(8,128)} %get-tuple-element.23.refs_4_, ...), custom_call_target="tpu_custom_call", output_to_operand_aliasing={{0}: (4, {})} | custom-call | flops 3623878656 | bytes 12582912 | tf_op jit(solution)/shard_map/pallas_call | solution.py:376
  102.4 5.8 %all-to-all-start.3 = ((bf16[32,32,128]{2,1,0:T(8,128)(2,1)}), bf16[32,32,128]{2,1,0:T(8,128)(2,1)S(1)}, u32[]{:S(2)}, u32[]{:S(2)}) async-start(bf16[32,32,128]{2,1,0:T(8,128)(2,1)} %shard_map.88), calls=%async_computation.4 | async-start | bytes 524288 | tf_op jit(solution)/shard_map/all_to_all | solution.py:613
  108.2 1.4 %collective-permute-start.12 = (bf16[256,256]{1,0:T(8,128)(2,1)}, bf16[256,256]{1,0:T(8,128)(2,1)S(1)}, u32[]{:S(2)}, u32[]{:S(2)}) collective-permute-start(bf16[256,256]{1,0:T(8,128)(2,1)} %copy-done.5), channel_id=1, source_target_pairs={{1,0},{2,1},{3,2},{4,3},{5,4},{6,5},{7,6},{8,7},{9,8},{10,9},{11,1... | collective-permute-start | bytes 393224 | tf_op jit(solution)/shard_map/ppermute | solution.py:535
  109.6 3.0 %collective-permute-start.11 = (bf16[256,256]{1,0:T(8,128)(2,1)}, bf16[256,256]{1,0:T(8,128)(2,1)S(1)}, u32[]{:S(2)}, u32[]{:S(2)}) collective-permute-start(bf16[256,256]{1,0:T(8,128)(2,1)} %copy-done.5), channel_id=1, source_target_pairs={{0,1},{1,2},{2,3},{3,4},{4,5},{5,6},{6,7},{7,8},{8,9},{9,10},{10,1... | collective-permute-start | bytes 393224 | tf_op jit(solution)/shard_map/ppermute | solution.py:534
  113.8 1.4 %shard_map.84 = bf16[32,2048]{1,0:T(8,128)(2,1)} custom-call(bf16[256,256]{1,0:T(8,128)(2,1)S(1)} %collective-permute-done.11.before_ref, bf16[256,256]{1,0:T(8,128)(2,1)S(1)} %copy-done.6, bf16[256,256]{1,0:T(8,128)(2,1)S(1)} %collective-permute-done.12.after_ref, bf16[3456,256]{1,0:T(8,128)(2,1)S(1)} %shard_map.83.w_ref), custom_call_target="tpu_custom_call" | custom-call | flops 452984832 | bytes 3145728 | tf_op jit(solution)/shard_map/pallas_call | solution.py:484
  115.2 3.3 %all-to-all-done.3.packed_ref = bf16[32,32,128]{2,1,0:T(8,128)(2,1)S(1)} async-done(((bf16[32,32,128]{2,1,0:T(8,128)(2,1)}), bf16[32,32,128]{2,1,0:T(8,128)(2,1)S(1)}, u32[]{:S(2)}, u32[]{:S(2)}) %all-to-all-start.3) | async-done | bytes 262176 | tf_op jit(solution)/shard_map/all_to_all | solution.py:613
  118.4 1.3 %shard_map.89 = f32[27,64,64]{2,1,0:T(8,128)} custom-call(bf16[32,32,128]{2,1,0:T(8,128)(2,1)S(1)} %all-to-all-done.3.packed_ref), custom_call_target="tpu_custom_call" | custom-call | bytes 1048576 | tf_op jit(solution)/shard_map/pallas_call | solution.py:522
  (72 shorter events, 10.0 us)
Async XLA Ops:
  7.2 11.9 %collective-permute-start.1 = (bf16[32,2048]{1,0:T(8,128)(2,1)}, bf16[32,2048]{1,0:T(8,128)(2,1)S(1)}, u32[]{:S(2)}, u32[]{:S(2)}) collective-permute-start(bf16[32,2048]{1,0:T(8,128)(2,1)} %bitcast.10), channel_id=1, source_target_pairs={{1,0},{2,1},{3,2},{4,3},{5,4},{6,5},{7,6},{8,7},{9,8},{10,9},{11,1... | collective-permute-start | bytes 393224 | tf_op jit(solution)/shard_map/ppermute | solution.py:535
  8.5 12.4 %collective-permute-start = (bf16[32,2048]{1,0:T(8,128)(2,1)}, bf16[32,2048]{1,0:T(8,128)(2,1)S(1)}, u32[]{:S(2)}, u32[]{:S(2)}) collective-permute-start(bf16[32,2048]{1,0:T(8,128)(2,1)} %bitcast.11), channel_id=1, source_target_pairs={{0,1},{1,2},{2,3},{3,4},{4,5},{5,6},{6,7},{7,8},{8,9},{9,10},{10,1... | collective-permute-start | bytes 393224 | tf_op jit(solution)/shard_map/ppermute | solution.py:534
  11.5 19.7 %collective-permute-start.6 = (bf16[64,1024]{1,0:T(8,128)(2,1)}, bf16[64,1024]{1,0:T(8,128)(2,1)S(1)}, u32[]{:S(2)}, u32[]{:S(2)}) collective-permute-start(bf16[64,1024]{1,0:T(8,128)(2,1)} %bitcast.13), channel_id=1, source_target_pairs={{0,12},{1,13},{2,14},{3,15},{4,8},{5,9},{6,10},{7,11},{8,4},{9,5},... | collective-permute-start | bytes 393224 | tf_op jit(solution)/shard_map/ppermute | solution.py:541
  17.0 14.3 %collective-permute-start.5 = (bf16[64,1024]{1,0:T(8,128)(2,1)}, bf16[64,1024]{1,0:T(8,128)(2,1)S(1)}, u32[]{:S(2)}, u32[]{:S(2)}) collective-permute-start(bf16[64,1024]{1,0:T(8,128)(2,1)} %bitcast.14), channel_id=1, source_target_pairs={{0,8},{1,9},{2,10},{3,11},{4,12},{5,13},{6,14},{7,15},{8,0},{9,1},... | collective-permute-start | bytes 393224 | tf_op jit(solution)/shard_map/ppermute | solution.py:541
  17.0 14.3 %collective-permute-start.4 = (bf16[64,1024]{1,0:T(8,128)(2,1)}, bf16[64,1024]{1,0:T(8,128)(2,1)S(1)}, u32[]{:S(2)}, u32[]{:S(2)}) collective-permute-start(bf16[64,1024]{1,0:T(8,128)(2,1)} %bitcast.15), channel_id=1, source_target_pairs={{0,4},{1,5},{2,6},{3,7},{4,0},{5,1},{6,2},{7,3},{8,12},{9,13},{10,... | collective-permute-start | bytes 393224 | tf_op jit(solution)/shard_map/ppermute | solution.py:541
  19.5 11.7 %collective-permute-start.2 = (bf16[64,1024]{1,0:T(8,128)(2,1)S(1)}, bf16[64,1024]{1,0:T(8,128)(2,1)S(1)}, u32[]{:S(2)}, u32[]{:S(2)}) collective-permute-start(bf16[64,1024]{1,0:T(8,128)(2,1)S(1)} %bitcast.16), channel_id=1, source_target_pairs={{0,2},{1,3},{2,0},{3,1},{4,6},{5,7},{6,4},{7,5},{8,10},{9,11},{10,... | collective-permute-start | bytes 393224 | tf_op jit(solution)/shard_map/ppermute | solution.py:541
  22.6 16.6 %all-to-all-start = ((bf16[16,32,128]{2,1,0:T(8,128)(2,1)}), bf16[16,32,128]{2,1,0:T(8,128)(2,1)S(1)}, u32[]{:S(2)}, u32[]{:S(2)}) async-start(bf16[16,32,128]{2,1,0:T(8,128)(2,1)} %get-tuple-element.15), calls=%async_computation | async-start | bytes 262144 | tf_op jit(solution)/shard_map/all_to_all | solution.py:571
  31.2 88.6 %reduce-scatter.2.cloned.1.call-start = ((), (), s32[]{:S(2)}) async-start(), calls=%async_computation.5 | async-start | bytes 2228224 | tf_op jit(solution)/shard_map/reduce_scatter | solution.py:582
  31.3 19.6 %copy-start.2 = (bf16[192,1024]{1,0:T(8,128)(2,1)}, bf16[192,1024]{1,0:T(8,128)(2,1)S(1)}, u32[]{:S(2)}) copy-start(bf16[192,1024]{1,0:T(8,128)(2,1)S(1)} %shard_map.78.refs_2_.refs_3_.refs_1_) | copy-start | bytes 1179652
  31.3 8.0 %collective-permute-start.7 = (bf16[192,1024]{1,0:T(8,128)(2,1)S(1)}, bf16[192,1024]{1,0:T(8,128)(2,1)S(1)}, u32[]{:S(2)}, u32[]{:S(2)}) collective-permute-start(bf16[192,1024]{1,0:T(8,128)(2,1)S(1)} %shard_map.78.refs_2_.refs_3_.refs_1_), channel_id=1, source_target_pairs={{0,1},{1,0},{2,3},{3,2},{4,5},{5,4},{6,7},{7,6},{8,9},{9,8},{10,11... | collective-permute-start | bytes 1179656 | tf_op jit(solution)/shard_map/ppermute | solution.py:541
  39.1 11.7 %copy-start.4 = (bf16[128,1024]{1,0:T(8,128)(2,1)}, bf16[128,1024]{1,0:T(8,128)(2,1)S(1)}, u32[]{:S(2)}) copy-start(bf16[128,1024]{1,0:T(8,128)(2,1)S(1)} %shard_map.77.refs_1_.refs_2_.refs_0_) | copy-start | bytes 786436
  39.1 1.6 %collective-permute-start.3 = (bf16[128,1024]{1,0:T(8,128)(2,1)S(1)}, bf16[128,1024]{1,0:T(8,128)(2,1)S(1)}, u32[]{:S(2)}, u32[]{:S(2)}) collective-permute-start(bf16[128,1024]{1,0:T(8,128)(2,1)S(1)} %shard_map.77.refs_1_.refs_2_.refs_0_), channel_id=1, source_target_pairs={{0,1},{1,0},{2,3},{3,2},{4,5},{5,4},{6,7},{7,6},{8,9},{9,8},{10,11... | collective-permute-start | bytes 786440 | tf_op jit(solution)/shard_map/ppermute | solution.py:541
  39.2 11.6 %collective-permute-start.8 = (bf16[192,1024]{1,0:T(8,128)(2,1)S(1)}, bf16[192,1024]{1,0:T(8,128)(2,1)}, u32[]{:S(2)}, u32[]{:S(2)}) collective-permute-start(bf16[192,1024]{1,0:T(8,128)(2,1)S(1)} %shard_map.78.refs_2_.refs_3_.refs_1_), channel_id=1, source_target_pairs={{0,2},{1,3},{2,0},{3,1},{4,6},{5,7},{6,4},{7,5},{8,10},{9,11},{10,... | collective-permute-start | bytes 1179656 | tf_op jit(solution)/shard_map/ppermute | solution.py:541
  50.9 4.1 %collective-permute-start.9 = (bf16[192,1024]{1,0:T(8,128)(2,1)}, bf16[192,1024]{1,0:T(8,128)(2,1)}, u32[]{:S(2)}, u32[]{:S(2)}) collective-permute-start(bf16[192,1024]{1,0:T(8,128)(2,1)} %collective-permute-done.8.refs_3_.refs_4_.refs_2_), channel_id=1, source_target_pairs={{0,1},{1,0},{2,3},{3,2},{4,5},{5,4},{6,7},{7,6},{8,9},{9,8},{10,11... | collective-permute-start | bytes 1179656 | tf_op jit(solution)/shard_map/ppermute | solution.py:541
  52.9 32.0 %collective-permute-start.13 = (bf16[512,1024]{1,0:T(8,128)(2,1)}, bf16[512,1024]{1,0:T(8,128)(2,1)S(1)}, u32[]{:S(2)}, u32[]{:S(2)}) collective-permute-start(bf16[512,1024]{1,0:T(8,128)(2,1)} %shard_map.85), channel_id=1, source_target_pairs={{0,16},{16,0},{1,17},{17,1},{2,18},{18,2},{3,19},{19,3},{4,20},{20... | collective-permute-start | bytes 3145736 | tf_op jit(solution)/shard_map/ppermute | solution.py:547
  54.4 27.1 %collective-permute-start.10 = (bf16[16,32,128]{2,1,0:T(8,128)(2,1)S(1)}, bf16[16,32,128]{2,1,0:T(8,128)(2,1)S(1)}, u32[]{:S(2)}, u32[]{:S(2)}) collective-permute-start(bf16[16,32,128]{2,1,0:T(8,128)(2,1)S(1)} %copy-done.8), channel_id=1, source_target_pairs={{0,16},{16,0},{1,17},{17,1},{2,18},{18,2},{3,19},{19,3},{4,20},{20... | collective-permute-start | bytes 393224 | tf_op jit(solution)/shard_map/ppermute | solution.py:547
  66.5 15.0 %all-to-all-start.1 = ((bf16[16,32,128]{2,1,0:T(8,128)(2,1)}), bf16[16,32,128]{2,1,0:T(8,128)(2,1)S(1)}, u32[]{:S(2)}, u32[]{:S(2)}) async-start(bf16[16,32,128]{2,1,0:T(8,128)(2,1)} %shard_map.80.refs_8_), calls=%async_computation.2 | async-start | bytes 262144 | tf_op jit(solution)/shard_map/all_to_all | solution.py:586
  84.9 3.8 %collective-permute-start.14 = (bf16[512,1024]{1,0:T(8,128)(2,1)S(1)}, bf16[512,1024]{1,0:T(8,128)(2,1)S(1)}, u32[]{:S(2)}, u32[]{:S(2)}) collective-permute-start(bf16[512,1024]{1,0:T(8,128)(2,1)S(1)} %shard_map.86.refs_2_), channel_id=1, source_target_pairs={{0,1},{1,0},{2,3},{3,2},{4,5},{5,4},{6,7},{7,6},{8,9},{9,8},{10,11... | collective-permute-start | bytes 3145736 | tf_op jit(solution)/shard_map/ppermute | solution.py:541
  85.6 15.4 %all-to-all-start.2 = ((bf16[32,32,128]{2,1,0:T(8,128)(2,1)}), bf16[32,32,128]{2,1,0:T(8,128)(2,1)S(1)}, u32[]{:S(2)}, u32[]{:S(2)}) async-start(bf16[32,32,128]{2,1,0:T(8,128)(2,1)} %copy-done.9), calls=%async_computation.3 | async-start | bytes 524288 | tf_op jit(solution)/shard_map/all_to_all | solution.py:607
  89.8 22.9 %copy-start.1 = (bf16[27,64,64]{2,1,0:T(8,128)(2,1)S(1)}, bf16[27,64,64]{2,1,0:T(8,128)(2,1)}, u32[]{:S(2)}) copy-start(bf16[27,64,64]{2,1,0:T(8,128)(2,1)} %w_ref.1) | copy-start | bytes 663556
  102.4 16.0 %all-to-all-start.3 = ((bf16[32,32,128]{2,1,0:T(8,128)(2,1)}), bf16[32,32,128]{2,1,0:T(8,128)(2,1)S(1)}, u32[]{:S(2)}, u32[]{:S(2)}) async-start(bf16[32,32,128]{2,1,0:T(8,128)(2,1)} %shard_map.88), calls=%async_computation.4 | async-start | bytes 524288 | tf_op jit(solution)/shard_map/all_to_all | solution.py:613
  108.2 5.7 %copy-start.6 = (bf16[256,256]{1,0:T(8,128)(2,1)S(1)}, bf16[256,256]{1,0:T(8,128)(2,1)}, u32[]{:S(2)}) copy-start(bf16[256,256]{1,0:T(8,128)(2,1)} %copy-done.5) | copy-start | bytes 393220
  108.2 5.2 %collective-permute-start.12 = (bf16[256,256]{1,0:T(8,128)(2,1)}, bf16[256,256]{1,0:T(8,128)(2,1)S(1)}, u32[]{:S(2)}, u32[]{:S(2)}) collective-permute-start(bf16[256,256]{1,0:T(8,128)(2,1)} %copy-done.5), channel_id=1, source_target_pairs={{1,0},{2,1},{3,2},{4,3},{5,4},{6,5},{7,6},{8,7},{9,8},{10,9},{11,1... | collective-permute-start | bytes 393224 | tf_op jit(solution)/shard_map/ppermute | solution.py:535
  109.6 4.2 %collective-permute-start.11 = (bf16[256,256]{1,0:T(8,128)(2,1)}, bf16[256,256]{1,0:T(8,128)(2,1)S(1)}, u32[]{:S(2)}, u32[]{:S(2)}) collective-permute-start(bf16[256,256]{1,0:T(8,128)(2,1)} %copy-done.5), channel_id=1, source_target_pairs={{0,1},{1,2},{2,3},{3,4},{4,5},{5,6},{6,7},{7,8},{8,9},{9,10},{10,1... | collective-permute-start | bytes 393224 | tf_op jit(solution)/shard_map/ppermute | solution.py:534
  (15 other events, 27.1 us)
Sparse Core Ops, SparseCore 0:
  50.4 59.4 reduce-scatter.1

commit v10 on v9

--- a/solution.py
+++ b/solution.py
@@ -397,7 +397,7 @@
             jax.ShapeDtypeStruct((8, PACK), f32),
         ),
         input_output_aliases={} if base is None else {2 + len(cots): 0},
-        compiler_params=params(60),
+        compiler_params=params(60 if base is None else 48),
         cost_estimate=pl.CostEstimate(
             flops=2 * cells * TAPS * C1 * C2, bytes_accessed=12 << 20, transcendentals=0
         ),

time: 128 us -> 127 us (level)
  local copies, waits for them, and re-layouts: 5.44 us -> 3.84 us
  Pallas kernels: 50.8 us -> 52.1 us
    unnamed x39 -> x27, local copies, waits for them, and re-layouts: 5.41 us -> 3.81 us
    pallas_call x2, Pallas kernels: 19.9 us -> 21.2 us  [weight_two(): pl.pallas_call(lambda *refs: weight_two_kernel(planes, pieces, scale, bas...]
  transfers between devices with their start and end apart: 20 -> 20, of which waited for: 6 -> 6; matrix products, arithmetic and copies ran while one was open for 0% -> 0% of each run, Pallas kernels for 40% -> 41%
where the time goes in v10:
time: 127 us; the launch traced here: 126 us
  Pallas kernels  52.1 us (41%)
  starting transfers between devices  40 us (31%)
  waiting for transfers between devices  16 us (13%)
  between operations  14.3 us (11%)
  local copies, waits for them, and re-layouts  3.84 us (3%)
    pallas_call x2, Pallas kernels, weight_two(): pl.pallas_call(lambda *refs: weight_two_kernel(planes, pieces, scale, bas...  21.2 us
    pallas_call x1, Pallas kernels, back_two(): pl.pallas_call(lambda *refs: back_two_kernel(planes, pieces, *refs), grid...  11.5 us
    pallas_call x1, Pallas kernels, conv_two(): pl.pallas_call(lambda *refs: conv_two_kernel(planes, *refs), grid=(C2 //...  8.77 us
    all_to_all x1, starting transfers between devices, on_device(): lax.all_to_all(moved, 'depth', split_axis=0, concat_axis=0, tiled=True)  8.61 us
    ppermute x9, starting transfers between devices, flipped(): lax.ppermute(value, 'depth', [(i, i ^ difference) for i in range(count)])  8.1 us
    all_to_all x1, waiting for transfers between devices, on_device(): lax.all_to_all(moved, 'depth', split_axis=0, concat_axis=0, tiled=True)  7.33 us
    ppermute x2, starting transfers between devices, neighbours(): before = lax.ppermute(value, axis, [(i, i + 1) for i in range(count - 1)])  6.07 us
    all_to_all x1, starting transfers between devices, on_device(): lax.all_to_all(summed, both, split_axis=0, concat_axis=0, tiled=True)  5.85 us
  transfers between devices with their start and end apart: 20, of which 6 were waited for; matrix products, arithmetic and copies ran while one was open for 0% of the time, Pallas kernels for 41%

profile of v10, /device:TPU:0, one launch (start us, length us, event | category | flops | bytes accessed | tf_op | source)
XLA Modules:
  0.0 126.3 jit_solution(14993416858771394631)
XLA Ops:
  7.2 1.3 %collective-permute-start.1 = (bf16[32,2048]{1,0:T(8,128)(2,1)}, bf16[32,2048]{1,0:T(8,128)(2,1)S(1)}, u32[]{:S(2)}, u32[]{:S(2)}) collective-permute-start(bf16[32,2048]{1,0:T(8,128)(2,1)} %bitcast.10), channel_id=1, source_target_pairs={{1,0},{2,1},{3,2},{4,3},{5,4},{6,5},{7,6},{8,7},{9,8},{10,9},{11,1... | collective-permute-start | bytes 393224 | tf_op jit(solution)/shard_map/ppermute | solution.py:535
  8.5 3.0 %collective-permute-start = (bf16[32,2048]{1,0:T(8,128)(2,1)}, bf16[32,2048]{1,0:T(8,128)(2,1)S(1)}, u32[]{:S(2)}, u32[]{:S(2)}) collective-permute-start(bf16[32,2048]{1,0:T(8,128)(2,1)} %bitcast.11), channel_id=1, source_target_pairs={{0,1},{1,2},{2,3},{3,4},{4,5},{5,6},{6,7},{7,8},{8,9},{9,10},{10,1... | collective-permute-start | bytes 393224 | tf_op jit(solution)/shard_map/ppermute | solution.py:534
  11.5 5.5 %collective-permute-start.6 = (bf16[64,1024]{1,0:T(8,128)(2,1)}, bf16[64,1024]{1,0:T(8,128)(2,1)S(1)}, u32[]{:S(2)}, u32[]{:S(2)}) collective-permute-start(bf16[64,1024]{1,0:T(8,128)(2,1)} %bitcast.13), channel_id=1, source_target_pairs={{0,12},{1,13},{2,14},{3,15},{4,8},{5,9},{6,10},{7,11},{8,4},{9,5},... | collective-permute-start | bytes 393224 | tf_op jit(solution)/shard_map/ppermute | solution.py:541
  19.5 1.3 %collective-permute-start.2 = (bf16[64,1024]{1,0:T(8,128)(2,1)S(1)}, bf16[64,1024]{1,0:T(8,128)(2,1)S(1)}, u32[]{:S(2)}, u32[]{:S(2)}) collective-permute-start(bf16[64,1024]{1,0:T(8,128)(2,1)S(1)} %bitcast.16), channel_id=1, source_target_pairs={{0,2},{1,3},{2,0},{3,1},{4,6},{5,7},{6,4},{7,5},{8,10},{9,11},{10,... | collective-permute-start | bytes 393224 | tf_op jit(solution)/shard_map/ppermute | solution.py:541
  20.9 1.7 %shard_map.76 = (bf16[16,32,128]{2,1,0:T(8,128)(2,1)}, f32[256,256]{1,0:T(8,128)S(1)}, bf16[256,3456]{1,0:T(8,128)(2,1)S(1)}) custom-call(bf16[32,2048]{1,0:T(8,128)(2,1)S(1)} %collective-permute-done.before_ref, bf16[32,2048]{1,0:T(8,128)(2,1)S(1)} %bitcast.12, bf16[32,2048]{1,0:T(8,128)(2,1)S(1)} %collective-permute-done.1.after_ref, ...), custom_call_target="tpu_custom_call" | custom-call | flops 452984832 | bytes 5242880 | tf_op jit(solution)/shard_map/pallas_call | solution.py:107
  22.6 8.6 %all-to-all-start = ((bf16[16,32,128]{2,1,0:T(8,128)(2,1)}), bf16[16,32,128]{2,1,0:T(8,128)(2,1)S(1)}, u32[]{:S(2)}, u32[]{:S(2)}) async-start(bf16[16,32,128]{2,1,0:T(8,128)(2,1)} %get-tuple-element.15), calls=%async_computation | async-start | bytes 262144 | tf_op jit(solution)/shard_map/all_to_all | solution.py:571
  31.8 7.3 %all-to-all-done.refs_2_.refs_0_.refs_1_ = bf16[16,32,128]{2,1,0:T(8,128)(2,1)S(1)} async-done(((bf16[16,32,128]{2,1,0:T(8,128)(2,1)}), bf16[16,32,128]{2,1,0:T(8,128)(2,1)S(1)}, u32[]{:S(2)}, u32[]{:S(2)}) %all-to-all-start) | async-done | bytes 131104 | tf_op jit(solution)/shard_map/all_to_all | solution.py:571
  39.3 1.4 %collective-permute-done.3.refs_2_.refs_4_.refs_5_ = bf16[128,1024]{1,0:T(8,128)(2,1)S(1)} collective-permute-done((bf16[128,1024]{1,0:T(8,128)(2,1)S(1)}, bf16[128,1024]{1,0:T(8,128)(2,1)S(1)}, u32[]{:S(2)}, u32[]{:S(2)}) %collective-permute-start.3) | collective-permute-done | bytes 262176 | tf_op jit(solution)/shard_map/ppermute | solution.py:541
  41.4 8.8 %shard_map.79 = (bf16[1024,1024]{1,0:T(8,128)(2,1)}, f32[8,128]{1,0:T(8,128)}) custom-call(bf16[16,32,128]{2,1,0:T(8,128)(2,1)} %copy-done.4, bf16[1728,1024]{1,0:T(8,128)(2,1)} %bitcast.19, bf16[128,1024]{1,0:T(8,128)(2,1)} %copy-done.12, bf16[192,1024]{1,0:T(8,128)(2,1)} %copy-done.11), custom_call_target="tpu_custom_call" | custom-call | flops 3623878656 | bytes 10485760 | tf_op jit(solution)/shard_map/pallas_call | solution.py:180
  50.9 2.0 %shard_map.85 = bf16[512,1024]{1,0:T(8,128)(2,1)} custom-call(bf16[128,1024]{1,0:T(8,128)(2,1)S(1)} %shard_map.77.refs_1_.refs_2_.refs_0_, bf16[192,1024]{1,0:T(8,128)(2,1)S(1)} %shard_map.78.refs_2_.refs_3_.refs_1_, bf16[192,1024]{1,0:T(8,128)(2,1)} %collective-permute-done.8.refs_3_.refs_4_.refs_2_, f32[8,128]{1,0:T(8,128)S(1)} %copy-done.9), custom_call_target="tpu_custom_call" | custom-call | bytes 2097152 | tf_op jit(solution)/shard_map/pallas_call | solution.py:215
  53.0 1.5 %collective-permute-start.13 = (bf16[512,1024]{1,0:T(8,128)(2,1)}, bf16[512,1024]{1,0:T(8,128)(2,1)S(1)}, u32[]{:S(2)}, u32[]{:S(2)}) collective-permute-start(bf16[512,1024]{1,0:T(8,128)(2,1)} %shard_map.85), channel_id=1, source_target_pairs={{0,16},{16,0},{1,17},{17,1},{2,18},{18,2},{3,19},{19,3},{4,20},{20... | collective-permute-start | bytes 3145736 | tf_op jit(solution)/shard_map/ppermute | solution.py:547
  55.0 11.5 %shard_map.80.refs_8_ = bf16[16,32,128]{2,1,0:T(8,128)(2,1)} custom-call(s32[1]{0:T(128)} %bitcast.4.refs_0_, bf16[128,1024]{1,0:T(8,128)(2,1)} %copy-done.3, bf16[192,1024]{1,0:T(8,128)(2,1)} %copy-done.2, bf16[192,1024]{1,0:T(8,128)(2,1)} %collective-permute-done.8.refs_3_.refs_4_.refs_2_, bf16[128,1024]{1,0:T(8,128)(2,1)} %copy-done.12, ...), custom_call_target="tpu_custom_call" | custom-call | flops 3623878656 | bytes 6291456 | tf_op jit(solution)/shard_map/pallas_call | solution.py:301
  66.5 3.5 %all-to-all-start.1 = ((bf16[16,32,128]{2,1,0:T(8,128)(2,1)}), bf16[16,32,128]{2,1,0:T(8,128)(2,1)S(1)}, u32[]{:S(2)}, u32[]{:S(2)}) async-start(bf16[16,32,128]{2,1,0:T(8,128)(2,1)} %shard_map.80.refs_8_), calls=%async_computation.2 | async-start | bytes 262144 | tf_op jit(solution)/shard_map/all_to_all | solution.py:586
  70.1 8.7 %shard_map.81 = (f32[1728,1024]{1,0:T(8,128)}, f32[8,128]{1,0:T(8,128)}) custom-call(s32[1]{0:T(128)} %bitcast.4.refs_0_, bf16[16,32,128]{2,1,0:T(8,128)(2,1)} %copy-done.4, bf16[128,1024]{1,0:T(8,128)(2,1)} %copy-done.3, bf16[192,1024]{1,0:T(8,128)(2,1)} %copy-done.2, bf16[192,1024]{1,0:T(8,128)(2,1)} %collective-permute-done.8.refs_3_.refs_4_.refs_2_, ...), custom_call_target="tpu_custom_call" | custom-call | flops 3623878656 | bytes 12582912 | tf_op jit(solution)/shard_map/pallas_call | solution.py:376
  78.8 2.7 %collective-permute-done.10.refs_1_ = bf16[16,32,128]{2,1,0:T(8,128)(2,1)S(1)} collective-permute-done((bf16[16,32,128]{2,1,0:T(8,128)(2,1)S(1)}, bf16[16,32,128]{2,1,0:T(8,128)(2,1)S(1)}, u32[]{:S(2)}, u32[]{:S(2)}) %collective-permute-start.10) | collective-permute-done | bytes 131104 | tf_op jit(solution)/shard_map/ppermute | solution.py:547
  82.2 2.7 %shard_map.82 = (bf16[256,256]{1,0:T(8,128)(2,1)S(1)}, bf16[32,32,128]{2,1,0:T(8,128)(2,1)S(1)}) custom-call(bf16[16,32,128]{2,1,0:T(8,128)(2,1)S(1)} %all-to-all-done.1.pieces_ref, f32[256,256]{1,0:T(8,128)S(1)} %get-tuple-element.16.refs_3_.slope_ref, bf16[256,3456]{1,0:T(8,128)(2,1)S(1)} %get-tuple-element.19.lhs_ref, f32[8,128]{1,0:T(8,128)S(1)} %copy-done.10, ...), custom_call_target="tpu_custom_call" | custom-call | flops 452984832 | bytes 3145728 | tf_op jit(solution)/shard_map/pallas_call | solution.py:456
  85.6 3.2 %all-to-all-start.2 = ((bf16[32,32,128]{2,1,0:T(8,128)(2,1)}), bf16[32,32,128]{2,1,0:T(8,128)(2,1)S(1)}, u32[]{:S(2)}, u32[]{:S(2)}) async-start(bf16[32,32,128]{2,1,0:T(8,128)(2,1)} %copy-done.6), calls=%async_computation.3 | async-start | bytes 524288 | tf_op jit(solution)/shard_map/all_to_all | solution.py:607
  88.8 12.4 %shard_map.87 = (f32[1728,1024]{1,0:T(8,128)}, f32[8,128]{1,0:T(8,128)S(1)}) custom-call(s32[1]{0:T(128)} %bitcast.4.refs_0_, bf16[16,32,128]{2,1,0:T(8,128)(2,1)S(1)} %collective-permute-done.10.refs_1_, bf16[512,1024]{1,0:T(8,128)(2,1)S(1)} %shard_map.86.refs_2_, ...), custom_call_target="tpu_custom_call", output_to_operand_aliasing={{0}: (4, {})} | custom-call | flops 3623878656 | bytes 12582912 | tf_op jit(solution)/shard_map/pallas_call | solution.py:376
  102.1 5.8 %all-to-all-start.3 = ((bf16[32,32,128]{2,1,0:T(8,128)(2,1)}), bf16[32,32,128]{2,1,0:T(8,128)(2,1)S(1)}, u32[]{:S(2)}, u32[]{:S(2)}) async-start(bf16[32,32,128]{2,1,0:T(8,128)(2,1)} %shard_map.88), calls=%async_computation.4 | async-start | bytes 524288 | tf_op jit(solution)/shard_map/all_to_all | solution.py:613
  107.9 1.3 %collective-permute-start.12 = (bf16[256,256]{1,0:T(8,128)(2,1)S(1)}, bf16[256,256]{1,0:T(8,128)(2,1)S(1)}, u32[]{:S(2)}, u32[]{:S(2)}) collective-permute-start(bf16[256,256]{1,0:T(8,128)(2,1)S(1)} %get-tuple-element.21.own_ref.refs_1_.refs_5_), channel_id=1, source_target_pairs={{1,0},{2,1},{3,2},{4,3},{5,4},{6,5},{7,6},{8,7},{9,8},{10,9},{11,1... | collective-permute-start | bytes 393224 | tf_op jit(solution)/shard_map/ppermute | solution.py:535
  109.2 3.0 %collective-permute-start.11 = (bf16[256,256]{1,0:T(8,128)(2,1)S(1)}, bf16[256,256]{1,0:T(8,128)(2,1)S(1)}, u32[]{:S(2)}, u32[]{:S(2)}) collective-permute-start(bf16[256,256]{1,0:T(8,128)(2,1)S(1)} %get-tuple-element.21.own_ref.refs_1_.refs_5_), channel_id=1, source_target_pairs={{0,1},{1,2},{2,3},{3,4},{4,5},{5,6},{6,7},{7,8},{8,9},{9,10},{10,1... | collective-permute-start | bytes 393224 | tf_op jit(solution)/shard_map/ppermute | solution.py:534
  113.2 1.4 %shard_map.84 = bf16[32,2048]{1,0:T(8,128)(2,1)} custom-call(bf16[256,256]{1,0:T(8,128)(2,1)S(1)} %collective-permute-done.11.before_ref, bf16[256,256]{1,0:T(8,128)(2,1)S(1)} %get-tuple-element.21.own_ref.refs_1_.refs_5_, bf16[256,256]{1,0:T(8,128)(2,1)S(1)} %collective-permute-done.12.after_ref, bf16[3456,256]{1,0:T(8,128)(2,1)S(1)} %shard_map.83.w_ref), custom_call_target="tpu_custom_call" | custom-call | flops 452984832 | bytes 3145728 | tf_op jit(solution)/shard_map/pallas_call | solution.py:484
  114.6 3.6 %all-to-all-done.3.packed_ref = bf16[32,32,128]{2,1,0:T(8,128)(2,1)S(1)} async-done(((bf16[32,32,128]{2,1,0:T(8,128)(2,1)}), bf16[32,32,128]{2,1,0:T(8,128)(2,1)S(1)}, u32[]{:S(2)}, u32[]{:S(2)}) %all-to-all-start.3) | async-done | bytes 262176 | tf_op jit(solution)/shard_map/all_to_all | solution.py:613
  118.2 1.3 %shard_map.89 = f32[27,64,64]{2,1,0:T(8,128)} custom-call(bf16[32,32,128]{2,1,0:T(8,128)(2,1)S(1)} %all-to-all-done.3.packed_ref), custom_call_target="tpu_custom_call" | custom-call | bytes 1048576 | tf_op jit(solution)/shard_map/pallas_call | solution.py:522
  (60 shorter events, 8.2 us)
Async XLA Ops:
  7.2 11.9 %collective-permute-start.1 = (bf16[32,2048]{1,0:T(8,128)(2,1)}, bf16[32,2048]{1,0:T(8,128)(2,1)S(1)}, u32[]{:S(2)}, u32[]{:S(2)}) collective-permute-start(bf16[32,2048]{1,0:T(8,128)(2,1)} %bitcast.10), channel_id=1, source_target_pairs={{1,0},{2,1},{3,2},{4,3},{5,4},{6,5},{7,6},{8,7},{9,8},{10,9},{11,1... | collective-permute-start | bytes 393224 | tf_op jit(solution)/shard_map/ppermute | solution.py:535
  8.5 12.4 %collective-permute-start = (bf16[32,2048]{1,0:T(8,128)(2,1)}, bf16[32,2048]{1,0:T(8,128)(2,1)S(1)}, u32[]{:S(2)}, u32[]{:S(2)}) collective-permute-start(bf16[32,2048]{1,0:T(8,128)(2,1)} %bitcast.11), channel_id=1, source_target_pairs={{0,1},{1,2},{2,3},{3,4},{4,5},{5,6},{6,7},{7,8},{8,9},{9,10},{10,1... | collective-permute-start | bytes 393224 | tf_op jit(solution)/shard_map/ppermute | solution.py:534
  11.5 19.7 %collective-permute-start.6 = (bf16[64,1024]{1,0:T(8,128)(2,1)}, bf16[64,1024]{1,0:T(8,128)(2,1)S(1)}, u32[]{:S(2)}, u32[]{:S(2)}) collective-permute-start(bf16[64,1024]{1,0:T(8,128)(2,1)} %bitcast.13), channel_id=1, source_target_pairs={{0,12},{1,13},{2,14},{3,15},{4,8},{5,9},{6,10},{7,11},{8,4},{9,5},... | collective-permute-start | bytes 393224 | tf_op jit(solution)/shard_map/ppermute | solution.py:541
  17.0 14.3 %collective-permute-start.5 = (bf16[64,1024]{1,0:T(8,128)(2,1)}, bf16[64,1024]{1,0:T(8,128)(2,1)S(1)}, u32[]{:S(2)}, u32[]{:S(2)}) collective-permute-start(bf16[64,1024]{1,0:T(8,128)(2,1)} %bitcast.14), channel_id=1, source_target_pairs={{0,8},{1,9},{2,10},{3,11},{4,12},{5,13},{6,14},{7,15},{8,0},{9,1},... | collective-permute-start | bytes 393224 | tf_op jit(solution)/shard_map/ppermute | solution.py:541
  17.0 14.3 %collective-permute-start.4 = (bf16[64,1024]{1,0:T(8,128)(2,1)}, bf16[64,1024]{1,0:T(8,128)(2,1)S(1)}, u32[]{:S(2)}, u32[]{:S(2)}) collective-permute-start(bf16[64,1024]{1,0:T(8,128)(2,1)} %bitcast.15), channel_id=1, source_target_pairs={{0,4},{1,5},{2,6},{3,7},{4,0},{5,1},{6,2},{7,3},{8,12},{9,13},{10,... | collective-permute-start | bytes 393224 | tf_op jit(solution)/shard_map/ppermute | solution.py:541
  19.5 11.7 %collective-permute-start.2 = (bf16[64,1024]{1,0:T(8,128)(2,1)S(1)}, bf16[64,1024]{1,0:T(8,128)(2,1)S(1)}, u32[]{:S(2)}, u32[]{:S(2)}) collective-permute-start(bf16[64,1024]{1,0:T(8,128)(2,1)S(1)} %bitcast.16), channel_id=1, source_target_pairs={{0,2},{1,3},{2,0},{3,1},{4,6},{5,7},{6,4},{7,5},{8,10},{9,11},{10,... | collective-permute-start | bytes 393224 | tf_op jit(solution)/shard_map/ppermute | solution.py:541
  22.6 16.6 %all-to-all-start = ((bf16[16,32,128]{2,1,0:T(8,128)(2,1)}), bf16[16,32,128]{2,1,0:T(8,128)(2,1)S(1)}, u32[]{:S(2)}, u32[]{:S(2)}) async-start(bf16[16,32,128]{2,1,0:T(8,128)(2,1)} %get-tuple-element.15), calls=%async_computation | async-start | bytes 262144 | tf_op jit(solution)/shard_map/all_to_all | solution.py:571
  31.2 88.3 %reduce-scatter.2.cloned.1.call-start = ((), (), s32[]{:S(2)}) async-start(), calls=%async_computation.5 | async-start | bytes 2228224 | tf_op jit(solution)/shard_map/reduce_scatter | solution.py:582
  31.3 19.6 %copy-start.2 = (bf16[192,1024]{1,0:T(8,128)(2,1)}, bf16[192,1024]{1,0:T(8,128)(2,1)S(1)}, u32[]{:S(2)}) copy-start(bf16[192,1024]{1,0:T(8,128)(2,1)S(1)} %shard_map.78.refs_2_.refs_3_.refs_1_) | copy-start | bytes 1179652
  31.3 8.0 %collective-permute-start.7 = (bf16[192,1024]{1,0:T(8,128)(2,1)S(1)}, bf16[192,1024]{1,0:T(8,128)(2,1)S(1)}, u32[]{:S(2)}, u32[]{:S(2)}) collective-permute-start(bf16[192,1024]{1,0:T(8,128)(2,1)S(1)} %shard_map.78.refs_2_.refs_3_.refs_1_), channel_id=1, source_target_pairs={{0,1},{1,0},{2,3},{3,2},{4,5},{5,4},{6,7},{7,6},{8,9},{9,8},{10,11... | collective-permute-start | bytes 1179656 | tf_op jit(solution)/shard_map/ppermute | solution.py:541
  39.1 11.7 %copy-start.3 = (bf16[128,1024]{1,0:T(8,128)(2,1)}, bf16[128,1024]{1,0:T(8,128)(2,1)S(1)}, u32[]{:S(2)}) copy-start(bf16[128,1024]{1,0:T(8,128)(2,1)S(1)} %shard_map.77.refs_1_.refs_2_.refs_0_) | copy-start | bytes 786436
  39.1 1.6 %collective-permute-start.3 = (bf16[128,1024]{1,0:T(8,128)(2,1)S(1)}, bf16[128,1024]{1,0:T(8,128)(2,1)S(1)}, u32[]{:S(2)}, u32[]{:S(2)}) collective-permute-start(bf16[128,1024]{1,0:T(8,128)(2,1)S(1)} %shard_map.77.refs_1_.refs_2_.refs_0_), channel_id=1, source_target_pairs={{0,1},{1,0},{2,3},{3,2},{4,5},{5,4},{6,7},{7,6},{8,9},{9,8},{10,11... | collective-permute-start | bytes 786440 | tf_op jit(solution)/shard_map/ppermute | solution.py:541
  39.2 11.6 %collective-permute-start.8 = (bf16[192,1024]{1,0:T(8,128)(2,1)S(1)}, bf16[192,1024]{1,0:T(8,128)(2,1)}, u32[]{:S(2)}, u32[]{:S(2)}) collective-permute-start(bf16[192,1024]{1,0:T(8,128)(2,1)S(1)} %shard_map.78.refs_2_.refs_3_.refs_1_), channel_id=1, source_target_pairs={{0,2},{1,3},{2,0},{3,1},{4,6},{5,7},{6,4},{7,5},{8,10},{9,11},{10,... | collective-permute-start | bytes 1179656 | tf_op jit(solution)/shard_map/ppermute | solution.py:541
  50.2 4.2 %copy-start.5 = (bf16[16,32,128]{2,1,0:T(8,128)(2,1)S(1)}, bf16[16,32,128]{2,1,0:T(8,128)(2,1)}, u32[]{:S(2)}) copy-start(bf16[16,32,128]{2,1,0:T(8,128)(2,1)} %copy-done.4) | copy-start | bytes 393220
  50.9 4.1 %collective-permute-start.9 = (bf16[192,1024]{1,0:T(8,128)(2,1)}, bf16[192,1024]{1,0:T(8,128)(2,1)}, u32[]{:S(2)}, u32[]{:S(2)}) collective-permute-start(bf16[192,1024]{1,0:T(8,128)(2,1)} %collective-permute-done.8.refs_3_.refs_4_.refs_2_), channel_id=1, source_target_pairs={{0,1},{1,0},{2,3},{3,2},{4,5},{5,4},{6,7},{7,6},{8,9},{9,8},{10,11... | collective-permute-start | bytes 1179656 | tf_op jit(solution)/shard_map/ppermute | solution.py:541
  53.0 32.0 %collective-permute-start.13 = (bf16[512,1024]{1,0:T(8,128)(2,1)}, bf16[512,1024]{1,0:T(8,128)(2,1)S(1)}, u32[]{:S(2)}, u32[]{:S(2)}) collective-permute-start(bf16[512,1024]{1,0:T(8,128)(2,1)} %shard_map.85), channel_id=1, source_target_pairs={{0,16},{16,0},{1,17},{17,1},{2,18},{18,2},{3,19},{19,3},{4,20},{20... | collective-permute-start | bytes 3145736 | tf_op jit(solution)/shard_map/ppermute | solution.py:547
  54.5 27.1 %collective-permute-start.10 = (bf16[16,32,128]{2,1,0:T(8,128)(2,1)S(1)}, bf16[16,32,128]{2,1,0:T(8,128)(2,1)S(1)}, u32[]{:S(2)}, u32[]{:S(2)}) collective-permute-start(bf16[16,32,128]{2,1,0:T(8,128)(2,1)S(1)} %copy-done.5), channel_id=1, source_target_pairs={{0,16},{16,0},{1,17},{17,1},{2,18},{18,2},{3,19},{19,3},{4,20},{20... | collective-permute-start | bytes 393224 | tf_op jit(solution)/shard_map/ppermute | solution.py:547
  66.5 15.0 %all-to-all-start.1 = ((bf16[16,32,128]{2,1,0:T(8,128)(2,1)}), bf16[16,32,128]{2,1,0:T(8,128)(2,1)S(1)}, u32[]{:S(2)}, u32[]{:S(2)}) async-start(bf16[16,32,128]{2,1,0:T(8,128)(2,1)} %shard_map.80.refs_8_), calls=%async_computation.2 | async-start | bytes 262144 | tf_op jit(solution)/shard_map/all_to_all | solution.py:586
  84.9 3.9 %collective-permute-start.14 = (bf16[512,1024]{1,0:T(8,128)(2,1)S(1)}, bf16[512,1024]{1,0:T(8,128)(2,1)S(1)}, u32[]{:S(2)}, u32[]{:S(2)}) collective-permute-start(bf16[512,1024]{1,0:T(8,128)(2,1)S(1)} %shard_map.86.refs_2_), channel_id=1, source_target_pairs={{0,1},{1,0},{2,3},{3,2},{4,5},{5,4},{6,7},{7,6},{8,9},{9,8},{10,11... | collective-permute-start | bytes 3145736 | tf_op jit(solution)/shard_map/ppermute | solution.py:541
  85.6 15.7 %all-to-all-start.2 = ((bf16[32,32,128]{2,1,0:T(8,128)(2,1)}), bf16[32,32,128]{2,1,0:T(8,128)(2,1)S(1)}, u32[]{:S(2)}, u32[]{:S(2)}) async-start(bf16[32,32,128]{2,1,0:T(8,128)(2,1)} %copy-done.6), calls=%async_computation.3 | async-start | bytes 524288 | tf_op jit(solution)/shard_map/all_to_all | solution.py:607
  88.8 23.4 %copy-start.1 = (bf16[27,64,64]{2,1,0:T(8,128)(2,1)S(1)}, bf16[27,64,64]{2,1,0:T(8,128)(2,1)}, u32[]{:S(2)}) copy-start(bf16[27,64,64]{2,1,0:T(8,128)(2,1)} %w_ref.1) | copy-start | bytes 663556
  102.1 16.1 %all-to-all-start.3 = ((bf16[32,32,128]{2,1,0:T(8,128)(2,1)}), bf16[32,32,128]{2,1,0:T(8,128)(2,1)S(1)}, u32[]{:S(2)}, u32[]{:S(2)}) async-start(bf16[32,32,128]{2,1,0:T(8,128)(2,1)} %shard_map.88), calls=%async_computation.4 | async-start | bytes 524288 | tf_op jit(solution)/shard_map/all_to_all | solution.py:613
  107.9 5.0 %collective-permute-start.12 = (bf16[256,256]{1,0:T(8,128)(2,1)S(1)}, bf16[256,256]{1,0:T(8,128)(2,1)S(1)}, u32[]{:S(2)}, u32[]{:S(2)}) collective-permute-start(bf16[256,256]{1,0:T(8,128)(2,1)S(1)} %get-tuple-element.21.own_ref.refs_1_.refs_5_), channel_id=1, source_target_pairs={{1,0},{2,1},{3,2},{4,3},{5,4},{6,5},{7,6},{8,7},{9,8},{10,9},{11,1... | collective-permute-start | bytes 393224 | tf_op jit(solution)/shard_map/ppermute | solution.py:535
  109.2 4.0 %collective-permute-start.11 = (bf16[256,256]{1,0:T(8,128)(2,1)S(1)}, bf16[256,256]{1,0:T(8,128)(2,1)S(1)}, u32[]{:S(2)}, u32[]{:S(2)}) collective-permute-start(bf16[256,256]{1,0:T(8,128)(2,1)S(1)} %get-tuple-element.21.own_ref.refs_1_.refs_5_), channel_id=1, source_target_pairs={{0,1},{1,2},{2,3},{3,4},{4,5},{5,6},{6,7},{7,8},{8,9},{9,10},{10,1... | collective-permute-start | bytes 393224 | tf_op jit(solution)/shard_map/ppermute | solution.py:534
  (9 other events, 10.0 us)
Sparse Core Ops, SparseCore 0:
  50.4 59.5 reduce-scatter.1
